TPU v7x, 32 devices: a whole 2x2x4 slice. The times are simulated.
32 devices in a mesh: groups: 2 (over y), row: 4 (over x, core), col: 4 (over z).
Axes of the slice: x: 2, y: 2, z: 4, core: 2. Of those that a mesh axis runs over, the one named last changes fastest.
Arguments:
- right_sides: float32 [32, 16384], P(None, ('groups', 'row')), parts along dimension 1
- nugget: float32 [16384], P(('groups', 'row')), parts along dimension 0, may hold values from 1 to 4
- cov_blocks: bfloat16 [8, 4, 32, 256, 256], P(('groups', 'row'), 'col'), parts along dimension 0
- block_rows: int32 [8, 4, 32], P(('groups', 'row'), 'col'), parts along dimension 0, may hold values from 0 to 7, as said below
- block_cols: int32 [8, 4, 32], P(('groups', 'row'), 'col'), parts along dimension 0, may hold values from 0 to 7, as said below
- block_count: int32 [8, 4], P(('groups', 'row'), 'col'), parts along dimension 0, may hold values from 4 to 32, as said below
Outputs:
- solution: float32 [32, 16384], P(None, ('groups', 'row')), parts along dimension 1
- residual: float32 [32, 16384], P(None, ('groups', 'row')), parts along dimension 1
There are 2 independent parts, one for each index of `groups`. A program takes and returns all parts, laid end to end along the dimension named above; each array names one. Nothing has to cross between parts.
Inputs may be any that keep to these rules, and one draw needn't show every extreme that they name: On each device the pairs (block_rows, block_cols) of all 32 slots are distinct; no stored block position of a problem is the mirror image of another (no pair is stored both as (g, h) and as (h, g)); on devices whose row and col index are equal, block_rows <= block_cols. `block_cols`: see block_rows. `block_count`: slots at or beyond the count are empty; some device of every problem has exactly 32 live slots.
All inputs are finite; a program needn't handle non-finite values.
Results may differ from a plain program's by a relative error of at most 0.0003.
Values sent between devices are 32-bit elements; how exact they have to be, the bound alone decides.
No kernel may reach another device: no remote copies, remote signals or barrier semaphores. Data moves between devices by JAX's collectives and lax.ppermute only.
A program may use at most 64 MiB of HBM per device.

v0:
```python
import jax
import jax.numpy as jnp
from jax import lax
from jax.sharding import PartitionSpec as P

ITERS = 2


def from_root(value, axis, source):
    kept = jnp.where(lax.axis_index(axis) == source, value, 0).astype(value.dtype)
    return lax.psum(kept, axis)


def on_device(right_sides, nugget, cov_blocks, block_rows, block_cols, block_count):
    blocks = cov_blocks[0, 0].astype(jnp.float32)
    slot_rows = block_rows[0, 0]
    slot_cols = block_cols[0, 0]
    live_count = block_count[0, 0]
    slot_total = blocks.shape[0]
    tile_size = blocks.shape[1]
    series, row_width = right_sides.shape
    tile_count = row_width // tile_size
    live_mask = (jnp.arange(slot_total, dtype=jnp.int32) < live_count).astype(jnp.float32)
    block_ids = jnp.arange(tile_count, dtype=jnp.int32)[:, None]
    row_selector = (slot_rows[None, :] == block_ids).astype(jnp.float32) * live_mask[None, :]
    col_selector = (slot_cols[None, :] == block_ids).astype(jnp.float32) * live_mask[None, :]

    def spread(selector, values):
        placed = jnp.einsum("bm,rmj->rbj", selector, values, precision=lax.Precision.HIGHEST)
        return placed.reshape(series, row_width)

    solution = jnp.zeros_like(right_sides)
    residual = right_sides
    direction = right_sides
    norm_now = lax.psum(jnp.sum(residual * residual, axis=1), "row")
    for turn_index in range(ITERS):
        far_rows = from_root(direction, "row", lax.axis_index("col"))
        near_tiles = direction.reshape(series, tile_count, tile_size)
        far_tiles = far_rows.reshape(series, tile_count, tile_size)
        local_direct = jnp.einsum(
            "rmk,mjk->rmj",
            jnp.take(far_tiles, slot_cols, axis=1),
            blocks,
            precision=lax.Precision.HIGHEST,
        )
        local_mirror = jnp.einsum(
            "rmj,mjk->rmk",
            jnp.take(near_tiles, slot_rows, axis=1),
            blocks,
            precision=lax.Precision.HIGHEST,
        )
        apply_direct = spread(row_selector, local_direct)
        apply_mirror = spread(col_selector, local_mirror)
        total = lax.psum(apply_direct, "col")
        summed = lax.psum(apply_mirror, "row")
        total = total + from_root(summed, "col", lax.axis_index("row"))
        applied = nugget[None, :] * direction + total
        curvature, crossed, squared = lax.psum(
            (
                jnp.sum(direction * applied, axis=1),
                jnp.sum(residual * applied, axis=1),
                jnp.sum(applied * applied, axis=1),
            ),
            "row",
        )
        step_size = norm_now / curvature
        solution = solution + step_size[:, None] * direction
        residual = residual - step_size[:, None] * applied
        norm_next = norm_now - 2.0 * step_size * crossed + step_size * step_size * squared
        direction = residual + (norm_next / norm_now)[:, None] * direction
        norm_now = norm_next
    return (solution, residual)


def solution(mesh):
    placed = (
        P(None, ("groups", "row")),
        P(("groups", "row")),
        P(("groups", "row"), "col", None, None, None),
        P(("groups", "row"), "col", None),
        P(("groups", "row"), "col", None),
        P(("groups", "row"), "col"),
    )
    return jax.shard_map(
        on_device,
        mesh=mesh,
        in_specs=placed,
        out_specs=(P(None, ("groups", "row")), P(None, ("groups", "row"))),
        check_vma=False,
    )
```

profile of v0, /device:TPU:0, one launch (start us, length us, event | category | flops | bytes accessed | tf_op | source)
XLA Modules:
  0.0 209.5 jit_solution(2557300919919235164)
XLA Ops:
  9.2 1.0 copy.38
  10.2 1.0 broadcast_select_fusion.1
  12.5 4.4 %fusion.11 = f32[32,32,256]{2,0,1:T(8,128)S(1)} fusion(bf16[1,1,32,256,256]{4,3,2,1,0:T(8,128)(2,1)} %param.10, f32[32,32,256]{2,1,0:T(8,128)S(1)} %gather_fusion.1, pred[32]{0:T(512)(128)(4,1)S(1)} %compare_and_fusion), kind=kOutput, calls=%fused_computation.13 | convolution fusion | flops 805568512 | bytes 6291488 | tf_op jit(solution)/shard_map/rmj,mjk->rmk/dot_general | solution.py:46
  16.9 1.2 fusion.28
  18.2 0.8 copy.21
  19.1 35.4 %all-reduce.14.cloned.1.call-done = (f32[32,8,256]{2,0,1:T(8,128)}, f32[32,2048]{1,0:T(8,128)}) async-done(((f32[32,8,256]{2,0,1:T(8,128)}, f32[32,2048]{1,0:T(8,128)}), (f32[32,8,256]{2,0,1:T(8,128)}, f32[32,2048]{1,0:T(8,128)})) %all-reduce.14.cloned.1.call-update) | async-done | bytes 524304 | tf_op jit(solution)/shard_map/psum | solution.py:11
  54.5 1.6 gather_fusion
  56.1 6.0 %fusion.8 = f32[32,32,256]{2,0,1:T(8,128)S(1)} fusion(bf16[1,1,32,256,256]{4,3,2,1,0:T(8,128)(2,1)} %param.10, f32[32,32,256]{2,1,0:T(8,128)S(1)} %gather_fusion, pred[32]{0:T(512)(128)(4,1)S(1)} %compare_and_fusion.1), kind=kOutput, calls=%fused_computation.12 | convolution fusion | flops 805568512 | bytes 6291488 | tf_op jit(solution)/shard_map/rmk,mjk->rmj/dot_general | solution.py:40
  62.1 1.2 fusion.30
  64.3 35.6 %all-reduce.8.cloned.1.call-done = f32[32,2048]{1,0:T(8,128)} async-done(((f32[32,2048]{1,0:T(8,128)}), f32[32,2048]{1,0:T(8,128)}) %all-reduce.8.cloned.1.call-update) | async-done | bytes 262160 | tf_op jit(solution)/shard_map/psum | solution.py:54
  99.9 1.2 multiply_reduce_fusion.2
  101.0 5.7 %all-reduce = (f32[32]{0:T(128)S(1)}, f32[32]{0:T(128)S(1)}, f32[32]{0:T(128)S(1)}) all-reduce(f32[32]{0:T(128)S(1)} %get-tuple-element.4, f32[32]{0:T(128)S(1)} %get-tuple-element.5, f32[32]{0:T(128)S(1)} %get-tuple-element.3), channel_id=1, replica_groups=mesh['groups'=2,'row'=4,'col'=4] {'row'}, use_global_device_ids=true, to_apply=%region_9.11 | all-reduce | flops 96 | bytes 768 | tf_op jit(solution)/shard_map/psum | solution.py:58
  106.7 1.1 broadcast_select_fusion
  109.2 4.4 %fusion.17 = f32[32,32,256]{2,0,1:T(8,128)S(1)} fusion(bf16[1,1,32,256,256]{4,3,2,1,0:T(8,128)(2,1)} %param.10, f32[32,32,256]{2,1,0:T(8,128)S(1)} %gather_fusion.3, pred[32]{0:T(512)(128)(4,1)S(1)} %compare_and_fusion), kind=kOutput, calls=%fused_computation.15 | convolution fusion | flops 805568512 | bytes 6291488 | tf_op jit(solution)/shard_map/rmj,mjk->rmk/dot_general | solution.py:46
  113.5 1.2 fusion.24
  114.8 0.8 copy.23
  115.8 33.1 %all-reduce.12.cloned.1.call-done = (f32[32,8,256]{2,0,1:T(8,128)}, f32[32,2048]{1,0:T(8,128)}) async-done(((f32[32,8,256]{2,0,1:T(8,128)}, f32[32,2048]{1,0:T(8,128)}), (f32[32,8,256]{2,0,1:T(8,128)}, f32[32,2048]{1,0:T(8,128)})) %all-reduce.12.cloned.1.call-update) | async-done | bytes 524304 | tf_op jit(solution)/shard_map/psum | solution.py:11
  149.0 1.6 gather_fusion.2
  150.5 6.0 %fusion.14 = f32[32,32,256]{2,0,1:T(8,128)S(1)} fusion(bf16[1,1,32,256,256]{4,3,2,1,0:T(8,128)(2,1)} %param.10, f32[32,32,256]{2,1,0:T(8,128)S(1)} %gather_fusion.2, pred[32]{0:T(512)(128)(4,1)S(1)} %compare_and_fusion.1), kind=kOutput, calls=%fused_computation.14 | convolution fusion | flops 805568512 | bytes 6291488 | tf_op jit(solution)/shard_map/rmk,mjk->rmj/dot_general | solution.py:40
  156.5 1.2 fusion.26
  158.7 35.7 %all-reduce.10.cloned.1.call-done = f32[32,2048]{1,0:T(8,128)} async-done(((f32[32,2048]{1,0:T(8,128)}), f32[32,2048]{1,0:T(8,128)}) %all-reduce.10.cloned.1.call-update) | async-done | bytes 262160 | tf_op jit(solution)/shard_map/psum | solution.py:54
  194.3 1.1 multiply_reduce_fusion
  195.4 5.7 %psum.98 = f32[32]{0:T(128)S(1)} all-reduce(f32[32]{0:T(128)S(1)} %multiply_reduce_fusion), channel_id=1, replica_groups=mesh['groups'=2,'row'=4,'col'=4] {'row'}, use_global_device_ids=true, to_apply=%region_15.17 | all-reduce | flops 32 | bytes 256 | tf_op jit(solution)/shard_map/psum | solution.py:58
  201.1 1.9 multiply_subtract_fusion
  (40 shorter events, 6.2 us)
Async XLA Ops:
  7.2 47.3 %all-reduce.14.cloned.1.call-start = ((), (), s32[]{:S(2)}) async-start(), calls=%async_computation.3 | async-start | bytes 1048576 | tf_op jit(solution)/shard_map/psum | solution.py:11
  11.9 5.0 %copy-start.5 = (s32[1,1,32]{2,1,0:T(1,128)S(1)}, s32[1,1,32]{2,1,0:T(1,128)}, u32[]{:S(2)}) copy-start(s32[1,1,32]{2,1,0:T(1,128)} %param.12) | copy-start | bytes 388
  19.0 80.9 %all-reduce.8.cloned.1.call-start = ((), (), s32[]{:S(2)}) async-start(), calls=%async_computation | async-start | bytes 524288 | tf_op jit(solution)/shard_map/psum | solution.py:54
  54.5 7.6 %copy-start.6 = (s32[1,1,32]{2,1,0:T(1,128)S(1)}, s32[1,1,32]{2,1,0:T(1,128)}, u32[]{:S(2)}) copy-start(s32[1,1,32]{2,1,0:T(1,128)} %param.11) | copy-start | bytes 388
  56.1 7.4 %copy-start.2 = (f32[32,2048]{1,0:T(8,128)S(1)}, f32[32,2048]{1,0:T(8,128)}, u32[]{:S(2)}) copy-start(f32[32,2048]{1,0:T(8,128)} %get-tuple-element.12) | copy-start | bytes 786436
  56.1 43.8 %copy-start = (f32[32,2048]{1,0:T(8,128)S(1)}, f32[32,2048]{1,0:T(8,128)}, u32[]{:S(2)}) copy-start(f32[32,2048]{1,0:T(8,128)} %param.8) | copy-start | bytes 786436
  56.1 43.8 %copy-start.4 = (f32[2048]{0:T(1024)S(1)}, f32[2048]{0:T(1024)}, u32[]{:S(2)}) copy-start(f32[2048]{0:T(1024)} %param.9) | copy-start | bytes 24580
  64.2 84.7 %all-reduce.12.cloned.1.call-start = ((), (), s32[]{:S(2)}) async-start(), calls=%async_computation.2 | async-start | bytes 1048576 | tf_op jit(solution)/shard_map/psum | solution.py:11
  115.6 78.7 %all-reduce.10.cloned.1.call-start = ((), (), s32[]{:S(2)}) async-start(), calls=%async_computation.1 | async-start | bytes 524288 | tf_op jit(solution)/shard_map/psum | solution.py:54
  150.5 7.4 %copy-start.3 = (f32[32,2048]{1,0:T(8,128)S(1)}, f32[32,2048]{1,0:T(8,128)}, u32[]{:S(2)}) copy-start(f32[32,2048]{1,0:T(8,128)} %get-tuple-element.10) | copy-start | bytes 786436
  150.5 50.5 %copy-start.1 = (f32[32,2048]{1,0:T(8,128)S(1)}, f32[32,2048]{1,0:T(8,128)}, u32[]{:S(2)}) copy-start(f32[32,2048]{1,0:T(8,128)} %all-reduce.8.cloned.1.call-done) | copy-start | bytes 786436
Sparse Core Ops, SparseCore 0:
  19.1 35.3 all-reduce.13
  64.3 35.4 all-reduce.7
  115.7 33.1 all-reduce.11
  158.8 35.4 all-reduce.9
where the time goes:
time: 210 us; the launch traced here: 209 us
  waiting for transfers between devices  140 us (67%)
  matrix products  25.7 us (12%)
  between operations  14.7 us (7%)
  blocking collectives  11.3 us (5%)
  other arithmetic  9.03 us (4%)
  local copies, waits for them, and re-layouts  8.58 us (4%)
    psum x2, waiting for transfers between devices, on_device(): total = lax.psum(apply_direct, 'col')  71.3 us
    psum x2, waiting for transfers between devices, from_root(): return lax.psum(kept, axis)  68.6 us
    dot_general x2, matrix products, on_device(): jnp.einsum('rmk,mjk->rmj', jnp.take(far_tiles, slot_cols, axis=1), blocks...  12 us
    psum x2, blocking collectives, on_device(): lax.psum((jnp.sum(direction * applied, axis=1), jnp.sum(residual * applie...  11.3 us
    dot_general x2, matrix products, on_device(): jnp.einsum('rmj,mjk->rmk', jnp.take(near_tiles, slot_rows, axis=1), block...  8.74 us
    dot_general x4, matrix products, spread(): jnp.einsum('bm,rmj->rbj', selector, values, precision=lax.Precision.HIGHEST)  4.95 us
  transfers between devices with their start and end apart: 4, of which 4 were waited for; matrix products, arithmetic and copies ran while one was open for 0% of the time, Pallas kernels for 0%

commit v1 on v0

v1 whole, which is shorter than its diff:
```python
import functools

import jax
import jax.numpy as jnp
from jax import lax
from jax.experimental import pallas as pl
from jax.experimental.pallas import tpu as pltpu
from jax.sharding import PartitionSpec as P

ITERS = 2
LANES = 128
GROUP = 8
BF16 = jnp.bfloat16
F32 = jnp.float32


def send_to(i, d, n):
    return i ^ d if n & (n - 1) == 0 else (i + d) % n


def shifted(value, axis, d, n):
    return lax.ppermute(value, axis, [(i, send_to(i, d, n)) for i in range(n)])


def transposed(value, n):
    pairs = [(r * n + c, c * n + r) for r in range(n) for c in range(n)]
    return lax.ppermute(value, ("row", "col"), pairs)


def load_pair(dst, tile, value):
    rhs = value.shape[0]
    high = value.astype(BF16)
    dst[tile, :rhs, :] = high
    dst[tile, rhs:, :] = (value - high.astype(F32)).astype(BF16)


def product(pair, block, contract):
    both = lax.dot_general(pair, block, (((1,), (contract,)), ((), ())), preferred_element_type=F32)
    rhs = both.shape[0] // 2
    return both[:rhs] + both[rhs:]


def pack_stats(columns, rhs):
    lane = lax.broadcasted_iota(jnp.int32, (8, LANES), 1)
    tile = jnp.zeros((8, LANES), F32)
    groups = rhs // 8
    for i, column in enumerate(columns):
        for g in range(groups):
            tile = jnp.where(lane == i * groups + g, column[g * 8:(g + 1) * 8], tile)
    return tile


def unpack_stat(tile, i, rhs):
    groups = rhs // 8
    return jnp.concatenate([tile[:, i * groups + g:i * groups + g + 1] for g in range(groups)], axis=0)


def accumulate(total, tile, value):
    width = value.shape[1] // LANES
    for part in range(width):
        total[tile * width + part] += value[:, part * LANES:(part + 1) * LANES]


def add_blocks(blocks, step, slot_of, live, pairs, total, read_index, write_index, contract):
    values = []
    for g in range(GROUP):
        slot = step * GROUP + g
        value = product(pairs[read_index[0, 0, slot]], blocks[g], contract)
        values.append((write_index[0, 0, slot], jnp.where(slot < live, value, 0.0)))
    for tile, value in values:
        accumulate(total, tile, value)


def write_chunks(outs, total, me, n, per, rhs):
    for d, out in enumerate(outs):
        first = send_to(me, d, n) * per
        for i in range(per):
            out[i * rhs:(i + 1) * rhs, :] = total[first + i]


def row_sums(value):
    return jnp.sum(value, axis=1, keepdims=True)


def first_kernel(n, per, mirror, slot_rows, slot_cols, live_ref, right, *rest):
    if mirror:
        blocks, (outs, (pairs, total)) = rest[0], (rest[1:1 + n], rest[1 + n:])
    else:
        near, nugget, blocks = rest[:3]
        outs, (pairs, total) = rest[3:3 + n], rest[3 + n:]
    step = pl.program_id(0)
    rhs = right.shape[0]
    tile_size = blocks.shape[1]
    tiles = right.shape[1] // tile_size

    @pl.when(step == 0)
    def _():
        total[...] = jnp.zeros_like(total)
        for tile in range(tiles):
            load_pair(pairs, tile, right[:, tile * tile_size:(tile + 1) * tile_size])

    live = live_ref[0, 0]

    @pl.when(step * GROUP < live)
    def _():
        if mirror:
            add_blocks(blocks, step, None, live, pairs, total, slot_rows, slot_cols, 0)
        else:
            add_blocks(blocks, step, None, live, pairs, total, slot_cols, slot_rows, 1)

    @pl.when(step == pl.num_programs(0) - 1)
    def _():
        data = per * rhs
        if mirror:
            write_chunks(outs, total, lax.axis_index("row"), n, per, rhs)
            value = right[...]
            stats = [row_sums(value * value)]
            tile = pack_stats(stats, rhs)
            for out in outs:
                out[data:, :] = tile
        else:
            write_chunks(outs, total, lax.axis_index("col"), n, per, rhs)
            value = near[...]
            cross = jnp.zeros((rhs, LANES), F32)
            for i in range(total.shape[0]):
                cross += total[i] * value[:, i * LANES:(i + 1) * LANES]
            cross = 2.0 * row_sums(cross)
            own = row_sums(value * value * nugget[...])
            tile = pack_stats([cross], rhs)
            outs[0][data:, :] = pack_stats([cross + own], rhs)
            for out in outs[1:]:
                out[data:, :] = tile


def add_all(refs):
    value = refs[0][...]
    for ref in refs[1:]:
        value += ref[...]
    return value


def sum_first_kernel(n, per, right, nugget, *refs):
    direct, mirror, out = refs[:n], refs[n:2 * n], refs[2 * n]
    rhs = right.shape[0]
    width = per * LANES
    size = direct[0].shape[0]
    out[:size, :] = add_all(direct)
    out[size:, :] = add_all(mirror)
    me = lax.axis_index("col")
    for k in range(n):
        @pl.when(me == k)
        def _():
            for i in range(per):
                lanes = slice(k * width + i * LANES, k * width + (i + 1) * LANES)
                out[i * rhs:(i + 1) * rhs, :] += right[:, lanes] * nugget[:, lanes]


def combine_first_kernel(data, mine, other, near, far, base):
    size = mine.shape[0] // 2
    near[...] = mine[:data, :] + other[size:size + data, :]
    far[:data, :] = other[:data, :] + mine[size:size + data, :]
    far[data:, :] = mine[data:size, :]
    base[...] = mine[size + data:, :]


def scatter_chunks(refs, me, n, per, rhs, total):
    for d in range(n):
        first = send_to(me, d, n) * per
        for i in range(per):
            total[first + i] = refs[d][i * rhs:(i + 1) * rhs, :]


def second_kernel(n, per, slot_rows, slot_cols, live_ref, near, far, nugget, base, *rest):
    near_parts, far_parts, blocks = rest[:n], rest[n:2 * n], rest[2 * n]
    direct, mirror = rest[2 * n + 1:3 * n + 1], rest[3 * n + 1:4 * n + 1]
    left, curve, near_pairs, far_pairs, direct_total, mirror_total = rest[4 * n + 1:]
    step = pl.program_id(0)
    rhs = near.shape[0]
    data = per * rhs
    tile_size = blocks.shape[1]
    width = tile_size // LANES
    tiles = near.shape[1] // tile_size

    @pl.when(step == 0)
    def _():
        norm = unpack_stat(base[...], 0, rhs)
        stat = far_parts[0][data:, :]
        for part in far_parts[1:]:
            stat += part[data:, :]
        curve[...] = stat
        size_now = norm / unpack_stat(stat, 0, rhs)
        scatter_chunks(near_parts, lax.axis_index("col"), n, per, rhs, direct_total)
        scatter_chunks(far_parts, lax.axis_index("row"), n, per, rhs, mirror_total)
        for source, image, pairs in ((near, direct_total, near_pairs), (far, mirror_total, far_pairs)):
            for tile in range(tiles):
                pieces = []
                for part in range(width):
                    i = tile * width + part
                    pieces.append(source[:, i * LANES:(i + 1) * LANES] - size_now * image[i])
                value = jnp.concatenate(pieces, axis=1)
                load_pair(pairs, tile, value)
                if source is near:
                    left[:, tile * tile_size:(tile + 1) * tile_size] = value
        direct_total[...] = jnp.zeros_like(direct_total)
        mirror_total[...] = jnp.zeros_like(mirror_total)

    live = live_ref[0, 0]

    @pl.when(step * GROUP < live)
    def _():
        add_blocks(blocks, step, None, live, near_pairs, mirror_total, slot_rows, slot_cols, 0)
        add_blocks(blocks, step, None, live, far_pairs, direct_total, slot_cols, slot_rows, 1)

    @pl.when(step == pl.num_programs(0) - 1)
    def _():
        write_chunks(direct, direct_total, lax.axis_index("col"), n, per, rhs)
        write_chunks(mirror, mirror_total, lax.axis_index("row"), n, per, rhs)
        value = left[...]
        cross = jnp.zeros((rhs, LANES), F32)
        for i in range(direct_total.shape[0]):
            cross += direct_total[i] * value[:, i * LANES:(i + 1) * LANES]
        square = value * value
        tile = pack_stats([row_sums(square), row_sums(square * nugget[...]), 2.0 * row_sums(cross)], rhs)
        for out in mirror:
            out[data:, :] = tile


def sum_second_kernel(n, data, *refs):
    direct, mirror, out_direct, out_mirror, stat = refs[:n], refs[n:2 * n], *refs[2 * n:]
    out_direct[...] = add_all(direct)
    value = add_all(mirror)
    out_mirror[...] = value[:data, :]
    stat[...] = value[data:, :]


def combine_second_kernel(data, mine, other, stat, out):
    out[:data, :] = mine[...] + other[...]
    out[data:, :] = stat[...]


def last_kernel(n, per, right, left, nugget, base, curve, *rest):
    parts, (solution, residual, total) = rest[:n], rest[n:]
    rhs = right.shape[0]
    data = per * rhs
    scatter_chunks(parts, lax.axis_index("col"), n, per, rhs, total)
    norm = unpack_stat(base[...], 0, rhs)
    size_now = norm / unpack_stat(curve[...], 0, rhs)
    stats = [part[data:, :] for part in parts]
    norm_next = unpack_stat(stats[0], 0, rhs)
    bend = unpack_stat(stats[0], 1, rhs)
    for stat in stats:
        bend += unpack_stat(stat, 2, rhs)
    ratio = norm_next / norm
    size_next = norm_next / (bend - ratio * norm_next / size_now)
    back = ratio / size_now
    for i in range(total.shape[0]):
        lanes = slice(i * LANES, (i + 1) * LANES)
        first = right[:, lanes]
        now = left[:, lanes]
        solution[:, lanes] = size_now * first + size_next * (now + ratio * first)
        image = nugget[:, lanes] * now + total[i] + back * (first - now)
        residual[:, lanes] = now - size_next * image


def whole(shape):
    return pl.BlockSpec(shape, lambda *_: (0,) * len(shape))


def shape_of(*shape):
    return jax.ShapeDtypeStruct(shape, F32)


def on_device(n, right_sides, nugget, cov_blocks, block_rows, block_cols, block_count):
    rhs, width = right_sides.shape
    slots, tile_size = cov_blocks.shape[2:4]
    per = width // n // LANES
    data = per * rhs
    size = data + 8
    tiles = width // tile_size
    steps = slots // GROUP
    noise = nugget.reshape(1, width)
    smem = [pl.BlockSpec(memory_space=pltpu.SMEM)] * 3
    index = (block_rows, block_cols, block_count)
    field = whole((rhs, width))
    thin = whole((1, width))
    chunk = whole((size, LANES))
    plain = whole((data, LANES))
    small = whole((8, LANES))
    block = pl.BlockSpec((None, None, GROUP, tile_size, tile_size), lambda i: (0, 0, i, 0, 0))
    pair = pltpu.VMEM((tiles, 2 * rhs, tile_size), BF16)
    total = pltpu.VMEM((width // LANES, rhs, LANES), F32)
    params = pltpu.CompilerParams(vmem_limit_bytes=32 * 1024 * 1024)
    cost = pl.CostEstimate(flops=4 * rhs * slots * tile_size * tile_size, transcendentals=0,
                           bytes_accessed=2 * slots * tile_size * tile_size)

    far_right = transposed(right_sides, n)
    mirror = pl.pallas_call(
        functools.partial(first_kernel, n, per, True),
        grid=(steps,),
        in_specs=smem + [field, block],
        out_specs=[chunk] * n,
        out_shape=[shape_of(size, LANES)] * n,
        scratch_shapes=[pair, total],
        compiler_params=params,
        cost_estimate=cost,
        name="mirror_first",
    )(*index, right_sides, cov_blocks)
    mirror = [mirror[0]] + [shifted(mirror[d], "row", d, n) for d in range(1, n)]
    direct = pl.pallas_call(
        functools.partial(first_kernel, n, per, False),
        grid=(steps,),
        in_specs=smem + [field, field, thin, block],
        out_specs=[chunk] * n,
        out_shape=[shape_of(size, LANES)] * n,
        scratch_shapes=[pair, total],
        compiler_params=params,
        cost_estimate=cost,
        name="direct_first",
    )(*index, far_right, right_sides, noise, cov_blocks)
    direct = [direct[0]] + [shifted(direct[d], "col", d, n) for d in range(1, n)]

    mine = pl.pallas_call(
        functools.partial(sum_first_kernel, n, per),
        out_shape=shape_of(2 * size, LANES),
        compiler_params=params,
        name="sum_first",
    )(right_sides, noise, *direct, *mirror)
    other = transposed(mine, n)
    near, far, base = pl.pallas_call(
        functools.partial(combine_first_kernel, data),
        out_shape=[shape_of(data, LANES), shape_of(size, LANES), shape_of(8, LANES)],
        compiler_params=params,
        name="combine_first",
    )(mine, other)
    near = [near] + [shifted(near, "col", d, n) for d in range(1, n)]
    far = [far] + [shifted(far, "row", d, n) for d in range(1, n)]

    out = pl.pallas_call(
        functools.partial(second_kernel, n, per),
        grid=(steps,),
        in_specs=smem + [field, field, thin, small] + [plain] * n + [chunk] * n + [block],
        out_specs=[plain] * n + [chunk] * n + [field, small],
        out_shape=[shape_of(data, LANES)] * n + [shape_of(size, LANES)] * n + [shape_of(rhs, width), shape_of(8, LANES)],
        scratch_shapes=[pair, pair, total, total],
        compiler_params=params,
        cost_estimate=cost,
        name="both_second",
    )(*index, right_sides, far_right, noise, base, *near, *far, cov_blocks)
    direct, mirror, left, curve = out[:n], out[n:2 * n], out[2 * n], out[2 * n + 1]
    direct = [direct[0]] + [shifted(direct[d], "col", d, n) for d in range(1, n)]
    mirror = [mirror[0]] + [shifted(mirror[d], "row", d, n) for d in range(1, n)]

    kept, sent, stat = pl.pallas_call(
        functools.partial(sum_second_kernel, n, data),
        out_shape=[shape_of(data, LANES), shape_of(data, LANES), shape_of(8, LANES)],
        compiler_params=params,
        name="sum_second",
    )(*direct, *mirror)
    other = transposed(sent, n)
    part = pl.pallas_call(
        functools.partial(combine_second_kernel, data),
        out_shape=shape_of(size, LANES),
        compiler_params=params,
        name="combine_second",
    )(kept, other, stat)
    parts = [part] + [shifted(part, "col", d, n) for d in range(1, n)]

    return pl.pallas_call(
        functools.partial(last_kernel, n, per),
        out_shape=(shape_of(rhs, width), shape_of(rhs, width)),
        scratch_shapes=[total],
        compiler_params=params,
        name="last",
    )(right_sides, left, noise, base, curve, *parts)


def solution(mesh):
    n = mesh.shape["row"]
    assert n == mesh.shape["col"]
    placed = (
        P(None, ("groups", "row")),
        P(("groups", "row")),
        P(("groups", "row"), "col", None, None, None),
        P(("groups", "row"), "col", None),
        P(("groups", "row"), "col", None),
        P(("groups", "row"), "col"),
    )
    return jax.shard_map(
        functools.partial(on_device, n),
        mesh=mesh,
        in_specs=placed,
        out_specs=(P(None, ("groups", "row")), P(None, ("groups", "row"))),
        check_vma=False,
    )
```

time: 210 us -> 83.1 us (0.40)
  waiting for transfers between devices: 140 us -> 17.4 us
  starting transfers between devices: 0.35 us -> 52.7 us
  matrix products: 25.7 us -> 0 us
  between operations: 14.7 us -> 1.45 us
  blocking collectives: 11.3 us -> 0 us
  other arithmetic: 9.03 us -> 0 us
  Pallas kernels: 0 us -> 6.87 us
  local copies, waits for them, and re-layouts: 8.58 us -> 4.46 us
    psum x4 -> x0, waiting for transfers between devices: 140 us -> none  [the longest x2 71.3 us: on_device(): total = lax.psum(apply_direct, 'col')]
    ppermute x0 -> x24, starting transfers between devices: none -> 52.7 us  [the longest x21 49.8 us: shifted(): return lax.ppermute(value, axis, [(i, send_to(i, d, n)) for i in range(n)])]
    dot_general x8 -> x0, matrix products: 25.7 us -> none  [the longest x2 12 us: on_device(): jnp.einsum('rmk,mjk->rmj', jnp.take(far_tiles, slot_cols, axis=1), blocks...]
    ppermute x0 -> x24, waiting for transfers between devices: none -> 17.4 us  [the longest x21 17.4 us: shifted(): return lax.ppermute(value, axis, [(i, send_to(i, d, n)) for i in range(n)])]
    psum x2 -> x0, blocking collectives: 11.3 us -> none  [on_device(): lax.psum((jnp.sum(direction * applied, axis=1), jnp.sum(residual * applie...]
    pallas_call x0 -> x8, Pallas kernels: none -> 6.87 us  [the longest x1 2.38 us: on_device(): pl.pallas_call(functools.partial(second_kernel, n, per), grid=(steps,), i...]
    gather x4 -> x0, local copies, waits for them, and re-layouts: 4.37 us -> none  [the longest x2 3.14 us: on_device(): jnp.take(far_tiles, slot_cols, axis=1)]
    select_n x4 -> x0, other arithmetic: 2.71 us -> none  [the longest x2 2.05 us: from_root(): jnp.where(lax.axis_index(axis) == source, value, 0).astype(value.dtype)]
  transfers between devices with their start and end apart: 4 -> 24, of which waited for: 4 -> 7; matrix products, arithmetic and copies ran while one was open for 0% -> 0% of each run, Pallas kernels for 0% -> 4%
where the time goes in v1:
time: 83.1 us; the launch traced here: 82.9 us
  starting transfers between devices  52.7 us (63%)
  waiting for transfers between devices  17.4 us (21%)
  Pallas kernels  6.87 us (8%)
  local copies, waits for them, and re-layouts  4.46 us (5%)
  between operations  1.45 us (2%)
    ppermute x21, starting transfers between devices, shifted(): return lax.ppermute(value, axis, [(i, send_to(i, d, n)) for i in range(n)])  49.8 us
    ppermute x21, waiting for transfers between devices, shifted(): return lax.ppermute(value, axis, [(i, send_to(i, d, n)) for i in range(n)])  17.4 us
    unnamed x18, local copies, waits for them, and re-layouts  4.46 us
    ppermute x3, starting transfers between devices, transposed(): return lax.ppermute(value, ('row', 'col'), pairs)  2.94 us
    pallas_call x1, Pallas kernels, on_device(): pl.pallas_call(functools.partial(second_kernel, n, per), grid=(steps,), i...  2.38 us
    pallas_call x1, Pallas kernels, on_device(): pl.pallas_call(functools.partial(first_kernel, n, per, False), grid=(step...  1.73 us
  transfers between devices with their start and end apart: 24, of which 7 were waited for; matrix products, arithmetic and copies ran while one was open for 0% of the time, Pallas kernels for 4%

profile of v1, /device:TPU:0, one launch (start us, length us, event | category | flops | bytes accessed | tf_op | source)
XLA Modules:
  0.0 82.9 jit_solution(9628988020805587428)
XLA Ops:
  0.6 1.6 %collective-permute-start = (f32[32,2048]{1,0:T(8,128)}, f32[32,2048]{1,0:T(8,128)S(1)}, u32[]{:S(2)}, u32[]{:S(2)}) collective-permute-start(f32[32,2048]{1,0:T(8,128)} %right.5), channel_id=1, source_target_pairs={{0,0},{1,4},{2,8},{3,12},{4,1},{5,5},{6,9},{7,13},{8,2},{9,6},{10,... | collective-permute-start | bytes 786440 | tf_op jit(solution)/shard_map/ppermute | solution.py:27
  2.9 2.2 %copy-done = bf16[1,1,32,256,256]{4,3,2,1,0:T(8,128)(2,1)S(1)} copy-done((bf16[1,1,32,256,256]{4,3,2,1,0:T(8,128)(2,1)S(1)}, bf16[1,1,32,256,256]{4,3,2,1,0:T(8,128)(2,1)}, u32[]{:S(2)}) %copy-start) | copy-done | bytes 4194328
  7.4 1.4 %mirror_first.1 = (f32[136,128]{1,0:T(8,128)S(1)}, f32[136,128]{1,0:T(8,128)S(1)}, f32[136,128]{1,0:T(8,128)S(1)}, f32[136,128]{1,0:T(8,128)S(1)}) custom-call(s32[1,1,32]{2,1,0:T(1,128)S(1)} %copy-done.5, s32[1,1,32]{2,1,0:T(1,128)S(1)} %copy-done.7, s32[1,1]{1,0:T(1,128)S(6)} %copy.8.live_ref, f32[32,2048]{1,0:T(8,128)S(1)} %copy-done.2, ...), custom_call_target="tpu_custom_call" | custom-call | flops 268435456 | bytes 4194304 | tf_op jit(solution)/shard_map/mirror_first/pallas_call | solution.py:297
  8.8 3.2 %collective-permute-start.4 = (f32[136,128]{1,0:T(8,128)S(1)}, f32[136,128]{1,0:T(8,128)S(1)}, u32[]{:S(2)}, u32[]{:S(2)}) collective-permute-start(f32[136,128]{1,0:T(8,128)S(1)} %get-tuple-element.31), channel_id=1, source_target_pairs={{0,4},{4,0},{8,12},{12,8},{1,5},{5,1},{9,13},{13,9},{2,6},{6,2},{1... | collective-permute-start | bytes 208904 | tf_op jit(solution)/shard_map/ppermute | solution.py:22
  12.0 3.5 %collective-permute-start.5 = (f32[136,128]{1,0:T(8,128)S(1)}, f32[136,128]{1,0:T(8,128)S(1)}, u32[]{:S(2)}, u32[]{:S(2)}) collective-permute-start(f32[136,128]{1,0:T(8,128)S(1)} %get-tuple-element.32), channel_id=1, source_target_pairs={{0,8},{4,12},{8,0},{12,4},{1,9},{5,13},{9,1},{13,5},{2,10},{6,14},... | collective-permute-start | bytes 208904 | tf_op jit(solution)/shard_map/ppermute | solution.py:22
  15.5 1.7 %direct_first.1 = (f32[136,128]{1,0:T(8,128)S(1)}, f32[136,128]{1,0:T(8,128)S(1)}, f32[136,128]{1,0:T(8,128)S(1)}, f32[136,128]{1,0:T(8,128)S(1)}) custom-call(s32[1,1,32]{2,1,0:T(1,128)S(1)} %copy-done.5, s32[1,1,32]{2,1,0:T(1,128)S(1)} %copy-done.7, s32[1,1]{1,0:T(1,128)S(6)} %copy.8.live_ref, f32[32,2048]{1,0:T(8,128)S(1)} %collective-permute-done.right.far, ...), custom_call_target="tpu_custom_call" | custom-call | flops 268435456 | bytes 4194304 | tf_op jit(solution)/shard_map/direct_first/pallas_call | solution.py:309
  17.2 1.4 %collective-permute-start.1 = (f32[136,128]{1,0:T(8,128)S(1)}, f32[136,128]{1,0:T(8,128)S(1)}, u32[]{:S(2)}, u32[]{:S(2)}) collective-permute-start(f32[136,128]{1,0:T(8,128)S(1)} %get-tuple-element.27), channel_id=1, source_target_pairs={{0,1},{1,0},{2,3},{3,2},{4,5},{5,4},{6,7},{7,6},{8,9},{9,8},{10,11... | collective-permute-start | bytes 208904 | tf_op jit(solution)/shard_map/ppermute | solution.py:22
  18.6 2.8 %collective-permute-start.2 = (f32[136,128]{1,0:T(8,128)S(1)}, f32[136,128]{1,0:T(8,128)S(1)}, u32[]{:S(2)}, u32[]{:S(2)}) collective-permute-start(f32[136,128]{1,0:T(8,128)S(1)} %get-tuple-element.28), channel_id=1, source_target_pairs={{0,2},{1,3},{2,0},{3,1},{4,6},{5,7},{6,4},{7,5},{8,10},{9,11},{10,... | collective-permute-start | bytes 208904 | tf_op jit(solution)/shard_map/ppermute | solution.py:22
  21.4 1.4 %collective-permute-start.3 = (f32[136,128]{1,0:T(8,128)S(1)}, f32[136,128]{1,0:T(8,128)S(1)}, u32[]{:S(2)}, u32[]{:S(2)}) collective-permute-start(f32[136,128]{1,0:T(8,128)S(1)} %get-tuple-element.29), channel_id=1, source_target_pairs={{0,3},{1,2},{2,1},{3,0},{4,7},{5,6},{6,5},{7,4},{8,11},{9,10},{10,... | collective-permute-start | bytes 208904 | tf_op jit(solution)/shard_map/ppermute | solution.py:22
  23.8 4.5 %collective-permute-done.3.refs_3_ = f32[136,128]{1,0:T(8,128)S(1)} collective-permute-done((f32[136,128]{1,0:T(8,128)S(1)}, f32[136,128]{1,0:T(8,128)S(1)}, u32[]{:S(2)}, u32[]{:S(2)}) %collective-permute-start.3) | collective-permute-done | bytes 69664 | tf_op jit(solution)/shard_map/ppermute | solution.py:22
  29.1 9.3 %collective-permute-start.10 = (f32[128,128]{1,0:T(8,128)S(1)}, f32[128,128]{1,0:T(8,128)S(1)}, u32[]{:S(2)}, u32[]{:S(2)}) collective-permute-start(f32[128,128]{1,0:T(8,128)S(1)} %get-tuple-element.35.rest_0_), channel_id=1, source_target_pairs={{0,3},{1,2},{2,1},{3,0},{4,7},{5,6},{6,5},{7,4},{8,11},{9,10},{10,... | collective-permute-start | bytes 196616 | tf_op jit(solution)/shard_map/ppermute | solution.py:22
  39.0 4.7 %collective-permute-start.12 = (f32[136,128]{1,0:T(8,128)S(1)}, f32[136,128]{1,0:T(8,128)S(1)}, u32[]{:S(2)}, u32[]{:S(2)}) collective-permute-start(f32[136,128]{1,0:T(8,128)S(1)} %get-tuple-element.36.rest_4_), channel_id=1, source_target_pairs={{0,8},{4,12},{8,0},{12,4},{1,9},{5,13},{9,1},{13,5},{2,10},{6,14},... | collective-permute-start | bytes 208904 | tf_op jit(solution)/shard_map/ppermute | solution.py:22
  43.7 1.6 %collective-permute-start.9 = (f32[128,128]{1,0:T(8,128)S(1)}, f32[128,128]{1,0:T(8,128)S(1)}, u32[]{:S(2)}, u32[]{:S(2)}) collective-permute-start(f32[128,128]{1,0:T(8,128)S(1)} %get-tuple-element.35.rest_0_), channel_id=1, source_target_pairs={{0,2},{1,3},{2,0},{3,1},{4,6},{5,7},{6,4},{7,5},{8,10},{9,11},{10,... | collective-permute-start | bytes 196616 | tf_op jit(solution)/shard_map/ppermute | solution.py:22
  45.3 2.5 %collective-permute-start.8 = (f32[128,128]{1,0:T(8,128)S(1)}, f32[128,128]{1,0:T(8,128)S(1)}, u32[]{:S(2)}, u32[]{:S(2)}) collective-permute-start(f32[128,128]{1,0:T(8,128)S(1)} %get-tuple-element.35.rest_0_), channel_id=1, source_target_pairs={{0,1},{1,0},{2,3},{3,2},{4,5},{5,4},{6,7},{7,6},{8,9},{9,8},{10,11... | collective-permute-start | bytes 196616 | tf_op jit(solution)/shard_map/ppermute | solution.py:22
  47.8 2.8 %collective-permute-done.9.rest_2_ = f32[128,128]{1,0:T(8,128)S(1)} collective-permute-done((f32[128,128]{1,0:T(8,128)S(1)}, f32[128,128]{1,0:T(8,128)S(1)}, u32[]{:S(2)}, u32[]{:S(2)}) %collective-permute-start.9) | collective-permute-done | bytes 65568 | tf_op jit(solution)/shard_map/ppermute | solution.py:22
  50.7 2.4 %both_second.1 = (f32[128,128]{1,0:T(8,128)S(1)}, f32[128,128]{1,0:T(8,128)S(1)}, f32[128,128]{1,0:T(8,128)S(1)}, f32[128,128]{1,0:T(8,128)S(1)}, f32[136,128]{1...) custom-call(s32[1,1,32]{2,1,0:T(1,128)S(1)} %copy-done.6, ...), custom_call_target="tpu_custom_call" | custom-call | flops 268435456 | bytes 4194304 | tf_op jit(solution)/shard_map/both_second/pallas_call | solution.py:338
  53.1 2.1 %collective-permute-start.14 = (f32[128,128]{1,0:T(8,128)S(1)}, f32[128,128]{1,0:T(8,128)S(1)}, u32[]{:S(2)}, u32[]{:S(2)}) collective-permute-start(f32[128,128]{1,0:T(8,128)S(1)} %get-tuple-element.40), channel_id=1, source_target_pairs={{0,1},{1,0},{2,3},{3,2},{4,5},{5,4},{6,7},{7,6},{8,9},{9,8},{10,11... | collective-permute-start | bytes 196616 | tf_op jit(solution)/shard_map/ppermute | solution.py:22
  55.2 1.8 %collective-permute-start.18 = (f32[136,128]{1,0:T(8,128)S(1)}, f32[136,128]{1,0:T(8,128)S(1)}, u32[]{:S(2)}, u32[]{:S(2)}) collective-permute-start(f32[136,128]{1,0:T(8,128)S(1)} %get-tuple-element.45), channel_id=1, source_target_pairs={{0,8},{4,12},{8,0},{12,4},{1,9},{5,13},{9,1},{13,5},{2,10},{6,14},... | collective-permute-start | bytes 208904 | tf_op jit(solution)/shard_map/ppermute | solution.py:22
  57.7 3.7 %collective-permute-start.16 = (f32[128,128]{1,0:T(8,128)S(1)}, f32[128,128]{1,0:T(8,128)S(1)}, u32[]{:S(2)}, u32[]{:S(2)}) collective-permute-start(f32[128,128]{1,0:T(8,128)S(1)} %get-tuple-element.42), channel_id=1, source_target_pairs={{0,3},{1,2},{2,1},{3,0},{4,7},{5,6},{6,5},{7,4},{8,11},{9,10},{10,... | collective-permute-start | bytes 196616 | tf_op jit(solution)/shard_map/ppermute | solution.py:22
  61.4 4.4 %collective-permute-done.15.refs_2_ = f32[128,128]{1,0:T(8,128)S(1)} collective-permute-done((f32[128,128]{1,0:T(8,128)S(1)}, f32[128,128]{1,0:T(8,128)S(1)}, u32[]{:S(2)}, u32[]{:S(2)}) %collective-permute-start.15) | collective-permute-done | bytes 65568 | tf_op jit(solution)/shard_map/ppermute | solution.py:22
  66.5 9.9 %collective-permute-start.23 = (f32[136,128]{1,0:T(8,128)S(1)}, f32[136,128]{1,0:T(8,128)S(1)}, u32[]{:S(2)}, u32[]{:S(2)}) collective-permute-start(f32[136,128]{1,0:T(8,128)S(1)} %combine_second.1.rest_0_), channel_id=1, source_target_pairs={{0,3},{1,2},{2,1},{3,0},{4,7},{5,6},{6,5},{7,4},{8,11},{9,10},{10,... | collective-permute-start | bytes 208904 | tf_op jit(solution)/shard_map/ppermute | solution.py:22
  77.1 2.5 %collective-permute-done.23.rest_3_ = f32[136,128]{1,0:T(8,128)S(1)} collective-permute-done((f32[136,128]{1,0:T(8,128)S(1)}, f32[136,128]{1,0:T(8,128)S(1)}, u32[]{:S(2)}, u32[]{:S(2)}) %collective-permute-start.23) | collective-permute-done | bytes 69664 | tf_op jit(solution)/shard_map/ppermute | solution.py:22
  79.5 2.2 %collective-permute-done.22.rest_2_ = f32[136,128]{1,0:T(8,128)S(1)} collective-permute-done((f32[136,128]{1,0:T(8,128)S(1)}, f32[136,128]{1,0:T(8,128)S(1)}, u32[]{:S(2)}, u32[]{:S(2)}) %collective-permute-start.22) | collective-permute-done | bytes 69664 | tf_op jit(solution)/shard_map/ppermute | solution.py:22
  81.8 1.2 %last.1 = (f32[32,2048]{1,0:T(8,128)}, f32[32,2048]{1,0:T(8,128)}) custom-call(f32[32,2048]{1,0:T(8,128)S(1)} %copy-done.3, f32[32,2048]{1,0:T(8,128)S(1)} %get-tuple-element.37.left, f32[1,2048]{1,0:T(1,128)S(1)} %bitcast.4, f32[8,128]{1,0:T(8,128)S(1)} %get-tuple-element.34.base, f32[8,128]{1,0:T(8,128)S(1)} %get-tuple-element.38.curve, ...), custom_call_target="tpu_custom_call" | custom-call | tf_op jit(solution)/shard_map/last/pallas_call | solution.py:368
  (50 shorter events, 6.8 us)
Async XLA Ops:
  0.6 14.8 %collective-permute-start = (f32[32,2048]{1,0:T(8,128)}, f32[32,2048]{1,0:T(8,128)S(1)}, u32[]{:S(2)}, u32[]{:S(2)}) collective-permute-start(f32[32,2048]{1,0:T(8,128)} %right.5), channel_id=1, source_target_pairs={{0,0},{1,4},{2,8},{3,12},{4,1},{5,5},{6,9},{7,13},{8,2},{9,6},{10,... | collective-permute-start | bytes 786440 | tf_op jit(solution)/shard_map/ppermute | solution.py:27
  8.8 12.6 %collective-permute-start.4 = (f32[136,128]{1,0:T(8,128)S(1)}, f32[136,128]{1,0:T(8,128)S(1)}, u32[]{:S(2)}, u32[]{:S(2)}) collective-permute-start(f32[136,128]{1,0:T(8,128)S(1)} %get-tuple-element.31), channel_id=1, source_target_pairs={{0,4},{4,0},{8,12},{12,8},{1,5},{5,1},{9,13},{13,9},{2,6},{6,2},{1... | collective-permute-start | bytes 208904 | tf_op jit(solution)/shard_map/ppermute | solution.py:22
  12.0 10.9 %collective-permute-start.5 = (f32[136,128]{1,0:T(8,128)S(1)}, f32[136,128]{1,0:T(8,128)S(1)}, u32[]{:S(2)}, u32[]{:S(2)}) collective-permute-start(f32[136,128]{1,0:T(8,128)S(1)} %get-tuple-element.32), channel_id=1, source_target_pairs={{0,8},{4,12},{8,0},{12,4},{1,9},{5,13},{9,1},{13,5},{2,10},{6,14},... | collective-permute-start | bytes 208904 | tf_op jit(solution)/shard_map/ppermute | solution.py:22
  15.4 7.4 %collective-permute-start.6 = (f32[136,128]{1,0:T(8,128)S(1)}, f32[136,128]{1,0:T(8,128)S(1)}, u32[]{:S(2)}, u32[]{:S(2)}) collective-permute-start(f32[136,128]{1,0:T(8,128)S(1)} %get-tuple-element.33), channel_id=1, source_target_pairs={{0,12},{4,8},{8,4},{12,0},{1,13},{5,9},{9,5},{13,1},{2,14},{6,10},... | collective-permute-start | bytes 208904 | tf_op jit(solution)/shard_map/ppermute | solution.py:22
  17.2 5.6 %collective-permute-start.1 = (f32[136,128]{1,0:T(8,128)S(1)}, f32[136,128]{1,0:T(8,128)S(1)}, u32[]{:S(2)}, u32[]{:S(2)}) collective-permute-start(f32[136,128]{1,0:T(8,128)S(1)} %get-tuple-element.27), channel_id=1, source_target_pairs={{0,1},{1,0},{2,3},{3,2},{4,5},{5,4},{6,7},{7,6},{8,9},{9,8},{10,11... | collective-permute-start | bytes 208904 | tf_op jit(solution)/shard_map/ppermute | solution.py:22
  18.6 5.2 %collective-permute-start.2 = (f32[136,128]{1,0:T(8,128)S(1)}, f32[136,128]{1,0:T(8,128)S(1)}, u32[]{:S(2)}, u32[]{:S(2)}) collective-permute-start(f32[136,128]{1,0:T(8,128)S(1)} %get-tuple-element.28), channel_id=1, source_target_pairs={{0,2},{1,3},{2,0},{3,1},{4,6},{5,7},{6,4},{7,5},{8,10},{9,11},{10,... | collective-permute-start | bytes 208904 | tf_op jit(solution)/shard_map/ppermute | solution.py:22
  21.4 6.9 %collective-permute-start.3 = (f32[136,128]{1,0:T(8,128)S(1)}, f32[136,128]{1,0:T(8,128)S(1)}, u32[]{:S(2)}, u32[]{:S(2)}) collective-permute-start(f32[136,128]{1,0:T(8,128)S(1)} %get-tuple-element.29), channel_id=1, source_target_pairs={{0,3},{1,2},{2,1},{3,0},{4,7},{5,6},{6,5},{7,4},{8,11},{9,10},{10,... | collective-permute-start | bytes 208904 | tf_op jit(solution)/shard_map/ppermute | solution.py:22
  28.4 0.7 collective-permute-start.7
  29.1 16.2 %collective-permute-start.10 = (f32[128,128]{1,0:T(8,128)S(1)}, f32[128,128]{1,0:T(8,128)S(1)}, u32[]{:S(2)}, u32[]{:S(2)}) collective-permute-start(f32[128,128]{1,0:T(8,128)S(1)} %get-tuple-element.35.rest_0_), channel_id=1, source_target_pairs={{0,3},{1,2},{2,1},{3,0},{4,7},{5,6},{6,5},{7,4},{8,11},{9,10},{10,... | collective-permute-start | bytes 196616 | tf_op jit(solution)/shard_map/ppermute | solution.py:22
  38.4 12.3 %collective-permute-start.13 = (f32[136,128]{1,0:T(8,128)S(1)}, f32[136,128]{1,0:T(8,128)S(1)}, u32[]{:S(2)}, u32[]{:S(2)}) collective-permute-start(f32[136,128]{1,0:T(8,128)S(1)} %get-tuple-element.36.rest_4_), channel_id=1, source_target_pairs={{0,12},{4,8},{8,4},{12,0},{1,13},{5,9},{9,5},{13,1},{2,14},{6,10},... | collective-permute-start | bytes 208904 | tf_op jit(solution)/shard_map/ppermute | solution.py:22
  39.0 11.7 %collective-permute-start.12 = (f32[136,128]{1,0:T(8,128)S(1)}, f32[136,128]{1,0:T(8,128)S(1)}, u32[]{:S(2)}, u32[]{:S(2)}) collective-permute-start(f32[136,128]{1,0:T(8,128)S(1)} %get-tuple-element.36.rest_4_), channel_id=1, source_target_pairs={{0,8},{4,12},{8,0},{12,4},{1,9},{5,13},{9,1},{13,5},{2,10},{6,14},... | collective-permute-start | bytes 208904 | tf_op jit(solution)/shard_map/ppermute | solution.py:22
  43.7 7.0 %collective-permute-start.11 = (f32[136,128]{1,0:T(8,128)S(1)}, f32[136,128]{1,0:T(8,128)S(1)}, u32[]{:S(2)}, u32[]{:S(2)}) collective-permute-start(f32[136,128]{1,0:T(8,128)S(1)} %get-tuple-element.36.rest_4_), channel_id=1, source_target_pairs={{0,4},{4,0},{8,12},{12,8},{1,5},{5,1},{9,13},{13,9},{2,6},{6,2},{1... | collective-permute-start | bytes 208904 | tf_op jit(solution)/shard_map/ppermute | solution.py:22
  43.7 6.9 %collective-permute-start.9 = (f32[128,128]{1,0:T(8,128)S(1)}, f32[128,128]{1,0:T(8,128)S(1)}, u32[]{:S(2)}, u32[]{:S(2)}) collective-permute-start(f32[128,128]{1,0:T(8,128)S(1)} %get-tuple-element.35.rest_0_), channel_id=1, source_target_pairs={{0,2},{1,3},{2,0},{3,1},{4,6},{5,7},{6,4},{7,5},{8,10},{9,11},{10,... | collective-permute-start | bytes 196616 | tf_op jit(solution)/shard_map/ppermute | solution.py:22
  45.3 5.4 %collective-permute-start.8 = (f32[128,128]{1,0:T(8,128)S(1)}, f32[128,128]{1,0:T(8,128)S(1)}, u32[]{:S(2)}, u32[]{:S(2)}) collective-permute-start(f32[128,128]{1,0:T(8,128)S(1)} %get-tuple-element.35.rest_0_), channel_id=1, source_target_pairs={{0,1},{1,0},{2,3},{3,2},{4,5},{5,4},{6,7},{7,6},{8,9},{9,8},{10,11... | collective-permute-start | bytes 196616 | tf_op jit(solution)/shard_map/ppermute | solution.py:22
  53.1 4.5 %collective-permute-start.14 = (f32[128,128]{1,0:T(8,128)S(1)}, f32[128,128]{1,0:T(8,128)S(1)}, u32[]{:S(2)}, u32[]{:S(2)}) collective-permute-start(f32[128,128]{1,0:T(8,128)S(1)} %get-tuple-element.40), channel_id=1, source_target_pairs={{0,1},{1,0},{2,3},{3,2},{4,5},{5,4},{6,7},{7,6},{8,9},{9,8},{10,11... | collective-permute-start | bytes 196616 | tf_op jit(solution)/shard_map/ppermute | solution.py:22
  55.2 10.5 %collective-permute-start.17 = (f32[136,128]{1,0:T(8,128)S(1)}, f32[136,128]{1,0:T(8,128)S(1)}, u32[]{:S(2)}, u32[]{:S(2)}) collective-permute-start(f32[136,128]{1,0:T(8,128)S(1)} %get-tuple-element.44), channel_id=1, source_target_pairs={{0,4},{4,0},{8,12},{12,8},{1,5},{5,1},{9,13},{13,9},{2,6},{6,2},{1... | collective-permute-start | bytes 208904 | tf_op jit(solution)/shard_map/ppermute | solution.py:22
  55.2 10.5 %collective-permute-start.18 = (f32[136,128]{1,0:T(8,128)S(1)}, f32[136,128]{1,0:T(8,128)S(1)}, u32[]{:S(2)}, u32[]{:S(2)}) collective-permute-start(f32[136,128]{1,0:T(8,128)S(1)} %get-tuple-element.45), channel_id=1, source_target_pairs={{0,8},{4,12},{8,0},{12,4},{1,9},{5,13},{9,1},{13,5},{2,10},{6,14},... | collective-permute-start | bytes 208904 | tf_op jit(solution)/shard_map/ppermute | solution.py:22
  57.0 8.8 %collective-permute-start.19 = (f32[136,128]{1,0:T(8,128)S(1)}, f32[136,128]{1,0:T(8,128)S(1)}, u32[]{:S(2)}, u32[]{:S(2)}) collective-permute-start(f32[136,128]{1,0:T(8,128)S(1)} %get-tuple-element.46), channel_id=1, source_target_pairs={{0,12},{4,8},{8,4},{12,0},{1,13},{5,9},{9,5},{13,1},{2,14},{6,10},... | collective-permute-start | bytes 208904 | tf_op jit(solution)/shard_map/ppermute | solution.py:22
  57.1 8.6 %collective-permute-start.15 = (f32[128,128]{1,0:T(8,128)S(1)}, f32[128,128]{1,0:T(8,128)S(1)}, u32[]{:S(2)}, u32[]{:S(2)}) collective-permute-start(f32[128,128]{1,0:T(8,128)S(1)} %get-tuple-element.41), channel_id=1, source_target_pairs={{0,2},{1,3},{2,0},{3,1},{4,6},{5,7},{6,4},{7,5},{8,10},{9,11},{10,... | collective-permute-start | bytes 196616 | tf_op jit(solution)/shard_map/ppermute | solution.py:22
  57.7 8.1 %collective-permute-start.16 = (f32[128,128]{1,0:T(8,128)S(1)}, f32[128,128]{1,0:T(8,128)S(1)}, u32[]{:S(2)}, u32[]{:S(2)}) collective-permute-start(f32[128,128]{1,0:T(8,128)S(1)} %get-tuple-element.42), channel_id=1, source_target_pairs={{0,3},{1,2},{2,1},{3,0},{4,7},{5,6},{6,5},{7,4},{8,11},{9,10},{10,... | collective-permute-start | bytes 196616 | tf_op jit(solution)/shard_map/ppermute | solution.py:22
  65.8 0.7 collective-permute-start.20
  66.5 13.0 %collective-permute-start.23 = (f32[136,128]{1,0:T(8,128)S(1)}, f32[136,128]{1,0:T(8,128)S(1)}, u32[]{:S(2)}, u32[]{:S(2)}) collective-permute-start(f32[136,128]{1,0:T(8,128)S(1)} %combine_second.1.rest_0_), channel_id=1, source_target_pairs={{0,3},{1,2},{2,1},{3,0},{4,7},{5,6},{6,5},{7,4},{8,11},{9,10},{10,... | collective-permute-start | bytes 208904 | tf_op jit(solution)/shard_map/ppermute | solution.py:22
  76.4 5.3 %collective-permute-start.22 = (f32[136,128]{1,0:T(8,128)S(1)}, f32[136,128]{1,0:T(8,128)S(1)}, u32[]{:S(2)}, u32[]{:S(2)}) collective-permute-start(f32[136,128]{1,0:T(8,128)S(1)} %combine_second.1.rest_0_), channel_id=1, source_target_pairs={{0,2},{1,3},{2,0},{3,1},{4,6},{5,7},{6,4},{7,5},{8,10},{9,11},{10,... | collective-permute-start | bytes 208904 | tf_op jit(solution)/shard_map/ppermute | solution.py:22
  76.4 5.3 %collective-permute-start.21 = (f32[136,128]{1,0:T(8,128)S(1)}, f32[136,128]{1,0:T(8,128)S(1)}, u32[]{:S(2)}, u32[]{:S(2)}) collective-permute-start(f32[136,128]{1,0:T(8,128)S(1)} %combine_second.1.rest_0_), channel_id=1, source_target_pairs={{0,1},{1,0},{2,3},{3,2},{4,5},{5,4},{6,7},{7,6},{8,9},{9,8},{10,11... | collective-permute-start | bytes 208904 | tf_op jit(solution)/shard_map/ppermute | solution.py:22
  (9 other events, 115.5 us)

commit v2 on v0

v2 whole, which is shorter than its diff:
```python
import functools

import jax
import jax.numpy as jnp
from jax import lax
from jax.experimental import pallas as pl
from jax.experimental.pallas import tpu as pltpu
from jax.sharding import PartitionSpec as P

ITERS = 2
LANES = 128
GROUP = 8
BF16 = jnp.bfloat16
F32 = jnp.float32


def shifted(value, axis, d, n):
    return lax.ppermute(value, axis, [(i, i ^ d) for i in range(n)])


def to_all(value, axis, n):
    return [value] + [shifted(value, axis, d, n) for d in range(1, n)]


def to_owners(values, axis, n):
    return [values[0]] + [shifted(values[d], axis, d, n) for d in range(1, n)]


def transposed(value, n):
    pairs = [(r * n + c, c * n + r) for r in range(n) for c in range(n)]
    return lax.ppermute(value, ("row", "col"), pairs)


def from_diagonal(value, n):
    held = [value]
    for o in range(1, n):
        pairs = [(c * n + c, (c ^ o) * n + c) for c in range(n)]
        held.append(lax.ppermute(value, ("row", "col"), pairs))
    return held


def load_pair(dst, tile, value):
    rhs = value.shape[0]
    high = value.astype(BF16)
    dst[tile, :rhs, :] = high
    dst[tile, rhs:, :] = (value - high.astype(F32)).astype(BF16)


def product(pair, block, contract):
    both = lax.dot_general(pair, block, (((1,), (contract,)), ((), ())), preferred_element_type=F32)
    rhs = both.shape[0] // 2
    return both[:rhs] + both[rhs:]


def pack_stats(columns, rhs):
    lane = lax.broadcasted_iota(jnp.int32, (8, LANES), 1)
    tile = jnp.zeros((8, LANES), F32)
    groups = rhs // 8
    for i, column in enumerate(columns):
        for g in range(groups):
            tile = jnp.where(lane == i * groups + g, column[g * 8:(g + 1) * 8], tile)
    return tile


def unpack_stat(tile, i, rhs):
    groups = rhs // 8
    return jnp.concatenate([tile[:, i * groups + g:i * groups + g + 1] for g in range(groups)], axis=0)


def accumulate(total, tile, value):
    width = value.shape[1] // LANES
    for part in range(width):
        total[tile * width + part] += value[:, part * LANES:(part + 1) * LANES]


def add_blocks(blocks, slot_rows, slot_cols, live, pairs, total, mirror, ready=None):
    read, write, contract = (slot_rows, slot_cols, 0) if mirror else (slot_cols, slot_rows, 1)

    def body(step, carry):
        if ready is not None:
            ready(step)
        values = []
        for g in range(GROUP):
            slot = step * GROUP + g
            value = product(pairs[read[0, 0, slot]], blocks[slot], contract)
            values.append((write[0, 0, slot], jnp.where(slot < live, value, 0.0)))
        for tile, value in values:
            accumulate(total, tile, value)
        return carry

    lax.fori_loop(0, (live + GROUP - 1) // GROUP, body, 0)


def write_chunks(outs, total, me, per, rhs):
    for d, out in enumerate(outs):
        first = (me ^ d) * per
        for i in range(per):
            out[i * rhs:(i + 1) * rhs, :] = total[first + i]


def read_chunks(parts, total, me, per, rhs):
    for d, part in enumerate(parts):
        first = (me ^ d) * per
        for i in range(per):
            total[first + i] = part[i * rhs:(i + 1) * rhs, :]


def row_sums(value):
    return jnp.sum(value, axis=1, keepdims=True)


def cross_sums(total, value):
    rhs = value.shape[0]
    cross = jnp.zeros((rhs, LANES), F32)
    for i in range(total.shape[0]):
        cross += total[i] * value[:, i * LANES:(i + 1) * LANES]
    return row_sums(cross)


def tree_sum(values):
    values = list(values)
    while len(values) > 1:
        values = [a + b for a, b in zip(values[::2], values[1::2])]
    return values[0]


def fetch_index(sources, targets, sems):
    copies = [pltpu.make_async_copy(s, t, sems.at[i]) for i, (s, t) in enumerate(zip(sources, targets))]
    for copy in copies:
        copy.start()
    return copies


def mirror_first_kernel(n, per, *refs):
    index, count, right_hbm, cov = refs[:2], refs[2], refs[3], refs[4]
    outs, blocks = refs[5:5 + n], refs[5 + n]
    slot_rows, slot_cols, right, pairs, total, index_sems, right_sem, block_sems = refs[6 + n:]
    slots, tile_size = blocks.shape[:2]
    rhs = right.shape[0]

    def block_copy(i):
        part = pl.ds(i * GROUP, GROUP)
        return pltpu.make_async_copy(cov.at[0, 0, part], blocks.at[part], block_sems.at[i])

    copies = fetch_index(index, (slot_rows, slot_cols), index_sems)
    load = pltpu.make_async_copy(right_hbm, right, right_sem)
    load.start()
    block_copy(0).start()
    total[...] = jnp.zeros_like(total)
    for copy in copies:
        copy.wait()
    live = count[0, 0]
    for i in range(1, slots // GROUP):
        @pl.when(i * GROUP < live)
        def _():
            block_copy(i).start()
    load.wait()
    for tile in range(right.shape[1] // tile_size):
        load_pair(pairs, tile, right[:, tile * tile_size:(tile + 1) * tile_size])
    add_blocks(blocks, slot_rows, slot_cols, live, pairs, total, True, lambda i: block_copy(i).wait())
    write_chunks(outs, total, lax.axis_index("row"), per, rhs)


def direct_first_kernel(n, per, *refs):
    index, count, held, noise, blocks = refs[:2], refs[2], refs[3:3 + n], refs[3 + n], refs[4 + n]
    outs, (stat, far), scratch = refs[5 + n:5 + 2 * n], refs[5 + 2 * n:7 + 2 * n], refs[7 + 2 * n:]
    slot_rows, slot_cols, pairs, total, index_sems = scratch
    tile_size = blocks.shape[1]
    rhs, width = far.shape
    copies = fetch_index(index, (slot_rows, slot_cols), index_sems)
    offset = lax.axis_index("row") ^ lax.axis_index("col")
    for o in range(n):
        @pl.when(offset == o)
        def _():
            for tile in range(width // tile_size):
                value = held[o][:, tile * tile_size:(tile + 1) * tile_size]
                load_pair(pairs, tile, value)
                far[:, tile * tile_size:(tile + 1) * tile_size] = value
    total[...] = jnp.zeros_like(total)
    for copy in copies:
        copy.wait()
    add_blocks(blocks, slot_rows, slot_cols, count[0, 0], pairs, total, False)
    write_chunks(outs, total, lax.axis_index("col"), per, rhs)
    right = held[0][...]
    square = right * right
    stat[...] = pack_stats([row_sums(square), row_sums(square * noise[...]), 2.0 * cross_sums(total, right)], rhs)


def sum_kernel(*refs):
    refs[-1][...] = tree_sum(ref[...] for ref in refs[:-1])


def combine_first_kernel(n, per, right, noise, other, *refs):
    direct, stats, (payload, finished) = refs[:n], refs[n:2 * n], refs[2 * n:]
    rhs = right.shape[0]
    data = per * rhs
    width = per * LANES
    finished[...] = tree_sum(ref[...] for ref in direct) + other[...]
    me = lax.axis_index("col")
    for k in range(n):
        @pl.when(me == k)
        def _():
            for i in range(per):
                lanes = slice(k * width + i * LANES, k * width + (i + 1) * LANES)
                finished[i * rhs:(i + 1) * rhs, :] += right[:, lanes] * noise[:, lanes]
    payload[:data, :] = finished[...]
    payload[data:, :] = tree_sum(ref[...] for ref in stats)


def mirror_second_kernel(n, per, *refs):
    index, count, right, parts, blocks = refs[:2], refs[2], refs[3], refs[4:4 + n], refs[4 + n]
    outs, (left, base), scratch = refs[5 + n:5 + 2 * n], refs[5 + 2 * n:7 + 2 * n], refs[7 + 2 * n:]
    slot_rows, slot_cols, pairs, total, index_sems = scratch
    copies = fetch_index(index, (slot_rows, slot_cols), index_sems)
    tile_size = blocks.shape[1]
    rhs, width = right.shape
    data = per * rhs
    stats = [part[data:, :] for part in parts]
    norm = unpack_stat(stats[0], 0, rhs)
    bend = unpack_stat(stats[0], 1, rhs) + tree_sum(unpack_stat(stat, 2, rhs) for stat in stats)
    base[...] = pack_stats([norm, bend], rhs)
    size_now = norm / bend
    read_chunks(parts, total, lax.axis_index("col"), per, rhs)
    for i in range(width // LANES):
        lanes = slice(i * LANES, (i + 1) * LANES)
        left[:, lanes] = right[:, lanes] - size_now * total[i]
    for tile in range(width // tile_size):
        load_pair(pairs, tile, left[:, tile * tile_size:(tile + 1) * tile_size])
    total[...] = jnp.zeros_like(total)
    for copy in copies:
        copy.wait()
    add_blocks(blocks, slot_rows, slot_cols, count[0, 0], pairs, total, True)
    write_chunks(outs, total, lax.axis_index("row"), per, rhs)


def direct_second_kernel(n, per, *refs):
    index, count, far, left, noise, base = refs[:2], refs[2], refs[3], refs[4], refs[5], refs[6]
    parts, blocks = refs[7:7 + n], refs[7 + n]
    outs, stat, scratch = refs[8 + n:8 + 2 * n], refs[8 + 2 * n], refs[9 + 2 * n:]
    slot_rows, slot_cols, pairs, total, index_sems = scratch
    copies = fetch_index(index, (slot_rows, slot_cols), index_sems)
    tile_size = blocks.shape[1]
    rhs, width = far.shape
    size_now = unpack_stat(base[...], 0, rhs) / unpack_stat(base[...], 1, rhs)
    read_chunks(parts, total, lax.axis_index("row"), per, rhs)
    pieces = tile_size // LANES
    for tile in range(width // tile_size):
        image = jnp.concatenate([total[tile * pieces + i] for i in range(pieces)], axis=1)
        load_pair(pairs, tile, far[:, tile * tile_size:(tile + 1) * tile_size] - size_now * image)
    total[...] = jnp.zeros_like(total)
    for copy in copies:
        copy.wait()
    add_blocks(blocks, slot_rows, slot_cols, count[0, 0], pairs, total, False)
    write_chunks(outs, total, lax.axis_index("col"), per, rhs)
    value = left[...]
    square = value * value
    stat[...] = pack_stats([row_sums(square), row_sums(square * noise[...]), 2.0 * cross_sums(total, value)], rhs)


def combine_second_kernel(n, data, other, *refs):
    direct, stats, payload = refs[:n], refs[n:2 * n], refs[2 * n]
    payload[:data, :] = tree_sum(ref[...] for ref in direct) + other[...]
    payload[data:, :] = tree_sum(ref[...] for ref in stats)


def last_kernel(n, per, right, left, noise, base, *rest):
    parts, (solution, residual, total) = rest[:n], rest[n:]
    rhs = right.shape[0]
    data = per * rhs
    read_chunks(parts, total, lax.axis_index("col"), per, rhs)
    norm = unpack_stat(base[...], 0, rhs)
    size_now = norm / unpack_stat(base[...], 1, rhs)
    stats = [part[data:, :] for part in parts]
    norm_next = unpack_stat(stats[0], 0, rhs)
    bend = unpack_stat(stats[0], 1, rhs) + tree_sum(unpack_stat(stat, 2, rhs) for stat in stats)
    ratio = norm_next / norm
    size_next = norm_next / (bend - ratio * norm_next / size_now)
    back = ratio / size_now
    for i in range(total.shape[0]):
        lanes = slice(i * LANES, (i + 1) * LANES)
        first = right[:, lanes]
        now = left[:, lanes]
        solution[:, lanes] = size_now * first + size_next * (now + ratio * first)
        image = noise[:, lanes] * now + total[i] + back * (first - now)
        residual[:, lanes] = now - size_next * image


def shape_of(*shape):
    return jax.ShapeDtypeStruct(shape, F32)


def on_device(n, right_sides, nugget, cov_blocks, block_rows, block_cols, block_count):
    rhs, width = right_sides.shape
    slots, tile_size = cov_blocks.shape[2:4]
    per = width // n // LANES
    data = per * rhs
    size = data + 8
    noise = nugget.reshape(1, width)
    index = (block_rows, block_cols, block_count)
    pair = pltpu.VMEM((width // tile_size, 2 * rhs, tile_size), BF16)
    total = pltpu.VMEM((width // LANES, rhs, LANES), F32)
    index_scratch = [pltpu.SMEM(item.shape, item.dtype) for item in index[:2]]
    index_sems = pltpu.SemaphoreType.DMA((2,))
    vmem = pl.BlockSpec(memory_space=pltpu.VMEM)
    any_spec = pl.BlockSpec(memory_space=pl.ANY)
    smem = pl.BlockSpec(memory_space=pltpu.SMEM)
    hbm = pl.BlockSpec(memory_space=pltpu.HBM)
    params = pltpu.CompilerParams(vmem_limit_bytes=16 * 1024 * 1024)
    cost = pl.CostEstimate(flops=4 * rhs * slots * tile_size * tile_size, transcendentals=0,
                           bytes_accessed=2 * slots * tile_size * tile_size)
    field = shape_of(rhs, width)
    plain = shape_of(data, LANES)
    tile = shape_of(8, LANES)
    payload = shape_of(size, LANES)

    def call(kernel, name, specs, outs, scratch, args, heavy=False):
        return pl.pallas_call(
            kernel,
            in_specs=specs,
            out_specs=jax.tree.map(lambda _: vmem, outs),
            out_shape=outs,
            scratch_shapes=scratch,
            compiler_params=params,
            cost_estimate=cost if heavy else None,
            name=name,
        )(*args)

    in_hbm = functools.partial(pltpu.with_memory_space_constraint, memory_space=pltpu.HBM)
    held = from_diagonal(right_sides, n)
    out = call(
        functools.partial(mirror_first_kernel, n, per), "mirror_first",
        [hbm] * 2 + [smem] + [hbm] * 2,
        [plain] * n + [jax.ShapeDtypeStruct(cov_blocks.shape[2:], cov_blocks.dtype)],
        index_scratch + [pltpu.VMEM((rhs, width), F32), pair, total, index_sems,
                         pltpu.SemaphoreType.DMA, pltpu.SemaphoreType.DMA((slots // GROUP,))],
        (*map(in_hbm, index[:2]), block_count, in_hbm(right_sides), in_hbm(cov_blocks)), True)
    mirror, blocks = to_owners(out[:n], "row", n), out[n]

    out = call(
        functools.partial(direct_first_kernel, n, per), "direct_first",
        [any_spec] * 2 + [smem] + [vmem] * (n + 2),
        [plain] * n + [tile, field],
        index_scratch + [pair, total, index_sems],
        (*index, *held, noise, blocks), True)
    direct, stats, far = to_owners(out[:n], "col", n), to_all(out[n], "row", n), out[n + 1]

    summed = call(sum_kernel, "sum_first", [vmem] * n, plain, [], mirror)
    other = transposed(summed, n)
    near, finished = call(
        functools.partial(combine_first_kernel, n, per), "combine_first",
        [vmem] * (2 * n + 3), [payload, plain], [],
        (right_sides, noise, other, *direct, *stats))
    near_parts = to_all(near, "col", n)
    far_parts = to_all(transposed(finished, n), "row", n)

    out = call(
        functools.partial(mirror_second_kernel, n, per), "mirror_second",
        [any_spec] * 2 + [smem] + [vmem] * (n + 2),
        [plain] * n + [field, tile],
        index_scratch + [pair, total, index_sems],
        (*index, right_sides, *near_parts, blocks), True)
    mirror, left, base = to_owners(out[:n], "row", n), out[n], out[n + 1]

    out = call(
        functools.partial(direct_second_kernel, n, per), "direct_second",
        [any_spec] * 2 + [smem] + [vmem] * (n + 5),
        [plain] * n + [tile],
        index_scratch + [pair, total, index_sems],
        (*index, far, left, noise, base, *far_parts, blocks), True)
    direct, stats = to_owners(out[:n], "col", n), to_all(out[n], "row", n)

    summed = call(sum_kernel, "sum_second", [vmem] * n, plain, [], mirror)
    other = transposed(summed, n)
    part = call(functools.partial(combine_second_kernel, n, data), "combine_second",
                [vmem] * (2 * n + 1), payload, [], (other, *direct, *stats))
    parts = to_all(part, "col", n)

    return tuple(call(functools.partial(last_kernel, n, per), "last",
                      [vmem] * (n + 4), [field, field], [total],
                      (right_sides, left, noise, base, *parts)))


def solution(mesh):
    n = mesh.shape["row"]
    assert n == mesh.shape["col"] and n & (n - 1) == 0
    placed = (
        P(None, ("groups", "row")),
        P(("groups", "row")),
        P(("groups", "row"), "col", None, None, None),
        P(("groups", "row"), "col", None),
        P(("groups", "row"), "col", None),
        P(("groups", "row"), "col"),
    )
    return jax.shard_map(
        functools.partial(on_device, n),
        mesh=mesh,
        in_specs=placed,
        out_specs=(P(None, ("groups", "row")), P(None, ("groups", "row"))),
        check_vma=False,
    )
```

time: 210 us -> 77.5 us (0.37)
  waiting for transfers between devices: 140 us -> 20.1 us
  starting transfers between devices: 0.35 us -> 48.8 us
  matrix products: 25.7 us -> 0 us
  between operations: 14.7 us -> 1.53 us
  blocking collectives: 11.3 us -> 0 us
  other arithmetic: 9.03 us -> 0 us
  local copies, waits for them, and re-layouts: 8.58 us -> 0.02 us
  Pallas kernels: 0 us -> 6.49 us
    psum x4 -> x0, waiting for transfers between devices: 140 us -> none  [the longest x2 71.3 us: on_device(): total = lax.psum(apply_direct, 'col')]
    ppermute x0 -> x33, starting transfers between devices: none -> 48.8 us  [the longest x27 39.8 us: shifted(): return lax.ppermute(value, axis, [(i, i ^ d) for i in range(n)])]
    dot_general x8 -> x0, matrix products: 25.7 us -> none  [the longest x2 12 us: on_device(): jnp.einsum('rmk,mjk->rmj', jnp.take(far_tiles, slot_cols, axis=1), blocks...]
    ppermute x0 -> x33, waiting for transfers between devices: none -> 20.1 us  [the longest x27 20.1 us: shifted(): return lax.ppermute(value, axis, [(i, i ^ d) for i in range(n)])]
    psum x2 -> x0, blocking collectives: 11.3 us -> none  [on_device(): lax.psum((jnp.sum(direction * applied, axis=1), jnp.sum(residual * applie...]
    pallas_call x0 -> x9, Pallas kernels: none -> 6.49 us  [call(): pl.pallas_call(kernel, in_specs=specs, out_specs=jax.tree.map(lambda _: v...]
    gather x4 -> x0, local copies, waits for them, and re-layouts: 4.37 us -> none  [the longest x2 3.14 us: on_device(): jnp.take(far_tiles, slot_cols, axis=1)]
    select_n x4 -> x0, other arithmetic: 2.71 us -> none  [the longest x2 2.05 us: from_root(): jnp.where(lax.axis_index(axis) == source, value, 0).astype(value.dtype)]
  transfers between devices with their start and end apart: 4 -> 33, of which waited for: 4 -> 12; matrix products, arithmetic and copies ran while one was open for 0% -> 0% of each run, Pallas kernels for 0% -> 7%
where the time goes in v2:
time: 77.5 us; the launch traced here: 76.9 us
  starting transfers between devices  48.8 us (63%)
  waiting for transfers between devices  20.1 us (26%)
  Pallas kernels  6.49 us (8%)
  between operations  1.53 us (2%)
    ppermute x27, starting transfers between devices, shifted(): return lax.ppermute(value, axis, [(i, i ^ d) for i in range(n)])  39.8 us
    ppermute x27, waiting for transfers between devices, shifted(): return lax.ppermute(value, axis, [(i, i ^ d) for i in range(n)])  20.1 us
    ppermute x3, starting transfers between devices, from_diagonal(): held.append(lax.ppermute(value, ('row', 'col'), pairs))  6.97 us
    pallas_call x9, Pallas kernels, call(): pl.pallas_call(kernel, in_specs=specs, out_specs=jax.tree.map(lambda _: v...  6.49 us
    ppermute x3, starting transfers between devices, transposed(): return lax.ppermute(value, ('row', 'col'), pairs)  1.99 us
  transfers between devices with their start and end apart: 33, of which 12 were waited for; matrix products, arithmetic and copies ran while one was open for 0% of the time, Pallas kernels for 7%

profile of v2, /device:TPU:0, one launch (start us, length us, event | category | flops | bytes accessed | tf_op | source)
XLA Modules:
  0.0 76.9 jit_solution(13363344753411783380)
XLA Ops:
  0.7 2.5 %collective-permute-start.4 = (f32[32,2048]{1,0:T(8,128)}, f32[32,2048]{1,0:T(8,128)S(1)}, u32[]{:S(2)}, u32[]{:S(2)}) collective-permute-start(f32[32,2048]{1,0:T(8,128)} %right.3), channel_id=1, source_target_pairs={{0,4},{5,1},{10,14},{15,11},{16,20},{21,17},{26,30},{31,27}} | collective-permute-start | bytes 786440 | tf_op jit(solution)/shard_map/ppermute | solution.py:38
  3.2 3.2 %collective-permute-start.5 = (f32[32,2048]{1,0:T(8,128)}, f32[32,2048]{1,0:T(8,128)S(1)}, u32[]{:S(2)}, u32[]{:S(2)}) collective-permute-start(f32[32,2048]{1,0:T(8,128)} %right.3), channel_id=1, source_target_pairs={{0,8},{5,13},{10,2},{15,7},{16,24},{21,29},{26,18},{31,23}} | collective-permute-start | bytes 786440 | tf_op jit(solution)/shard_map/ppermute | solution.py:38
  6.4 1.3 %collective-permute-start.6 = (f32[32,2048]{1,0:T(8,128)}, f32[32,2048]{1,0:T(8,128)S(1)}, u32[]{:S(2)}, u32[]{:S(2)}) collective-permute-start(f32[32,2048]{1,0:T(8,128)} %right.3), channel_id=1, source_target_pairs={{0,12},{5,9},{10,6},{15,3},{16,28},{21,25},{26,22},{31,19}} | collective-permute-start | bytes 786440 | tf_op jit(solution)/shard_map/ppermute | solution.py:38
  8.3 1.7 %mirror_first.1 = (f32[128,128]{1,0:T(8,128)S(1)}, f32[128,128]{1,0:T(8,128)S(1)}, f32[128,128]{1,0:T(8,128)S(1)}, f32[128,128]{1,0:T(8,128)S(1)}, bf16[32,256,256]{2,1,0:T(8,128)(2,1)S(1)}) custom-call(s32[1,1,32]{2,1,0:T(1,128)} %refs_0_.7, s32[1,1,32]{2,1,0:T(1,128)} %refs_1_.7, s32[1,1]{1,0:T(1,128)S(6)} %copy.8.refs_2_, f32[32,2048]{1,0:T(8,128)} %right.3, ...), custom_call_target="tpu_custom_call" | custom-call | flops 268435456 | bytes 4194304 | tf_op jit(solution)/shard_map/mirror_first/pallas_call | solution.py:317
  12.0 3.4 %collective-permute-done.1.refs_2_ = f32[128,128]{1,0:T(8,128)S(1)} collective-permute-done((f32[128,128]{1,0:T(8,128)S(1)}, f32[128,128]{1,0:T(8,128)S(1)}, u32[]{:S(2)}, u32[]{:S(2)}) %collective-permute-start.1) | collective-permute-done | bytes 65568 | tf_op jit(solution)/shard_map/ppermute | solution.py:18
  18.0 2.9 %collective-permute-start.7 = (f32[128,128]{1,0:T(8,128)S(1)}, f32[128,128]{1,0:T(8,128)S(1)}, u32[]{:S(2)}, u32[]{:S(2)}) collective-permute-start(f32[128,128]{1,0:T(8,128)S(1)} %get-tuple-element.32), channel_id=1, source_target_pairs={{0,1},{1,0},{2,3},{3,2},{4,5},{5,4},{6,7},{7,6},{8,9},{9,8},{10,11... | collective-permute-start | bytes 196616 | tf_op jit(solution)/shard_map/ppermute | solution.py:18
  20.9 4.1 %collective-permute-start.8 = (f32[128,128]{1,0:T(8,128)S(1)}, f32[128,128]{1,0:T(8,128)S(1)}, u32[]{:S(2)}, u32[]{:S(2)}) collective-permute-start(f32[128,128]{1,0:T(8,128)S(1)} %get-tuple-element.33), channel_id=1, source_target_pairs={{0,2},{1,3},{2,0},{3,1},{4,6},{5,7},{6,4},{7,5},{8,10},{9,11},{10,... | collective-permute-start | bytes 196616 | tf_op jit(solution)/shard_map/ppermute | solution.py:18
  25.0 4.8 %collective-permute-start.11 = (f32[8,128]{1,0:T(8,128)S(1)}, f32[8,128]{1,0:T(8,128)S(1)}, u32[]{:S(2)}, u32[]{:S(2)}) collective-permute-start(f32[8,128]{1,0:T(8,128)S(1)} %get-tuple-element.35.refs_4_), channel_id=1, source_target_pairs={{0,8},{4,12},{8,0},{12,4},{1,9},{5,13},{9,1},{13,5},{2,10},{6,14},... | collective-permute-start | bytes 12296 | tf_op jit(solution)/shard_map/ppermute | solution.py:18
  31.4 1.5 %collective-permute-done.12.refs_7_ = f32[8,128]{1,0:T(8,128)S(1)} collective-permute-done((f32[8,128]{1,0:T(8,128)S(1)}, f32[8,128]{1,0:T(8,128)S(1)}, u32[]{:S(2)}, u32[]{:S(2)}) %collective-permute-start.12) | collective-permute-done | bytes 4128 | tf_op jit(solution)/shard_map/ppermute | solution.py:18
  33.6 2.7 %collective-permute-start.13 = (f32[136,128]{1,0:T(8,128)S(1)}, f32[136,128]{1,0:T(8,128)S(1)}, u32[]{:S(2)}, u32[]{:S(2)}) collective-permute-start(f32[136,128]{1,0:T(8,128)S(1)} %get-tuple-element.36.refs_4_), channel_id=1, source_target_pairs={{0,1},{1,0},{2,3},{3,2},{4,5},{5,4},{6,7},{7,6},{8,9},{9,8},{10,11... | collective-permute-start | bytes 208904 | tf_op jit(solution)/shard_map/ppermute | solution.py:18
  36.3 3.2 %collective-permute-start.14 = (f32[136,128]{1,0:T(8,128)S(1)}, f32[136,128]{1,0:T(8,128)S(1)}, u32[]{:S(2)}, u32[]{:S(2)}) collective-permute-start(f32[136,128]{1,0:T(8,128)S(1)} %get-tuple-element.36.refs_4_), channel_id=1, source_target_pairs={{0,2},{1,3},{2,0},{3,1},{4,6},{5,7},{6,4},{7,5},{8,10},{9,11},{10,... | collective-permute-start | bytes 208904 | tf_op jit(solution)/shard_map/ppermute | solution.py:18
  39.6 4.7 %collective-permute-start.22 = (f32[128,128]{1,0:T(8,128)S(1)}, f32[128,128]{1,0:T(8,128)S(1)}, u32[]{:S(2)}, u32[]{:S(2)}) collective-permute-start(f32[128,128]{1,0:T(8,128)S(1)} %collective-permute-done.20.refs_7_), channel_id=1, source_target_pairs={{0,8},{4,12},{8,0},{12,4},{1,9},{5,13},{9,1},{13,5},{2,10},{6,14},... | collective-permute-start | bytes 196616 | tf_op jit(solution)/shard_map/ppermute | solution.py:18
  44.5 2.3 %collective-permute-done.14.refs_6_ = f32[136,128]{1,0:T(8,128)S(1)} collective-permute-done((f32[136,128]{1,0:T(8,128)S(1)}, f32[136,128]{1,0:T(8,128)S(1)}, u32[]{:S(2)}, u32[]{:S(2)}) %collective-permute-start.14) | collective-permute-done | bytes 69664 | tf_op jit(solution)/shard_map/ppermute | solution.py:18
  48.2 1.5 %collective-permute-start.18 = (f32[128,128]{1,0:T(8,128)S(1)}, f32[128,128]{1,0:T(8,128)S(1)}, u32[]{:S(2)}, u32[]{:S(2)}) collective-permute-start(f32[128,128]{1,0:T(8,128)S(1)} %get-tuple-element.42), channel_id=1, source_target_pairs={{0,12},{4,8},{8,4},{12,0},{1,13},{5,9},{9,5},{13,1},{2,14},{6,10},... | collective-permute-start | bytes 196616 | tf_op jit(solution)/shard_map/ppermute | solution.py:18
  50.9 1.5 %collective-permute-start.24 = (f32[128,128]{1,0:T(8,128)S(1)}, f32[128,128]{1,0:T(8,128)S(1)}, u32[]{:S(2)}, u32[]{:S(2)}) collective-permute-start(f32[128,128]{1,0:T(8,128)S(1)} %get-tuple-element.46), channel_id=1, source_target_pairs={{0,1},{1,0},{2,3},{3,2},{4,5},{5,4},{6,7},{7,6},{8,9},{9,8},{10,11... | collective-permute-start | bytes 196616 | tf_op jit(solution)/shard_map/ppermute | solution.py:18
  52.7 2.7 %collective-permute-start.26 = (f32[128,128]{1,0:T(8,128)S(1)}, f32[128,128]{1,0:T(8,128)S(1)}, u32[]{:S(2)}, u32[]{:S(2)}) collective-permute-start(f32[128,128]{1,0:T(8,128)S(1)} %get-tuple-element.48), channel_id=1, source_target_pairs={{0,3},{1,2},{2,1},{3,0},{4,7},{5,6},{6,5},{7,4},{8,11},{9,10},{10,... | collective-permute-start | bytes 196616 | tf_op jit(solution)/shard_map/ppermute | solution.py:18
  56.1 2.0 %collective-permute-start.27 = (f32[8,128]{1,0:T(8,128)S(1)}, f32[8,128]{1,0:T(8,128)S(1)}, u32[]{:S(2)}, u32[]{:S(2)}) collective-permute-start(f32[8,128]{1,0:T(8,128)S(1)} %get-tuple-element.49.refs_4_), channel_id=1, source_target_pairs={{0,4},{4,0},{8,12},{12,8},{1,5},{5,1},{9,13},{13,9},{2,6},{6,2},{1... | collective-permute-start | bytes 12296 | tf_op jit(solution)/shard_map/ppermute | solution.py:18
  58.9 2.0 %collective-permute-start.28 = (f32[8,128]{1,0:T(8,128)S(1)}, f32[8,128]{1,0:T(8,128)S(1)}, u32[]{:S(2)}, u32[]{:S(2)}) collective-permute-start(f32[8,128]{1,0:T(8,128)S(1)} %get-tuple-element.49.refs_4_), channel_id=1, source_target_pairs={{0,8},{4,12},{8,0},{12,4},{1,9},{5,13},{9,1},{13,5},{2,10},{6,14},... | collective-permute-start | bytes 12296 | tf_op jit(solution)/shard_map/ppermute | solution.py:18
  60.9 1.6 %collective-permute-done.28.refs_6_ = f32[8,128]{1,0:T(8,128)S(1)} collective-permute-done((f32[8,128]{1,0:T(8,128)S(1)}, f32[8,128]{1,0:T(8,128)S(1)}, u32[]{:S(2)}, u32[]{:S(2)}) %collective-permute-start.28) | collective-permute-done | bytes 4128 | tf_op jit(solution)/shard_map/ppermute | solution.py:18
  63.3 2.2 %collective-permute-done.29.refs_7_ = f32[8,128]{1,0:T(8,128)S(1)} collective-permute-done((f32[8,128]{1,0:T(8,128)S(1)}, f32[8,128]{1,0:T(8,128)S(1)}, u32[]{:S(2)}, u32[]{:S(2)}) %collective-permute-start.29) | collective-permute-done | bytes 4128 | tf_op jit(solution)/shard_map/ppermute | solution.py:18
  65.6 1.7 %collective-permute-start.30 = (f32[136,128]{1,0:T(8,128)S(1)}, f32[136,128]{1,0:T(8,128)S(1)}, u32[]{:S(2)}, u32[]{:S(2)}) collective-permute-start(f32[136,128]{1,0:T(8,128)S(1)} %combine_second.1.rest_0_), channel_id=1, source_target_pairs={{0,1},{1,0},{2,3},{3,2},{4,5},{5,4},{6,7},{7,6},{8,9},{9,8},{10,11... | collective-permute-start | bytes 208904 | tf_op jit(solution)/shard_map/ppermute | solution.py:18
  67.3 2.2 %collective-permute-start.31 = (f32[136,128]{1,0:T(8,128)S(1)}, f32[136,128]{1,0:T(8,128)S(1)}, u32[]{:S(2)}, u32[]{:S(2)}) collective-permute-start(f32[136,128]{1,0:T(8,128)S(1)} %combine_second.1.rest_0_), channel_id=1, source_target_pairs={{0,2},{1,3},{2,0},{3,1},{4,6},{5,7},{6,4},{7,5},{8,10},{9,11},{10,... | collective-permute-start | bytes 208904 | tf_op jit(solution)/shard_map/ppermute | solution.py:18
  70.3 4.5 %collective-permute-done.31.rest_2_ = f32[136,128]{1,0:T(8,128)S(1)} collective-permute-done((f32[136,128]{1,0:T(8,128)S(1)}, f32[136,128]{1,0:T(8,128)S(1)}, u32[]{:S(2)}, u32[]{:S(2)}) %collective-permute-start.31) | collective-permute-done | bytes 69664 | tf_op jit(solution)/shard_map/ppermute | solution.py:18
  75.7 1.3 %last.1 = (f32[32,2048]{1,0:T(8,128)}, f32[32,2048]{1,0:T(8,128)}) custom-call(f32[32,2048]{1,0:T(8,128)S(1)} %copy-done, f32[32,2048]{1,0:T(8,128)S(1)} %get-tuple-element.37.refs_4_.left, f32[1,2048]{1,0:T(1,128)S(1)} %bitcast.4, f32[8,128]{1,0:T(8,128)S(1)} %get-tuple-element.38.refs_6_.base, f32[136,128]{1,0:T(8,128)S(1)} %combine_second.1.rest_0_, ...), custom_call_target="tpu_custom_call" | custom-call | tf_op jit(solution)/shard_map/last/pallas_call | solution.py:317
  (59 shorter events, 14.0 us)
Async XLA Ops:
  0.7 16.1 %collective-permute-start.4 = (f32[32,2048]{1,0:T(8,128)}, f32[32,2048]{1,0:T(8,128)S(1)}, u32[]{:S(2)}, u32[]{:S(2)}) collective-permute-start(f32[32,2048]{1,0:T(8,128)} %right.3), channel_id=1, source_target_pairs={{0,4},{5,1},{10,14},{15,11},{16,20},{21,17},{26,30},{31,27}} | collective-permute-start | bytes 786440 | tf_op jit(solution)/shard_map/ppermute | solution.py:38
  3.2 13.6 %collective-permute-start.5 = (f32[32,2048]{1,0:T(8,128)}, f32[32,2048]{1,0:T(8,128)S(1)}, u32[]{:S(2)}, u32[]{:S(2)}) collective-permute-start(f32[32,2048]{1,0:T(8,128)} %right.3), channel_id=1, source_target_pairs={{0,8},{5,13},{10,2},{15,7},{16,24},{21,29},{26,18},{31,23}} | collective-permute-start | bytes 786440 | tf_op jit(solution)/shard_map/ppermute | solution.py:38
  6.4 10.4 %collective-permute-start.6 = (f32[32,2048]{1,0:T(8,128)}, f32[32,2048]{1,0:T(8,128)S(1)}, u32[]{:S(2)}, u32[]{:S(2)}) collective-permute-start(f32[32,2048]{1,0:T(8,128)} %right.3), channel_id=1, source_target_pairs={{0,12},{5,9},{10,6},{15,3},{16,28},{21,25},{26,22},{31,19}} | collective-permute-start | bytes 786440 | tf_op jit(solution)/shard_map/ppermute | solution.py:38
  10.1 5.2 %collective-permute-start.1 = (f32[128,128]{1,0:T(8,128)S(1)}, f32[128,128]{1,0:T(8,128)S(1)}, u32[]{:S(2)}, u32[]{:S(2)}) collective-permute-start(f32[128,128]{1,0:T(8,128)S(1)} %get-tuple-element.28), channel_id=1, source_target_pairs={{0,8},{4,12},{8,0},{12,4},{1,9},{5,13},{9,1},{13,5},{2,10},{6,14},... | collective-permute-start | bytes 196616 | tf_op jit(solution)/shard_map/ppermute | solution.py:18
  16.1 9.0 %collective-permute-start.3 = (f32[128,128]{1,0:T(8,128)S(1)}, f32[128,128]{1,0:T(8,128)S(1)}, u32[]{:S(2)}, u32[]{:S(2)}) collective-permute-start(f32[128,128]{1,0:T(8,128)S(1)} %sum_first.1), channel_id=1, source_target_pairs={{0,0},{1,4},{2,8},{3,12},{4,1},{5,5},{6,9},{7,13},{8,2},{9,6},{10,... | collective-permute-start | bytes 196616 | tf_op jit(solution)/shard_map/ppermute | solution.py:31
  18.0 14.9 %collective-permute-start.7 = (f32[128,128]{1,0:T(8,128)S(1)}, f32[128,128]{1,0:T(8,128)S(1)}, u32[]{:S(2)}, u32[]{:S(2)}) collective-permute-start(f32[128,128]{1,0:T(8,128)S(1)} %get-tuple-element.32), channel_id=1, source_target_pairs={{0,1},{1,0},{2,3},{3,2},{4,5},{5,4},{6,7},{7,6},{8,9},{9,8},{10,11... | collective-permute-start | bytes 196616 | tf_op jit(solution)/shard_map/ppermute | solution.py:18
  20.9 12.0 %collective-permute-start.8 = (f32[128,128]{1,0:T(8,128)S(1)}, f32[128,128]{1,0:T(8,128)S(1)}, u32[]{:S(2)}, u32[]{:S(2)}) collective-permute-start(f32[128,128]{1,0:T(8,128)S(1)} %get-tuple-element.33), channel_id=1, source_target_pairs={{0,2},{1,3},{2,0},{3,1},{4,6},{5,7},{6,4},{7,5},{8,10},{9,11},{10,... | collective-permute-start | bytes 196616 | tf_op jit(solution)/shard_map/ppermute | solution.py:18
  25.0 7.8 %collective-permute-start.9 = (f32[128,128]{1,0:T(8,128)S(1)}, f32[128,128]{1,0:T(8,128)S(1)}, u32[]{:S(2)}, u32[]{:S(2)}) collective-permute-start(f32[128,128]{1,0:T(8,128)S(1)} %get-tuple-element.34), channel_id=1, source_target_pairs={{0,3},{1,2},{2,1},{3,0},{4,7},{5,6},{6,5},{7,4},{8,11},{9,10},{10,... | collective-permute-start | bytes 196616 | tf_op jit(solution)/shard_map/ppermute | solution.py:18
  25.0 6.4 %collective-permute-start.11 = (f32[8,128]{1,0:T(8,128)S(1)}, f32[8,128]{1,0:T(8,128)S(1)}, u32[]{:S(2)}, u32[]{:S(2)}) collective-permute-start(f32[8,128]{1,0:T(8,128)S(1)} %get-tuple-element.35.refs_4_), channel_id=1, source_target_pairs={{0,8},{4,12},{8,0},{12,4},{1,9},{5,13},{9,1},{13,5},{2,10},{6,14},... | collective-permute-start | bytes 12296 | tf_op jit(solution)/shard_map/ppermute | solution.py:18
  32.9 6.6 %collective-permute-start.20 = (f32[128,128]{1,0:T(8,128)S(1)}, f32[128,128]{1,0:T(8,128)S(1)}, u32[]{:S(2)}, u32[]{:S(2)}) collective-permute-start(f32[128,128]{1,0:T(8,128)S(1)} %get-tuple-element.44), channel_id=1, source_target_pairs={{0,0},{1,4},{2,8},{3,12},{4,1},{5,5},{6,9},{7,13},{8,2},{9,6},{10,... | collective-permute-start | bytes 196616 | tf_op jit(solution)/shard_map/ppermute | solution.py:31
  33.6 10.7 %collective-permute-start.13 = (f32[136,128]{1,0:T(8,128)S(1)}, f32[136,128]{1,0:T(8,128)S(1)}, u32[]{:S(2)}, u32[]{:S(2)}) collective-permute-start(f32[136,128]{1,0:T(8,128)S(1)} %get-tuple-element.36.refs_4_), channel_id=1, source_target_pairs={{0,1},{1,0},{2,3},{3,2},{4,5},{5,4},{6,7},{7,6},{8,9},{9,8},{10,11... | collective-permute-start | bytes 208904 | tf_op jit(solution)/shard_map/ppermute | solution.py:18
  36.3 10.4 %collective-permute-start.14 = (f32[136,128]{1,0:T(8,128)S(1)}, f32[136,128]{1,0:T(8,128)S(1)}, u32[]{:S(2)}, u32[]{:S(2)}) collective-permute-start(f32[136,128]{1,0:T(8,128)S(1)} %get-tuple-element.36.refs_4_), channel_id=1, source_target_pairs={{0,2},{1,3},{2,0},{3,1},{4,6},{5,7},{6,4},{7,5},{8,10},{9,11},{10,... | collective-permute-start | bytes 208904 | tf_op jit(solution)/shard_map/ppermute | solution.py:18
  39.5 7.2 %collective-permute-start.15 = (f32[136,128]{1,0:T(8,128)S(1)}, f32[136,128]{1,0:T(8,128)S(1)}, u32[]{:S(2)}, u32[]{:S(2)}) collective-permute-start(f32[136,128]{1,0:T(8,128)S(1)} %get-tuple-element.36.refs_4_), channel_id=1, source_target_pairs={{0,3},{1,2},{2,1},{3,0},{4,7},{5,6},{6,5},{7,4},{8,11},{9,10},{10,... | collective-permute-start | bytes 208904 | tf_op jit(solution)/shard_map/ppermute | solution.py:18
  39.6 8.7 %collective-permute-start.21 = (f32[128,128]{1,0:T(8,128)S(1)}, f32[128,128]{1,0:T(8,128)S(1)}, u32[]{:S(2)}, u32[]{:S(2)}) collective-permute-start(f32[128,128]{1,0:T(8,128)S(1)} %collective-permute-done.20.refs_7_), channel_id=1, source_target_pairs={{0,4},{4,0},{8,12},{12,8},{1,5},{5,1},{9,13},{13,9},{2,6},{6,2},{1... | collective-permute-start | bytes 196616 | tf_op jit(solution)/shard_map/ppermute | solution.py:18
  39.6 10.2 %collective-permute-start.22 = (f32[128,128]{1,0:T(8,128)S(1)}, f32[128,128]{1,0:T(8,128)S(1)}, u32[]{:S(2)}, u32[]{:S(2)}) collective-permute-start(f32[128,128]{1,0:T(8,128)S(1)} %collective-permute-done.20.refs_7_), channel_id=1, source_target_pairs={{0,8},{4,12},{8,0},{12,4},{1,9},{5,13},{9,1},{13,5},{2,10},{6,14},... | collective-permute-start | bytes 196616 | tf_op jit(solution)/shard_map/ppermute | solution.py:18
  44.3 5.4 %collective-permute-start.23 = (f32[128,128]{1,0:T(8,128)S(1)}, f32[128,128]{1,0:T(8,128)S(1)}, u32[]{:S(2)}, u32[]{:S(2)}) collective-permute-start(f32[128,128]{1,0:T(8,128)S(1)} %collective-permute-done.20.refs_7_), channel_id=1, source_target_pairs={{0,12},{4,8},{8,4},{12,0},{1,13},{5,9},{9,5},{13,1},{2,14},{6,10},... | collective-permute-start | bytes 196616 | tf_op jit(solution)/shard_map/ppermute | solution.py:18
  47.9 7.5 %collective-permute-start.17 = (f32[128,128]{1,0:T(8,128)S(1)}, f32[128,128]{1,0:T(8,128)S(1)}, u32[]{:S(2)}, u32[]{:S(2)}) collective-permute-start(f32[128,128]{1,0:T(8,128)S(1)} %get-tuple-element.41), channel_id=1, source_target_pairs={{0,8},{4,12},{8,0},{12,4},{1,9},{5,13},{9,1},{13,5},{2,10},{6,14},... | collective-permute-start | bytes 196616 | tf_op jit(solution)/shard_map/ppermute | solution.py:18
  48.2 7.2 %collective-permute-start.18 = (f32[128,128]{1,0:T(8,128)S(1)}, f32[128,128]{1,0:T(8,128)S(1)}, u32[]{:S(2)}, u32[]{:S(2)}) collective-permute-start(f32[128,128]{1,0:T(8,128)S(1)} %get-tuple-element.42), channel_id=1, source_target_pairs={{0,12},{4,8},{8,4},{12,0},{1,13},{5,9},{9,5},{13,1},{2,14},{6,10},... | collective-permute-start | bytes 196616 | tf_op jit(solution)/shard_map/ppermute | solution.py:18
  50.9 14.6 %collective-permute-start.24 = (f32[128,128]{1,0:T(8,128)S(1)}, f32[128,128]{1,0:T(8,128)S(1)}, u32[]{:S(2)}, u32[]{:S(2)}) collective-permute-start(f32[128,128]{1,0:T(8,128)S(1)} %get-tuple-element.46), channel_id=1, source_target_pairs={{0,1},{1,0},{2,3},{3,2},{4,5},{5,4},{6,7},{7,6},{8,9},{9,8},{10,11... | collective-permute-start | bytes 196616 | tf_op jit(solution)/shard_map/ppermute | solution.py:18
  52.4 13.1 %collective-permute-start.25 = (f32[128,128]{1,0:T(8,128)S(1)}, f32[128,128]{1,0:T(8,128)S(1)}, u32[]{:S(2)}, u32[]{:S(2)}) collective-permute-start(f32[128,128]{1,0:T(8,128)S(1)} %get-tuple-element.47), channel_id=1, source_target_pairs={{0,2},{1,3},{2,0},{3,1},{4,6},{5,7},{6,4},{7,5},{8,10},{9,11},{10,... | collective-permute-start | bytes 196616 | tf_op jit(solution)/shard_map/ppermute | solution.py:18
  52.7 12.9 %collective-permute-start.26 = (f32[128,128]{1,0:T(8,128)S(1)}, f32[128,128]{1,0:T(8,128)S(1)}, u32[]{:S(2)}, u32[]{:S(2)}) collective-permute-start(f32[128,128]{1,0:T(8,128)S(1)} %get-tuple-element.48), channel_id=1, source_target_pairs={{0,3},{1,2},{2,1},{3,0},{4,7},{5,6},{6,5},{7,4},{8,11},{9,10},{10,... | collective-permute-start | bytes 196616 | tf_op jit(solution)/shard_map/ppermute | solution.py:18
  55.4 10.1 %collective-permute-start.19 = (f32[128,128]{1,0:T(8,128)S(1)}, f32[128,128]{1,0:T(8,128)S(1)}, u32[]{:S(2)}, u32[]{:S(2)}) collective-permute-start(f32[128,128]{1,0:T(8,128)S(1)} %sum_second.1), channel_id=1, source_target_pairs={{0,0},{1,4},{2,8},{3,12},{4,1},{5,5},{6,9},{7,13},{8,2},{9,6},{10,... | collective-permute-start | bytes 196616 | tf_op jit(solution)/shard_map/ppermute | solution.py:31
  67.3 7.5 %collective-permute-start.31 = (f32[136,128]{1,0:T(8,128)S(1)}, f32[136,128]{1,0:T(8,128)S(1)}, u32[]{:S(2)}, u32[]{:S(2)}) collective-permute-start(f32[136,128]{1,0:T(8,128)S(1)} %combine_second.1.rest_0_), channel_id=1, source_target_pairs={{0,2},{1,3},{2,0},{3,1},{4,6},{5,7},{6,4},{7,5},{8,10},{9,11},{10,... | collective-permute-start | bytes 208904 | tf_op jit(solution)/shard_map/ppermute | solution.py:18
  69.5 6.2 %collective-permute-start.32 = (f32[136,128]{1,0:T(8,128)S(1)}, f32[136,128]{1,0:T(8,128)S(1)}, u32[]{:S(2)}, u32[]{:S(2)}) collective-permute-start(f32[136,128]{1,0:T(8,128)S(1)} %combine_second.1.rest_0_), channel_id=1, source_target_pairs={{0,3},{1,2},{2,1},{3,0},{4,7},{5,6},{6,5},{7,4},{8,11},{9,10},{10,... | collective-permute-start | bytes 208904 | tf_op jit(solution)/shard_map/ppermute | solution.py:18
  (13 other events, 97.4 us)

commit v3 on v2

v3 whole, which is shorter than its diff:
```python
import functools

import jax
import jax.numpy as jnp
from jax import lax
from jax.experimental import pallas as pl
from jax.experimental.pallas import tpu as pltpu
from jax.sharding import PartitionSpec as P

ITERS = 2
LANES = 128
GROUP = 8
BF16 = jnp.bfloat16
F32 = jnp.float32


def swapped(values, axis):
    return lax.all_to_all(values, axis, 0, 0)


def transposed(value, n):
    pairs = [(r * n + c, c * n + r) for r in range(n) for c in range(n)]
    return lax.ppermute(value, ("row", "col"), pairs)


def from_diagonal(value, n):
    held = [value]
    for o in range(1, n):
        pairs = [(c * n + c, (c ^ o) * n + c) for c in range(n)]
        held.append(lax.ppermute(value, ("row", "col"), pairs))
    return held


def load_pair(dst, tile, value):
    rhs = value.shape[0]
    high = value.astype(BF16)
    dst[tile, :rhs, :] = high
    dst[tile, rhs:, :] = (value - high.astype(F32)).astype(BF16)


def product(pair, block, contract):
    both = lax.dot_general(pair, block, (((1,), (contract,)), ((), ())), preferred_element_type=F32)
    rhs = both.shape[0] // 2
    return both[:rhs] + both[rhs:]


def pack_stats(columns, rhs):
    lane = lax.broadcasted_iota(jnp.int32, (8, LANES), 1)
    tile = jnp.zeros((8, LANES), F32)
    groups = rhs // 8
    for i, column in enumerate(columns):
        for g in range(groups):
            tile = jnp.where(lane == i * groups + g, column[g * 8:(g + 1) * 8], tile)
    return tile


def unpack_stat(tile, i, rhs):
    groups = rhs // 8
    return jnp.concatenate([tile[:, i * groups + g:i * groups + g + 1] for g in range(groups)], axis=0)


def accumulate(total, tile, value):
    width = value.shape[1] // LANES
    for part in range(width):
        total[tile * width + part] += value[:, part * LANES:(part + 1) * LANES]


def add_blocks(blocks, slot_rows, slot_cols, live, pairs, total, mirror, ready=None):
    read, write, contract = (slot_rows, slot_cols, 0) if mirror else (slot_cols, slot_rows, 1)

    def body(step, carry):
        if ready is not None:
            ready(step)
        values = []
        for g in range(GROUP):
            slot = step * GROUP + g
            value = product(pairs[read[0, 0, slot]], blocks[slot], contract)
            values.append((write[0, 0, slot], jnp.where(slot < live, value, 0.0)))
        for tile, value in values:
            accumulate(total, tile, value)
        return carry

    lax.fori_loop(0, (live + GROUP - 1) // GROUP, body, 0)


def write_chunks(out, total, per, rhs):
    for j in range(out.shape[0]):
        for i in range(per):
            out[j, i * rhs:(i + 1) * rhs, :] = total[j * per + i]


def image_part(parts, i, per, rhs):
    return parts[i // per, (i % per) * rhs:(i % per + 1) * rhs, :]


def row_sums(value):
    return jnp.sum(value, axis=1, keepdims=True)


def cross_sums(total, value):
    rhs = value.shape[0]
    cross = jnp.zeros((rhs, LANES), F32)
    for i in range(total.shape[0]):
        cross += total[i] * value[:, i * LANES:(i + 1) * LANES]
    return row_sums(cross)


def fetch_index(sources, targets, sems):
    copies = [pltpu.make_async_copy(s, t, sems.at[i]) for i, (s, t) in enumerate(zip(sources, targets))]
    for copy in copies:
        copy.start()
    return copies


def mirror_first_kernel(per, *refs):
    rows_hbm, cols_hbm, count, right_hbm, cov, out, blocks = refs[:7]
    slot_rows, slot_cols, right, pairs, total, index_sems, right_sem, block_sems = refs[7:]
    slots, tile_size = blocks.shape[:2]
    rhs = right.shape[0]

    def block_copy(i):
        part = pl.ds(i * GROUP, GROUP)
        return pltpu.make_async_copy(cov.at[0, 0, part], blocks.at[part], block_sems.at[i])

    copies = fetch_index((rows_hbm, cols_hbm), (slot_rows, slot_cols), index_sems)
    load = pltpu.make_async_copy(right_hbm, right, right_sem)
    load.start()
    live = count[0, 0]
    for i in range(slots // GROUP):
        @pl.when(i * GROUP < live)
        def _():
            block_copy(i).start()
    total[...] = jnp.zeros_like(total)
    for copy in copies:
        copy.wait()
    load.wait()
    for tile in range(right.shape[1] // tile_size):
        load_pair(pairs, tile, right[:, tile * tile_size:(tile + 1) * tile_size])
    add_blocks(blocks, slot_rows, slot_cols, live, pairs, total, True, lambda i: block_copy(i).wait())
    write_chunks(out, total, per, rhs)


def direct_first_kernel(n, per, *refs):
    rows_any, cols_any, count, noise, blocks = refs[:5]
    held, (out, far), scratch = refs[5:5 + n], refs[5 + n:7 + n], refs[7 + n:]
    slot_rows, slot_cols, pairs, total, index_sems = scratch
    tile_size = blocks.shape[1]
    rhs, width = far.shape
    copies = fetch_index((rows_any, cols_any), (slot_rows, slot_cols), index_sems)
    offset = lax.axis_index("row") ^ lax.axis_index("col")
    for o in range(n):
        @pl.when(offset == o)
        def _():
            for tile in range(width // tile_size):
                value = held[o][:, tile * tile_size:(tile + 1) * tile_size]
                load_pair(pairs, tile, value)
                far[:, tile * tile_size:(tile + 1) * tile_size] = value
    total[...] = jnp.zeros_like(total)
    for copy in copies:
        copy.wait()
    add_blocks(blocks, slot_rows, slot_cols, count[0, 0], pairs, total, False)
    write_chunks(out, total, per, rhs)
    right = held[0][...]
    square = right * right
    share = 1.0 / n
    norm = share * row_sums(square)
    bend = share * row_sums(square * noise[...]) + 2.0 * cross_sums(total, right)
    tile = pack_stats([norm, bend], rhs)
    for j in range(n):
        out[j, per * rhs:, :] = tile


def sum_kernel(parts, *outs):
    value = jnp.sum(parts[...], axis=0)
    first = 0
    for out in outs:
        out[...] = value[first:first + out.shape[0]]
        first += out.shape[0]


def combine_first_kernel(n, per, right, noise, other, direct, near, finished, stat):
    rhs = right.shape[0]
    data = per * rhs
    width = per * LANES
    value = jnp.sum(direct[...], axis=0)
    stat[...] = value[data:]
    finished[...] = value[:data] + other[...]
    me = lax.axis_index("col")
    for k in range(n):
        @pl.when(me == k)
        def _():
            for i in range(per):
                lanes = slice(k * width + i * LANES, k * width + (i + 1) * LANES)
                finished[i * rhs:(i + 1) * rhs, :] += right[:, lanes] * noise[:, lanes]
    for j in range(n):
        near[j] = finished[...]


def repeat_kernel(n, chunk, stat, out):
    data = chunk.shape[0]
    for j in range(n):
        out[j, :data, :] = chunk[...]
        out[j, data:, :] = stat[...]


def second_kernel(per, *refs):
    rows_any, cols_any, count, right, far, noise, near_parts, far_parts, blocks = refs[:9]
    direct, mirror, left, base = refs[9:13]
    slot_rows, slot_cols, near_pairs, far_pairs, direct_total, mirror_total, index_sems = refs[13:]
    copies = fetch_index((rows_any, cols_any), (slot_rows, slot_cols), index_sems)
    tile_size = blocks.shape[1]
    pieces = tile_size // LANES
    rhs, width = right.shape
    data = per * rhs
    stat = jnp.sum(far_parts[:, data:, :], axis=0)
    base[...] = stat
    size_now = unpack_stat(stat, 0, rhs) / unpack_stat(stat, 1, rhs)
    for tile in range(width // tile_size):
        lanes = slice(tile * tile_size, (tile + 1) * tile_size)
        image = [image_part(near_parts, tile * pieces + i, per, rhs) for i in range(pieces)]
        value = right[:, lanes] - size_now * jnp.concatenate(image, axis=1)
        left[:, lanes] = value
        load_pair(near_pairs, tile, value)
        image = [image_part(far_parts, tile * pieces + i, per, rhs) for i in range(pieces)]
        load_pair(far_pairs, tile, far[:, lanes] - size_now * jnp.concatenate(image, axis=1))
    direct_total[...] = jnp.zeros_like(direct_total)
    mirror_total[...] = jnp.zeros_like(mirror_total)
    for copy in copies:
        copy.wait()
    live = count[0, 0]
    add_blocks(blocks, slot_rows, slot_cols, live, near_pairs, mirror_total, True)
    add_blocks(blocks, slot_rows, slot_cols, live, far_pairs, direct_total, False)
    write_chunks(mirror, mirror_total, per, rhs)
    write_chunks(direct, direct_total, per, rhs)
    value = left[...]
    square = value * value
    cross = 2.0 * cross_sums(direct_total, value)
    tile = pack_stats([row_sums(square), row_sums(square * noise[...]), cross], rhs)
    for j in range(mirror.shape[0]):
        mirror[j, data:, :] = tile


def combine_second_kernel(n, other, stat, direct, out):
    data = other.shape[0]
    value = jnp.sum(direct[...], axis=0) + other[...]
    for j in range(n):
        out[j, :data, :] = value
        out[j, data:, :] = stat[...]


def last_kernel(per, right, left, noise, base, parts, solution, residual):
    rhs, width = right.shape
    data = per * rhs
    norm = unpack_stat(base[...], 0, rhs)
    size_now = norm / unpack_stat(base[...], 1, rhs)
    norm_next = unpack_stat(parts[0, data:, :], 0, rhs)
    cross = unpack_stat(jnp.sum(parts[:, data:, :], axis=0), 2, rhs)
    bend = unpack_stat(parts[0, data:, :], 1, rhs) + cross
    ratio = norm_next / norm
    size_next = norm_next / (bend - ratio * norm_next / size_now)
    back = ratio / size_now
    for i in range(width // LANES):
        lanes = slice(i * LANES, (i + 1) * LANES)
        first = right[:, lanes]
        now = left[:, lanes]
        solution[:, lanes] = size_now * first + size_next * (now + ratio * first)
        image = noise[:, lanes] * now + image_part(parts, i, per, rhs) + back * (first - now)
        residual[:, lanes] = now - size_next * image


def shape_of(*shape):
    return jax.ShapeDtypeStruct(shape, F32)


def on_device(n, right_sides, nugget, cov_blocks, block_rows, block_cols, block_count):
    rhs, width = right_sides.shape
    slots, tile_size = cov_blocks.shape[2:4]
    per = width // n // LANES
    data = per * rhs
    size = data + 8
    noise = nugget.reshape(1, width)
    index = (block_rows, block_cols, block_count)
    pair = pltpu.VMEM((width // tile_size, 2 * rhs, tile_size), BF16)
    total = pltpu.VMEM((width // LANES, rhs, LANES), F32)
    index_scratch = [pltpu.SMEM(item.shape, item.dtype) for item in index[:2]]
    index_sems = pltpu.SemaphoreType.DMA((2,))
    vmem = pl.BlockSpec(memory_space=pltpu.VMEM)
    any_spec = pl.BlockSpec(memory_space=pl.ANY)
    smem = pl.BlockSpec(memory_space=pltpu.SMEM)
    hbm = pl.BlockSpec(memory_space=pltpu.HBM)
    params = pltpu.CompilerParams(vmem_limit_bytes=16 * 1024 * 1024)
    cost = pl.CostEstimate(flops=4 * rhs * slots * tile_size * tile_size, transcendentals=0,
                           bytes_accessed=2 * slots * tile_size * tile_size)
    field = shape_of(rhs, width)
    chunk = shape_of(data, LANES)
    tile = shape_of(8, LANES)
    chunks = shape_of(n, data, LANES)
    loaded = shape_of(n, size, LANES)

    def call(kernel, name, specs, outs, scratch, args, heavy=False):
        return pl.pallas_call(
            kernel,
            in_specs=specs,
            out_specs=jax.tree.map(lambda _: vmem, outs),
            out_shape=outs,
            scratch_shapes=scratch,
            compiler_params=params,
            cost_estimate=cost if heavy else None,
            name=name,
        )(*args)

    in_hbm = functools.partial(pltpu.with_memory_space_constraint, memory_space=pltpu.HBM)
    held = from_diagonal(right_sides, n)
    mirror, blocks = call(
        functools.partial(mirror_first_kernel, per), "mirror_first",
        [hbm] * 2 + [smem] + [hbm] * 2,
        [chunks, jax.ShapeDtypeStruct(cov_blocks.shape[2:], cov_blocks.dtype)],
        index_scratch + [pltpu.VMEM((rhs, width), F32), pair, total, index_sems,
                         pltpu.SemaphoreType.DMA, pltpu.SemaphoreType.DMA((slots // GROUP,))],
        (*map(in_hbm, index[:2]), block_count, in_hbm(right_sides), in_hbm(cov_blocks)), True)
    summed, = call(sum_kernel, "sum_first", [vmem], [chunk], [], (swapped(mirror, "row"),))
    other = transposed(summed, n)
    direct, far = call(
        functools.partial(direct_first_kernel, n, per), "direct_first",
        [any_spec] * 2 + [smem] + [vmem] * (n + 2),
        [loaded, field],
        index_scratch + [pair, total, index_sems],
        (*index, noise, blocks, *held), True)
    near, finished, stat = call(
        functools.partial(combine_first_kernel, n, per), "combine_first",
        [vmem] * 4, [chunks, chunk, tile], [],
        (right_sides, noise, other, swapped(direct, "col")))
    near_parts = swapped(near, "col")
    repeated, = call(functools.partial(repeat_kernel, n), "repeat_far", [vmem] * 2, [loaded], [],
                     (transposed(finished, n), stat))
    far_parts = swapped(repeated, "row")

    direct, mirror, left, base = call(
        functools.partial(second_kernel, per), "both_second",
        [any_spec] * 2 + [smem] + [vmem] * 6,
        [chunks, loaded, field, tile],
        index_scratch + [pair, pair, total, total, index_sems],
        (*index, right_sides, far, noise, near_parts, far_parts, blocks), True)
    summed, stat = call(sum_kernel, "sum_second", [vmem], [chunk, tile], [], (swapped(mirror, "row"),))
    other = transposed(summed, n)
    part, = call(functools.partial(combine_second_kernel, n), "combine_second",
                 [vmem] * 3, [loaded], [], (other, stat, swapped(direct, "col")))
    return tuple(call(functools.partial(last_kernel, per), "last", [vmem] * 5, [field, field], [],
                      (right_sides, left, noise, base, swapped(part, "col"))))


def solution(mesh):
    n = mesh.shape["row"]
    assert n == mesh.shape["col"] and n & (n - 1) == 0
    placed = (
        P(None, ("groups", "row")),
        P(("groups", "row")),
        P(("groups", "row"), "col", None, None, None),
        P(("groups", "row"), "col", None),
        P(("groups", "row"), "col", None),
        P(("groups", "row"), "col"),
    )
    return jax.shard_map(
        functools.partial(on_device, n),
        mesh=mesh,
        in_specs=placed,
        out_specs=(P(None, ("groups", "row")), P(None, ("groups", "row"))),
        check_vma=False,
    )
```

time: 77.5 us -> 110 us (1.42)
  blocking collectives: 0 us -> 48.7 us
  starting transfers between devices: 48.8 us -> 19.3 us
  local copies, waits for them, and re-layouts: 0.02 us -> 6.31 us
  Pallas kernels: 6.49 us -> 11.5 us
  waiting for transfers between devices: 20.1 us -> 22.4 us
    all_to_all x0 -> x4, blocking collectives: none -> 48.7 us  [swapped(): return lax.all_to_all(values, axis, 0, 0)]
    ppermute x27 -> x0, starting transfers between devices: 39.8 us -> none  [shifted(): return lax.ppermute(value, axis, [(i, i ^ d) for i in range(n)])]
    all_to_all x0 -> x3, waiting for transfers between devices: none -> 22.3 us  [swapped(): return lax.all_to_all(values, axis, 0, 0)]
    ppermute x27 -> x0, waiting for transfers between devices: 20.1 us -> none  [shifted(): return lax.ppermute(value, axis, [(i, i ^ d) for i in range(n)])]
    all_to_all x0 -> x3, starting transfers between devices: none -> 10.3 us  [swapped(): return lax.all_to_all(values, axis, 0, 0)]
    unnamed x8 -> x14, local copies, waits for them, and re-layouts: 0.02 us -> 6.31 us
    pallas_call x9, Pallas kernels: 6.49 us -> 11.5 us  [call(): pl.pallas_call(kernel, in_specs=specs, out_specs=jax.tree.map(lambda _: v...]
  transfers between devices with their start and end apart: 33 -> 9, of which waited for: 12 -> 3; matrix products, arithmetic and copies ran while one was open for 0% -> 0% of each run, Pallas kernels for 7% -> 6%
where the time goes in v3:
time: 110 us
  blocking collectives  48.7 us (44%)
  waiting for transfers between devices  22.4 us (20%)
  starting transfers between devices  19.3 us (18%)
  Pallas kernels  11.5 us (10%)
  local copies, waits for them, and re-layouts  6.31 us (6%)
  between operations  1.54 us (1%)
    all_to_all x4, blocking collectives, swapped(): return lax.all_to_all(values, axis, 0, 0)  48.7 us
    all_to_all x3, waiting for transfers between devices, swapped(): return lax.all_to_all(values, axis, 0, 0)  22.3 us
    pallas_call x9, Pallas kernels, call(): pl.pallas_call(kernel, in_specs=specs, out_specs=jax.tree.map(lambda _: v...  11.5 us
    all_to_all x3, starting transfers between devices, swapped(): return lax.all_to_all(values, axis, 0, 0)  10.3 us
    ppermute x3, starting transfers between devices, from_diagonal(): held.append(lax.ppermute(value, ('row', 'col'), pairs))  7.04 us
    unnamed x14, local copies, waits for them, and re-layouts  6.31 us
  transfers between devices with their start and end apart: 9, of which 3 were waited for; matrix products, arithmetic and copies ran while one was open for 0% of the time, Pallas kernels for 6%

profile of v3, /device:TPU:0, one launch (start us, length us, event | category | flops | bytes accessed | tf_op | source)
XLA Modules:
  0.0 109.6 jit_solution(7372843841840273587)
XLA Ops:
  0.7 4.4 %collective-permute-start.2 = (f32[32,2048]{1,0:T(8,128)}, f32[32,2048]{1,0:T(8,128)S(1)}, u32[]{:S(2)}, u32[]{:S(2)}) collective-permute-start(f32[32,2048]{1,0:T(8,128)} %right.3), channel_id=1, source_target_pairs={{0,12},{5,9},{10,6},{15,3},{16,28},{21,25},{26,22},{31,19}} | collective-permute-start | bytes 786440 | tf_op jit(solution)/shard_map/ppermute | solution.py:30
  5.1 1.3 %collective-permute-start.1 = (f32[32,2048]{1,0:T(8,128)}, f32[32,2048]{1,0:T(8,128)S(1)}, u32[]{:S(2)}, u32[]{:S(2)}) collective-permute-start(f32[32,2048]{1,0:T(8,128)} %right.3), channel_id=1, source_target_pairs={{0,8},{5,13},{10,2},{15,7},{16,24},{21,29},{26,18},{31,23}} | collective-permute-start | bytes 786440 | tf_op jit(solution)/shard_map/ppermute | solution.py:30
  6.4 1.3 %collective-permute-start = (f32[32,2048]{1,0:T(8,128)}, f32[32,2048]{1,0:T(8,128)S(1)}, u32[]{:S(2)}, u32[]{:S(2)}) collective-permute-start(f32[32,2048]{1,0:T(8,128)} %right.3), channel_id=1, source_target_pairs={{0,4},{5,1},{10,14},{15,11},{16,20},{21,17},{26,30},{31,27}} | collective-permute-start | bytes 786440 | tf_op jit(solution)/shard_map/ppermute | solution.py:30
  8.4 3.6 %mirror_first.1 = (f32[4,128,128]{2,1,0:T(8,128)}, bf16[32,256,256]{2,1,0:T(8,128)(2,1)S(1)}) custom-call(s32[1,1,32]{2,1,0:T(1,128)} %refs_0_.5, s32[1,1,32]{2,1,0:T(1,128)} %refs_1_.5, s32[1,1]{1,0:T(1,128)S(6)} %copy.8.refs_2_, f32[32,2048]{1,0:T(8,128)} %right.3, bf16[1,1,32,256,256]{4,3,2,1,0:T(8,128)(2,1)} %refs_4_.1), custom_call_target="tpu_custom_call" | custom-call | flops 268435456 | bytes 4194304 | tf_op jit(solution)/shard_map/mirror_first/pallas_call | solution.py:301
  12.0 1.9 %copy-done = bf16[32,256,256]{2,1,0:T(8,128)(2,1)} copy-done((bf16[32,256,256]{2,1,0:T(8,128)(2,1)}, bf16[32,256,256]{2,1,0:T(8,128)(2,1)S(1)}, u32[]{:S(2)}) %copy-start) | copy-done | bytes 4194328
  14.0 3.4 %all-to-all-start = ((f32[4,128,128]{2,1,0:T(8,128)}), f32[4,128,128]{2,1,0:T(8,128)S(1)}, u32[]{:S(2)}, u32[]{:S(2)}) async-start(f32[4,128,128]{2,1,0:T(8,128)} %get-tuple-element.17), calls=%async_computation | async-start | bytes 524288 | tf_op jit(solution)/shard_map/all_to_all | solution.py:18
  17.5 2.2 %copy-done.1 = bf16[32,256,256]{2,1,0:T(8,128)(2,1)S(1)} copy-done((bf16[32,256,256]{2,1,0:T(8,128)(2,1)S(1)}, bf16[32,256,256]{2,1,0:T(8,128)(2,1)}, u32[]{:S(2)}) %copy-start.1) | copy-done | bytes 4194328
  19.6 2.8 %direct_first.1 = (f32[4,136,128]{2,1,0:T(8,128)}, f32[32,2048]{1,0:T(8,128)S(1)}) custom-call(s32[1,1,32]{2,1,0:T(1,128)S(1)} %copy-done.5, s32[1,1,32]{2,1,0:T(1,128)S(1)} %copy-done.6, s32[1,1]{1,0:T(1,128)S(6)} %copy.8.refs_2_, f32[1,2048]{1,0:T(1,128)S(1)} %bitcast.1, bf16[32,256,256]{2,1,0:T(8,128)(2,1)S(1)} %copy-done.1, f32[32,2048]{1,0:T(8,128)S(1)} %copy-done.3, ...), custom_call_target="tpu_custom_call" | custom-call | flops 268435456 | bytes 4194304 | tf_op jit(solution)/shard_map/direct_first/pallas_call | solution.py:301
  22.5 0.9 all-to-all-done.parts
  23.4 3.4 %all-to-all-start.1 = ((f32[4,136,128]{2,1,0:T(8,128)}), f32[4,136,128]{2,1,0:T(8,128)S(1)}, u32[]{:S(2)}, u32[]{:S(2)}) async-start(f32[4,136,128]{2,1,0:T(8,128)} %get-tuple-element.18), calls=%async_computation.1 | async-start | bytes 557056 | tf_op jit(solution)/shard_map/all_to_all | solution.py:18
  26.9 0.7 collective-permute-start.3
  27.5 10.7 %all-to-all-done.1.direct = f32[4,136,128]{2,1,0:T(8,128)S(1)} async-done(((f32[4,136,128]{2,1,0:T(8,128)}), f32[4,136,128]{2,1,0:T(8,128)S(1)}, u32[]{:S(2)}, u32[]{:S(2)}) %all-to-all-start.1) | async-done | bytes 278560 | tf_op jit(solution)/shard_map/all_to_all | solution.py:18
  38.3 0.1 combine_first.1
  38.3 0.7 collective-permute-start.4
  39.0 16.7 %all_to_all.35.refs_7_ = f32[4,136,128]{2,1,0:T(8,128)S(1)} all-to-all(f32[4,136,128]{2,1,0:T(8,128)S(1)} %repeat_far.1), channel_id=1, replica_groups=mesh['groups'=2,'row'=4,'col'=4] {'row'}, dimensions={0} | all-to-all | bytes 557056 | tf_op jit(solution)/shard_map/all_to_all | solution.py:18
  55.7 11.7 %all_to_all.36.refs_6_ = f32[4,128,128]{2,1,0:T(8,128)S(1)} all-to-all(f32[4,128,128]{2,1,0:T(8,128)S(1)} %get-tuple-element.19), channel_id=1, replica_groups=mesh['groups'=2,'row'=4,'col'=4] {'col'}, dimensions={0} | all-to-all | bytes 524288 | tf_op jit(solution)/shard_map/all_to_all | solution.py:18
  67.5 2.2 %copy-done.2 = bf16[32,256,256]{2,1,0:T(8,128)(2,1)S(1)} copy-done((bf16[32,256,256]{2,1,0:T(8,128)(2,1)S(1)}, bf16[32,256,256]{2,1,0:T(8,128)(2,1)}, u32[]{:S(2)}) %copy-start.2) | copy-done | bytes 4194328
  69.7 3.7 %both_second.1 = (f32[4,128,128]{2,1,0:T(8,128)}, f32[4,136,128]{2,1,0:T(8,128)S(1)}, f32[32,2048]{1,0:T(8,128)S(1)}, f32[8,128]{1,0:T(8,128)S(1)}) custom-call(s32[1,1,32]{2,1,0:T(1,128)S(1)} %copy-done.5, s32[1,1,32]{2,1,0:T(1,128)S(1)} %copy-done.6, s32[1,1]{1,0:T(1,128)S(6)} %copy.8.refs_2_, f32[32,2048]{1,0:T(8,128)S(1)} %copy-done.3, ...), custom_call_target="tpu_custom_call" | custom-call | flops 268435456 | bytes 4194304 | tf_op jit(solution)/shard_map/both_second/pallas_call | solution.py:301
  73.3 8.6 %all_to_all.37.parts = f32[4,136,128]{2,1,0:T(8,128)S(1)} all-to-all(f32[4,136,128]{2,1,0:T(8,128)S(1)} %get-tuple-element.24), channel_id=1, replica_groups=mesh['groups'=2,'row'=4,'col'=4] {'row'}, dimensions={0} | all-to-all | bytes 557056 | tf_op jit(solution)/shard_map/all_to_all | solution.py:18
  81.9 3.4 %all-to-all-start.5 = ((f32[4,128,128]{2,1,0:T(8,128)}), f32[4,128,128]{2,1,0:T(8,128)S(1)}, u32[]{:S(2)}, u32[]{:S(2)}) async-start(f32[4,128,128]{2,1,0:T(8,128)} %get-tuple-element.27), calls=%async_computation.5 | async-start | bytes 524288 | tf_op jit(solution)/shard_map/all_to_all | solution.py:18
  85.3 0.7 collective-permute-start.5
  86.0 10.7 %all-to-all-done.5.direct = f32[4,128,128]{2,1,0:T(8,128)S(1)} async-done(((f32[4,128,128]{2,1,0:T(8,128)}), f32[4,128,128]{2,1,0:T(8,128)S(1)}, u32[]{:S(2)}, u32[]{:S(2)}) %all-to-all-start.5) | async-done | bytes 262176 | tf_op jit(solution)/shard_map/all_to_all | solution.py:18
  96.7 11.7 %all_to_all.38.parts = f32[4,136,128]{2,1,0:T(8,128)S(1)} all-to-all(f32[4,136,128]{2,1,0:T(8,128)S(1)} %combine_second.1), channel_id=1, replica_groups=mesh['groups'=2,'row'=4,'col'=4] {'col'}, dimensions={0} | all-to-all | bytes 557056 | tf_op jit(solution)/shard_map/all_to_all | solution.py:18
  108.4 1.2 %last.1 = (f32[32,2048]{1,0:T(8,128)}, f32[32,2048]{1,0:T(8,128)}) custom-call(f32[32,2048]{1,0:T(8,128)S(1)} %copy-done.3, f32[32,2048]{1,0:T(8,128)S(1)} %get-tuple-element.22.left, f32[1,2048]{1,0:T(1,128)S(1)} %bitcast.4, f32[8,128]{1,0:T(8,128)S(1)} %get-tuple-element.23.base, f32[4,136,128]{2,1,0:T(8,128)S(1)} %all_to_all.38.parts), custom_call_target="tpu_custom_call" | custom-call | tf_op jit(solution)/shard_map/last/pallas_call | solution.py:301
  (21 shorter events, 0.1 us)
Async XLA Ops:
  0.6 16.8 %copy-start.3 = (f32[32,2048]{1,0:T(8,128)S(1)}, f32[32,2048]{1,0:T(8,128)}, u32[]{:S(2)}) copy-start(f32[32,2048]{1,0:T(8,128)} %right.3) | copy-start | bytes 786436
  0.6 16.8 %copy-start.6 = (s32[1,1,32]{2,1,0:T(1,128)S(1)}, s32[1,1,32]{2,1,0:T(1,128)}, u32[]{:S(2)}) copy-start(s32[1,1,32]{2,1,0:T(1,128)} %refs_1_.5) | copy-start | bytes 388
  0.7 16.8 %copy-start.5 = (s32[1,1,32]{2,1,0:T(1,128)S(1)}, s32[1,1,32]{2,1,0:T(1,128)}, u32[]{:S(2)}) copy-start(s32[1,1,32]{2,1,0:T(1,128)} %refs_0_.5) | copy-start | bytes 388
  0.7 16.8 %copy-start.4 = (f32[2048]{0:T(1024)S(1)}, f32[2048]{0:T(1024)}, u32[]{:S(2)}) copy-start(f32[2048]{0:T(1024)} %param.7) | copy-start | bytes 24580
  0.7 16.7 %collective-permute-start.2 = (f32[32,2048]{1,0:T(8,128)}, f32[32,2048]{1,0:T(8,128)S(1)}, u32[]{:S(2)}, u32[]{:S(2)}) collective-permute-start(f32[32,2048]{1,0:T(8,128)} %right.3), channel_id=1, source_target_pairs={{0,12},{5,9},{10,6},{15,3},{16,28},{21,25},{26,22},{31,19}} | collective-permute-start | bytes 786440 | tf_op jit(solution)/shard_map/ppermute | solution.py:30
  5.1 12.3 %collective-permute-start.1 = (f32[32,2048]{1,0:T(8,128)}, f32[32,2048]{1,0:T(8,128)S(1)}, u32[]{:S(2)}, u32[]{:S(2)}) collective-permute-start(f32[32,2048]{1,0:T(8,128)} %right.3), channel_id=1, source_target_pairs={{0,8},{5,13},{10,2},{15,7},{16,24},{21,29},{26,18},{31,23}} | collective-permute-start | bytes 786440 | tf_op jit(solution)/shard_map/ppermute | solution.py:30
  6.4 11.0 %collective-permute-start = (f32[32,2048]{1,0:T(8,128)}, f32[32,2048]{1,0:T(8,128)S(1)}, u32[]{:S(2)}, u32[]{:S(2)}) collective-permute-start(f32[32,2048]{1,0:T(8,128)} %right.3), channel_id=1, source_target_pairs={{0,4},{5,1},{10,14},{15,11},{16,20},{21,17},{26,30},{31,27}} | collective-permute-start | bytes 786440 | tf_op jit(solution)/shard_map/ppermute | solution.py:30
  12.0 1.9 %copy-start = (bf16[32,256,256]{2,1,0:T(8,128)(2,1)}, bf16[32,256,256]{2,1,0:T(8,128)(2,1)S(1)}, u32[]{:S(2)}) copy-start(bf16[32,256,256]{2,1,0:T(8,128)(2,1)S(1)} %get-tuple-element.15.refs_4_.refs_8_) | copy-start | bytes 12582916
  14.0 9.4 %all-to-all-start = ((f32[4,128,128]{2,1,0:T(8,128)}), f32[4,128,128]{2,1,0:T(8,128)S(1)}, u32[]{:S(2)}, u32[]{:S(2)}) async-start(f32[4,128,128]{2,1,0:T(8,128)} %get-tuple-element.17), calls=%async_computation | async-start | bytes 524288 | tf_op jit(solution)/shard_map/all_to_all | solution.py:18
  17.4 2.2 %copy-start.1 = (bf16[32,256,256]{2,1,0:T(8,128)(2,1)S(1)}, bf16[32,256,256]{2,1,0:T(8,128)(2,1)}, u32[]{:S(2)}) copy-start(bf16[32,256,256]{2,1,0:T(8,128)(2,1)} %copy-done) | copy-start | bytes 12582916
  23.4 14.9 %all-to-all-start.1 = ((f32[4,136,128]{2,1,0:T(8,128)}), f32[4,136,128]{2,1,0:T(8,128)S(1)}, u32[]{:S(2)}, u32[]{:S(2)}) async-start(f32[4,136,128]{2,1,0:T(8,128)} %get-tuple-element.18), calls=%async_computation.1 | async-start | bytes 557056 | tf_op jit(solution)/shard_map/all_to_all | solution.py:18
  26.9 0.7 collective-permute-start.3
  38.3 0.7 collective-permute-start.4
  67.5 2.2 %copy-start.2 = (bf16[32,256,256]{2,1,0:T(8,128)(2,1)S(1)}, bf16[32,256,256]{2,1,0:T(8,128)(2,1)}, u32[]{:S(2)}) copy-start(bf16[32,256,256]{2,1,0:T(8,128)(2,1)} %copy-done) | copy-start | bytes 12582916
  81.9 14.8 %all-to-all-start.5 = ((f32[4,128,128]{2,1,0:T(8,128)}), f32[4,128,128]{2,1,0:T(8,128)S(1)}, u32[]{:S(2)}, u32[]{:S(2)}) async-start(f32[4,128,128]{2,1,0:T(8,128)} %get-tuple-element.27), calls=%async_computation.5 | async-start | bytes 524288 | tf_op jit(solution)/shard_map/all_to_all | solution.py:18
  85.3 0.7 collective-permute-start.5

commit v4 on v3

v4 whole, which is shorter than its diff:
```python
import functools

import jax
import jax.numpy as jnp
from jax import lax
from jax.experimental import pallas as pl
from jax.experimental.pallas import tpu as pltpu
from jax.sharding import PartitionSpec as P

ITERS = 2
LANES = 128
GROUP = 8
BF16 = jnp.bfloat16
F32 = jnp.float32


def shifted(value, axis, d, n):
    return lax.ppermute(value, axis, [(i, i ^ d) for i in range(n)])


def distances(n):
    return [d for d in range(n) if d > 1] + [1]


def hop(value, n, moves):
    pairs = [((c ^ s) * n + c, (c ^ t) * n + c) for c in range(n) for s, t in moves]
    return lax.ppermute(value, ("row", "col"), pairs)


def bits(n):
    return [1 << i for i in range(n.bit_length() - 1)]


def load_pair(dst, tile, value):
    rhs = value.shape[0]
    high = value.astype(BF16)
    dst[tile, :rhs, :] = high
    dst[tile, rhs:, :] = (value - high.astype(F32)).astype(BF16)


def product(pair, block, contract):
    both = lax.dot_general(pair, block, (((1,), (contract,)), ((), ())), preferred_element_type=F32)
    rhs = both.shape[0] // 2
    return both[:rhs] + both[rhs:]


def pack_stats(columns, rhs):
    lane = lax.broadcasted_iota(jnp.int32, (8, LANES), 1)
    tile = jnp.zeros((8, LANES), F32)
    groups = rhs // 8
    for i, column in enumerate(columns):
        for g in range(groups):
            tile = jnp.where(lane == i * groups + g, column[g * 8:(g + 1) * 8], tile)
    return tile


def unpack_stat(tile, i, rhs):
    groups = rhs // 8
    return jnp.concatenate([tile[:, i * groups + g:i * groups + g + 1] for g in range(groups)], axis=0)


def accumulate(total, tile, value):
    width = value.shape[1] // LANES
    for part in range(width):
        total[tile * width + part] += value[:, part * LANES:(part + 1) * LANES]


def add_blocks(blocks, slot_rows, slot_cols, live, pairs, total, mirror, ready=None):
    read, write, contract = (slot_rows, slot_cols, 0) if mirror else (slot_cols, slot_rows, 1)

    def body(step, carry):
        if ready is not None:
            ready(step)
        values = []
        for g in range(GROUP):
            slot = step * GROUP + g
            value = product(pairs[read[0, 0, slot]], blocks[slot], contract)
            values.append((write[0, 0, slot], jnp.where(slot < live, value, 0.0)))
        for tile, value in values:
            accumulate(total, tile, value)
        return carry

    lax.fori_loop(0, (live + GROUP - 1) // GROUP, body, 0)


def image_part(parts, me, i, per, rhs):
    rows = slice((i % per) * rhs, (i % per + 1) * rhs)
    value = parts[0][rows, :]
    for d in range(1, len(parts)):
        value = jnp.where(me ^ d == i // per, parts[d][rows, :], value)
    return value


def row_sums(value):
    return jnp.sum(value, axis=1, keepdims=True)


def cross_sums(total, value):
    rhs = value.shape[0]
    cross = jnp.zeros((rhs, LANES), F32)
    for i in range(total.shape[0]):
        cross += total[i] * value[:, i * LANES:(i + 1) * LANES]
    return row_sums(cross)


def tree_sum(values):
    values = list(values)
    while len(values) > 1:
        values = [a + b for a, b in zip(values[::2], values[1::2])]
    return values[0]


def fetch_index(sources, targets, sems):
    copies = [pltpu.make_async_copy(s, t, sems.at[i]) for i, (s, t) in enumerate(zip(sources, targets))]
    for copy in copies:
        copy.start()
    return copies


def mirror_first_kernel(rows_hbm, cols_hbm, count, right_hbm, cov, total, blocks, mark, *scratch):
    slot_rows, slot_cols, right, pairs, index_sems, right_sem, block_sems = scratch
    slots, tile_size = blocks.shape[:2]

    def block_copy(i):
        part = pl.ds(i * GROUP, GROUP)
        return pltpu.make_async_copy(cov.at[0, 0, part], blocks.at[part], block_sems.at[i])

    copies = fetch_index((rows_hbm, cols_hbm), (slot_rows, slot_cols), index_sems)
    load = pltpu.make_async_copy(right_hbm, right, right_sem)
    load.start()
    live = count[0, 0]
    for i in range(slots // GROUP):
        @pl.when(i * GROUP < live)
        def _():
            block_copy(i).start()
    total[...] = jnp.zeros_like(total)
    mark[...] = jnp.zeros_like(mark)
    load.wait()
    for tile in range(right.shape[1] // tile_size):
        load_pair(pairs, tile, right[:, tile * tile_size:(tile + 1) * tile_size])
    for copy in copies:
        copy.wait()
    add_blocks(blocks, slot_rows, slot_cols, live, pairs, total, True, lambda i: block_copy(i).wait())


def mirror_second_kernel(rows_any, cols_any, count, near, blocks, total, mark, *scratch):
    slot_rows, slot_cols, pairs, index_sems = scratch
    tile_size = blocks.shape[1]
    copies = fetch_index((rows_any, cols_any), (slot_rows, slot_cols), index_sems)
    total[...] = jnp.zeros_like(total)
    mark[...] = jnp.zeros_like(mark)
    for tile in range(near.shape[1] // tile_size):
        load_pair(pairs, tile, near[:, tile * tile_size:(tile + 1) * tile_size])
    for copy in copies:
        copy.wait()
    add_blocks(blocks, slot_rows, slot_cols, count[0, 0], pairs, total, True)


def direct_kernel(n, *refs):
    rows_any, cols_any, count, noise, blocks = refs[:5]
    held, (total, stat), scratch = refs[5:5 + n], refs[5 + n:7 + n], refs[7 + n:]
    slot_rows, slot_cols, pairs, index_sems = scratch
    tile_size = blocks.shape[1]
    near = held[0]
    rhs, width = near.shape
    copies = fetch_index((rows_any, cols_any), (slot_rows, slot_cols), index_sems)
    offset = lax.axis_index("row") ^ lax.axis_index("col")
    for o in range(n):
        @pl.when(offset == o)
        def _():
            for tile in range(width // tile_size):
                load_pair(pairs, tile, held[o][:, tile * tile_size:(tile + 1) * tile_size])
    total[...] = jnp.zeros_like(total)
    for copy in copies:
        copy.wait()
    add_blocks(blocks, slot_rows, slot_cols, count[0, 0], pairs, total, False)
    value = near[...]
    square = value * value
    share = 1.0 / n
    bend = share * row_sums(square * noise[...]) + 2.0 * cross_sums(total, value)
    stat[...] = pack_stats([share * row_sums(square), bend], rhs)


def add_kernel(one, two, out):
    out[...] = one[...] + two[...]


def pass_kernel(value, mark, out):
    out[...] = value[...]


def merge_kernel(n, direct, stat, held, arrived, *outs):
    per = direct.shape[0] // n
    rhs = direct.shape[1]
    me = lax.axis_index("col")
    diagonal = lax.axis_index("row") == me
    for d, out in enumerate(outs):
        first = (me ^ d) * per
        out[per * rhs:, :] = stat[...]

        @pl.when(diagonal)
        def _():
            for i in range(per):
                out[i * rhs:(i + 1) * rhs, :] = direct[first + i] + held[first + i] + arrived[first + i]

        @pl.when(jnp.logical_not(diagonal))
        def _():
            for i in range(per):
                out[i * rhs:(i + 1) * rhs, :] = direct[first + i]


def combine_kernel(n, near, noise, *refs):
    parts, (chunk, stat) = refs[:n], refs[n:]
    rhs = near.shape[0]
    data = chunk.shape[0]
    per = data // rhs
    value = tree_sum(ref[...] for ref in parts)
    chunk[...] = value[:data]
    stat[...] = value[data:]
    me = lax.axis_index("col")
    for k in range(n):
        @pl.when(me == k)
        def _():
            for i in range(per):
                lanes = slice((k * per + i) * LANES, (k * per + i + 1) * LANES)
                chunk[i * rhs:(i + 1) * rhs, :] += near[:, lanes] * noise[:, lanes]


def left_kernel(right, stat, *refs):
    parts, left = refs[:-1], refs[-1]
    rhs, width = right.shape
    per = parts[0].shape[0] // rhs
    me = lax.axis_index("col")
    size_now = unpack_stat(stat[...], 0, rhs) / unpack_stat(stat[...], 1, rhs)
    for i in range(width // LANES):
        lanes = slice(i * LANES, (i + 1) * LANES)
        left[:, lanes] = right[:, lanes] - size_now * image_part(parts, me, i, per, rhs)


def last_kernel(right, left, stat_now, stat_next, *refs):
    parts, (solution, residual) = refs[:-2], refs[-2:]
    rhs, width = right.shape
    per = parts[0].shape[0] // rhs
    me = lax.axis_index("col")
    norm = unpack_stat(stat_now[...], 0, rhs)
    norm_next = unpack_stat(stat_next[...], 0, rhs)
    size_now = norm / unpack_stat(stat_now[...], 1, rhs)
    ratio = norm_next / norm
    size_next = norm_next / (unpack_stat(stat_next[...], 1, rhs) - ratio * norm_next / size_now)
    back = ratio / size_now
    for i in range(width // LANES):
        lanes = slice(i * LANES, (i + 1) * LANES)
        first = right[:, lanes]
        now = left[:, lanes]
        solution[:, lanes] = size_now * first + size_next * (now + ratio * first)
        image = image_part(parts, me, i, per, rhs) + back * (first - now)
        residual[:, lanes] = now - size_next * image


def shape_of(*shape):
    return jax.ShapeDtypeStruct(shape, F32)


def on_device(n, right_sides, nugget, cov_blocks, block_rows, block_cols, block_count):
    rhs, width = right_sides.shape
    slots, tile_size = cov_blocks.shape[2:4]
    per = width // n // LANES
    data = per * rhs
    size = data + 8
    noise = nugget.reshape(1, width)
    index = (block_rows, block_cols, block_count)
    pair = pltpu.VMEM((width // tile_size, 2 * rhs, tile_size), BF16)
    index_scratch = [pltpu.SMEM(item.shape, item.dtype) for item in index[:2]]
    index_sems = pltpu.SemaphoreType.DMA((2,))
    vmem = pl.BlockSpec(memory_space=pltpu.VMEM)
    any_spec = pl.BlockSpec(memory_space=pl.ANY)
    smem = pl.BlockSpec(memory_space=pltpu.SMEM)
    hbm = pl.BlockSpec(memory_space=pltpu.HBM)
    params = pltpu.CompilerParams(vmem_limit_bytes=16 * 1024 * 1024)
    cost = pl.CostEstimate(flops=4 * rhs * slots * tile_size * tile_size, transcendentals=0,
                           bytes_accessed=2 * slots * tile_size * tile_size)
    field = shape_of(rhs, width)
    total = shape_of(width // LANES, rhs, LANES)
    chunk = shape_of(data, LANES)
    tile = shape_of(8, LANES)
    loaded = shape_of(size, LANES)

    def call(kernel, name, specs, outs, scratch, args, heavy=False):
        return pl.pallas_call(
            kernel,
            in_specs=specs,
            out_specs=jax.tree.map(lambda _: vmem, outs),
            out_shape=outs,
            scratch_shapes=scratch,
            compiler_params=params,
            cost_estimate=cost if heavy else None,
            name=name,
        )(*args)

    in_hbm = functools.partial(pltpu.with_memory_space_constraint, memory_space=pltpu.HBM)

    def image_of(value, mirrored):
        held = [value] + [None] * (n - 1)
        for o in distances(n):
            if o & (o - 1) == 0:
                held[o] = hop(value, n, [(0, o)])
        mirror, blocks, mark = mirrored(value)
        for o in range(n):
            if held[o] is None:
                parent = held[o & (o - 1)]
                passed, = call(pass_kernel, "pass_on", [vmem] * 2, [field], [], (parent, mark))
                held[o] = hop(passed, n, [(o & (o - 1), o)])
        for b in bits(n):
            arrived = hop(mirror, n, [(o, o ^ b) for o in range(n) if o & -o == b])
            if 2 * b < n:
                mirror, = call(add_kernel, "add_mirror", [vmem] * 2, [total], [], (mirror, arrived))
        direct, stat = call(
            functools.partial(direct_kernel, n), "direct",
            [any_spec] * 2 + [smem] + [vmem] * (n + 2),
            [total, tile], index_scratch + [pair, index_sems],
            (*index, noise, blocks, *held), True)
        merged = call(functools.partial(merge_kernel, n), "merge", [vmem] * 4, [loaded] * n, [],
                      (direct, stat, mirror, arrived))
        parts = [merged[0]] + [None] * (n - 1)
        for d in distances(n):
            parts[d] = shifted(merged[d], "col", d, n)
        own, stat = call(functools.partial(combine_kernel, n), "combine", [vmem] * (n + 2), [chunk, tile], [],
                         (value, noise, *parts))
        parts = [own] + [None] * (n - 1)
        for d in distances(n):
            parts[d] = shifted(own, "col", d, n)
        for b in bits(n):
            stat, = call(add_kernel, "add_stat", [vmem] * 2, [tile], [], (stat, shifted(stat, "row", b, n)))
        return parts, stat, blocks

    def mirror_first(value):
        return call(
            mirror_first_kernel, "mirror_first", [hbm] * 2 + [smem] + [hbm] * 2,
            [total, jax.ShapeDtypeStruct(cov_blocks.shape[2:], cov_blocks.dtype), tile],
            index_scratch + [pltpu.VMEM((rhs, width), F32), pair, index_sems,
                             pltpu.SemaphoreType.DMA, pltpu.SemaphoreType.DMA((slots // GROUP,))],
            (*map(in_hbm, index[:2]), block_count, in_hbm(value), in_hbm(cov_blocks)), True)

    parts, stat_now, blocks = image_of(right_sides, mirror_first)
    left, = call(left_kernel, "left", [vmem] * (n + 2), [field], [], (right_sides, stat_now, *parts))

    def mirror_second(value):
        mirror, mark = call(
            mirror_second_kernel, "mirror_second", [any_spec] * 2 + [smem] + [vmem] * 2,
            [total, tile], index_scratch + [pair, index_sems], (*index, value, blocks), True)
        return mirror, blocks, mark

    parts, stat_next, _ = image_of(left, mirror_second)
    return tuple(call(last_kernel, "last", [vmem] * (n + 4), [field, field], [],
                      (right_sides, left, stat_now, stat_next, *parts)))


def solution(mesh):
    n = mesh.shape["row"]
    assert n == mesh.shape["col"] and n & (n - 1) == 0
    placed = (
        P(None, ("groups", "row")),
        P(("groups", "row")),
        P(("groups", "row"), "col", None, None, None),
        P(("groups", "row"), "col", None),
        P(("groups", "row"), "col", None),
        P(("groups", "row"), "col"),
    )
    return jax.shard_map(
        functools.partial(on_device, n),
        mesh=mesh,
        in_specs=placed,
        out_specs=(P(None, ("groups", "row")), P(None, ("groups", "row"))),
        check_vma=False,
    )
```

time: 110 us -> 76.7 us (0.70)
  blocking collectives: 48.7 us -> 0 us
  starting transfers between devices: 19.3 us -> 41.7 us
  local copies, waits for them, and re-layouts: 6.31 us -> 0.02 us
  Pallas kernels: 11.5 us -> 6.71 us
  waiting for transfers between devices: 22.4 us -> 26.2 us
    all_to_all x4 -> x0, blocking collectives: 48.7 us -> none  [swapped(): return lax.all_to_all(values, axis, 0, 0)]
    ppermute x6 -> x26, starting transfers between devices: 9.03 us -> 41.7 us  [the longest x16 21.2 us: shifted(): return lax.ppermute(value, axis, [(i, i ^ d) for i in range(n)])]
    ppermute x6 -> x26, waiting for transfers between devices: 0.02 us -> 26.2 us  [the longest x16 14.7 us: shifted(): return lax.ppermute(value, axis, [(i, i ^ d) for i in range(n)])]
    all_to_all x3 -> x0, waiting for transfers between devices: 22.3 us -> none  [swapped(): return lax.all_to_all(values, axis, 0, 0)]
    all_to_all x3 -> x0, starting transfers between devices: 10.3 us -> none  [swapped(): return lax.all_to_all(values, axis, 0, 0)]
    unnamed x14 -> x8, local copies, waits for them, and re-layouts: 6.31 us -> 0.02 us
    pallas_call x9 -> x18, Pallas kernels: 11.5 us -> 6.71 us  [call(): pl.pallas_call(kernel, in_specs=specs, out_specs=jax.tree.map(lambda _: v...]
  transfers between devices with their start and end apart: 9 -> 26, of which waited for: 3 -> 12; matrix products, arithmetic and copies ran while one was open for 0% -> 0% of each run, Pallas kernels for 6% -> 7%
where the time goes in v4:
time: 76.7 us; the launch traced here: 76.3 us
  starting transfers between devices  41.7 us (54%)
  waiting for transfers between devices  26.2 us (34%)
  Pallas kernels  6.71 us (9%)
  between operations  1.62 us (2%)
    ppermute x16, starting transfers between devices, shifted(): return lax.ppermute(value, axis, [(i, i ^ d) for i in range(n)])  21.2 us
    ppermute x10, starting transfers between devices, hop(): return lax.ppermute(value, ('row', 'col'), pairs)  20.5 us
    ppermute x16, waiting for transfers between devices, shifted(): return lax.ppermute(value, axis, [(i, i ^ d) for i in range(n)])  14.7 us
    ppermute x10, waiting for transfers between devices, hop(): return lax.ppermute(value, ('row', 'col'), pairs)  11.5 us
    pallas_call x18, Pallas kernels, call(): pl.pallas_call(kernel, in_specs=specs, out_specs=jax.tree.map(lambda _: v...  6.71 us
  transfers between devices with their start and end apart: 26, of which 12 were waited for; matrix products, arithmetic and copies ran while one was open for 0% of the time, Pallas kernels for 7%

profile of v4, /device:TPU:0, one launch (start us, length us, event | category | flops | bytes accessed | tf_op | source)
XLA Modules:
  0.0 76.3 jit_solution(1079862241040472482)
XLA Ops:
  0.7 5.0 %collective-permute-start.1 = (f32[32,2048]{1,0:T(8,128)}, f32[32,2048]{1,0:T(8,128)S(1)}, u32[]{:S(2)}, u32[]{:S(2)}) collective-permute-start(f32[32,2048]{1,0:T(8,128)} %right.3), channel_id=1, source_target_pairs={{0,8},{5,13},{10,2},{15,7},{16,24},{21,29},{26,18},{31,23}} | collective-permute-start | bytes 786440 | tf_op jit(solution)/shard_map/ppermute | solution.py:27
  6.3 1.7 %mirror_first.1 = (f32[16,32,128]{2,1,0:T(8,128)S(1)}, bf16[32,256,256]{2,1,0:T(8,128)(2,1)S(1)}, f32[8,128]{1,0:T(8,128)S(1)}) custom-call(s32[1,1,32]{2,1,0:T(1,128)} %refs_0_.3, s32[1,1,32]{2,1,0:T(1,128)} %refs_1_.3, s32[1,1]{1,0:T(1,128)S(6)} %copy.8.count.refs_2_, f32[32,2048]{1,0:T(8,128)} %right.3, bf16[1,1,32,256,256]{4,3,2,1,0:T(8,128)(2,1)} %cov.1), custom_call_target="tpu_custom_call" | custom-call | flops 268435456 | bytes 4194304 | tf_op jit(solution)/shard_map/mirror_first/pallas_call | solution.py:289
  8.0 1.3 %collective-permute-start.3 = (f32[16,32,128]{2,1,0:T(8,128)S(1)}, f32[16,32,128]{2,1,0:T(8,128)S(1)}, u32[]{:S(2)}, u32[]{:S(2)}) collective-permute-start(f32[16,32,128]{2,1,0:T(8,128)S(1)} %get-tuple-element.27.one), channel_id=1, source_target_pairs={{4,0},{12,8},{1,5},{9,13},{14,10},{6,2},{11,15},{3,7},{20,16},{28,... | collective-permute-start | bytes 786440 | tf_op jit(solution)/shard_map/ppermute | solution.py:27
  9.3 3.1 %collective-permute-start = (f32[32,2048]{1,0:T(8,128)S(1)}, f32[32,2048]{1,0:T(8,128)S(1)}, u32[]{:S(2)}, u32[]{:S(2)}) collective-permute-start(f32[32,2048]{1,0:T(8,128)S(1)} %copy-done), channel_id=1, source_target_pairs={{0,4},{5,1},{10,14},{15,11},{16,20},{21,17},{26,30},{31,27}} | collective-permute-start | bytes 786440 | tf_op jit(solution)/shard_map/ppermute | solution.py:27
  13.2 1.3 %collective-permute-start.4 = (f32[16,32,128]{2,1,0:T(8,128)S(1)}, f32[16,32,128]{2,1,0:T(8,128)S(1)}, u32[]{:S(2)}, u32[]{:S(2)}) collective-permute-start(f32[16,32,128]{2,1,0:T(8,128)S(1)} %add_mirror.2.held), channel_id=1, source_target_pairs={{8,0},{13,5},{2,10},{7,15},{24,16},{29,21},{18,26},{23,31}} | collective-permute-start | bytes 786440 | tf_op jit(solution)/shard_map/ppermute | solution.py:27
  15.7 5.7 %collective-permute-done.4.arrived = f32[16,32,128]{2,1,0:T(8,128)S(1)} collective-permute-done((f32[16,32,128]{2,1,0:T(8,128)S(1)}, f32[16,32,128]{2,1,0:T(8,128)S(1)}, u32[]{:S(2)}, u32[]{:S(2)}) %collective-permute-start.4) | collective-permute-done | bytes 262176 | tf_op jit(solution)/shard_map/ppermute | solution.py:27
  21.6 1.3 %collective-permute-start.6 = (f32[136,128]{1,0:T(8,128)S(1)}, f32[136,128]{1,0:T(8,128)S(1)}, u32[]{:S(2)}, u32[]{:S(2)}) collective-permute-start(f32[136,128]{1,0:T(8,128)S(1)} %get-tuple-element.30), channel_id=1, source_target_pairs={{0,2},{1,3},{2,0},{3,1},{4,6},{5,7},{6,4},{7,5},{8,10},{9,11},{10,... | collective-permute-start | bytes 208904 | tf_op jit(solution)/shard_map/ppermute | solution.py:18
  22.9 3.1 %collective-permute-start.7 = (f32[136,128]{1,0:T(8,128)S(1)}, f32[136,128]{1,0:T(8,128)S(1)}, u32[]{:S(2)}, u32[]{:S(2)}) collective-permute-start(f32[136,128]{1,0:T(8,128)S(1)} %get-tuple-element.31), channel_id=1, source_target_pairs={{0,3},{1,2},{2,1},{3,0},{4,7},{5,6},{6,5},{7,4},{8,11},{9,10},{10,... | collective-permute-start | bytes 208904 | tf_op jit(solution)/shard_map/ppermute | solution.py:18
  26.0 4.2 %collective-permute-done.6.refs_2_ = f32[136,128]{1,0:T(8,128)S(1)} collective-permute-done((f32[136,128]{1,0:T(8,128)S(1)}, f32[136,128]{1,0:T(8,128)S(1)}, u32[]{:S(2)}, u32[]{:S(2)}) %collective-permute-start.6) | collective-permute-done | bytes 69664 | tf_op jit(solution)/shard_map/ppermute | solution.py:18
  30.2 2.0 %collective-permute-start.10 = (f32[128,128]{1,0:T(8,128)S(1)}, f32[128,128]{1,0:T(8,128)S(1)}, u32[]{:S(2)}, u32[]{:S(2)}) collective-permute-start(f32[128,128]{1,0:T(8,128)S(1)} %get-tuple-element.33.refs_0_), channel_id=1, source_target_pairs={{0,1},{1,0},{2,3},{3,2},{4,5},{5,4},{6,7},{7,6},{8,9},{9,8},{10,11... | collective-permute-start | bytes 196616 | tf_op jit(solution)/shard_map/ppermute | solution.py:18
  32.1 1.3 %collective-permute-start.11 = (f32[128,128]{1,0:T(8,128)S(1)}, f32[128,128]{1,0:T(8,128)S(1)}, u32[]{:S(2)}, u32[]{:S(2)}) collective-permute-start(f32[128,128]{1,0:T(8,128)S(1)} %get-tuple-element.33.refs_0_), channel_id=1, source_target_pairs={{0,2},{1,3},{2,0},{3,1},{4,6},{5,7},{6,4},{7,5},{8,10},{9,11},{10,... | collective-permute-start | bytes 196616 | tf_op jit(solution)/shard_map/ppermute | solution.py:18
  35.8 1.4 %collective-permute-start.9 = (f32[8,128]{1,0:T(8,128)S(1)}, f32[8,128]{1,0:T(8,128)S(1)}, u32[]{:S(2)}, u32[]{:S(2)}) collective-permute-start(f32[8,128]{1,0:T(8,128)S(1)} %add_stat.4.one), channel_id=1, source_target_pairs={{0,8},{4,12},{8,0},{12,4},{1,9},{5,13},{9,1},{13,5},{2,10},{6,14},... | collective-permute-start | bytes 12296 | tf_op jit(solution)/shard_map/ppermute | solution.py:18
  37.2 2.2 %collective-permute-done.9.two = f32[8,128]{1,0:T(8,128)S(1)} collective-permute-done((f32[8,128]{1,0:T(8,128)S(1)}, f32[8,128]{1,0:T(8,128)S(1)}, u32[]{:S(2)}, u32[]{:S(2)}) %collective-permute-start.9) | collective-permute-done | bytes 4128 | tf_op jit(solution)/shard_map/ppermute | solution.py:18
  40.2 2.9 %collective-permute-start.14 = (f32[32,2048]{1,0:T(8,128)S(1)}, f32[32,2048]{1,0:T(8,128)S(1)}, u32[]{:S(2)}, u32[]{:S(2)}) collective-permute-start(f32[32,2048]{1,0:T(8,128)S(1)} %left.1.near.refs_5_), channel_id=1, source_target_pairs={{0,8},{5,13},{10,2},{15,7},{16,24},{21,29},{26,18},{31,23}} | collective-permute-start | bytes 786440 | tf_op jit(solution)/shard_map/ppermute | solution.py:27
  44.0 1.3 %collective-permute-start.16 = (f32[16,32,128]{2,1,0:T(8,128)S(1)}, f32[16,32,128]{2,1,0:T(8,128)S(1)}, u32[]{:S(2)}, u32[]{:S(2)}) collective-permute-start(f32[16,32,128]{2,1,0:T(8,128)S(1)} %get-tuple-element.37.one), channel_id=1, source_target_pairs={{4,0},{12,8},{1,5},{9,13},{14,10},{6,2},{11,15},{3,7},{20,16},{28,... | collective-permute-start | bytes 786440 | tf_op jit(solution)/shard_map/ppermute | solution.py:27
  45.3 3.1 %collective-permute-start.13 = (f32[32,2048]{1,0:T(8,128)S(1)}, f32[32,2048]{1,0:T(8,128)S(1)}, u32[]{:S(2)}, u32[]{:S(2)}) collective-permute-start(f32[32,2048]{1,0:T(8,128)S(1)} %left.1.near.refs_5_), channel_id=1, source_target_pairs={{0,4},{5,1},{10,14},{15,11},{16,20},{21,17},{26,30},{31,27}} | collective-permute-start | bytes 786440 | tf_op jit(solution)/shard_map/ppermute | solution.py:27
  49.1 1.3 %collective-permute-start.17 = (f32[16,32,128]{2,1,0:T(8,128)S(1)}, f32[16,32,128]{2,1,0:T(8,128)S(1)}, u32[]{:S(2)}, u32[]{:S(2)}) collective-permute-start(f32[16,32,128]{2,1,0:T(8,128)S(1)} %add_mirror.3.held), channel_id=1, source_target_pairs={{8,0},{13,5},{2,10},{7,15},{24,16},{29,21},{18,26},{23,31}} | collective-permute-start | bytes 786440 | tf_op jit(solution)/shard_map/ppermute | solution.py:27
  51.6 5.8 %collective-permute-done.17.arrived = f32[16,32,128]{2,1,0:T(8,128)S(1)} collective-permute-done((f32[16,32,128]{2,1,0:T(8,128)S(1)}, f32[16,32,128]{2,1,0:T(8,128)S(1)}, u32[]{:S(2)}, u32[]{:S(2)}) %collective-permute-start.17) | collective-permute-done | bytes 262176 | tf_op jit(solution)/shard_map/ppermute | solution.py:27
  58.3 3.6 %collective-permute-start.20 = (f32[136,128]{1,0:T(8,128)S(1)}, f32[136,128]{1,0:T(8,128)S(1)}, u32[]{:S(2)}, u32[]{:S(2)}) collective-permute-start(f32[136,128]{1,0:T(8,128)S(1)} %get-tuple-element.41), channel_id=1, source_target_pairs={{0,3},{1,2},{2,1},{3,0},{4,7},{5,6},{6,5},{7,4},{8,11},{9,10},{10,... | collective-permute-start | bytes 208904 | tf_op jit(solution)/shard_map/ppermute | solution.py:18
  63.3 1.7 %collective-permute-done.20.refs_3_ = f32[136,128]{1,0:T(8,128)S(1)} collective-permute-done((f32[136,128]{1,0:T(8,128)S(1)}, f32[136,128]{1,0:T(8,128)S(1)}, u32[]{:S(2)}, u32[]{:S(2)}) %collective-permute-start.20) | collective-permute-done | bytes 69664 | tf_op jit(solution)/shard_map/ppermute | solution.py:18
  66.3 2.8 %collective-permute-start.24 = (f32[128,128]{1,0:T(8,128)S(1)}, f32[128,128]{1,0:T(8,128)S(1)}, u32[]{:S(2)}, u32[]{:S(2)}) collective-permute-start(f32[128,128]{1,0:T(8,128)S(1)} %get-tuple-element.43.refs_0_), channel_id=1, source_target_pairs={{0,2},{1,3},{2,0},{3,1},{4,6},{5,7},{6,4},{7,5},{8,10},{9,11},{10,... | collective-permute-start | bytes 196616 | tf_op jit(solution)/shard_map/ppermute | solution.py:18
  70.7 2.0 %collective-permute-start.22 = (f32[8,128]{1,0:T(8,128)S(1)}, f32[8,128]{1,0:T(8,128)S(1)}, u32[]{:S(2)}, u32[]{:S(2)}) collective-permute-start(f32[8,128]{1,0:T(8,128)S(1)} %add_stat.6.one), channel_id=1, source_target_pairs={{0,8},{4,12},{8,0},{12,4},{1,9},{5,13},{9,1},{13,5},{2,10},{6,14},... | collective-permute-start | bytes 12296 | tf_op jit(solution)/shard_map/ppermute | solution.py:18
  72.7 1.6 %collective-permute-done.22.two = f32[8,128]{1,0:T(8,128)S(1)} collective-permute-done((f32[8,128]{1,0:T(8,128)S(1)}, f32[8,128]{1,0:T(8,128)S(1)}, u32[]{:S(2)}, u32[]{:S(2)}) %collective-permute-start.22) | collective-permute-done | bytes 4128 | tf_op jit(solution)/shard_map/ppermute | solution.py:18
  75.1 1.2 %last.1 = (f32[32,2048]{1,0:T(8,128)}, f32[32,2048]{1,0:T(8,128)}) custom-call(f32[32,2048]{1,0:T(8,128)S(1)} %copy-done, f32[32,2048]{1,0:T(8,128)S(1)} %left.1.near.refs_5_, f32[8,128]{1,0:T(8,128)S(1)} %add_stat.5.stat.stat_now, f32[8,128]{1,0:T(8,128)S(1)} %add_stat.7.stat_next, f32[128,128]{1,0:T(8,128)S(1)} %get-tuple-element.43.refs_0_, ...), custom_call_target="tpu_custom_call" | custom-call | tf_op jit(solution)/shard_map/last/pallas_call | solution.py:289
  (54 shorter events, 14.0 us)
Async XLA Ops:
  0.7 11.7 %collective-permute-start.1 = (f32[32,2048]{1,0:T(8,128)}, f32[32,2048]{1,0:T(8,128)S(1)}, u32[]{:S(2)}, u32[]{:S(2)}) collective-permute-start(f32[32,2048]{1,0:T(8,128)} %right.3), channel_id=1, source_target_pairs={{0,8},{5,13},{10,2},{15,7},{16,24},{21,29},{26,18},{31,23}} | collective-permute-start | bytes 786440 | tf_op jit(solution)/shard_map/ppermute | solution.py:27
  8.0 5.1 %collective-permute-start.3 = (f32[16,32,128]{2,1,0:T(8,128)S(1)}, f32[16,32,128]{2,1,0:T(8,128)S(1)}, u32[]{:S(2)}, u32[]{:S(2)}) collective-permute-start(f32[16,32,128]{2,1,0:T(8,128)S(1)} %get-tuple-element.27.one), channel_id=1, source_target_pairs={{4,0},{12,8},{1,5},{9,13},{14,10},{6,2},{11,15},{3,7},{20,16},{28,... | collective-permute-start | bytes 786440 | tf_op jit(solution)/shard_map/ppermute | solution.py:27
  9.3 5.1 %collective-permute-start = (f32[32,2048]{1,0:T(8,128)S(1)}, f32[32,2048]{1,0:T(8,128)S(1)}, u32[]{:S(2)}, u32[]{:S(2)}) collective-permute-start(f32[32,2048]{1,0:T(8,128)S(1)} %copy-done), channel_id=1, source_target_pairs={{0,4},{5,1},{10,14},{15,11},{16,20},{21,17},{26,30},{31,27}} | collective-permute-start | bytes 786440 | tf_op jit(solution)/shard_map/ppermute | solution.py:27
  12.4 2.0 %collective-permute-start.2 = (f32[32,2048]{1,0:T(8,128)S(1)}, f32[32,2048]{1,0:T(8,128)S(1)}, u32[]{:S(2)}, u32[]{:S(2)}) collective-permute-start(f32[32,2048]{1,0:T(8,128)S(1)} %pass_on.2), channel_id=1, source_target_pairs={{8,12},{13,9},{2,6},{7,3},{24,28},{29,25},{18,22},{23,19}} | collective-permute-start | bytes 786440 | tf_op jit(solution)/shard_map/ppermute | solution.py:27
  13.2 8.3 %collective-permute-start.4 = (f32[16,32,128]{2,1,0:T(8,128)S(1)}, f32[16,32,128]{2,1,0:T(8,128)S(1)}, u32[]{:S(2)}, u32[]{:S(2)}) collective-permute-start(f32[16,32,128]{2,1,0:T(8,128)S(1)} %add_mirror.2.held), channel_id=1, source_target_pairs={{8,0},{13,5},{2,10},{7,15},{24,16},{29,21},{18,26},{23,31}} | collective-permute-start | bytes 786440 | tf_op jit(solution)/shard_map/ppermute | solution.py:27
  21.5 4.5 %collective-permute-start.5 = (f32[136,128]{1,0:T(8,128)S(1)}, f32[136,128]{1,0:T(8,128)S(1)}, u32[]{:S(2)}, u32[]{:S(2)}) collective-permute-start(f32[136,128]{1,0:T(8,128)S(1)} %get-tuple-element.29), channel_id=1, source_target_pairs={{0,1},{1,0},{2,3},{3,2},{4,5},{5,4},{6,7},{7,6},{8,9},{9,8},{10,11... | collective-permute-start | bytes 208904 | tf_op jit(solution)/shard_map/ppermute | solution.py:18
  21.6 8.5 %collective-permute-start.6 = (f32[136,128]{1,0:T(8,128)S(1)}, f32[136,128]{1,0:T(8,128)S(1)}, u32[]{:S(2)}, u32[]{:S(2)}) collective-permute-start(f32[136,128]{1,0:T(8,128)S(1)} %get-tuple-element.30), channel_id=1, source_target_pairs={{0,2},{1,3},{2,0},{3,1},{4,6},{5,7},{6,4},{7,5},{8,10},{9,11},{10,... | collective-permute-start | bytes 208904 | tf_op jit(solution)/shard_map/ppermute | solution.py:18
  22.9 7.2 %collective-permute-start.7 = (f32[136,128]{1,0:T(8,128)S(1)}, f32[136,128]{1,0:T(8,128)S(1)}, u32[]{:S(2)}, u32[]{:S(2)}) collective-permute-start(f32[136,128]{1,0:T(8,128)S(1)} %get-tuple-element.31), channel_id=1, source_target_pairs={{0,3},{1,2},{2,1},{3,0},{4,7},{5,6},{6,5},{7,4},{8,11},{9,10},{10,... | collective-permute-start | bytes 208904 | tf_op jit(solution)/shard_map/ppermute | solution.py:18
  30.2 9.2 %collective-permute-start.10 = (f32[128,128]{1,0:T(8,128)S(1)}, f32[128,128]{1,0:T(8,128)S(1)}, u32[]{:S(2)}, u32[]{:S(2)}) collective-permute-start(f32[128,128]{1,0:T(8,128)S(1)} %get-tuple-element.33.refs_0_), channel_id=1, source_target_pairs={{0,1},{1,0},{2,3},{3,2},{4,5},{5,4},{6,7},{7,6},{8,9},{9,8},{10,11... | collective-permute-start | bytes 196616 | tf_op jit(solution)/shard_map/ppermute | solution.py:18
  32.1 7.8 %collective-permute-start.11 = (f32[128,128]{1,0:T(8,128)S(1)}, f32[128,128]{1,0:T(8,128)S(1)}, u32[]{:S(2)}, u32[]{:S(2)}) collective-permute-start(f32[128,128]{1,0:T(8,128)S(1)} %get-tuple-element.33.refs_0_), channel_id=1, source_target_pairs={{0,2},{1,3},{2,0},{3,1},{4,6},{5,7},{6,4},{7,5},{8,10},{9,11},{10,... | collective-permute-start | bytes 196616 | tf_op jit(solution)/shard_map/ppermute | solution.py:18
  33.5 6.4 %collective-permute-start.12 = (f32[128,128]{1,0:T(8,128)S(1)}, f32[128,128]{1,0:T(8,128)S(1)}, u32[]{:S(2)}, u32[]{:S(2)}) collective-permute-start(f32[128,128]{1,0:T(8,128)S(1)} %get-tuple-element.33.refs_0_), channel_id=1, source_target_pairs={{0,3},{1,2},{2,1},{3,0},{4,7},{5,6},{6,5},{7,4},{8,11},{9,10},{10,... | collective-permute-start | bytes 196616 | tf_op jit(solution)/shard_map/ppermute | solution.py:18
  35.8 3.6 %collective-permute-start.9 = (f32[8,128]{1,0:T(8,128)S(1)}, f32[8,128]{1,0:T(8,128)S(1)}, u32[]{:S(2)}, u32[]{:S(2)}) collective-permute-start(f32[8,128]{1,0:T(8,128)S(1)} %add_stat.4.one), channel_id=1, source_target_pairs={{0,8},{4,12},{8,0},{12,4},{1,9},{5,13},{9,1},{13,5},{2,10},{6,14},... | collective-permute-start | bytes 12296 | tf_op jit(solution)/shard_map/ppermute | solution.py:18
  40.2 8.2 %collective-permute-start.14 = (f32[32,2048]{1,0:T(8,128)S(1)}, f32[32,2048]{1,0:T(8,128)S(1)}, u32[]{:S(2)}, u32[]{:S(2)}) collective-permute-start(f32[32,2048]{1,0:T(8,128)S(1)} %left.1.near.refs_5_), channel_id=1, source_target_pairs={{0,8},{5,13},{10,2},{15,7},{16,24},{21,29},{26,18},{31,23}} | collective-permute-start | bytes 786440 | tf_op jit(solution)/shard_map/ppermute | solution.py:27
  44.0 5.1 %collective-permute-start.16 = (f32[16,32,128]{2,1,0:T(8,128)S(1)}, f32[16,32,128]{2,1,0:T(8,128)S(1)}, u32[]{:S(2)}, u32[]{:S(2)}) collective-permute-start(f32[16,32,128]{2,1,0:T(8,128)S(1)} %get-tuple-element.37.one), channel_id=1, source_target_pairs={{4,0},{12,8},{1,5},{9,13},{14,10},{6,2},{11,15},{3,7},{20,16},{28,... | collective-permute-start | bytes 786440 | tf_op jit(solution)/shard_map/ppermute | solution.py:27
  45.3 5.1 %collective-permute-start.13 = (f32[32,2048]{1,0:T(8,128)S(1)}, f32[32,2048]{1,0:T(8,128)S(1)}, u32[]{:S(2)}, u32[]{:S(2)}) collective-permute-start(f32[32,2048]{1,0:T(8,128)S(1)} %left.1.near.refs_5_), channel_id=1, source_target_pairs={{0,4},{5,1},{10,14},{15,11},{16,20},{21,17},{26,30},{31,27}} | collective-permute-start | bytes 786440 | tf_op jit(solution)/shard_map/ppermute | solution.py:27
  48.4 2.0 %collective-permute-start.15 = (f32[32,2048]{1,0:T(8,128)S(1)}, f32[32,2048]{1,0:T(8,128)S(1)}, u32[]{:S(2)}, u32[]{:S(2)}) collective-permute-start(f32[32,2048]{1,0:T(8,128)S(1)} %pass_on.3), channel_id=1, source_target_pairs={{8,12},{13,9},{2,6},{7,3},{24,28},{29,25},{18,22},{23,19}} | collective-permute-start | bytes 786440 | tf_op jit(solution)/shard_map/ppermute | solution.py:27
  49.1 8.3 %collective-permute-start.17 = (f32[16,32,128]{2,1,0:T(8,128)S(1)}, f32[16,32,128]{2,1,0:T(8,128)S(1)}, u32[]{:S(2)}, u32[]{:S(2)}) collective-permute-start(f32[16,32,128]{2,1,0:T(8,128)S(1)} %add_mirror.3.held), channel_id=1, source_target_pairs={{8,0},{13,5},{2,10},{7,15},{24,16},{29,21},{18,26},{23,31}} | collective-permute-start | bytes 786440 | tf_op jit(solution)/shard_map/ppermute | solution.py:27
  57.4 5.4 %collective-permute-start.18 = (f32[136,128]{1,0:T(8,128)S(1)}, f32[136,128]{1,0:T(8,128)S(1)}, u32[]{:S(2)}, u32[]{:S(2)}) collective-permute-start(f32[136,128]{1,0:T(8,128)S(1)} %get-tuple-element.39), channel_id=1, source_target_pairs={{0,1},{1,0},{2,3},{3,2},{4,5},{5,4},{6,7},{7,6},{8,9},{9,8},{10,11... | collective-permute-start | bytes 208904 | tf_op jit(solution)/shard_map/ppermute | solution.py:18
  57.5 5.8 %collective-permute-start.19 = (f32[136,128]{1,0:T(8,128)S(1)}, f32[136,128]{1,0:T(8,128)S(1)}, u32[]{:S(2)}, u32[]{:S(2)}) collective-permute-start(f32[136,128]{1,0:T(8,128)S(1)} %get-tuple-element.40), channel_id=1, source_target_pairs={{0,2},{1,3},{2,0},{3,1},{4,6},{5,7},{6,4},{7,5},{8,10},{9,11},{10,... | collective-permute-start | bytes 208904 | tf_op jit(solution)/shard_map/ppermute | solution.py:18
  58.3 6.7 %collective-permute-start.20 = (f32[136,128]{1,0:T(8,128)S(1)}, f32[136,128]{1,0:T(8,128)S(1)}, u32[]{:S(2)}, u32[]{:S(2)}) collective-permute-start(f32[136,128]{1,0:T(8,128)S(1)} %get-tuple-element.41), channel_id=1, source_target_pairs={{0,3},{1,2},{2,1},{3,0},{4,7},{5,6},{6,5},{7,4},{8,11},{9,10},{10,... | collective-permute-start | bytes 208904 | tf_op jit(solution)/shard_map/ppermute | solution.py:18
  65.1 9.2 %collective-permute-start.23 = (f32[128,128]{1,0:T(8,128)S(1)}, f32[128,128]{1,0:T(8,128)S(1)}, u32[]{:S(2)}, u32[]{:S(2)}) collective-permute-start(f32[128,128]{1,0:T(8,128)S(1)} %get-tuple-element.43.refs_0_), channel_id=1, source_target_pairs={{0,1},{1,0},{2,3},{3,2},{4,5},{5,4},{6,7},{7,6},{8,9},{9,8},{10,11... | collective-permute-start | bytes 196616 | tf_op jit(solution)/shard_map/ppermute | solution.py:18
  66.3 8.1 %collective-permute-start.24 = (f32[128,128]{1,0:T(8,128)S(1)}, f32[128,128]{1,0:T(8,128)S(1)}, u32[]{:S(2)}, u32[]{:S(2)}) collective-permute-start(f32[128,128]{1,0:T(8,128)S(1)} %get-tuple-element.43.refs_0_), channel_id=1, source_target_pairs={{0,2},{1,3},{2,0},{3,1},{4,6},{5,7},{6,4},{7,5},{8,10},{9,11},{10,... | collective-permute-start | bytes 196616 | tf_op jit(solution)/shard_map/ppermute | solution.py:18
  69.0 6.1 %collective-permute-start.25 = (f32[128,128]{1,0:T(8,128)S(1)}, f32[128,128]{1,0:T(8,128)S(1)}, u32[]{:S(2)}, u32[]{:S(2)}) collective-permute-start(f32[128,128]{1,0:T(8,128)S(1)} %get-tuple-element.43.refs_0_), channel_id=1, source_target_pairs={{0,3},{1,2},{2,1},{3,0},{4,7},{5,6},{6,5},{7,4},{8,11},{9,10},{10,... | collective-permute-start | bytes 196616 | tf_op jit(solution)/shard_map/ppermute | solution.py:18
  70.7 3.6 %collective-permute-start.22 = (f32[8,128]{1,0:T(8,128)S(1)}, f32[8,128]{1,0:T(8,128)S(1)}, u32[]{:S(2)}, u32[]{:S(2)}) collective-permute-start(f32[8,128]{1,0:T(8,128)S(1)} %add_stat.6.one), channel_id=1, source_target_pairs={{0,8},{4,12},{8,0},{12,4},{1,9},{5,13},{9,1},{13,5},{2,10},{6,14},... | collective-permute-start | bytes 12296 | tf_op jit(solution)/shard_map/ppermute | solution.py:18
  (6 other events, 52.6 us)

commit v5 on v4

v5 whole, which is shorter than its diff:
```python
import functools

import jax
import jax.numpy as jnp
from jax import lax
from jax.experimental import pallas as pl
from jax.experimental.pallas import tpu as pltpu
from jax.sharding import PartitionSpec as P

ITERS = 2
LANES = 128
GROUP = 8
BF16 = jnp.bfloat16
F32 = jnp.float32


def shifted(value, axis, d, n):
    return lax.ppermute(value, axis, [(i, i ^ d) for i in range(n)])


def distances(n):
    return [d for d in range(n) if d > 1] + [1]


def moved(value, n, target):
    pairs = [(r * n + c, target(r, c)) for r in range(n) for c in range(n)]
    return lax.ppermute(value, ("row", "col"), [(s, t[0] * n + t[1]) for s, t in pairs])


def far_target(j):
    def target(r, c):
        d = r ^ c
        return (c ^ 2 * j, r) if d ^ 2 * j >= 2 else (c ^ (d & 1), c)

    return target


def far_source(j, n):
    back = {far_target(j)(r, c): (r, c) for r in range(n) for c in range(n)}
    return lambda r, c: back[r, c]


def spread_target(b):
    return lambda r, c: (r ^ b, c) if (r ^ c) % b == 0 else (r, c)


def bits(n):
    return [1 << i for i in range(n.bit_length() - 1)]


def load_pair(dst, tile, value):
    rhs = value.shape[0]
    high = value.astype(BF16)
    dst[tile, :rhs, :] = high
    dst[tile, rhs:, :] = (value - high.astype(F32)).astype(BF16)


def product(pair, block, contract):
    both = lax.dot_general(pair, block, (((1,), (contract,)), ((), ())), preferred_element_type=F32)
    rhs = both.shape[0] // 2
    return both[:rhs] + both[rhs:]


def pack_stats(columns, rhs):
    lane = lax.broadcasted_iota(jnp.int32, (8, LANES), 1)
    tile = jnp.zeros((8, LANES), F32)
    groups = rhs // 8
    for i, column in enumerate(columns):
        for g in range(groups):
            tile = jnp.where(lane == i * groups + g, column[g * 8:(g + 1) * 8], tile)
    return tile


def unpack_stat(tile, i, rhs):
    groups = rhs // 8
    return jnp.concatenate([tile[:, i * groups + g:i * groups + g + 1] for g in range(groups)], axis=0)


def accumulate(total, tile, value):
    width = value.shape[1] // LANES
    for part in range(width):
        total[tile * width + part] += value[:, part * LANES:(part + 1) * LANES]


def add_blocks(blocks, slot_rows, slot_cols, live, pairs, total, mirror, ready=None):
    read, write, contract = (slot_rows, slot_cols, 0) if mirror else (slot_cols, slot_rows, 1)

    def body(step, carry):
        if ready is not None:
            ready(step)
        values = []
        for g in range(GROUP):
            slot = step * GROUP + g
            value = product(pairs[read[0, 0, slot]], blocks[slot], contract)
            values.append((write[0, 0, slot], jnp.where(slot < live, value, 0.0)))
        for tile, value in values:
            accumulate(total, tile, value)
        return carry

    lax.fori_loop(0, (live + GROUP - 1) // GROUP, body, 0)


def image_part(parts, me, i, per, rhs):
    rows = slice((i % per) * rhs, (i % per + 1) * rhs)
    value = parts[0][rows, :]
    for d, part in zip(distances(len(parts)), parts[1:]):
        value = jnp.where(me ^ d == i // per, part[rows, :], value)
    return value


def row_sums(value):
    return jnp.sum(value, axis=1, keepdims=True)


def cross_sums(total, value):
    rhs = value.shape[0]
    cross = jnp.zeros((rhs, LANES), F32)
    for i in range(total.shape[0]):
        cross += total[i] * value[:, i * LANES:(i + 1) * LANES]
    return row_sums(cross)


def tree_sum(values):
    values = list(values)
    while len(values) > 1:
        values = [a + b for a, b in zip(values[::2], values[1::2])]
    return values[0]


def fetch_index(sources, targets, sems):
    copies = [pltpu.make_async_copy(s, t, sems.at[i]) for i, (s, t) in enumerate(zip(sources, targets))]
    for copy in copies:
        copy.start()
    return copies


def mirror_first_kernel(rows_hbm, cols_hbm, count, right_hbm, cov, total, blocks, *scratch):
    slot_rows, slot_cols, right, pairs, index_sems, right_sem, block_sems = scratch
    slots, tile_size = blocks.shape[:2]

    def block_copy(i):
        part = pl.ds(i * GROUP, GROUP)
        return pltpu.make_async_copy(cov.at[0, 0, part], blocks.at[part], block_sems.at[i])

    copies = fetch_index((rows_hbm, cols_hbm), (slot_rows, slot_cols), index_sems)
    load = pltpu.make_async_copy(right_hbm, right, right_sem)
    load.start()
    live = count[0, 0]
    for i in range(slots // GROUP):
        @pl.when(i * GROUP < live)
        def _():
            block_copy(i).start()
    total[...] = jnp.zeros_like(total)
    load.wait()
    for tile in range(right.shape[1] // tile_size):
        load_pair(pairs, tile, right[:, tile * tile_size:(tile + 1) * tile_size])
    for copy in copies:
        copy.wait()
    add_blocks(blocks, slot_rows, slot_cols, live, pairs, total, True, lambda i: block_copy(i).wait())


def mirror_second_kernel(rows_any, cols_any, count, near, blocks, total, *scratch):
    slot_rows, slot_cols, pairs, index_sems = scratch
    tile_size = blocks.shape[1]
    copies = fetch_index((rows_any, cols_any), (slot_rows, slot_cols), index_sems)
    total[...] = jnp.zeros_like(total)
    for tile in range(near.shape[1] // tile_size):
        load_pair(pairs, tile, near[:, tile * tile_size:(tile + 1) * tile_size])
    for copy in copies:
        copy.wait()
    add_blocks(blocks, slot_rows, slot_cols, count[0, 0], pairs, total, True)


def finish_direct(total, near, noise, stat, n):
    value = near[...]
    rhs = value.shape[0]
    square = value * value
    share = 1.0 / n
    bend = share * row_sums(square * noise[...]) + 2.0 * cross_sums(total, value)
    stat[...] = pack_stats([share * row_sums(square), bend], rhs)


def direct_first_kernel(n, rows_any, cols_any, count, noise, blocks, near, current, twin, mark, total, stat, far, *scratch):
    slot_rows, slot_cols, pairs, index_sems = scratch
    tile_size = blocks.shape[1]
    pieces = tile_size // LANES
    copies = fetch_index((rows_any, cols_any), (slot_rows, slot_cols), index_sems)
    odd = (lax.axis_index("row") ^ lax.axis_index("col")) & 1
    for o, source in enumerate((current, twin)):
        @pl.when(odd == o)
        def _():
            for tile in range(near.shape[1] // tile_size):
                value = source[:, tile * tile_size:(tile + 1) * tile_size]
                load_pair(pairs, tile, value)
                for i in range(pieces):
                    far[tile * pieces + i] = value[:, i * LANES:(i + 1) * LANES]
    total[...] = jnp.zeros_like(total)
    for copy in copies:
        copy.wait()
    add_blocks(blocks, slot_rows, slot_cols, count[0, 0], pairs, total, False)
    finish_direct(total, near, noise, stat, n)


def direct_second_kernel(n, rows_any, cols_any, count, noise, blocks, near, held, twin, mark, total, stat, *scratch):
    slot_rows, slot_cols, pairs, index_sems = scratch
    tile_size = blocks.shape[1]
    pieces = tile_size // LANES
    per = held.shape[0] // n
    copies = fetch_index((rows_any, cols_any), (slot_rows, slot_cols), index_sems)
    row = lax.axis_index("row")
    offset = row ^ lax.axis_index("col")
    for tile in range(near.shape[1] // tile_size):
        value = []
        for i in range(tile * pieces, (tile + 1) * pieces):
            own = jnp.logical_or(offset == 0, jnp.logical_and(offset >= 2, ((i // per) ^ row) & 1 == 0))
            value.append(jnp.where(own, held[i], twin[i]))
        load_pair(pairs, tile, jnp.concatenate(value, axis=1))
    total[...] = jnp.zeros_like(total)
    for copy in copies:
        copy.wait()
    add_blocks(blocks, slot_rows, slot_cols, count[0, 0], pairs, total, False)
    finish_direct(total, near, noise, stat, n)


def add_kernel(one, two, *refs):
    refs[-1][...] = one[...] + two[...]


def pick_kernel(b, current, arrived, mark, out):
    there = (lax.axis_index("row") ^ lax.axis_index("col")) & b
    out[...] = jnp.where(there != 0, arrived[...], current[...])


def split_kernel(n, mirror, twin, *outs):
    per = mirror.shape[0] // n
    rhs = mirror.shape[1]
    row = lax.axis_index("row")
    for j, out in enumerate(outs):
        first = (row ^ 2 * j) * per
        for i in range(per):
            out[i * rhs:(i + 1) * rhs, :] = mirror[first + i] + twin[first + i]


def merge_kernel(n, direct, mirror, twin, stat, *outs):
    per = direct.shape[0] // n
    rhs = direct.shape[1]
    me = lax.axis_index("col")
    diagonal = lax.axis_index("row") == me
    outs[n][...] = stat[...]
    for d, out in zip([0] + distances(n), outs):
        first = (me ^ d) * per

        @pl.when(diagonal)
        def _():
            for i in range(per):
                out[i * rhs:(i + 1) * rhs, :] = direct[first + i] + (mirror[first + i] + twin[first + i])

        @pl.when(jnp.logical_not(diagonal))
        def _():
            for i in range(per):
                out[i * rhs:(i + 1) * rhs, :] = direct[first + i]


def combine_kernel(n, near, noise, stat, *refs):
    parts, others, chunk = refs[:n], refs[n:-1], refs[-1]
    rhs = near.shape[0]
    data = parts[0].shape[0]
    per = data // rhs
    me = lax.axis_index("col")
    group = (lax.axis_index("row") ^ me) // 2
    value = tree_sum(ref[...] for ref in parts)
    for j, other in enumerate(others):
        value += jnp.where(group == j, 0.0, other[...])
    chunk[:data, :] = value
    chunk[data:, :] = stat[...]
    for k in range(n):
        @pl.when(me == k)
        def _():
            for i in range(per):
                lanes = slice((k * per + i) * LANES, (k * per + i + 1) * LANES)
                chunk[i * rhs:(i + 1) * rhs, :] += near[:, lanes] * noise[:, lanes]


def left_kernel(right, *refs):
    parts, (left, stat) = refs[:-2], refs[-2:]
    rhs, width = right.shape
    data = parts[0].shape[0] - 8
    per = data // rhs
    me = lax.axis_index("col")
    both = tree_sum(part[data:, :] for part in parts)
    stat[...] = both
    size_now = unpack_stat(both, 0, rhs) / unpack_stat(both, 1, rhs)
    for i in range(width // LANES):
        lanes = slice(i * LANES, (i + 1) * LANES)
        left[:, lanes] = right[:, lanes] - size_now * image_part(parts, me, i, per, rhs)


def held_kernel(n, left, stat, far, mark, *refs):
    parts, held = refs[:-1], refs[-1]
    rhs = left.shape[0]
    per = held.shape[0] // n
    row = lax.axis_index("row")
    diagonal = (row ^ lax.axis_index("col")) < 2
    size_now = unpack_stat(stat[...], 0, rhs) / unpack_stat(stat[...], 1, rhs)

    @pl.when(diagonal)
    def _():
        for i in range(held.shape[0]):
            held[i] = left[:, i * LANES:(i + 1) * LANES]

    @pl.when(jnp.logical_not(diagonal))
    def _():
        for j, part in enumerate(parts):
            first = (row ^ 2 * j) * per
            for i in range(per):
                held[first + i] = far[first + i] - size_now * part[i * rhs:(i + 1) * rhs, :]


def last_kernel(right, left, stat_now, *refs):
    parts, (solution, residual) = refs[:-2], refs[-2:]
    rhs, width = right.shape
    data = parts[0].shape[0] - 8
    per = data // rhs
    me = lax.axis_index("col")
    both = tree_sum(part[data:, :] for part in parts)
    norm = unpack_stat(stat_now[...], 0, rhs)
    norm_next = unpack_stat(both, 0, rhs)
    size_now = norm / unpack_stat(stat_now[...], 1, rhs)
    ratio = norm_next / norm
    size_next = norm_next / (unpack_stat(both, 1, rhs) - ratio * norm_next / size_now)
    back = ratio / size_now
    for i in range(width // LANES):
        lanes = slice(i * LANES, (i + 1) * LANES)
        first = right[:, lanes]
        now = left[:, lanes]
        solution[:, lanes] = size_now * first + size_next * (now + ratio * first)
        image = image_part(parts, me, i, per, rhs) + back * (first - now)
        residual[:, lanes] = now - size_next * image


def shape_of(*shape):
    return jax.ShapeDtypeStruct(shape, F32)


def on_device(n, right_sides, nugget, cov_blocks, block_rows, block_cols, block_count):
    rhs, width = right_sides.shape
    slots, tile_size = cov_blocks.shape[2:4]
    per = width // n // LANES
    data = per * rhs
    size = data + 8
    noise = nugget.reshape(1, width)
    index = (block_rows, block_cols, block_count)
    pair = pltpu.VMEM((width // tile_size, 2 * rhs, tile_size), BF16)
    index_scratch = [pltpu.SMEM(item.shape, item.dtype) for item in index[:2]]
    index_sems = pltpu.SemaphoreType.DMA((2,))
    vmem = pl.BlockSpec(memory_space=pltpu.VMEM)
    any_spec = pl.BlockSpec(memory_space=pl.ANY)
    smem = pl.BlockSpec(memory_space=pltpu.SMEM)
    hbm = pl.BlockSpec(memory_space=pltpu.HBM)
    params = pltpu.CompilerParams(vmem_limit_bytes=16 * 1024 * 1024)
    cost = pl.CostEstimate(flops=4 * rhs * slots * tile_size * tile_size, transcendentals=0,
                           bytes_accessed=2 * slots * tile_size * tile_size)
    field = shape_of(rhs, width)
    total = shape_of(width // LANES, rhs, LANES)
    chunk = shape_of(data, LANES)
    tile = shape_of(8, LANES)
    loaded = shape_of(size, LANES)

    def call(kernel, name, specs, outs, scratch, args, heavy=False):
        return pl.pallas_call(
            kernel,
            in_specs=specs,
            out_specs=jax.tree.map(lambda _: vmem, outs),
            out_shape=outs,
            scratch_shapes=scratch,
            compiler_params=params,
            cost_estimate=cost if heavy else None,
            name=name,
        )(*args)

    in_hbm = functools.partial(pltpu.with_memory_space_constraint, memory_space=pltpu.HBM)
    kernel_index = index_scratch + [pair, index_sems]

    def to_owners(mirror, twin):
        sent = call(functools.partial(split_kernel, n), "split", [vmem] * 2, [chunk] * (n // 2), [], (mirror, twin))
        return [moved(value, n, far_source(j, n)) for j, value in enumerate(sent)], sent[0]

    def gathered(near, mirror, twin, others, direct, stat):
        merged = call(functools.partial(merge_kernel, n), "merge", [vmem] * 4, [chunk] * n + [tile], [],
                      (direct, mirror, twin, stat))
        parts = [merged[0]] + [shifted(value, "col", d, n) for d, value in zip(distances(n), merged[1:n])]
        stat = merged[n]
        for b in bits(n):
            stat, = call(add_kernel, "add_stat", [vmem] * (2 + n // 2), [tile], [],
                         (stat, shifted(stat, "row", b, n), *others))
        own, = call(functools.partial(combine_kernel, n), "combine", [vmem] * (3 + n + n // 2), [loaded], [],
                    (near, noise, stat, *parts, *others))
        return [own] + [shifted(own, "col", d, n) for d in distances(n)]

    current = right_sides
    for b in bits(n)[:0:-1]:
        arrived = moved(current, n, spread_target(b))
        if b == n // 2:
            mirror, blocks = call(
                mirror_first_kernel, "mirror_first", [hbm] * 2 + [smem] + [hbm] * 2,
                [total, jax.ShapeDtypeStruct(cov_blocks.shape[2:], cov_blocks.dtype)],
                index_scratch + [pltpu.VMEM((rhs, width), F32), pair, index_sems,
                                 pltpu.SemaphoreType.DMA, pltpu.SemaphoreType.DMA((slots // GROUP,))],
                (*map(in_hbm, index[:2]), block_count, in_hbm(right_sides), in_hbm(cov_blocks)), True)
            twin_mirror = shifted(mirror, "row", 1, n)
        current, = call(functools.partial(pick_kernel, b), "pick", [vmem] * 3, [field], [], (current, arrived, mirror))
    twin = shifted(current, "row", 1, n)
    others, mark = to_owners(mirror, twin_mirror)
    direct, stat, far = call(
        functools.partial(direct_first_kernel, n), "direct_first", [any_spec] * 2 + [smem] + [vmem] * 6,
        [total, tile, total], kernel_index, (*index, noise, blocks, right_sides, current, twin, mark), True)
    parts = gathered(right_sides, mirror, twin_mirror, others, direct, stat)
    far_parts = [moved(parts[0], n, far_target(j)) for j in range(n // 2)]

    left, stat_now = call(left_kernel, "left", [vmem] * (n + 1), [field, tile], [], (right_sides, *parts))
    mirror, = call(mirror_second_kernel, "mirror_second", [any_spec] * 2 + [smem] + [vmem] * 2,
                   [total], kernel_index, (*index, left, blocks), True)
    twin_mirror = shifted(mirror, "row", 1, n)
    held, = call(functools.partial(held_kernel, n), "held", [vmem] * (4 + n // 2), [total], [],
                 (left, stat_now, far, mirror, *far_parts))
    twin = shifted(held, "row", 1, n)
    others, mark = to_owners(mirror, twin_mirror)
    direct, stat = call(
        functools.partial(direct_second_kernel, n), "direct_second", [any_spec] * 2 + [smem] + [vmem] * 6,
        [total, tile], kernel_index, (*index, noise, blocks, left, held, twin, mark), True)
    parts = gathered(left, mirror, twin_mirror, others, direct, stat)
    return tuple(call(last_kernel, "last", [vmem] * (n + 3), [field, field], [],
                      (right_sides, left, stat_now, *parts)))


def solution(mesh):
    n = mesh.shape["row"]
    assert n == mesh.shape["col"] and n & (n - 1) == 0 and n >= 4
    placed = (
        P(None, ("groups", "row")),
        P(("groups", "row")),
        P(("groups", "row"), "col", None, None, None),
        P(("groups", "row"), "col", None),
        P(("groups", "row"), "col", None),
        P(("groups", "row"), "col"),
    )
    return jax.shard_map(
        functools.partial(on_device, n),
        mesh=mesh,
        in_specs=placed,
        out_specs=(P(None, ("groups", "row")), P(None, ("groups", "row"))),
        check_vma=False,
    )
```

time: 76.7 us -> 67.7 us (0.88)
  waiting for transfers between devices: 26.2 us -> 18.9 us
  starting transfers between devices: 41.7 us -> 38.1 us
  Pallas kernels: 6.71 us -> 8.73 us
    ppermute x10 -> x7, waiting for transfers between devices: 11.5 us -> 1.5 us  [moved(): lax.ppermute(value, ('row', 'col'), [(s, t[0] * n + t[1]) for s, t in pai...]
    ppermute x10 -> x7, starting transfers between devices: 20.5 us -> 14.7 us  [moved(): lax.ppermute(value, ('row', 'col'), [(s, t[0] * n + t[1]) for s, t in pai...]
    ppermute x16 -> x20, waiting for transfers between devices: 14.7 us -> 17.4 us  [shifted(): return lax.ppermute(value, axis, [(i, i ^ d) for i in range(n)])]
    ppermute x16 -> x20, starting transfers between devices: 21.2 us -> 23.4 us  [shifted(): return lax.ppermute(value, axis, [(i, i ^ d) for i in range(n)])]
    pallas_call x18, Pallas kernels: 6.71 us -> 8.73 us  [call(): pl.pallas_call(kernel, in_specs=specs, out_specs=jax.tree.map(lambda _: v...]
  transfers between devices with their start and end apart: 26 -> 27, of which waited for: 12 -> 12; matrix products, arithmetic and copies ran while one was open for 0% -> 0% of each run, Pallas kernels for 7% -> 11%
where the time goes in v5:
time: 67.7 us; the launch traced here: 67.3 us
  starting transfers between devices  38.1 us (56%)
  waiting for transfers between devices  18.9 us (28%)
  Pallas kernels  8.73 us (13%)
  between operations  1.56 us (2%)
    ppermute x20, starting transfers between devices, shifted(): return lax.ppermute(value, axis, [(i, i ^ d) for i in range(n)])  23.4 us
    ppermute x20, waiting for transfers between devices, shifted(): return lax.ppermute(value, axis, [(i, i ^ d) for i in range(n)])  17.4 us
    ppermute x7, starting transfers between devices, moved(): lax.ppermute(value, ('row', 'col'), [(s, t[0] * n + t[1]) for s, t in pai...  14.7 us
    pallas_call x18, Pallas kernels, call(): pl.pallas_call(kernel, in_specs=specs, out_specs=jax.tree.map(lambda _: v...  8.73 us
    ppermute x7, waiting for transfers between devices, moved(): lax.ppermute(value, ('row', 'col'), [(s, t[0] * n + t[1]) for s, t in pai...  1.5 us
  transfers between devices with their start and end apart: 27, of which 12 were waited for; matrix products, arithmetic and copies ran while one was open for 0% of the time, Pallas kernels for 11%

profile of v5, /device:TPU:0, one launch (start us, length us, event | category | flops | bytes accessed | tf_op | source)
XLA Modules:
  0.0 67.3 jit_solution(1637826841718698205)
XLA Ops:
  0.7 5.0 %collective-permute-start = (f32[32,2048]{1,0:T(8,128)}, f32[32,2048]{1,0:T(8,128)S(1)}, u32[]{:S(2)}, u32[]{:S(2)}) collective-permute-start(f32[32,2048]{1,0:T(8,128)} %right.3), channel_id=1, source_target_pairs={{0,8},{1,1},{2,10},{3,3},{4,4},{5,13},{6,6},{7,15},{8,0},{9,9},{10... | collective-permute-start | bytes 786440 | tf_op jit(solution)/shard_map/ppermute | solution.py:27
  6.3 2.3 %mirror_first.1 = (f32[16,32,128]{2,1,0:T(8,128)S(1)}, bf16[32,256,256]{2,1,0:T(8,128)(2,1)S(1)}) custom-call(s32[1,1,32]{2,1,0:T(1,128)} %rows_any.5, s32[1,1,32]{2,1,0:T(1,128)} %cols_any.5, s32[1,1]{1,0:T(1,128)S(6)} %copy.8.count, f32[32,2048]{1,0:T(8,128)} %right.3, bf16[1,1,32,256,256]{4,3,2,1,0:T(8,128)(2,1)} %cov.1), custom_call_target="tpu_custom_call" | custom-call | flops 268435456 | bytes 4194304 | tf_op jit(solution)/shard_map/mirror_first/pallas_call | solution.py:370
  8.7 1.5 %collective-permute-done.arrived = f32[32,2048]{1,0:T(8,128)S(1)} collective-permute-done((f32[32,2048]{1,0:T(8,128)}, f32[32,2048]{1,0:T(8,128)S(1)}, u32[]{:S(2)}, u32[]{:S(2)}) %collective-permute-start) | collective-permute-done | bytes 262176 | tf_op jit(solution)/shard_map/ppermute | solution.py:27
  10.4 2.1 %collective-permute-start.5 = (f32[128,128]{1,0:T(8,128)S(1)}, f32[128,128]{1,0:T(8,128)S(1)}, u32[]{:S(2)}, u32[]{:S(2)}) collective-permute-start(f32[128,128]{1,0:T(8,128)S(1)} %get-tuple-element.31), channel_id=1, source_target_pairs={{0,8},{1,9},{2,10},{3,14},{4,12},{5,13},{6,11},{7,15},{8,0},{9,4},... | collective-permute-start | bytes 196616 | tf_op jit(solution)/shard_map/ppermute | solution.py:27
  13.1 1.6 %direct_first.1 = (f32[16,32,128]{2,1,0:T(8,128)S(1)}, f32[8,128]{1,0:T(8,128)S(1)}, f32[16,32,128]{2,1,0:T(8,128)S(1)}) custom-call(s32[1,1,32]{2,1,0:T(1,128)S(1)} %copy-done.2, s32[1,1,32]{2,1,0:T(1,128)S(1)} %copy-done.3, s32[1,1]{1,0:T(1,128)S(6)} %copy.8.count, f32[1,2048]{1,0:T(1,128)S(1)} %bitcast.1, ...), custom_call_target="tpu_custom_call" | custom-call | flops 268435456 | bytes 4194304 | tf_op jit(solution)/shard_map/direct_first/pallas_call | solution.py:370
  14.9 4.3 %collective-permute-start.7 = (f32[128,128]{1,0:T(8,128)S(1)}, f32[128,128]{1,0:T(8,128)S(1)}, u32[]{:S(2)}, u32[]{:S(2)}) collective-permute-start(f32[128,128]{1,0:T(8,128)S(1)} %get-tuple-element.33), channel_id=1, source_target_pairs={{0,2},{1,3},{2,0},{3,1},{4,6},{5,7},{6,4},{7,5},{8,10},{9,11},{10,... | collective-permute-start | bytes 196616 | tf_op jit(solution)/shard_map/ppermute | solution.py:18
  20.3 1.2 %collective-permute-done.3.two = f32[8,128]{1,0:T(8,128)S(1)} collective-permute-done((f32[8,128]{1,0:T(8,128)S(1)}, f32[8,128]{1,0:T(8,128)S(1)}, u32[]{:S(2)}, u32[]{:S(2)}) %collective-permute-start.3) | collective-permute-done | bytes 4128 | tf_op jit(solution)/shard_map/ppermute | solution.py:18
  21.5 3.3 %collective-permute-start.6 = (f32[8,128]{1,0:T(8,128)S(1)}, f32[8,128]{1,0:T(8,128)S(1)}, u32[]{:S(2)}, u32[]{:S(2)}) collective-permute-start(f32[8,128]{1,0:T(8,128)S(1)} %add_stat.4.one), channel_id=1, source_target_pairs={{0,8},{4,12},{8,0},{12,4},{1,9},{5,13},{9,1},{13,5},{2,10},{6,14},... | collective-permute-start | bytes 12296 | tf_op jit(solution)/shard_map/ppermute | solution.py:18
  24.8 1.6 %collective-permute-done.6.two = f32[8,128]{1,0:T(8,128)S(1)} collective-permute-done((f32[8,128]{1,0:T(8,128)S(1)}, f32[8,128]{1,0:T(8,128)S(1)}, u32[]{:S(2)}, u32[]{:S(2)}) %collective-permute-start.6) | collective-permute-done | bytes 4128 | tf_op jit(solution)/shard_map/ppermute | solution.py:18
  26.4 1.0 %collective-permute-start.12 = (f32[136,128]{1,0:T(8,128)S(1)}, f32[136,128]{1,0:T(8,128)S(1)}, u32[]{:S(2)}, u32[]{:S(2)}) collective-permute-start(f32[136,128]{1,0:T(8,128)S(1)} %combine.2.refs_0_), channel_id=1, source_target_pairs={{0,1},{1,0},{2,3},{3,2},{4,5},{5,4},{6,7},{7,6},{8,9},{9,8},{10,11... | collective-permute-start | bytes 208904 | tf_op jit(solution)/shard_map/ppermute | solution.py:18
  27.4 2.5 %collective-permute-start.11 = (f32[136,128]{1,0:T(8,128)S(1)}, f32[136,128]{1,0:T(8,128)S(1)}, u32[]{:S(2)}, u32[]{:S(2)}) collective-permute-start(f32[136,128]{1,0:T(8,128)S(1)} %combine.2.refs_0_), channel_id=1, source_target_pairs={{0,3},{1,2},{2,1},{3,0},{4,7},{5,6},{6,5},{7,4},{8,11},{9,10},{10,... | collective-permute-start | bytes 208904 | tf_op jit(solution)/shard_map/ppermute | solution.py:18
  30.0 2.6 %collective-permute-start.14 = (f32[136,128]{1,0:T(8,128)S(1)}, f32[136,128]{1,0:T(8,128)S(1)}, u32[]{:S(2)}, u32[]{:S(2)}) collective-permute-start(f32[136,128]{1,0:T(8,128)S(1)} %combine.2.refs_0_), channel_id=1, source_target_pairs={{0,8},{1,12},{2,10},{3,11},{4,9},{5,13},{6,14},{7,15},{8,0},{9,1},... | collective-permute-start | bytes 208904 | tf_op jit(solution)/shard_map/ppermute | solution.py:27
  33.8 2.3 %collective-permute-done.10.refs_1_ = f32[136,128]{1,0:T(8,128)S(1)} collective-permute-done((f32[136,128]{1,0:T(8,128)S(1)}, f32[136,128]{1,0:T(8,128)S(1)}, u32[]{:S(2)}, u32[]{:S(2)}) %collective-permute-start.10) | collective-permute-done | bytes 69664 | tf_op jit(solution)/shard_map/ppermute | solution.py:18
  36.4 1.2 %mirror_second.1.mark.mirror = f32[16,32,128]{2,1,0:T(8,128)S(1)} custom-call(s32[1,1,32]{2,1,0:T(1,128)S(1)} %copy-done.2, s32[1,1,32]{2,1,0:T(1,128)S(1)} %copy-done.3, s32[1,1]{1,0:T(1,128)S(6)} %copy.8.count, f32[32,2048]{1,0:T(8,128)S(1)} %get-tuple-element.36.near.left, bf16[32,256,256]{2,1,0:T(8,128)(2,1)S(1)} %get-tuple-element.25.blocks), custom_call_target="tpu_custom_call" | custom-call | flops 268435456 | bytes 4194304 | tf_op jit(solution)/shard_map/mirror_second/pallas_call | solution.py:370
  39.3 3.1 %collective-permute-start.19 = (f32[128,128]{1,0:T(8,128)S(1)}, f32[128,128]{1,0:T(8,128)S(1)}, u32[]{:S(2)}, u32[]{:S(2)}) collective-permute-start(f32[128,128]{1,0:T(8,128)S(1)} %get-tuple-element.43), channel_id=1, source_target_pairs={{0,8},{1,9},{2,10},{3,14},{4,12},{5,13},{6,11},{7,15},{8,0},{9,4},... | collective-permute-start | bytes 196616 | tf_op jit(solution)/shard_map/ppermute | solution.py:27
  43.1 1.6 %direct_second.1 = (f32[16,32,128]{2,1,0:T(8,128)S(1)}, f32[8,128]{1,0:T(8,128)S(1)}) custom-call(s32[1,1,32]{2,1,0:T(1,128)S(1)} %copy-done.2, s32[1,1,32]{2,1,0:T(1,128)S(1)} %copy-done.3, s32[1,1]{1,0:T(1,128)S(6)} %copy.8.count, f32[1,2048]{1,0:T(1,128)S(1)} %bitcast.3, bf16[32,256,256]{2,1,0:T(8,128)(2,1)S(1)} %get-tuple-element.25.blocks, ...), custom_call_target="tpu_custom_call" | custom-call | flops 268435456 | bytes 4194304 | tf_op jit(solution)/shard_map/direct_second/pallas_call | solution.py:370
  45.0 4.0 %collective-permute-start.21 = (f32[128,128]{1,0:T(8,128)S(1)}, f32[128,128]{1,0:T(8,128)S(1)}, u32[]{:S(2)}, u32[]{:S(2)}) collective-permute-start(f32[128,128]{1,0:T(8,128)S(1)} %get-tuple-element.45), channel_id=1, source_target_pairs={{0,2},{1,3},{2,0},{3,1},{4,6},{5,7},{6,4},{7,5},{8,10},{9,11},{10,... | collective-permute-start | bytes 196616 | tf_op jit(solution)/shard_map/ppermute | solution.py:18
  50.1 1.2 %collective-permute-start.20 = (f32[8,128]{1,0:T(8,128)S(1)}, f32[8,128]{1,0:T(8,128)S(1)}, u32[]{:S(2)}, u32[]{:S(2)}) collective-permute-start(f32[8,128]{1,0:T(8,128)S(1)} %add_stat.6.one), channel_id=1, source_target_pairs={{0,8},{4,12},{8,0},{12,4},{1,9},{5,13},{9,1},{13,5},{2,10},{6,14},... | collective-permute-start | bytes 12296 | tf_op jit(solution)/shard_map/ppermute | solution.py:18
  51.3 2.5 %collective-permute-done.20.two = f32[8,128]{1,0:T(8,128)S(1)} collective-permute-done((f32[8,128]{1,0:T(8,128)S(1)}, f32[8,128]{1,0:T(8,128)S(1)}, u32[]{:S(2)}, u32[]{:S(2)}) %collective-permute-start.20) | collective-permute-done | bytes 4128 | tf_op jit(solution)/shard_map/ppermute | solution.py:18
  53.8 1.9 %collective-permute-done.22.refs_2_ = f32[128,128]{1,0:T(8,128)S(1)} collective-permute-done((f32[128,128]{1,0:T(8,128)S(1)}, f32[128,128]{1,0:T(8,128)S(1)}, u32[]{:S(2)}, u32[]{:S(2)}) %collective-permute-start.22) | collective-permute-done | bytes 65568 | tf_op jit(solution)/shard_map/ppermute | solution.py:18
  56.6 3.2 %collective-permute-start.25 = (f32[136,128]{1,0:T(8,128)S(1)}, f32[136,128]{1,0:T(8,128)S(1)}, u32[]{:S(2)}, u32[]{:S(2)}) collective-permute-start(f32[136,128]{1,0:T(8,128)S(1)} %combine.3.refs_0_), channel_id=1, source_target_pairs={{0,3},{1,2},{2,1},{3,0},{4,7},{5,6},{6,5},{7,4},{8,11},{9,10},{10,... | collective-permute-start | bytes 208904 | tf_op jit(solution)/shard_map/ppermute | solution.py:18
  60.3 3.5 %collective-permute-done.25.refs_2_ = f32[136,128]{1,0:T(8,128)S(1)} collective-permute-done((f32[136,128]{1,0:T(8,128)S(1)}, f32[136,128]{1,0:T(8,128)S(1)}, u32[]{:S(2)}, u32[]{:S(2)}) %collective-permute-start.25) | collective-permute-done | bytes 69664 | tf_op jit(solution)/shard_map/ppermute | solution.py:18
  63.8 2.2 %collective-permute-done.24.refs_1_ = f32[136,128]{1,0:T(8,128)S(1)} collective-permute-done((f32[136,128]{1,0:T(8,128)S(1)}, f32[136,128]{1,0:T(8,128)S(1)}, u32[]{:S(2)}, u32[]{:S(2)}) %collective-permute-start.24) | collective-permute-done | bytes 69664 | tf_op jit(solution)/shard_map/ppermute | solution.py:18
  66.1 1.2 %last.1 = (f32[32,2048]{1,0:T(8,128)}, f32[32,2048]{1,0:T(8,128)}) custom-call(f32[32,2048]{1,0:T(8,128)S(1)} %copy-done, f32[32,2048]{1,0:T(8,128)S(1)} %get-tuple-element.36.near.left, f32[8,128]{1,0:T(8,128)S(1)} %get-tuple-element.37.stat.stat_now, f32[136,128]{1,0:T(8,128)S(1)} %combine.3.refs_0_, f32[136,128]{1,0:T(8,128)S(1)} %collective-permute-done.24.refs_1_, ...), custom_call_target="tpu_custom_call" | custom-call | tf_op jit(solution)/shard_map/last/pallas_call | solution.py:370
  (56 shorter events, 8.7 us)
Async XLA Ops:
  0.7 9.5 %collective-permute-start = (f32[32,2048]{1,0:T(8,128)}, f32[32,2048]{1,0:T(8,128)S(1)}, u32[]{:S(2)}, u32[]{:S(2)}) collective-permute-start(f32[32,2048]{1,0:T(8,128)} %right.3), channel_id=1, source_target_pairs={{0,8},{1,1},{2,10},{3,3},{4,4},{5,13},{6,6},{7,15},{8,0},{9,9},{10... | collective-permute-start | bytes 786440 | tf_op jit(solution)/shard_map/ppermute | solution.py:27
  10.2 2.9 %collective-permute-start.1 = (f32[32,2048]{1,0:T(8,128)S(1)}, f32[32,2048]{1,0:T(8,128)S(1)}, u32[]{:S(2)}, u32[]{:S(2)}) collective-permute-start(f32[32,2048]{1,0:T(8,128)S(1)} %pick.1.current), channel_id=1, source_target_pairs={{0,4},{4,0},{8,12},{12,8},{1,5},{5,1},{9,13},{13,9},{2,6},{6,2},{1... | collective-permute-start | bytes 786440 | tf_op jit(solution)/shard_map/ppermute | solution.py:18
  10.4 9.9 %collective-permute-start.5 = (f32[128,128]{1,0:T(8,128)S(1)}, f32[128,128]{1,0:T(8,128)S(1)}, u32[]{:S(2)}, u32[]{:S(2)}) collective-permute-start(f32[128,128]{1,0:T(8,128)S(1)} %get-tuple-element.31), channel_id=1, source_target_pairs={{0,8},{1,9},{2,10},{3,14},{4,12},{5,13},{6,11},{7,15},{8,0},{9,4},... | collective-permute-start | bytes 196616 | tf_op jit(solution)/shard_map/ppermute | solution.py:27
  12.4 7.9 %collective-permute-start.4 = (f32[128,128]{1,0:T(8,128)S(1)}, f32[128,128]{1,0:T(8,128)S(1)}, u32[]{:S(2)}, u32[]{:S(2)}) collective-permute-start(f32[128,128]{1,0:T(8,128)S(1)} %get-tuple-element.27.mark), channel_id=1, source_target_pairs={{0,0},{1,1},{2,8},{3,12},{4,4},{5,5},{6,9},{7,13},{8,2},{9,6},{10,... | collective-permute-start | bytes 196616 | tf_op jit(solution)/shard_map/ppermute | solution.py:27
  14.9 11.5 %collective-permute-start.7 = (f32[128,128]{1,0:T(8,128)S(1)}, f32[128,128]{1,0:T(8,128)S(1)}, u32[]{:S(2)}, u32[]{:S(2)}) collective-permute-start(f32[128,128]{1,0:T(8,128)S(1)} %get-tuple-element.33), channel_id=1, source_target_pairs={{0,2},{1,3},{2,0},{3,1},{4,6},{5,7},{6,4},{7,5},{8,10},{9,11},{10,... | collective-permute-start | bytes 196616 | tf_op jit(solution)/shard_map/ppermute | solution.py:18
  19.2 7.2 %collective-permute-start.8 = (f32[128,128]{1,0:T(8,128)S(1)}, f32[128,128]{1,0:T(8,128)S(1)}, u32[]{:S(2)}, u32[]{:S(2)}) collective-permute-start(f32[128,128]{1,0:T(8,128)S(1)} %get-tuple-element.34), channel_id=1, source_target_pairs={{0,3},{1,2},{2,1},{3,0},{4,7},{5,6},{6,5},{7,4},{8,11},{9,10},{10,... | collective-permute-start | bytes 196616 | tf_op jit(solution)/shard_map/ppermute | solution.py:18
  19.8 6.6 %collective-permute-start.9 = (f32[128,128]{1,0:T(8,128)S(1)}, f32[128,128]{1,0:T(8,128)S(1)}, u32[]{:S(2)}, u32[]{:S(2)}) collective-permute-start(f32[128,128]{1,0:T(8,128)S(1)} %get-tuple-element.35), channel_id=1, source_target_pairs={{0,1},{1,0},{2,3},{3,2},{4,5},{5,4},{6,7},{7,6},{8,9},{9,8},{10,11... | collective-permute-start | bytes 196616 | tf_op jit(solution)/shard_map/ppermute | solution.py:18
  21.5 4.9 %collective-permute-start.6 = (f32[8,128]{1,0:T(8,128)S(1)}, f32[8,128]{1,0:T(8,128)S(1)}, u32[]{:S(2)}, u32[]{:S(2)}) collective-permute-start(f32[8,128]{1,0:T(8,128)S(1)} %add_stat.4.one), channel_id=1, source_target_pairs={{0,8},{4,12},{8,0},{12,4},{1,9},{5,13},{9,1},{13,5},{2,10},{6,14},... | collective-permute-start | bytes 12296 | tf_op jit(solution)/shard_map/ppermute | solution.py:18
  26.4 6.8 %collective-permute-start.12 = (f32[136,128]{1,0:T(8,128)S(1)}, f32[136,128]{1,0:T(8,128)S(1)}, u32[]{:S(2)}, u32[]{:S(2)}) collective-permute-start(f32[136,128]{1,0:T(8,128)S(1)} %combine.2.refs_0_), channel_id=1, source_target_pairs={{0,1},{1,0},{2,3},{3,2},{4,5},{5,4},{6,7},{7,6},{8,9},{9,8},{10,11... | collective-permute-start | bytes 208904 | tf_op jit(solution)/shard_map/ppermute | solution.py:18
  27.4 6.4 %collective-permute-start.11 = (f32[136,128]{1,0:T(8,128)S(1)}, f32[136,128]{1,0:T(8,128)S(1)}, u32[]{:S(2)}, u32[]{:S(2)}) collective-permute-start(f32[136,128]{1,0:T(8,128)S(1)} %combine.2.refs_0_), channel_id=1, source_target_pairs={{0,3},{1,2},{2,1},{3,0},{4,7},{5,6},{6,5},{7,4},{8,11},{9,10},{10,... | collective-permute-start | bytes 208904 | tf_op jit(solution)/shard_map/ppermute | solution.py:18
  30.0 6.2 %collective-permute-start.10 = (f32[136,128]{1,0:T(8,128)S(1)}, f32[136,128]{1,0:T(8,128)S(1)}, u32[]{:S(2)}, u32[]{:S(2)}) collective-permute-start(f32[136,128]{1,0:T(8,128)S(1)} %combine.2.refs_0_), channel_id=1, source_target_pairs={{0,2},{1,3},{2,0},{3,1},{4,6},{5,7},{6,4},{7,5},{8,10},{9,11},{10,... | collective-permute-start | bytes 208904 | tf_op jit(solution)/shard_map/ppermute | solution.py:18
  30.0 7.7 %collective-permute-start.14 = (f32[136,128]{1,0:T(8,128)S(1)}, f32[136,128]{1,0:T(8,128)S(1)}, u32[]{:S(2)}, u32[]{:S(2)}) collective-permute-start(f32[136,128]{1,0:T(8,128)S(1)} %combine.2.refs_0_), channel_id=1, source_target_pairs={{0,8},{1,12},{2,10},{3,11},{4,9},{5,13},{6,14},{7,15},{8,0},{9,1},... | collective-permute-start | bytes 208904 | tf_op jit(solution)/shard_map/ppermute | solution.py:27
  32.6 5.2 %collective-permute-start.13 = (f32[136,128]{1,0:T(8,128)S(1)}, f32[136,128]{1,0:T(8,128)S(1)}, u32[]{:S(2)}, u32[]{:S(2)}) collective-permute-start(f32[136,128]{1,0:T(8,128)S(1)} %combine.2.refs_0_), channel_id=1, source_target_pairs={{0,0},{1,1},{2,8},{3,12},{4,4},{5,5},{6,9},{7,13},{8,2},{9,6},{10,... | collective-permute-start | bytes 208904 | tf_op jit(solution)/shard_map/ppermute | solution.py:27
  37.9 5.2 %collective-permute-start.15 = (f32[16,32,128]{2,1,0:T(8,128)S(1)}, f32[16,32,128]{2,1,0:T(8,128)S(1)}, u32[]{:S(2)}, u32[]{:S(2)}) collective-permute-start(f32[16,32,128]{2,1,0:T(8,128)S(1)} %held.1), channel_id=1, source_target_pairs={{0,4},{4,0},{8,12},{12,8},{1,5},{5,1},{9,13},{13,9},{2,6},{6,2},{1... | collective-permute-start | bytes 786440 | tf_op jit(solution)/shard_map/ppermute | solution.py:18
  39.3 10.8 %collective-permute-start.19 = (f32[128,128]{1,0:T(8,128)S(1)}, f32[128,128]{1,0:T(8,128)S(1)}, u32[]{:S(2)}, u32[]{:S(2)}) collective-permute-start(f32[128,128]{1,0:T(8,128)S(1)} %get-tuple-element.43), channel_id=1, source_target_pairs={{0,8},{1,9},{2,10},{3,14},{4,12},{5,13},{6,11},{7,15},{8,0},{9,4},... | collective-permute-start | bytes 196616 | tf_op jit(solution)/shard_map/ppermute | solution.py:27
  42.4 7.7 %collective-permute-start.18 = (f32[128,128]{1,0:T(8,128)S(1)}, f32[128,128]{1,0:T(8,128)S(1)}, u32[]{:S(2)}, u32[]{:S(2)}) collective-permute-start(f32[128,128]{1,0:T(8,128)S(1)} %get-tuple-element.39.mark), channel_id=1, source_target_pairs={{0,0},{1,1},{2,8},{3,12},{4,4},{5,5},{6,9},{7,13},{8,2},{9,6},{10,... | collective-permute-start | bytes 196616 | tf_op jit(solution)/shard_map/ppermute | solution.py:27
  44.8 4.8 %collective-permute-start.17 = (f32[8,128]{1,0:T(8,128)S(1)}, f32[8,128]{1,0:T(8,128)S(1)}, u32[]{:S(2)}, u32[]{:S(2)}) collective-permute-start(f32[8,128]{1,0:T(8,128)S(1)} %get-tuple-element.42.one), channel_id=1, source_target_pairs={{0,4},{4,0},{8,12},{12,8},{1,5},{5,1},{9,13},{13,9},{2,6},{6,2},{1... | collective-permute-start | bytes 12296 | tf_op jit(solution)/shard_map/ppermute | solution.py:18
  45.0 8.8 %collective-permute-start.21 = (f32[128,128]{1,0:T(8,128)S(1)}, f32[128,128]{1,0:T(8,128)S(1)}, u32[]{:S(2)}, u32[]{:S(2)}) collective-permute-start(f32[128,128]{1,0:T(8,128)S(1)} %get-tuple-element.45), channel_id=1, source_target_pairs={{0,2},{1,3},{2,0},{3,1},{4,6},{5,7},{6,4},{7,5},{8,10},{9,11},{10,... | collective-permute-start | bytes 196616 | tf_op jit(solution)/shard_map/ppermute | solution.py:18
  49.0 6.7 %collective-permute-start.22 = (f32[128,128]{1,0:T(8,128)S(1)}, f32[128,128]{1,0:T(8,128)S(1)}, u32[]{:S(2)}, u32[]{:S(2)}) collective-permute-start(f32[128,128]{1,0:T(8,128)S(1)} %get-tuple-element.46), channel_id=1, source_target_pairs={{0,3},{1,2},{2,1},{3,0},{4,7},{5,6},{6,5},{7,4},{8,11},{9,10},{10,... | collective-permute-start | bytes 196616 | tf_op jit(solution)/shard_map/ppermute | solution.py:18
  49.6 6.3 %collective-permute-start.23 = (f32[128,128]{1,0:T(8,128)S(1)}, f32[128,128]{1,0:T(8,128)S(1)}, u32[]{:S(2)}, u32[]{:S(2)}) collective-permute-start(f32[128,128]{1,0:T(8,128)S(1)} %get-tuple-element.47), channel_id=1, source_target_pairs={{0,1},{1,0},{2,3},{3,2},{4,5},{5,4},{6,7},{7,6},{8,9},{9,8},{10,11... | collective-permute-start | bytes 196616 | tf_op jit(solution)/shard_map/ppermute | solution.py:18
  50.1 3.7 %collective-permute-start.20 = (f32[8,128]{1,0:T(8,128)S(1)}, f32[8,128]{1,0:T(8,128)S(1)}, u32[]{:S(2)}, u32[]{:S(2)}) collective-permute-start(f32[8,128]{1,0:T(8,128)S(1)} %add_stat.6.one), channel_id=1, source_target_pairs={{0,8},{4,12},{8,0},{12,4},{1,9},{5,13},{9,1},{13,5},{2,10},{6,14},... | collective-permute-start | bytes 12296 | tf_op jit(solution)/shard_map/ppermute | solution.py:18
  55.9 4.4 %collective-permute-start.26 = (f32[136,128]{1,0:T(8,128)S(1)}, f32[136,128]{1,0:T(8,128)S(1)}, u32[]{:S(2)}, u32[]{:S(2)}) collective-permute-start(f32[136,128]{1,0:T(8,128)S(1)} %combine.3.refs_0_), channel_id=1, source_target_pairs={{0,1},{1,0},{2,3},{3,2},{4,5},{5,4},{6,7},{7,6},{8,9},{9,8},{10,11... | collective-permute-start | bytes 208904 | tf_op jit(solution)/shard_map/ppermute | solution.py:18
  56.6 7.2 %collective-permute-start.25 = (f32[136,128]{1,0:T(8,128)S(1)}, f32[136,128]{1,0:T(8,128)S(1)}, u32[]{:S(2)}, u32[]{:S(2)}) collective-permute-start(f32[136,128]{1,0:T(8,128)S(1)} %combine.3.refs_0_), channel_id=1, source_target_pairs={{0,3},{1,2},{2,1},{3,0},{4,7},{5,6},{6,5},{7,4},{8,11},{9,10},{10,... | collective-permute-start | bytes 208904 | tf_op jit(solution)/shard_map/ppermute | solution.py:18
  59.8 6.2 %collective-permute-start.24 = (f32[136,128]{1,0:T(8,128)S(1)}, f32[136,128]{1,0:T(8,128)S(1)}, u32[]{:S(2)}, u32[]{:S(2)}) collective-permute-start(f32[136,128]{1,0:T(8,128)S(1)} %combine.3.refs_0_), channel_id=1, source_target_pairs={{0,2},{1,3},{2,0},{3,1},{4,6},{5,7},{6,4},{7,5},{8,10},{9,11},{10,... | collective-permute-start | bytes 208904 | tf_op jit(solution)/shard_map/ppermute | solution.py:18
  (7 other events, 51.4 us)

commit v6 on v5

--- a/solution.py
+++ b/solution.py
@@ -30,7 +30,9 @@
 def far_target(j):
     def target(r, c):
         d = r ^ c
-        return (c ^ 2 * j, r) if d ^ 2 * j >= 2 else (c ^ (d & 1), c)
+        if d ^ 2 * j >= 2:
+            return c ^ 2 * j, r
+        return c ^ (d & 1) ^ (j == 0), c
 
     return target
 
@@ -41,7 +43,12 @@
 
 
 def spread_target(b):
-    return lambda r, c: (r ^ b, c) if (r ^ c) % b == 0 else (r, c)
+    def target(r, c):
+        o = r ^ c
+        move = {0: b, b: 1, b + 1: b, 1: 1}.get(o % (2 * b), 1)
+        return r ^ move, c
+
+    return target
 
 
 def bits(n):
@@ -103,7 +110,7 @@
 def image_part(parts, me, i, per, rhs):
     rows = slice((i % per) * rhs, (i % per + 1) * rhs)
     value = parts[0][rows, :]
-    for d, part in zip(distances(len(parts)), parts[1:]):
+    for d, part in zip(distances(len(parts))[::-1], parts[1:]):
         value = jnp.where(me ^ d == i // per, part[rows, :], value)
     return value
 
@@ -125,6 +132,11 @@
     while len(values) > 1:
         values = [a + b for a, b in zip(values[::2], values[1::2])]
     return values[0]
+
+
+def stat_sum(parts, data):
+    order = [0] + distances(len(parts))[::-1]
+    return tree_sum(parts[order.index(d)][data:, :] for d in range(len(parts)))
 
 
 def fetch_index(sources, targets, sems):
@@ -287,7 +299,7 @@
     data = parts[0].shape[0] - 8
     per = data // rhs
     me = lax.axis_index("col")
-    both = tree_sum(part[data:, :] for part in parts)
+    both = stat_sum(parts, data)
     stat[...] = both
     size_now = unpack_stat(both, 0, rhs) / unpack_stat(both, 1, rhs)
     for i in range(width // LANES):
@@ -322,7 +334,7 @@
     data = parts[0].shape[0] - 8
     per = data // rhs
     me = lax.axis_index("col")
-    both = tree_sum(part[data:, :] for part in parts)
+    both = stat_sum(parts, data)
     norm = unpack_stat(stat_now[...], 0, rhs)
     norm_next = unpack_stat(both, 0, rhs)
     size_now = norm / unpack_stat(stat_now[...], 1, rhs)
@@ -395,7 +407,7 @@
                          (stat, shifted(stat, "row", b, n), *others))
         own, = call(functools.partial(combine_kernel, n), "combine", [vmem] * (3 + n + n // 2), [loaded], [],
                     (near, noise, stat, *parts, *others))
-        return [own] + [shifted(own, "col", d, n) for d in distances(n)]
+        return [own] + [shifted(own, "col", d, n) for d in distances(n)[::-1]]
 
     current = right_sides
     for b in bits(n)[:0:-1]:

time: 67.7 us -> 61 us (0.901)
  waiting for transfers between devices: 18.9 us -> 15 us
  Pallas kernels: 8.73 us -> 6.89 us
  starting transfers between devices: 38.1 us -> 36.8 us
    ppermute x20, waiting for transfers between devices: 17.4 us -> 13.2 us  [shifted(): return lax.ppermute(value, axis, [(i, i ^ d) for i in range(n)])]
    ppermute x7, starting transfers between devices: 14.7 us -> 11.7 us  [moved(): lax.ppermute(value, ('row', 'col'), [(s, t[0] * n + t[1]) for s, t in pai...]
    pallas_call x18, Pallas kernels: 8.73 us -> 6.89 us  [call(): pl.pallas_call(kernel, in_specs=specs, out_specs=jax.tree.map(lambda _: v...]
    ppermute x20, starting transfers between devices: 23.4 us -> 25.2 us  [shifted(): return lax.ppermute(value, axis, [(i, i ^ d) for i in range(n)])]
  transfers between devices with their start and end apart: 27 -> 27, of which waited for: 12 -> 10; matrix products, arithmetic and copies ran while one was open for 0% -> 0% of each run, Pallas kernels for 11% -> 9%
where the time goes in v6:
time: 61 us; the launch traced here: 60.2 us
  starting transfers between devices  36.8 us (60%)
  waiting for transfers between devices  15 us (25%)
  Pallas kernels  6.89 us (11%)
  between operations  1.51 us (2%)
    ppermute x20, starting transfers between devices, shifted(): return lax.ppermute(value, axis, [(i, i ^ d) for i in range(n)])  25.2 us
    ppermute x20, waiting for transfers between devices, shifted(): return lax.ppermute(value, axis, [(i, i ^ d) for i in range(n)])  13.2 us
    ppermute x7, starting transfers between devices, moved(): lax.ppermute(value, ('row', 'col'), [(s, t[0] * n + t[1]) for s, t in pai...  11.7 us
    pallas_call x18, Pallas kernels, call(): pl.pallas_call(kernel, in_specs=specs, out_specs=jax.tree.map(lambda _: v...  6.89 us
    ppermute x7, waiting for transfers between devices, moved(): lax.ppermute(value, ('row', 'col'), [(s, t[0] * n + t[1]) for s, t in pai...  1.78 us
  transfers between devices with their start and end apart: 27, of which 10 were waited for; matrix products, arithmetic and copies ran while one was open for 0% of the time, Pallas kernels for 9%

profile of v6, /device:TPU:0, one launch (start us, length us, event | category | flops | bytes accessed | tf_op | source)
XLA Modules:
  0.0 60.2 jit_solution(5722396585248036061)
XLA Ops:
  0.7 3.0 %collective-permute-start = (f32[32,2048]{1,0:T(8,128)}, f32[32,2048]{1,0:T(8,128)S(1)}, u32[]{:S(2)}, u32[]{:S(2)}) collective-permute-start(f32[32,2048]{1,0:T(8,128)} %right.3), channel_id=1, source_target_pairs={{0,8},{1,5},{2,6},{3,11},{4,0},{5,13},{6,14},{7,3},{8,12},{9,1},{1... | collective-permute-start | bytes 786440 | tf_op jit(solution)/shard_map/ppermute | solution.py:27
  4.3 1.7 %mirror_first.1 = (f32[16,32,128]{2,1,0:T(8,128)S(1)}, bf16[32,256,256]{2,1,0:T(8,128)(2,1)S(1)}) custom-call(s32[1,1,32]{2,1,0:T(1,128)} %rows_any.5, s32[1,1,32]{2,1,0:T(1,128)} %cols_any.5, s32[1,1]{1,0:T(1,128)S(6)} %copy.8.count, f32[32,2048]{1,0:T(8,128)} %right.3, bf16[1,1,32,256,256]{4,3,2,1,0:T(8,128)(2,1)} %cov.1), custom_call_target="tpu_custom_call" | custom-call | flops 268435456 | bytes 4194304 | tf_op jit(solution)/shard_map/mirror_first/pallas_call | solution.py:382
  6.1 1.8 %collective-permute-done.arrived = f32[32,2048]{1,0:T(8,128)S(1)} collective-permute-done((f32[32,2048]{1,0:T(8,128)}, f32[32,2048]{1,0:T(8,128)S(1)}, u32[]{:S(2)}, u32[]{:S(2)}) %collective-permute-start) | collective-permute-done | bytes 262176 | tf_op jit(solution)/shard_map/ppermute | solution.py:27
  8.0 2.4 %collective-permute-start.5 = (f32[128,128]{1,0:T(8,128)S(1)}, f32[128,128]{1,0:T(8,128)S(1)}, u32[]{:S(2)}, u32[]{:S(2)}) collective-permute-start(f32[128,128]{1,0:T(8,128)S(1)} %get-tuple-element.31), channel_id=1, source_target_pairs={{0,8},{1,9},{2,10},{3,14},{4,12},{5,13},{6,11},{7,15},{8,0},{9,4},... | collective-permute-start | bytes 196616 | tf_op jit(solution)/shard_map/ppermute | solution.py:27
  10.7 1.2 %direct_first.1 = (f32[16,32,128]{2,1,0:T(8,128)S(1)}, f32[8,128]{1,0:T(8,128)S(1)}, f32[16,32,128]{2,1,0:T(8,128)S(1)}) custom-call(s32[1,1,32]{2,1,0:T(1,128)S(1)} %copy-done.2, s32[1,1,32]{2,1,0:T(1,128)S(1)} %copy-done.3, s32[1,1]{1,0:T(1,128)S(6)} %copy.8.count, f32[1,2048]{1,0:T(1,128)S(1)} %bitcast.1, ...), custom_call_target="tpu_custom_call" | custom-call | flops 268435456 | bytes 4194304 | tf_op jit(solution)/shard_map/direct_first/pallas_call | solution.py:382
  12.0 2.8 %collective-permute-start.7 = (f32[128,128]{1,0:T(8,128)S(1)}, f32[128,128]{1,0:T(8,128)S(1)}, u32[]{:S(2)}, u32[]{:S(2)}) collective-permute-start(f32[128,128]{1,0:T(8,128)S(1)} %get-tuple-element.33), channel_id=1, source_target_pairs={{0,2},{1,3},{2,0},{3,1},{4,6},{5,7},{6,4},{7,5},{8,10},{9,11},{10,... | collective-permute-start | bytes 196616 | tf_op jit(solution)/shard_map/ppermute | solution.py:18
  14.8 2.5 %collective-permute-start.8 = (f32[128,128]{1,0:T(8,128)S(1)}, f32[128,128]{1,0:T(8,128)S(1)}, u32[]{:S(2)}, u32[]{:S(2)}) collective-permute-start(f32[128,128]{1,0:T(8,128)S(1)} %get-tuple-element.34), channel_id=1, source_target_pairs={{0,3},{1,2},{2,1},{3,0},{4,7},{5,6},{6,5},{7,4},{8,11},{9,10},{10,... | collective-permute-start | bytes 196616 | tf_op jit(solution)/shard_map/ppermute | solution.py:18
  17.8 1.2 %collective-permute-done.3.two = f32[8,128]{1,0:T(8,128)S(1)} collective-permute-done((f32[8,128]{1,0:T(8,128)S(1)}, f32[8,128]{1,0:T(8,128)S(1)}, u32[]{:S(2)}, u32[]{:S(2)}) %collective-permute-start.3) | collective-permute-done | bytes 4128 | tf_op jit(solution)/shard_map/ppermute | solution.py:18
  19.0 2.2 %collective-permute-start.6 = (f32[8,128]{1,0:T(8,128)S(1)}, f32[8,128]{1,0:T(8,128)S(1)}, u32[]{:S(2)}, u32[]{:S(2)}) collective-permute-start(f32[8,128]{1,0:T(8,128)S(1)} %add_stat.4.one), channel_id=1, source_target_pairs={{0,8},{4,12},{8,0},{12,4},{1,9},{5,13},{9,1},{13,5},{2,10},{6,14},... | collective-permute-start | bytes 12296 | tf_op jit(solution)/shard_map/ppermute | solution.py:18
  21.1 1.6 %collective-permute-done.6.two = f32[8,128]{1,0:T(8,128)S(1)} collective-permute-done((f32[8,128]{1,0:T(8,128)S(1)}, f32[8,128]{1,0:T(8,128)S(1)}, u32[]{:S(2)}, u32[]{:S(2)}) %collective-permute-start.6) | collective-permute-done | bytes 4128 | tf_op jit(solution)/shard_map/ppermute | solution.py:18
  22.8 1.6 %collective-permute-start.12 = (f32[136,128]{1,0:T(8,128)S(1)}, f32[136,128]{1,0:T(8,128)S(1)}, u32[]{:S(2)}, u32[]{:S(2)}) collective-permute-start(f32[136,128]{1,0:T(8,128)S(1)} %combine.2.refs_0_), channel_id=1, source_target_pairs={{0,2},{1,3},{2,0},{3,1},{4,6},{5,7},{6,4},{7,5},{8,10},{9,11},{10,... | collective-permute-start | bytes 208904 | tf_op jit(solution)/shard_map/ppermute | solution.py:18
  24.4 2.8 %collective-permute-start.11 = (f32[136,128]{1,0:T(8,128)S(1)}, f32[136,128]{1,0:T(8,128)S(1)}, u32[]{:S(2)}, u32[]{:S(2)}) collective-permute-start(f32[136,128]{1,0:T(8,128)S(1)} %combine.2.refs_0_), channel_id=1, source_target_pairs={{0,3},{1,2},{2,1},{3,0},{4,7},{5,6},{6,5},{7,4},{8,11},{9,10},{10,... | collective-permute-start | bytes 208904 | tf_op jit(solution)/shard_map/ppermute | solution.py:18
  27.3 2.0 %collective-permute-start.14 = (f32[136,128]{1,0:T(8,128)S(1)}, f32[136,128]{1,0:T(8,128)S(1)}, u32[]{:S(2)}, u32[]{:S(2)}) collective-permute-start(f32[136,128]{1,0:T(8,128)S(1)} %combine.2.refs_0_), channel_id=1, source_target_pairs={{0,8},{1,12},{2,10},{3,11},{4,9},{5,13},{6,14},{7,15},{8,0},{9,1},... | collective-permute-start | bytes 208904 | tf_op jit(solution)/shard_map/ppermute | solution.py:27
  29.3 1.6 %collective-permute-start.13 = (f32[136,128]{1,0:T(8,128)S(1)}, f32[136,128]{1,0:T(8,128)S(1)}, u32[]{:S(2)}, u32[]{:S(2)}) collective-permute-start(f32[136,128]{1,0:T(8,128)S(1)} %combine.2.refs_0_), channel_id=1, source_target_pairs={{0,4},{1,5},{2,8},{3,12},{4,0},{5,1},{6,9},{7,13},{8,2},{9,6},{10,... | collective-permute-start | bytes 208904 | tf_op jit(solution)/shard_map/ppermute | solution.py:27
  35.0 2.3 %collective-permute-start.19 = (f32[128,128]{1,0:T(8,128)S(1)}, f32[128,128]{1,0:T(8,128)S(1)}, u32[]{:S(2)}, u32[]{:S(2)}) collective-permute-start(f32[128,128]{1,0:T(8,128)S(1)} %get-tuple-element.43), channel_id=1, source_target_pairs={{0,8},{1,9},{2,10},{3,14},{4,12},{5,13},{6,11},{7,15},{8,0},{9,4},... | collective-permute-start | bytes 196616 | tf_op jit(solution)/shard_map/ppermute | solution.py:27
  37.4 1.2 %direct_second.1 = (f32[16,32,128]{2,1,0:T(8,128)S(1)}, f32[8,128]{1,0:T(8,128)S(1)}) custom-call(s32[1,1,32]{2,1,0:T(1,128)S(1)} %copy-done.2, s32[1,1,32]{2,1,0:T(1,128)S(1)} %copy-done.3, s32[1,1]{1,0:T(1,128)S(6)} %copy.8.count, f32[1,2048]{1,0:T(1,128)S(1)} %bitcast.3, bf16[32,256,256]{2,1,0:T(8,128)(2,1)S(1)} %get-tuple-element.25.blocks, ...), custom_call_target="tpu_custom_call" | custom-call | flops 268435456 | bytes 4194304 | tf_op jit(solution)/shard_map/direct_second/pallas_call | solution.py:382
  39.1 2.5 %collective-permute-start.21 = (f32[128,128]{1,0:T(8,128)S(1)}, f32[128,128]{1,0:T(8,128)S(1)}, u32[]{:S(2)}, u32[]{:S(2)}) collective-permute-start(f32[128,128]{1,0:T(8,128)S(1)} %get-tuple-element.45), channel_id=1, source_target_pairs={{0,2},{1,3},{2,0},{3,1},{4,6},{5,7},{6,4},{7,5},{8,10},{9,11},{10,... | collective-permute-start | bytes 196616 | tf_op jit(solution)/shard_map/ppermute | solution.py:18
  41.5 2.8 %collective-permute-start.22 = (f32[128,128]{1,0:T(8,128)S(1)}, f32[128,128]{1,0:T(8,128)S(1)}, u32[]{:S(2)}, u32[]{:S(2)}) collective-permute-start(f32[128,128]{1,0:T(8,128)S(1)} %get-tuple-element.46), channel_id=1, source_target_pairs={{0,3},{1,2},{2,1},{3,0},{4,7},{5,6},{6,5},{7,4},{8,11},{9,10},{10,... | collective-permute-start | bytes 196616 | tf_op jit(solution)/shard_map/ppermute | solution.py:18
  44.9 2.3 %collective-permute-start.20 = (f32[8,128]{1,0:T(8,128)S(1)}, f32[8,128]{1,0:T(8,128)S(1)}, u32[]{:S(2)}, u32[]{:S(2)}) collective-permute-start(f32[8,128]{1,0:T(8,128)S(1)} %add_stat.6.one), channel_id=1, source_target_pairs={{0,8},{4,12},{8,0},{12,4},{1,9},{5,13},{9,1},{13,5},{2,10},{6,14},... | collective-permute-start | bytes 12296 | tf_op jit(solution)/shard_map/ppermute | solution.py:18
  47.1 1.6 %collective-permute-done.20.two = f32[8,128]{1,0:T(8,128)S(1)} collective-permute-done((f32[8,128]{1,0:T(8,128)S(1)}, f32[8,128]{1,0:T(8,128)S(1)}, u32[]{:S(2)}, u32[]{:S(2)}) %collective-permute-start.20) | collective-permute-done | bytes 4128 | tf_op jit(solution)/shard_map/ppermute | solution.py:18
  49.7 1.9 %collective-permute-start.26 = (f32[136,128]{1,0:T(8,128)S(1)}, f32[136,128]{1,0:T(8,128)S(1)}, u32[]{:S(2)}, u32[]{:S(2)}) collective-permute-start(f32[136,128]{1,0:T(8,128)S(1)} %combine.3.refs_0_), channel_id=1, source_target_pairs={{0,2},{1,3},{2,0},{3,1},{4,6},{5,7},{6,4},{7,5},{8,10},{9,11},{10,... | collective-permute-start | bytes 208904 | tf_op jit(solution)/shard_map/ppermute | solution.py:18
  51.7 1.2 %collective-permute-start.25 = (f32[136,128]{1,0:T(8,128)S(1)}, f32[136,128]{1,0:T(8,128)S(1)}, u32[]{:S(2)}, u32[]{:S(2)}) collective-permute-start(f32[136,128]{1,0:T(8,128)S(1)} %combine.3.refs_0_), channel_id=1, source_target_pairs={{0,3},{1,2},{2,1},{3,0},{4,7},{5,6},{6,5},{7,4},{8,11},{9,10},{10,... | collective-permute-start | bytes 208904 | tf_op jit(solution)/shard_map/ppermute | solution.py:18
  53.3 4.8 %collective-permute-done.26.refs_3_ = f32[136,128]{1,0:T(8,128)S(1)} collective-permute-done((f32[136,128]{1,0:T(8,128)S(1)}, f32[136,128]{1,0:T(8,128)S(1)}, u32[]{:S(2)}, u32[]{:S(2)}) %collective-permute-start.26) | collective-permute-done | bytes 69664 | tf_op jit(solution)/shard_map/ppermute | solution.py:18
  59.0 1.2 %last.1 = (f32[32,2048]{1,0:T(8,128)}, f32[32,2048]{1,0:T(8,128)}) custom-call(f32[32,2048]{1,0:T(8,128)S(1)} %copy-done, f32[32,2048]{1,0:T(8,128)S(1)} %get-tuple-element.36.near.left, f32[8,128]{1,0:T(8,128)S(1)} %get-tuple-element.37.stat.stat_now, f32[136,128]{1,0:T(8,128)S(1)} %combine.3.refs_0_, f32[136,128]{1,0:T(8,128)S(1)} %collective-permute-done.24.refs_1_, ...), custom_call_target="tpu_custom_call" | custom-call | tf_op jit(solution)/shard_map/last/pallas_call | solution.py:382
  (56 shorter events, 8.7 us)
Async XLA Ops:
  0.7 7.2 %collective-permute-start = (f32[32,2048]{1,0:T(8,128)}, f32[32,2048]{1,0:T(8,128)S(1)}, u32[]{:S(2)}, u32[]{:S(2)}) collective-permute-start(f32[32,2048]{1,0:T(8,128)} %right.3), channel_id=1, source_target_pairs={{0,8},{1,5},{2,6},{3,11},{4,0},{5,13},{6,14},{7,3},{8,12},{9,1},{1... | collective-permute-start | bytes 786440 | tf_op jit(solution)/shard_map/ppermute | solution.py:27
  7.9 2.8 %collective-permute-start.1 = (f32[32,2048]{1,0:T(8,128)S(1)}, f32[32,2048]{1,0:T(8,128)S(1)}, u32[]{:S(2)}, u32[]{:S(2)}) collective-permute-start(f32[32,2048]{1,0:T(8,128)S(1)} %pick.1.current), channel_id=1, source_target_pairs={{0,4},{4,0},{8,12},{12,8},{1,5},{5,1},{9,13},{13,9},{2,6},{6,2},{1... | collective-permute-start | bytes 786440 | tf_op jit(solution)/shard_map/ppermute | solution.py:18
  8.0 9.8 %collective-permute-start.5 = (f32[128,128]{1,0:T(8,128)S(1)}, f32[128,128]{1,0:T(8,128)S(1)}, u32[]{:S(2)}, u32[]{:S(2)}) collective-permute-start(f32[128,128]{1,0:T(8,128)S(1)} %get-tuple-element.31), channel_id=1, source_target_pairs={{0,8},{1,9},{2,10},{3,14},{4,12},{5,13},{6,11},{7,15},{8,0},{9,4},... | collective-permute-start | bytes 196616 | tf_op jit(solution)/shard_map/ppermute | solution.py:27
  10.5 7.3 %collective-permute-start.4 = (f32[128,128]{1,0:T(8,128)S(1)}, f32[128,128]{1,0:T(8,128)S(1)}, u32[]{:S(2)}, u32[]{:S(2)}) collective-permute-start(f32[128,128]{1,0:T(8,128)S(1)} %get-tuple-element.27.mark), channel_id=1, source_target_pairs={{0,4},{1,5},{2,8},{3,12},{4,0},{5,1},{6,9},{7,13},{8,2},{9,6},{10,... | collective-permute-start | bytes 196616 | tf_op jit(solution)/shard_map/ppermute | solution.py:27
  12.0 10.8 %collective-permute-start.7 = (f32[128,128]{1,0:T(8,128)S(1)}, f32[128,128]{1,0:T(8,128)S(1)}, u32[]{:S(2)}, u32[]{:S(2)}) collective-permute-start(f32[128,128]{1,0:T(8,128)S(1)} %get-tuple-element.33), channel_id=1, source_target_pairs={{0,2},{1,3},{2,0},{3,1},{4,6},{5,7},{6,4},{7,5},{8,10},{9,11},{10,... | collective-permute-start | bytes 196616 | tf_op jit(solution)/shard_map/ppermute | solution.py:18
  14.8 8.0 %collective-permute-start.8 = (f32[128,128]{1,0:T(8,128)S(1)}, f32[128,128]{1,0:T(8,128)S(1)}, u32[]{:S(2)}, u32[]{:S(2)}) collective-permute-start(f32[128,128]{1,0:T(8,128)S(1)} %get-tuple-element.34), channel_id=1, source_target_pairs={{0,3},{1,2},{2,1},{3,0},{4,7},{5,6},{6,5},{7,4},{8,11},{9,10},{10,... | collective-permute-start | bytes 196616 | tf_op jit(solution)/shard_map/ppermute | solution.py:18
  17.3 5.4 %collective-permute-start.9 = (f32[128,128]{1,0:T(8,128)S(1)}, f32[128,128]{1,0:T(8,128)S(1)}, u32[]{:S(2)}, u32[]{:S(2)}) collective-permute-start(f32[128,128]{1,0:T(8,128)S(1)} %get-tuple-element.35), channel_id=1, source_target_pairs={{0,1},{1,0},{2,3},{3,2},{4,5},{5,4},{6,7},{7,6},{8,9},{9,8},{10,11... | collective-permute-start | bytes 196616 | tf_op jit(solution)/shard_map/ppermute | solution.py:18
  19.0 3.8 %collective-permute-start.6 = (f32[8,128]{1,0:T(8,128)S(1)}, f32[8,128]{1,0:T(8,128)S(1)}, u32[]{:S(2)}, u32[]{:S(2)}) collective-permute-start(f32[8,128]{1,0:T(8,128)S(1)} %add_stat.4.one), channel_id=1, source_target_pairs={{0,8},{4,12},{8,0},{12,4},{1,9},{5,13},{9,1},{13,5},{2,10},{6,14},... | collective-permute-start | bytes 12296 | tf_op jit(solution)/shard_map/ppermute | solution.py:18
  22.8 8.8 %collective-permute-start.12 = (f32[136,128]{1,0:T(8,128)S(1)}, f32[136,128]{1,0:T(8,128)S(1)}, u32[]{:S(2)}, u32[]{:S(2)}) collective-permute-start(f32[136,128]{1,0:T(8,128)S(1)} %combine.2.refs_0_), channel_id=1, source_target_pairs={{0,2},{1,3},{2,0},{3,1},{4,6},{5,7},{6,4},{7,5},{8,10},{9,11},{10,... | collective-permute-start | bytes 208904 | tf_op jit(solution)/shard_map/ppermute | solution.py:18
  24.4 7.2 %collective-permute-start.11 = (f32[136,128]{1,0:T(8,128)S(1)}, f32[136,128]{1,0:T(8,128)S(1)}, u32[]{:S(2)}, u32[]{:S(2)}) collective-permute-start(f32[136,128]{1,0:T(8,128)S(1)} %combine.2.refs_0_), channel_id=1, source_target_pairs={{0,3},{1,2},{2,1},{3,0},{4,7},{5,6},{6,5},{7,4},{8,11},{9,10},{10,... | collective-permute-start | bytes 208904 | tf_op jit(solution)/shard_map/ppermute | solution.py:18
  27.3 4.9 %collective-permute-start.10 = (f32[136,128]{1,0:T(8,128)S(1)}, f32[136,128]{1,0:T(8,128)S(1)}, u32[]{:S(2)}, u32[]{:S(2)}) collective-permute-start(f32[136,128]{1,0:T(8,128)S(1)} %combine.2.refs_0_), channel_id=1, source_target_pairs={{0,1},{1,0},{2,3},{3,2},{4,5},{5,4},{6,7},{7,6},{8,9},{9,8},{10,11... | collective-permute-start | bytes 208904 | tf_op jit(solution)/shard_map/ppermute | solution.py:18
  27.3 6.2 %collective-permute-start.14 = (f32[136,128]{1,0:T(8,128)S(1)}, f32[136,128]{1,0:T(8,128)S(1)}, u32[]{:S(2)}, u32[]{:S(2)}) collective-permute-start(f32[136,128]{1,0:T(8,128)S(1)} %combine.2.refs_0_), channel_id=1, source_target_pairs={{0,8},{1,12},{2,10},{3,11},{4,9},{5,13},{6,14},{7,15},{8,0},{9,1},... | collective-permute-start | bytes 208904 | tf_op jit(solution)/shard_map/ppermute | solution.py:27
  29.3 4.1 %collective-permute-start.13 = (f32[136,128]{1,0:T(8,128)S(1)}, f32[136,128]{1,0:T(8,128)S(1)}, u32[]{:S(2)}, u32[]{:S(2)}) collective-permute-start(f32[136,128]{1,0:T(8,128)S(1)} %combine.2.refs_0_), channel_id=1, source_target_pairs={{0,4},{1,5},{2,8},{3,12},{4,0},{5,1},{6,9},{7,13},{8,2},{9,6},{10,... | collective-permute-start | bytes 208904 | tf_op jit(solution)/shard_map/ppermute | solution.py:27
  33.6 3.8 %collective-permute-start.15 = (f32[16,32,128]{2,1,0:T(8,128)S(1)}, f32[16,32,128]{2,1,0:T(8,128)S(1)}, u32[]{:S(2)}, u32[]{:S(2)}) collective-permute-start(f32[16,32,128]{2,1,0:T(8,128)S(1)} %held.1), channel_id=1, source_target_pairs={{0,4},{4,0},{8,12},{12,8},{1,5},{5,1},{9,13},{13,9},{2,6},{6,2},{1... | collective-permute-start | bytes 786440 | tf_op jit(solution)/shard_map/ppermute | solution.py:18
  35.0 9.9 %collective-permute-start.19 = (f32[128,128]{1,0:T(8,128)S(1)}, f32[128,128]{1,0:T(8,128)S(1)}, u32[]{:S(2)}, u32[]{:S(2)}) collective-permute-start(f32[128,128]{1,0:T(8,128)S(1)} %get-tuple-element.43), channel_id=1, source_target_pairs={{0,8},{1,9},{2,10},{3,14},{4,12},{5,13},{6,11},{7,15},{8,0},{9,4},... | collective-permute-start | bytes 196616 | tf_op jit(solution)/shard_map/ppermute | solution.py:27
  37.2 7.6 %collective-permute-start.18 = (f32[128,128]{1,0:T(8,128)S(1)}, f32[128,128]{1,0:T(8,128)S(1)}, u32[]{:S(2)}, u32[]{:S(2)}) collective-permute-start(f32[128,128]{1,0:T(8,128)S(1)} %get-tuple-element.39.mark), channel_id=1, source_target_pairs={{0,4},{1,5},{2,8},{3,12},{4,0},{5,1},{6,9},{7,13},{8,2},{9,6},{10,... | collective-permute-start | bytes 196616 | tf_op jit(solution)/shard_map/ppermute | solution.py:27
  38.7 5.7 %collective-permute-start.17 = (f32[8,128]{1,0:T(8,128)S(1)}, f32[8,128]{1,0:T(8,128)S(1)}, u32[]{:S(2)}, u32[]{:S(2)}) collective-permute-start(f32[8,128]{1,0:T(8,128)S(1)} %get-tuple-element.42.one), channel_id=1, source_target_pairs={{0,4},{4,0},{8,12},{12,8},{1,5},{5,1},{9,13},{13,9},{2,6},{6,2},{1... | collective-permute-start | bytes 12296 | tf_op jit(solution)/shard_map/ppermute | solution.py:18
  39.1 9.7 %collective-permute-start.21 = (f32[128,128]{1,0:T(8,128)S(1)}, f32[128,128]{1,0:T(8,128)S(1)}, u32[]{:S(2)}, u32[]{:S(2)}) collective-permute-start(f32[128,128]{1,0:T(8,128)S(1)} %get-tuple-element.45), channel_id=1, source_target_pairs={{0,2},{1,3},{2,0},{3,1},{4,6},{5,7},{6,4},{7,5},{8,10},{9,11},{10,... | collective-permute-start | bytes 196616 | tf_op jit(solution)/shard_map/ppermute | solution.py:18
  41.5 7.2 %collective-permute-start.22 = (f32[128,128]{1,0:T(8,128)S(1)}, f32[128,128]{1,0:T(8,128)S(1)}, u32[]{:S(2)}, u32[]{:S(2)}) collective-permute-start(f32[128,128]{1,0:T(8,128)S(1)} %get-tuple-element.46), channel_id=1, source_target_pairs={{0,3},{1,2},{2,1},{3,0},{4,7},{5,6},{6,5},{7,4},{8,11},{9,10},{10,... | collective-permute-start | bytes 196616 | tf_op jit(solution)/shard_map/ppermute | solution.py:18
  44.4 5.3 %collective-permute-start.23 = (f32[128,128]{1,0:T(8,128)S(1)}, f32[128,128]{1,0:T(8,128)S(1)}, u32[]{:S(2)}, u32[]{:S(2)}) collective-permute-start(f32[128,128]{1,0:T(8,128)S(1)} %get-tuple-element.47), channel_id=1, source_target_pairs={{0,1},{1,0},{2,3},{3,2},{4,5},{5,4},{6,7},{7,6},{8,9},{9,8},{10,11... | collective-permute-start | bytes 196616 | tf_op jit(solution)/shard_map/ppermute | solution.py:18
  44.9 3.9 %collective-permute-start.20 = (f32[8,128]{1,0:T(8,128)S(1)}, f32[8,128]{1,0:T(8,128)S(1)}, u32[]{:S(2)}, u32[]{:S(2)}) collective-permute-start(f32[8,128]{1,0:T(8,128)S(1)} %add_stat.6.one), channel_id=1, source_target_pairs={{0,8},{4,12},{8,0},{12,4},{1,9},{5,13},{9,1},{13,5},{2,10},{6,14},... | collective-permute-start | bytes 12296 | tf_op jit(solution)/shard_map/ppermute | solution.py:18
  49.7 8.3 %collective-permute-start.26 = (f32[136,128]{1,0:T(8,128)S(1)}, f32[136,128]{1,0:T(8,128)S(1)}, u32[]{:S(2)}, u32[]{:S(2)}) collective-permute-start(f32[136,128]{1,0:T(8,128)S(1)} %combine.3.refs_0_), channel_id=1, source_target_pairs={{0,2},{1,3},{2,0},{3,1},{4,6},{5,7},{6,4},{7,5},{8,10},{9,11},{10,... | collective-permute-start | bytes 208904 | tf_op jit(solution)/shard_map/ppermute | solution.py:18
  51.7 6.4 %collective-permute-start.25 = (f32[136,128]{1,0:T(8,128)S(1)}, f32[136,128]{1,0:T(8,128)S(1)}, u32[]{:S(2)}, u32[]{:S(2)}) collective-permute-start(f32[136,128]{1,0:T(8,128)S(1)} %combine.3.refs_0_), channel_id=1, source_target_pairs={{0,3},{1,2},{2,1},{3,0},{4,7},{5,6},{6,5},{7,4},{8,11},{9,10},{10,... | collective-permute-start | bytes 208904 | tf_op jit(solution)/shard_map/ppermute | solution.py:18
  52.8 6.2 %collective-permute-start.24 = (f32[136,128]{1,0:T(8,128)S(1)}, f32[136,128]{1,0:T(8,128)S(1)}, u32[]{:S(2)}, u32[]{:S(2)}) collective-permute-start(f32[136,128]{1,0:T(8,128)S(1)} %combine.3.refs_0_), channel_id=1, source_target_pairs={{0,1},{1,0},{2,3},{3,2},{4,5},{5,4},{6,7},{7,6},{8,9},{9,8},{10,11... | collective-permute-start | bytes 208904 | tf_op jit(solution)/shard_map/ppermute | solution.py:18
  (7 other events, 42.1 us)

commit v7 on v6

--- a/solution.py
+++ b/solution.py
@@ -192,7 +192,7 @@
     stat[...] = pack_stats([share * row_sums(square), bend], rhs)
 
 
-def direct_first_kernel(n, rows_any, cols_any, count, noise, blocks, near, current, twin, mark, total, stat, far, *scratch):
+def direct_first_kernel(n, rows_any, cols_any, count, noise, blocks, near, current, twin, total, stat, far, *scratch):
     slot_rows, slot_cols, pairs, index_sems = scratch
     tile_size = blocks.shape[1]
     pieces = tile_size // LANES
@@ -213,7 +213,7 @@
     finish_direct(total, near, noise, stat, n)
 
 
-def direct_second_kernel(n, rows_any, cols_any, count, noise, blocks, near, held, twin, mark, total, stat, *scratch):
+def direct_second_kernel(n, rows_any, cols_any, count, noise, blocks, near, held, twin, total, stat, *scratch):
     slot_rows, slot_cols, pairs, index_sems = scratch
     tile_size = blocks.shape[1]
     pieces = tile_size // LANES
@@ -234,8 +234,8 @@
     finish_direct(total, near, noise, stat, n)
 
 
-def add_kernel(one, two, *refs):
-    refs[-1][...] = one[...] + two[...]
+def add_kernel(one, two, mark, out):
+    out[...] = one[...] + two[...]
 
 
 def pick_kernel(b, current, arrived, mark, out):
@@ -243,7 +243,7 @@
     out[...] = jnp.where(there != 0, arrived[...], current[...])
 
 
-def split_kernel(n, mirror, twin, *outs):
+def split_kernel(n, mirror, twin, mark, *outs):
     per = mirror.shape[0] // n
     rhs = mirror.shape[1]
     row = lax.axis_index("row")
@@ -393,18 +393,16 @@
     in_hbm = functools.partial(pltpu.with_memory_space_constraint, memory_space=pltpu.HBM)
     kernel_index = index_scratch + [pair, index_sems]
 
-    def to_owners(mirror, twin):
-        sent = call(functools.partial(split_kernel, n), "split", [vmem] * 2, [chunk] * (n // 2), [], (mirror, twin))
-        return [moved(value, n, far_source(j, n)) for j, value in enumerate(sent)], sent[0]
-
-    def gathered(near, mirror, twin, others, direct, stat):
+    def gathered(near, mirror, twin, direct, stat):
         merged = call(functools.partial(merge_kernel, n), "merge", [vmem] * 4, [chunk] * n + [tile], [],
                       (direct, mirror, twin, stat))
         parts = [merged[0]] + [shifted(value, "col", d, n) for d, value in zip(distances(n), merged[1:n])]
+        sent = call(functools.partial(split_kernel, n), "split", [vmem] * 3, [chunk] * (n // 2), [],
+                    (mirror, twin, merged[n]))
+        others = [moved(value, n, far_source(j, n)) for j, value in enumerate(sent)]
         stat = merged[n]
         for b in bits(n):
-            stat, = call(add_kernel, "add_stat", [vmem] * (2 + n // 2), [tile], [],
-                         (stat, shifted(stat, "row", b, n), *others))
+            stat, = call(add_kernel, "add_stat", [vmem] * 3, [tile], [], (stat, shifted(stat, "row", b, n), parts[1]))
         own, = call(functools.partial(combine_kernel, n), "combine", [vmem] * (3 + n + n // 2), [loaded], [],
                     (near, noise, stat, *parts, *others))
         return [own] + [shifted(own, "col", d, n) for d in distances(n)[::-1]]
@@ -422,11 +420,10 @@
             twin_mirror = shifted(mirror, "row", 1, n)
         current, = call(functools.partial(pick_kernel, b), "pick", [vmem] * 3, [field], [], (current, arrived, mirror))
     twin = shifted(current, "row", 1, n)
-    others, mark = to_owners(mirror, twin_mirror)
     direct, stat, far = call(
-        functools.partial(direct_first_kernel, n), "direct_first", [any_spec] * 2 + [smem] + [vmem] * 6,
-        [total, tile, total], kernel_index, (*index, noise, blocks, right_sides, current, twin, mark), True)
-    parts = gathered(right_sides, mirror, twin_mirror, others, direct, stat)
+        functools.partial(direct_first_kernel, n), "direct_first", [any_spec] * 2 + [smem] + [vmem] * 5,
+        [total, tile, total], kernel_index, (*index, noise, blocks, right_sides, current, twin), True)
+    parts = gathered(right_sides, mirror, twin_mirror, direct, stat)
     far_parts = [moved(parts[0], n, far_target(j)) for j in range(n // 2)]
 
     left, stat_now = call(left_kernel, "left", [vmem] * (n + 1), [field, tile], [], (right_sides, *parts))
@@ -436,11 +433,10 @@
     held, = call(functools.partial(held_kernel, n), "held", [vmem] * (4 + n // 2), [total], [],
                  (left, stat_now, far, mirror, *far_parts))
     twin = shifted(held, "row", 1, n)
-    others, mark = to_owners(mirror, twin_mirror)
     direct, stat = call(
-        functools.partial(direct_second_kernel, n), "direct_second", [any_spec] * 2 + [smem] + [vmem] * 6,
-        [total, tile], kernel_index, (*index, noise, blocks, left, held, twin, mark), True)
-    parts = gathered(left, mirror, twin_mirror, others, direct, stat)
+        functools.partial(direct_second_kernel, n), "direct_second", [any_spec] * 2 + [smem] + [vmem] * 5,
+        [total, tile], kernel_index, (*index, noise, blocks, left, held, twin), True)
+    parts = gathered(left, mirror, twin_mirror, direct, stat)
     return tuple(call(last_kernel, "last", [vmem] * (n + 3), [field, field], [],
                       (right_sides, left, stat_now, *parts)))
 

time: 61 us -> 61.3 us (level); the launches traced: 60.2 us -> 61.4 us
  Pallas kernels: 6.89 us -> 8.73 us
  starting transfers between devices: 36.8 us -> 36 us
    ppermute x20, starting transfers between devices: 25.2 us -> 21.7 us  [shifted(): return lax.ppermute(value, axis, [(i, i ^ d) for i in range(n)])]
    ppermute x7, starting transfers between devices: 11.7 us -> 14.3 us  [moved(): lax.ppermute(value, ('row', 'col'), [(s, t[0] * n + t[1]) for s, t in pai...]
    pallas_call x18, Pallas kernels: 6.89 us -> 8.73 us  [call(): pl.pallas_call(kernel, in_specs=specs, out_specs=jax.tree.map(lambda _: v...]
    ppermute x20, waiting for transfers between devices: 13.2 us -> 13.9 us  [shifted(): return lax.ppermute(value, axis, [(i, i ^ d) for i in range(n)])]
  transfers between devices with their start and end apart: 27 -> 27, of which waited for: 10 -> 10; matrix products, arithmetic and copies ran while one was open for 0% -> 0% of each run, Pallas kernels for 9% -> 11%
where the time goes in v7:
time: 61.3 us; the launch traced here: 61.4 us
  starting transfers between devices  36 us (59%)
  waiting for transfers between devices  15.2 us (25%)
  Pallas kernels  8.73 us (14%)
  between operations  1.51 us (2%)
    ppermute x20, starting transfers between devices, shifted(): return lax.ppermute(value, axis, [(i, i ^ d) for i in range(n)])  21.7 us
    ppermute x7, starting transfers between devices, moved(): lax.ppermute(value, ('row', 'col'), [(s, t[0] * n + t[1]) for s, t in pai...  14.3 us
    ppermute x20, waiting for transfers between devices, shifted(): return lax.ppermute(value, axis, [(i, i ^ d) for i in range(n)])  13.9 us
    pallas_call x18, Pallas kernels, call(): pl.pallas_call(kernel, in_specs=specs, out_specs=jax.tree.map(lambda _: v...  8.73 us
    ppermute x7, waiting for transfers between devices, moved(): lax.ppermute(value, ('row', 'col'), [(s, t[0] * n + t[1]) for s, t in pai...  1.23 us
  transfers between devices with their start and end apart: 27, of which 10 were waited for; matrix products, arithmetic and copies ran while one was open for 0% of the time, Pallas kernels for 11%

profile of v7, /device:TPU:0, one launch (start us, length us, event | category | flops | bytes accessed | tf_op | source)
XLA Modules:
  0.0 61.4 jit_solution(3255403659028435125)
XLA Ops:
  0.7 3.0 %collective-permute-start = (f32[32,2048]{1,0:T(8,128)}, f32[32,2048]{1,0:T(8,128)S(1)}, u32[]{:S(2)}, u32[]{:S(2)}) collective-permute-start(f32[32,2048]{1,0:T(8,128)} %right.3), channel_id=1, source_target_pairs={{0,8},{1,5},{2,6},{3,11},{4,0},{5,13},{6,14},{7,3},{8,12},{9,1},{1... | collective-permute-start | bytes 786440 | tf_op jit(solution)/shard_map/ppermute | solution.py:27
  4.3 2.3 %mirror_first.1 = (f32[16,32,128]{2,1,0:T(8,128)S(1)}, bf16[32,256,256]{2,1,0:T(8,128)(2,1)S(1)}) custom-call(s32[1,1,32]{2,1,0:T(1,128)} %rows_any.5, s32[1,1,32]{2,1,0:T(1,128)} %cols_any.5, s32[1,1]{1,0:T(1,128)S(6)} %copy.8.count, f32[32,2048]{1,0:T(8,128)} %right.3, bf16[1,1,32,256,256]{4,3,2,1,0:T(8,128)(2,1)} %cov.1), custom_call_target="tpu_custom_call" | custom-call | flops 268435456 | bytes 4194304 | tf_op jit(solution)/shard_map/mirror_first/pallas_call | solution.py:382
  6.7 1.2 %collective-permute-done.arrived = f32[32,2048]{1,0:T(8,128)S(1)} collective-permute-done((f32[32,2048]{1,0:T(8,128)}, f32[32,2048]{1,0:T(8,128)S(1)}, u32[]{:S(2)}, u32[]{:S(2)}) %collective-permute-start) | collective-permute-done | bytes 262176 | tf_op jit(solution)/shard_map/ppermute | solution.py:27
  8.5 1.0 %collective-permute-done.1.twin = f32[32,2048]{1,0:T(8,128)S(1)} collective-permute-done((f32[32,2048]{1,0:T(8,128)S(1)}, f32[32,2048]{1,0:T(8,128)S(1)}, u32[]{:S(2)}, u32[]{:S(2)}) %collective-permute-start.1) | collective-permute-done | bytes 262176 | tf_op jit(solution)/shard_map/ppermute | solution.py:18
  9.5 1.6 %direct_first.1 = (f32[16,32,128]{2,1,0:T(8,128)S(1)}, f32[8,128]{1,0:T(8,128)S(1)}, f32[16,32,128]{2,1,0:T(8,128)S(1)}) custom-call(s32[1,1,32]{2,1,0:T(1,128)S(1)} %copy-done.2, s32[1,1,32]{2,1,0:T(1,128)S(1)} %copy-done.3, s32[1,1]{1,0:T(1,128)S(6)} %copy.8.count, f32[1,2048]{1,0:T(1,128)S(1)} %bitcast.1, ...), custom_call_target="tpu_custom_call" | custom-call | flops 268435456 | bytes 4194304 | tf_op jit(solution)/shard_map/direct_first/pallas_call | solution.py:382
  11.3 3.5 %collective-permute-start.4 = (f32[128,128]{1,0:T(8,128)S(1)}, f32[128,128]{1,0:T(8,128)S(1)}, u32[]{:S(2)}, u32[]{:S(2)}) collective-permute-start(f32[128,128]{1,0:T(8,128)S(1)} %get-tuple-element.30), channel_id=1, source_target_pairs={{0,2},{1,3},{2,0},{3,1},{4,6},{5,7},{6,4},{7,5},{8,10},{9,11},{10,... | collective-permute-start | bytes 196616 | tf_op jit(solution)/shard_map/ppermute | solution.py:18
  15.1 1.1 %collective-permute-start.6 = (f32[128,128]{1,0:T(8,128)S(1)}, f32[128,128]{1,0:T(8,128)S(1)}, u32[]{:S(2)}, u32[]{:S(2)}) collective-permute-start(f32[128,128]{1,0:T(8,128)S(1)} %get-tuple-element.32), channel_id=1, source_target_pairs={{0,3},{1,2},{2,1},{3,0},{4,7},{5,6},{6,5},{7,4},{8,11},{9,10},{10,... | collective-permute-start | bytes 196616 | tf_op jit(solution)/shard_map/ppermute | solution.py:18
  16.4 4.6 %collective-permute-start.9 = (f32[128,128]{1,0:T(8,128)S(1)}, f32[128,128]{1,0:T(8,128)S(1)}, u32[]{:S(2)}, u32[]{:S(2)}) collective-permute-start(f32[128,128]{1,0:T(8,128)S(1)} %get-tuple-element.35), channel_id=1, source_target_pairs={{0,8},{1,9},{2,10},{3,14},{4,12},{5,13},{6,11},{7,15},{8,0},{9,4},... | collective-permute-start | bytes 196616 | tf_op jit(solution)/shard_map/ppermute | solution.py:27
  21.0 1.5 %collective-permute-start.5 = (f32[8,128]{1,0:T(8,128)S(1)}, f32[8,128]{1,0:T(8,128)S(1)}, u32[]{:S(2)}, u32[]{:S(2)}) collective-permute-start(f32[8,128]{1,0:T(8,128)S(1)} %add_stat.4.one), channel_id=1, source_target_pairs={{0,8},{4,12},{8,0},{12,4},{1,9},{5,13},{9,1},{13,5},{2,10},{6,14},... | collective-permute-start | bytes 12296 | tf_op jit(solution)/shard_map/ppermute | solution.py:18
  22.5 2.1 %collective-permute-done.5.two = f32[8,128]{1,0:T(8,128)S(1)} collective-permute-done((f32[8,128]{1,0:T(8,128)S(1)}, f32[8,128]{1,0:T(8,128)S(1)}, u32[]{:S(2)}, u32[]{:S(2)}) %collective-permute-start.5) | collective-permute-done | bytes 4128 | tf_op jit(solution)/shard_map/ppermute | solution.py:18
  24.7 1.8 %collective-permute-start.12 = (f32[136,128]{1,0:T(8,128)S(1)}, f32[136,128]{1,0:T(8,128)S(1)}, u32[]{:S(2)}, u32[]{:S(2)}) collective-permute-start(f32[136,128]{1,0:T(8,128)S(1)} %combine.2.refs_0_), channel_id=1, source_target_pairs={{0,2},{1,3},{2,0},{3,1},{4,6},{5,7},{6,4},{7,5},{8,10},{9,11},{10,... | collective-permute-start | bytes 208904 | tf_op jit(solution)/shard_map/ppermute | solution.py:18
  28.3 1.8 %collective-permute-start.14 = (f32[136,128]{1,0:T(8,128)S(1)}, f32[136,128]{1,0:T(8,128)S(1)}, u32[]{:S(2)}, u32[]{:S(2)}) collective-permute-start(f32[136,128]{1,0:T(8,128)S(1)} %combine.2.refs_0_), channel_id=1, source_target_pairs={{0,8},{1,12},{2,10},{3,11},{4,9},{5,13},{6,14},{7,15},{8,0},{9,1},... | collective-permute-start | bytes 208904 | tf_op jit(solution)/shard_map/ppermute | solution.py:27
  30.7 1.8 %collective-permute-done.12.refs_3_ = f32[136,128]{1,0:T(8,128)S(1)} collective-permute-done((f32[136,128]{1,0:T(8,128)S(1)}, f32[136,128]{1,0:T(8,128)S(1)}, u32[]{:S(2)}, u32[]{:S(2)}) %collective-permute-start.12) | collective-permute-done | bytes 69664 | tf_op jit(solution)/shard_map/ppermute | solution.py:18
  34.0 1.2 %mirror_second.1.mark.mirror = f32[16,32,128]{2,1,0:T(8,128)S(1)} custom-call(s32[1,1,32]{2,1,0:T(1,128)S(1)} %copy-done.2, s32[1,1,32]{2,1,0:T(1,128)S(1)} %copy-done.3, s32[1,1]{1,0:T(1,128)S(6)} %copy.8.count, f32[32,2048]{1,0:T(8,128)S(1)} %get-tuple-element.36.near.left, bf16[32,256,256]{2,1,0:T(8,128)(2,1)S(1)} %get-tuple-element.25.blocks), custom_call_target="tpu_custom_call" | custom-call | flops 268435456 | bytes 4194304 | tf_op jit(solution)/shard_map/mirror_second/pallas_call | solution.py:382
  36.9 1.6 %direct_second.1 = (f32[16,32,128]{2,1,0:T(8,128)S(1)}, f32[8,128]{1,0:T(8,128)S(1)}) custom-call(s32[1,1,32]{2,1,0:T(1,128)S(1)} %copy-done.2, s32[1,1,32]{2,1,0:T(1,128)S(1)} %copy-done.3, s32[1,1]{1,0:T(1,128)S(6)} %copy.8.count, f32[1,2048]{1,0:T(1,128)S(1)} %bitcast.3, bf16[32,256,256]{2,1,0:T(8,128)(2,1)S(1)} %get-tuple-element.25.blocks, ...), custom_call_target="tpu_custom_call" | custom-call | flops 268435456 | bytes 4194304 | tf_op jit(solution)/shard_map/direct_second/pallas_call | solution.py:382
  38.7 2.5 %collective-permute-start.18 = (f32[128,128]{1,0:T(8,128)S(1)}, f32[128,128]{1,0:T(8,128)S(1)}, u32[]{:S(2)}, u32[]{:S(2)}) collective-permute-start(f32[128,128]{1,0:T(8,128)S(1)} %get-tuple-element.42), channel_id=1, source_target_pairs={{0,2},{1,3},{2,0},{3,1},{4,6},{5,7},{6,4},{7,5},{8,10},{9,11},{10,... | collective-permute-start | bytes 196616 | tf_op jit(solution)/shard_map/ppermute | solution.py:18
  41.7 1.8 %collective-permute-start.20 = (f32[128,128]{1,0:T(8,128)S(1)}, f32[128,128]{1,0:T(8,128)S(1)}, u32[]{:S(2)}, u32[]{:S(2)}) collective-permute-start(f32[128,128]{1,0:T(8,128)S(1)} %get-tuple-element.44), channel_id=1, source_target_pairs={{0,3},{1,2},{2,1},{3,0},{4,7},{5,6},{6,5},{7,4},{8,11},{9,10},{10,... | collective-permute-start | bytes 196616 | tf_op jit(solution)/shard_map/ppermute | solution.py:18
  43.8 3.9 %collective-permute-start.23 = (f32[128,128]{1,0:T(8,128)S(1)}, f32[128,128]{1,0:T(8,128)S(1)}, u32[]{:S(2)}, u32[]{:S(2)}) collective-permute-start(f32[128,128]{1,0:T(8,128)S(1)} %get-tuple-element.47), channel_id=1, source_target_pairs={{0,8},{1,9},{2,10},{3,14},{4,12},{5,13},{6,11},{7,15},{8,0},{9,4},... | collective-permute-start | bytes 196616 | tf_op jit(solution)/shard_map/ppermute | solution.py:27
  47.6 2.3 %collective-permute-start.19 = (f32[8,128]{1,0:T(8,128)S(1)}, f32[8,128]{1,0:T(8,128)S(1)}, u32[]{:S(2)}, u32[]{:S(2)}) collective-permute-start(f32[8,128]{1,0:T(8,128)S(1)} %add_stat.6.one), channel_id=1, source_target_pairs={{0,8},{4,12},{8,0},{12,4},{1,9},{5,13},{9,1},{13,5},{2,10},{6,14},... | collective-permute-start | bytes 12296 | tf_op jit(solution)/shard_map/ppermute | solution.py:18
  49.9 1.6 %collective-permute-done.19.two = f32[8,128]{1,0:T(8,128)S(1)} collective-permute-done((f32[8,128]{1,0:T(8,128)S(1)}, f32[8,128]{1,0:T(8,128)S(1)}, u32[]{:S(2)}, u32[]{:S(2)}) %collective-permute-start.19) | collective-permute-done | bytes 4128 | tf_op jit(solution)/shard_map/ppermute | solution.py:18
  51.6 2.4 %collective-permute-start.26 = (f32[136,128]{1,0:T(8,128)S(1)}, f32[136,128]{1,0:T(8,128)S(1)}, u32[]{:S(2)}, u32[]{:S(2)}) collective-permute-start(f32[136,128]{1,0:T(8,128)S(1)} %combine.3.refs_0_), channel_id=1, source_target_pairs={{0,2},{1,3},{2,0},{3,1},{4,6},{5,7},{6,4},{7,5},{8,10},{9,11},{10,... | collective-permute-start | bytes 208904 | tf_op jit(solution)/shard_map/ppermute | solution.py:18
  55.2 4.0 %collective-permute-done.26.refs_3_ = f32[136,128]{1,0:T(8,128)S(1)} collective-permute-done((f32[136,128]{1,0:T(8,128)S(1)}, f32[136,128]{1,0:T(8,128)S(1)}, u32[]{:S(2)}, u32[]{:S(2)}) %collective-permute-start.26) | collective-permute-done | bytes 69664 | tf_op jit(solution)/shard_map/ppermute | solution.py:18
  59.2 1.1 %collective-permute-done.25.refs_2_ = f32[136,128]{1,0:T(8,128)S(1)} collective-permute-done((f32[136,128]{1,0:T(8,128)S(1)}, f32[136,128]{1,0:T(8,128)S(1)}, u32[]{:S(2)}, u32[]{:S(2)}) %collective-permute-start.25) | collective-permute-done | bytes 69664 | tf_op jit(solution)/shard_map/ppermute | solution.py:18
  60.2 1.2 %last.1 = (f32[32,2048]{1,0:T(8,128)}, f32[32,2048]{1,0:T(8,128)}) custom-call(f32[32,2048]{1,0:T(8,128)S(1)} %copy-done, f32[32,2048]{1,0:T(8,128)S(1)} %get-tuple-element.36.near.left, f32[8,128]{1,0:T(8,128)S(1)} %get-tuple-element.37.stat.stat_now, f32[136,128]{1,0:T(8,128)S(1)} %combine.3.refs_0_, f32[136,128]{1,0:T(8,128)S(1)} %collective-permute-done.24.refs_1_, ...), custom_call_target="tpu_custom_call" | custom-call | tf_op jit(solution)/shard_map/last/pallas_call | solution.py:382
  (56 shorter events, 9.0 us)
Async XLA Ops:
  0.7 7.2 %collective-permute-start = (f32[32,2048]{1,0:T(8,128)}, f32[32,2048]{1,0:T(8,128)S(1)}, u32[]{:S(2)}, u32[]{:S(2)}) collective-permute-start(f32[32,2048]{1,0:T(8,128)} %right.3), channel_id=1, source_target_pairs={{0,8},{1,5},{2,6},{3,11},{4,0},{5,13},{6,14},{7,3},{8,12},{9,1},{1... | collective-permute-start | bytes 786440 | tf_op jit(solution)/shard_map/ppermute | solution.py:27
  8.0 3.2 %collective-permute-start.2 = (f32[16,32,128]{2,1,0:T(8,128)S(1)}, f32[16,32,128]{2,1,0:T(8,128)S(1)}, u32[]{:S(2)}, u32[]{:S(2)}) collective-permute-start(f32[16,32,128]{2,1,0:T(8,128)S(1)} %get-tuple-element.26.mark.mirror), channel_id=1, source_target_pairs={{0,4},{4,0},{8,12},{12,8},{1,5},{5,1},{9,13},{13,9},{2,6},{6,2},{1... | collective-permute-start | bytes 786440 | tf_op jit(solution)/shard_map/ppermute | solution.py:18
  11.3 9.7 %collective-permute-start.4 = (f32[128,128]{1,0:T(8,128)S(1)}, f32[128,128]{1,0:T(8,128)S(1)}, u32[]{:S(2)}, u32[]{:S(2)}) collective-permute-start(f32[128,128]{1,0:T(8,128)S(1)} %get-tuple-element.30), channel_id=1, source_target_pairs={{0,2},{1,3},{2,0},{3,1},{4,6},{5,7},{6,4},{7,5},{8,10},{9,11},{10,... | collective-permute-start | bytes 196616 | tf_op jit(solution)/shard_map/ppermute | solution.py:18
  15.1 9.6 %collective-permute-start.6 = (f32[128,128]{1,0:T(8,128)S(1)}, f32[128,128]{1,0:T(8,128)S(1)}, u32[]{:S(2)}, u32[]{:S(2)}) collective-permute-start(f32[128,128]{1,0:T(8,128)S(1)} %get-tuple-element.32), channel_id=1, source_target_pairs={{0,3},{1,2},{2,1},{3,0},{4,7},{5,6},{6,5},{7,4},{8,11},{9,10},{10,... | collective-permute-start | bytes 196616 | tf_op jit(solution)/shard_map/ppermute | solution.py:18
  16.1 8.5 %collective-permute-start.7 = (f32[128,128]{1,0:T(8,128)S(1)}, f32[128,128]{1,0:T(8,128)S(1)}, u32[]{:S(2)}, u32[]{:S(2)}) collective-permute-start(f32[128,128]{1,0:T(8,128)S(1)} %get-tuple-element.33), channel_id=1, source_target_pairs={{0,1},{1,0},{2,3},{3,2},{4,5},{5,4},{6,7},{7,6},{8,9},{9,8},{10,11... | collective-permute-start | bytes 196616 | tf_op jit(solution)/shard_map/ppermute | solution.py:18
  16.2 8.4 %collective-permute-start.8 = (f32[128,128]{1,0:T(8,128)S(1)}, f32[128,128]{1,0:T(8,128)S(1)}, u32[]{:S(2)}, u32[]{:S(2)}) collective-permute-start(f32[128,128]{1,0:T(8,128)S(1)} %get-tuple-element.34), channel_id=1, source_target_pairs={{0,4},{1,5},{2,8},{3,12},{4,0},{5,1},{6,9},{7,13},{8,2},{9,6},{10,... | collective-permute-start | bytes 196616 | tf_op jit(solution)/shard_map/ppermute | solution.py:27
  16.4 8.2 %collective-permute-start.9 = (f32[128,128]{1,0:T(8,128)S(1)}, f32[128,128]{1,0:T(8,128)S(1)}, u32[]{:S(2)}, u32[]{:S(2)}) collective-permute-start(f32[128,128]{1,0:T(8,128)S(1)} %get-tuple-element.35), channel_id=1, source_target_pairs={{0,8},{1,9},{2,10},{3,14},{4,12},{5,13},{6,11},{7,15},{8,0},{9,4},... | collective-permute-start | bytes 196616 | tf_op jit(solution)/shard_map/ppermute | solution.py:27
  21.0 3.6 %collective-permute-start.5 = (f32[8,128]{1,0:T(8,128)S(1)}, f32[8,128]{1,0:T(8,128)S(1)}, u32[]{:S(2)}, u32[]{:S(2)}) collective-permute-start(f32[8,128]{1,0:T(8,128)S(1)} %add_stat.4.one), channel_id=1, source_target_pairs={{0,8},{4,12},{8,0},{12,4},{1,9},{5,13},{9,1},{13,5},{2,10},{6,14},... | collective-permute-start | bytes 12296 | tf_op jit(solution)/shard_map/ppermute | solution.py:18
  24.7 7.8 %collective-permute-start.12 = (f32[136,128]{1,0:T(8,128)S(1)}, f32[136,128]{1,0:T(8,128)S(1)}, u32[]{:S(2)}, u32[]{:S(2)}) collective-permute-start(f32[136,128]{1,0:T(8,128)S(1)} %combine.2.refs_0_), channel_id=1, source_target_pairs={{0,2},{1,3},{2,0},{3,1},{4,6},{5,7},{6,4},{7,5},{8,10},{9,11},{10,... | collective-permute-start | bytes 208904 | tf_op jit(solution)/shard_map/ppermute | solution.py:18
  26.6 6.6 %collective-permute-start.11 = (f32[136,128]{1,0:T(8,128)S(1)}, f32[136,128]{1,0:T(8,128)S(1)}, u32[]{:S(2)}, u32[]{:S(2)}) collective-permute-start(f32[136,128]{1,0:T(8,128)S(1)} %combine.2.refs_0_), channel_id=1, source_target_pairs={{0,3},{1,2},{2,1},{3,0},{4,7},{5,6},{6,5},{7,4},{8,11},{9,10},{10,... | collective-permute-start | bytes 208904 | tf_op jit(solution)/shard_map/ppermute | solution.py:18
  27.5 6.2 %collective-permute-start.10 = (f32[136,128]{1,0:T(8,128)S(1)}, f32[136,128]{1,0:T(8,128)S(1)}, u32[]{:S(2)}, u32[]{:S(2)}) collective-permute-start(f32[136,128]{1,0:T(8,128)S(1)} %combine.2.refs_0_), channel_id=1, source_target_pairs={{0,1},{1,0},{2,3},{3,2},{4,5},{5,4},{6,7},{7,6},{8,9},{9,8},{10,11... | collective-permute-start | bytes 208904 | tf_op jit(solution)/shard_map/ppermute | solution.py:18
  28.3 6.9 %collective-permute-start.14 = (f32[136,128]{1,0:T(8,128)S(1)}, f32[136,128]{1,0:T(8,128)S(1)}, u32[]{:S(2)}, u32[]{:S(2)}) collective-permute-start(f32[136,128]{1,0:T(8,128)S(1)} %combine.2.refs_0_), channel_id=1, source_target_pairs={{0,8},{1,12},{2,10},{3,11},{4,9},{5,13},{6,14},{7,15},{8,0},{9,1},... | collective-permute-start | bytes 208904 | tf_op jit(solution)/shard_map/ppermute | solution.py:27
  30.1 5.1 %collective-permute-start.13 = (f32[136,128]{1,0:T(8,128)S(1)}, f32[136,128]{1,0:T(8,128)S(1)}, u32[]{:S(2)}, u32[]{:S(2)}) collective-permute-start(f32[136,128]{1,0:T(8,128)S(1)} %combine.2.refs_0_), channel_id=1, source_target_pairs={{0,4},{1,5},{2,8},{3,12},{4,0},{5,1},{6,9},{7,13},{8,2},{9,6},{10,... | collective-permute-start | bytes 208904 | tf_op jit(solution)/shard_map/ppermute | solution.py:27
  35.4 3.1 %collective-permute-start.16 = (f32[16,32,128]{2,1,0:T(8,128)S(1)}, f32[16,32,128]{2,1,0:T(8,128)S(1)}, u32[]{:S(2)}, u32[]{:S(2)}) collective-permute-start(f32[16,32,128]{2,1,0:T(8,128)S(1)} %mirror_second.1.mark.mirror), channel_id=1, source_target_pairs={{0,4},{4,0},{8,12},{12,8},{1,5},{5,1},{9,13},{13,9},{2,6},{6,2},{1... | collective-permute-start | bytes 786440 | tf_op jit(solution)/shard_map/ppermute | solution.py:18
  38.7 9.0 %collective-permute-start.18 = (f32[128,128]{1,0:T(8,128)S(1)}, f32[128,128]{1,0:T(8,128)S(1)}, u32[]{:S(2)}, u32[]{:S(2)}) collective-permute-start(f32[128,128]{1,0:T(8,128)S(1)} %get-tuple-element.42), channel_id=1, source_target_pairs={{0,2},{1,3},{2,0},{3,1},{4,6},{5,7},{6,4},{7,5},{8,10},{9,11},{10,... | collective-permute-start | bytes 196616 | tf_op jit(solution)/shard_map/ppermute | solution.py:18
  41.1 2.6 %collective-permute-start.17 = (f32[8,128]{1,0:T(8,128)S(1)}, f32[8,128]{1,0:T(8,128)S(1)}, u32[]{:S(2)}, u32[]{:S(2)}) collective-permute-start(f32[8,128]{1,0:T(8,128)S(1)} %get-tuple-element.41.one.mark), channel_id=1, source_target_pairs={{0,4},{4,0},{8,12},{12,8},{1,5},{5,1},{9,13},{13,9},{2,6},{6,2},{1... | collective-permute-start | bytes 12296 | tf_op jit(solution)/shard_map/ppermute | solution.py:18
  41.7 9.8 %collective-permute-start.20 = (f32[128,128]{1,0:T(8,128)S(1)}, f32[128,128]{1,0:T(8,128)S(1)}, u32[]{:S(2)}, u32[]{:S(2)}) collective-permute-start(f32[128,128]{1,0:T(8,128)S(1)} %get-tuple-element.44), channel_id=1, source_target_pairs={{0,3},{1,2},{2,1},{3,0},{4,7},{5,6},{6,5},{7,4},{8,11},{9,10},{10,... | collective-permute-start | bytes 196616 | tf_op jit(solution)/shard_map/ppermute | solution.py:18
  43.4 8.1 %collective-permute-start.21 = (f32[128,128]{1,0:T(8,128)S(1)}, f32[128,128]{1,0:T(8,128)S(1)}, u32[]{:S(2)}, u32[]{:S(2)}) collective-permute-start(f32[128,128]{1,0:T(8,128)S(1)} %get-tuple-element.45), channel_id=1, source_target_pairs={{0,1},{1,0},{2,3},{3,2},{4,5},{5,4},{6,7},{7,6},{8,9},{9,8},{10,11... | collective-permute-start | bytes 196616 | tf_op jit(solution)/shard_map/ppermute | solution.py:18
  43.5 8.0 %collective-permute-start.22 = (f32[128,128]{1,0:T(8,128)S(1)}, f32[128,128]{1,0:T(8,128)S(1)}, u32[]{:S(2)}, u32[]{:S(2)}) collective-permute-start(f32[128,128]{1,0:T(8,128)S(1)} %get-tuple-element.46), channel_id=1, source_target_pairs={{0,4},{1,5},{2,8},{3,12},{4,0},{5,1},{6,9},{7,13},{8,2},{9,6},{10,... | collective-permute-start | bytes 196616 | tf_op jit(solution)/shard_map/ppermute | solution.py:27
  43.8 7.8 %collective-permute-start.23 = (f32[128,128]{1,0:T(8,128)S(1)}, f32[128,128]{1,0:T(8,128)S(1)}, u32[]{:S(2)}, u32[]{:S(2)}) collective-permute-start(f32[128,128]{1,0:T(8,128)S(1)} %get-tuple-element.47), channel_id=1, source_target_pairs={{0,8},{1,9},{2,10},{3,14},{4,12},{5,13},{6,11},{7,15},{8,0},{9,4},... | collective-permute-start | bytes 196616 | tf_op jit(solution)/shard_map/ppermute | solution.py:27
  47.6 3.9 %collective-permute-start.19 = (f32[8,128]{1,0:T(8,128)S(1)}, f32[8,128]{1,0:T(8,128)S(1)}, u32[]{:S(2)}, u32[]{:S(2)}) collective-permute-start(f32[8,128]{1,0:T(8,128)S(1)} %add_stat.6.one), channel_id=1, source_target_pairs={{0,8},{4,12},{8,0},{12,4},{1,9},{5,13},{9,1},{13,5},{2,10},{6,14},... | collective-permute-start | bytes 12296 | tf_op jit(solution)/shard_map/ppermute | solution.py:18
  51.6 7.6 %collective-permute-start.26 = (f32[136,128]{1,0:T(8,128)S(1)}, f32[136,128]{1,0:T(8,128)S(1)}, u32[]{:S(2)}, u32[]{:S(2)}) collective-permute-start(f32[136,128]{1,0:T(8,128)S(1)} %combine.3.refs_0_), channel_id=1, source_target_pairs={{0,2},{1,3},{2,0},{3,1},{4,6},{5,7},{6,4},{7,5},{8,10},{9,11},{10,... | collective-permute-start | bytes 208904 | tf_op jit(solution)/shard_map/ppermute | solution.py:18
  54.0 6.2 %collective-permute-start.25 = (f32[136,128]{1,0:T(8,128)S(1)}, f32[136,128]{1,0:T(8,128)S(1)}, u32[]{:S(2)}, u32[]{:S(2)}) collective-permute-start(f32[136,128]{1,0:T(8,128)S(1)} %combine.3.refs_0_), channel_id=1, source_target_pairs={{0,3},{1,2},{2,1},{3,0},{4,7},{5,6},{6,5},{7,4},{8,11},{9,10},{10,... | collective-permute-start | bytes 208904 | tf_op jit(solution)/shard_map/ppermute | solution.py:18
  54.7 5.5 %collective-permute-start.24 = (f32[136,128]{1,0:T(8,128)S(1)}, f32[136,128]{1,0:T(8,128)S(1)}, u32[]{:S(2)}, u32[]{:S(2)}) collective-permute-start(f32[136,128]{1,0:T(8,128)S(1)} %combine.3.refs_0_), channel_id=1, source_target_pairs={{0,1},{1,0},{2,3},{3,2},{4,5},{5,4},{6,7},{7,6},{8,9},{9,8},{10,11... | collective-permute-start | bytes 208904 | tf_op jit(solution)/shard_map/ppermute | solution.py:18
  (7 other events, 38.7 us)

commit v8 on v7

--- a/solution.py
+++ b/solution.py
@@ -110,7 +110,7 @@
 def image_part(parts, me, i, per, rhs):
     rows = slice((i % per) * rhs, (i % per + 1) * rhs)
     value = parts[0][rows, :]
-    for d, part in zip(distances(len(parts))[::-1], parts[1:]):
+    for d, part in zip(distances(len(parts)), parts[1:]):
         value = jnp.where(me ^ d == i // per, part[rows, :], value)
     return value
 
@@ -135,7 +135,7 @@
 
 
 def stat_sum(parts, data):
-    order = [0] + distances(len(parts))[::-1]
+    order = [0] + distances(len(parts))
     return tree_sum(parts[order.index(d)][data:, :] for d in range(len(parts)))
 
 
@@ -234,8 +234,8 @@
     finish_direct(total, near, noise, stat, n)
 
 
-def add_kernel(one, two, mark, out):
-    out[...] = one[...] + two[...]
+def add_kernel(one, two, *refs):
+    refs[-1][...] = one[...] + two[...]
 
 
 def pick_kernel(b, current, arrived, mark, out):
@@ -293,39 +293,28 @@
                 chunk[i * rhs:(i + 1) * rhs, :] += near[:, lanes] * noise[:, lanes]
 
 
-def left_kernel(right, *refs):
-    parts, (left, stat) = refs[:-2], refs[-2:]
+def left_kernel(n, right, far, *refs):
+    parts, others, (left, stat, held) = refs[:n], refs[n:-3], refs[-3:]
     rhs, width = right.shape
     data = parts[0].shape[0] - 8
     per = data // rhs
-    me = lax.axis_index("col")
+    row, me = lax.axis_index("row"), lax.axis_index("col")
+    diagonal = (row ^ me) < 2
     both = stat_sum(parts, data)
     stat[...] = both
     size_now = unpack_stat(both, 0, rhs) / unpack_stat(both, 1, rhs)
     for i in range(width // LANES):
         lanes = slice(i * LANES, (i + 1) * LANES)
-        left[:, lanes] = right[:, lanes] - size_now * image_part(parts, me, i, per, rhs)
-
-
-def held_kernel(n, left, stat, far, mark, *refs):
-    parts, held = refs[:-1], refs[-1]
-    rhs = left.shape[0]
-    per = held.shape[0] // n
-    row = lax.axis_index("row")
-    diagonal = (row ^ lax.axis_index("col")) < 2
-    size_now = unpack_stat(stat[...], 0, rhs) / unpack_stat(stat[...], 1, rhs)
-
-    @pl.when(diagonal)
-    def _():
-        for i in range(held.shape[0]):
-            held[i] = left[:, i * LANES:(i + 1) * LANES]
+        value = right[:, lanes] - size_now * image_part(parts, me, i, per, rhs)
+        left[:, lanes] = value
+        held[i] = value
 
     @pl.when(jnp.logical_not(diagonal))
     def _():
-        for j, part in enumerate(parts):
+        for j, other in enumerate(others):
             first = (row ^ 2 * j) * per
             for i in range(per):
-                held[first + i] = far[first + i] - size_now * part[i * rhs:(i + 1) * rhs, :]
+                held[first + i] = far[first + i] - size_now * other[i * rhs:(i + 1) * rhs, :]
 
 
 def last_kernel(right, left, stat_now, *refs):
@@ -394,18 +383,19 @@
     kernel_index = index_scratch + [pair, index_sems]
 
     def gathered(near, mirror, twin, direct, stat):
+        sent = call(functools.partial(split_kernel, n), "split", [vmem] * 3, [chunk] * (n // 2), [],
+                    (mirror, twin, stat))
+        others = [moved(value, n, far_source(j, n)) for j, value in enumerate(sent)]
         merged = call(functools.partial(merge_kernel, n), "merge", [vmem] * 4, [chunk] * n + [tile], [],
                       (direct, mirror, twin, stat))
         parts = [merged[0]] + [shifted(value, "col", d, n) for d, value in zip(distances(n), merged[1:n])]
-        sent = call(functools.partial(split_kernel, n), "split", [vmem] * 3, [chunk] * (n // 2), [],
-                    (mirror, twin, merged[n]))
-        others = [moved(value, n, far_source(j, n)) for j, value in enumerate(sent)]
         stat = merged[n]
         for b in bits(n):
-            stat, = call(add_kernel, "add_stat", [vmem] * 3, [tile], [], (stat, shifted(stat, "row", b, n), parts[1]))
+            stat, = call(add_kernel, "add_stat", [vmem] * (2 + n // 2), [tile], [],
+                         (stat, shifted(stat, "row", b, n), *others))
         own, = call(functools.partial(combine_kernel, n), "combine", [vmem] * (3 + n + n // 2), [loaded], [],
                     (near, noise, stat, *parts, *others))
-        return [own] + [shifted(own, "col", d, n) for d in distances(n)[::-1]]
+        return [own] + [shifted(own, "col", d, n) for d in distances(n)]
 
     current = right_sides
     for b in bits(n)[:0:-1]:
@@ -426,13 +416,13 @@
     parts = gathered(right_sides, mirror, twin_mirror, direct, stat)
     far_parts = [moved(parts[0], n, far_target(j)) for j in range(n // 2)]
 
-    left, stat_now = call(left_kernel, "left", [vmem] * (n + 1), [field, tile], [], (right_sides, *parts))
+    left, stat_now, held = call(
+        functools.partial(left_kernel, n), "left", [vmem] * (2 + n + n // 2), [field, tile, total], [],
+        (right_sides, far, *parts, *far_parts))
+    twin = shifted(held, "row", 1, n)
     mirror, = call(mirror_second_kernel, "mirror_second", [any_spec] * 2 + [smem] + [vmem] * 2,
                    [total], kernel_index, (*index, left, blocks), True)
     twin_mirror = shifted(mirror, "row", 1, n)
-    held, = call(functools.partial(held_kernel, n), "held", [vmem] * (4 + n // 2), [total], [],
-                 (left, stat_now, far, mirror, *far_parts))
-    twin = shifted(held, "row", 1, n)
     direct, stat = call(
         functools.partial(direct_second_kernel, n), "direct_second", [any_spec] * 2 + [smem] + [vmem] * 5,
         [total, tile], kernel_index, (*index, noise, blocks, left, held, twin), True)

time: 61.3 us -> 63.9 us (1.042); the launches traced: 61.4 us -> 63 us
  waiting for transfers between devices: 15.2 us -> 16.8 us
    ppermute x7, waiting for transfers between devices: 1.23 us -> 2.97 us  [moved(): lax.ppermute(value, ('row', 'col'), [(s, t[0] * n + t[1]) for s, t in pai...]
    ppermute x7, starting transfers between devices: 14.3 us -> 15 us  [moved(): lax.ppermute(value, ('row', 'col'), [(s, t[0] * n + t[1]) for s, t in pai...]
    pallas_call x18 -> x17, Pallas kernels: 8.73 us -> 8.57 us  [call(): pl.pallas_call(kernel, in_specs=specs, out_specs=jax.tree.map(lambda _: v...]
  transfers between devices with their start and end apart: 27 -> 27, of which waited for: 10 -> 12; matrix products, arithmetic and copies ran while one was open for 0% -> 0% of each run, Pallas kernels for 11% -> 11%
where the time goes in v8:
time: 63.9 us; the launch traced here: 63 us
  starting transfers between devices  36.1 us (56%)
  waiting for transfers between devices  16.8 us (26%)
  Pallas kernels  8.57 us (13%)
  between operations  1.48 us (2%)
    ppermute x20, starting transfers between devices, shifted(): return lax.ppermute(value, axis, [(i, i ^ d) for i in range(n)])  21.1 us
    ppermute x7, starting transfers between devices, moved(): lax.ppermute(value, ('row', 'col'), [(s, t[0] * n + t[1]) for s, t in pai...  15 us
    ppermute x20, waiting for transfers between devices, shifted(): return lax.ppermute(value, axis, [(i, i ^ d) for i in range(n)])  13.9 us
    pallas_call x17, Pallas kernels, call(): pl.pallas_call(kernel, in_specs=specs, out_specs=jax.tree.map(lambda _: v...  8.57 us
    ppermute x7, waiting for transfers between devices, moved(): lax.ppermute(value, ('row', 'col'), [(s, t[0] * n + t[1]) for s, t in pai...  2.97 us
  transfers between devices with their start and end apart: 27, of which 12 were waited for; matrix products, arithmetic and copies ran while one was open for 0% of the time, Pallas kernels for 11%

profile of v8, /device:TPU:0, one launch (start us, length us, event | category | flops | bytes accessed | tf_op | source)
XLA Modules:
  0.0 63.0 jit_solution(17519490993144940925)
XLA Ops:
  0.7 3.0 %collective-permute-start = (f32[32,2048]{1,0:T(8,128)}, f32[32,2048]{1,0:T(8,128)S(1)}, u32[]{:S(2)}, u32[]{:S(2)}) collective-permute-start(f32[32,2048]{1,0:T(8,128)} %right.3), channel_id=1, source_target_pairs={{0,8},{1,5},{2,6},{3,11},{4,0},{5,13},{6,14},{7,3},{8,12},{9,1},{1... | collective-permute-start | bytes 786440 | tf_op jit(solution)/shard_map/ppermute | solution.py:27
  4.3 2.3 %mirror_first.1 = (f32[16,32,128]{2,1,0:T(8,128)S(1)}, bf16[32,256,256]{2,1,0:T(8,128)(2,1)S(1)}) custom-call(s32[1,1,32]{2,1,0:T(1,128)} %rows_any.5, s32[1,1,32]{2,1,0:T(1,128)} %cols_any.5, s32[1,1]{1,0:T(1,128)S(6)} %copy.8.count, f32[32,2048]{1,0:T(8,128)} %right.3, bf16[1,1,32,256,256]{4,3,2,1,0:T(8,128)(2,1)} %cov.1), custom_call_target="tpu_custom_call" | custom-call | flops 268435456 | bytes 4194304 | tf_op jit(solution)/shard_map/mirror_first/pallas_call | solution.py:371
  6.7 1.2 %collective-permute-done.arrived = f32[32,2048]{1,0:T(8,128)S(1)} collective-permute-done((f32[32,2048]{1,0:T(8,128)}, f32[32,2048]{1,0:T(8,128)S(1)}, u32[]{:S(2)}, u32[]{:S(2)}) %collective-permute-start) | collective-permute-done | bytes 262176 | tf_op jit(solution)/shard_map/ppermute | solution.py:27
  9.5 1.6 %direct_first.1 = (f32[16,32,128]{2,1,0:T(8,128)S(1)}, f32[8,128]{1,0:T(8,128)S(1)}, f32[16,32,128]{2,1,0:T(8,128)S(1)}) custom-call(s32[1,1,32]{2,1,0:T(1,128)S(1)} %copy-done.2, s32[1,1,32]{2,1,0:T(1,128)S(1)} %copy-done.3, s32[1,1]{1,0:T(1,128)S(6)} %copy.8.count, f32[1,2048]{1,0:T(1,128)S(1)} %bitcast.1, ...), custom_call_target="tpu_custom_call" | custom-call | flops 268435456 | bytes 4194304 | tf_op jit(solution)/shard_map/direct_first/pallas_call | solution.py:371
  11.4 4.4 %collective-permute-start.5 = (f32[128,128]{1,0:T(8,128)S(1)}, f32[128,128]{1,0:T(8,128)S(1)}, u32[]{:S(2)}, u32[]{:S(2)}) collective-permute-start(f32[128,128]{1,0:T(8,128)S(1)} %get-tuple-element.33), channel_id=1, source_target_pairs={{0,8},{1,9},{2,10},{3,14},{4,12},{5,13},{6,11},{7,15},{8,0},{9,4},... | collective-permute-start | bytes 196616 | tf_op jit(solution)/shard_map/ppermute | solution.py:27
  15.9 2.5 %collective-permute-start.7 = (f32[128,128]{1,0:T(8,128)S(1)}, f32[128,128]{1,0:T(8,128)S(1)}, u32[]{:S(2)}, u32[]{:S(2)}) collective-permute-start(f32[128,128]{1,0:T(8,128)S(1)} %get-tuple-element.35), channel_id=1, source_target_pairs={{0,2},{1,3},{2,0},{3,1},{4,6},{5,7},{6,4},{7,5},{8,10},{9,11},{10,... | collective-permute-start | bytes 196616 | tf_op jit(solution)/shard_map/ppermute | solution.py:18
  19.5 1.9 %collective-permute-start.6 = (f32[8,128]{1,0:T(8,128)S(1)}, f32[8,128]{1,0:T(8,128)S(1)}, u32[]{:S(2)}, u32[]{:S(2)}) collective-permute-start(f32[8,128]{1,0:T(8,128)S(1)} %add_stat.4.one), channel_id=1, source_target_pairs={{0,8},{4,12},{8,0},{12,4},{1,9},{5,13},{9,1},{13,5},{2,10},{6,14},... | collective-permute-start | bytes 12296 | tf_op jit(solution)/shard_map/ppermute | solution.py:18
  21.4 1.7 %collective-permute-done.6.two = f32[8,128]{1,0:T(8,128)S(1)} collective-permute-done((f32[8,128]{1,0:T(8,128)S(1)}, f32[8,128]{1,0:T(8,128)S(1)}, u32[]{:S(2)}, u32[]{:S(2)}) %collective-permute-start.6) | collective-permute-done | bytes 4128 | tf_op jit(solution)/shard_map/ppermute | solution.py:18
  23.2 1.6 %collective-permute-done.8.refs_2_ = f32[128,128]{1,0:T(8,128)S(1)} collective-permute-done((f32[128,128]{1,0:T(8,128)S(1)}, f32[128,128]{1,0:T(8,128)S(1)}, u32[]{:S(2)}, u32[]{:S(2)}) %collective-permute-start.8) | collective-permute-done | bytes 65568 | tf_op jit(solution)/shard_map/ppermute | solution.py:18
  25.2 1.7 %collective-permute-start.10 = (f32[136,128]{1,0:T(8,128)S(1)}, f32[136,128]{1,0:T(8,128)S(1)}, u32[]{:S(2)}, u32[]{:S(2)}) collective-permute-start(f32[136,128]{1,0:T(8,128)S(1)} %combine.2.refs_0_), channel_id=1, source_target_pairs={{0,2},{1,3},{2,0},{3,1},{4,6},{5,7},{6,4},{7,5},{8,10},{9,11},{10,... | collective-permute-start | bytes 208904 | tf_op jit(solution)/shard_map/ppermute | solution.py:18
  26.9 1.4 %collective-permute-start.11 = (f32[136,128]{1,0:T(8,128)S(1)}, f32[136,128]{1,0:T(8,128)S(1)}, u32[]{:S(2)}, u32[]{:S(2)}) collective-permute-start(f32[136,128]{1,0:T(8,128)S(1)} %combine.2.refs_0_), channel_id=1, source_target_pairs={{0,3},{1,2},{2,1},{3,0},{4,7},{5,6},{6,5},{7,4},{8,11},{9,10},{10,... | collective-permute-start | bytes 208904 | tf_op jit(solution)/shard_map/ppermute | solution.py:18
  28.7 4.0 %collective-permute-start.14 = (f32[136,128]{1,0:T(8,128)S(1)}, f32[136,128]{1,0:T(8,128)S(1)}, u32[]{:S(2)}, u32[]{:S(2)}) collective-permute-start(f32[136,128]{1,0:T(8,128)S(1)} %combine.2.refs_0_), channel_id=1, source_target_pairs={{0,8},{1,12},{2,10},{3,11},{4,9},{5,13},{6,14},{7,15},{8,0},{9,1},... | collective-permute-start | bytes 208904 | tf_op jit(solution)/shard_map/ppermute | solution.py:27
  32.7 1.5 %collective-permute-done.10.refs_1_ = f32[136,128]{1,0:T(8,128)S(1)} collective-permute-done((f32[136,128]{1,0:T(8,128)S(1)}, f32[136,128]{1,0:T(8,128)S(1)}, u32[]{:S(2)}, u32[]{:S(2)}) %collective-permute-start.10) | collective-permute-done | bytes 69664 | tf_op jit(solution)/shard_map/ppermute | solution.py:18
  34.2 1.7 %collective-permute-done.14.refs_5_ = f32[136,128]{1,0:T(8,128)S(1)} collective-permute-done((f32[136,128]{1,0:T(8,128)S(1)}, f32[136,128]{1,0:T(8,128)S(1)}, u32[]{:S(2)}, u32[]{:S(2)}) %collective-permute-start.14) | collective-permute-done | bytes 69664 | tf_op jit(solution)/shard_map/ppermute | solution.py:27
  38.1 1.6 %direct_second.1 = (f32[16,32,128]{2,1,0:T(8,128)S(1)}, f32[8,128]{1,0:T(8,128)S(1)}) custom-call(s32[1,1,32]{2,1,0:T(1,128)S(1)} %copy-done.2, s32[1,1,32]{2,1,0:T(1,128)S(1)} %copy-done.3, s32[1,1]{1,0:T(1,128)S(6)} %copy.8.count, f32[1,2048]{1,0:T(1,128)S(1)} %bitcast.3, bf16[32,256,256]{2,1,0:T(8,128)(2,1)S(1)} %get-tuple-element.26.blocks, ...), custom_call_target="tpu_custom_call" | custom-call | flops 268435456 | bytes 4194304 | tf_op jit(solution)/shard_map/direct_second/pallas_call | solution.py:371
  39.8 3.4 %collective-permute-start.19 = (f32[128,128]{1,0:T(8,128)S(1)}, f32[128,128]{1,0:T(8,128)S(1)}, u32[]{:S(2)}, u32[]{:S(2)}) collective-permute-start(f32[128,128]{1,0:T(8,128)S(1)} %get-tuple-element.45), channel_id=1, source_target_pairs={{0,8},{1,9},{2,10},{3,14},{4,12},{5,13},{6,11},{7,15},{8,0},{9,4},... | collective-permute-start | bytes 196616 | tf_op jit(solution)/shard_map/ppermute | solution.py:27
  43.6 1.6 %collective-permute-start.21 = (f32[128,128]{1,0:T(8,128)S(1)}, f32[128,128]{1,0:T(8,128)S(1)}, u32[]{:S(2)}, u32[]{:S(2)}) collective-permute-start(f32[128,128]{1,0:T(8,128)S(1)} %get-tuple-element.47), channel_id=1, source_target_pairs={{0,2},{1,3},{2,0},{3,1},{4,6},{5,7},{6,4},{7,5},{8,10},{9,11},{10,... | collective-permute-start | bytes 196616 | tf_op jit(solution)/shard_map/ppermute | solution.py:18
  45.2 1.7 %collective-permute-start.22 = (f32[128,128]{1,0:T(8,128)S(1)}, f32[128,128]{1,0:T(8,128)S(1)}, u32[]{:S(2)}, u32[]{:S(2)}) collective-permute-start(f32[128,128]{1,0:T(8,128)S(1)} %get-tuple-element.48), channel_id=1, source_target_pairs={{0,3},{1,2},{2,1},{3,0},{4,7},{5,6},{6,5},{7,4},{8,11},{9,10},{10,... | collective-permute-start | bytes 196616 | tf_op jit(solution)/shard_map/ppermute | solution.py:18
  47.1 3.3 %collective-permute-start.20 = (f32[8,128]{1,0:T(8,128)S(1)}, f32[8,128]{1,0:T(8,128)S(1)}, u32[]{:S(2)}, u32[]{:S(2)}) collective-permute-start(f32[8,128]{1,0:T(8,128)S(1)} %add_stat.6.one), channel_id=1, source_target_pairs={{0,8},{4,12},{8,0},{12,4},{1,9},{5,13},{9,1},{13,5},{2,10},{6,14},... | collective-permute-start | bytes 12296 | tf_op jit(solution)/shard_map/ppermute | solution.py:18
  50.4 1.6 %collective-permute-done.20.two = f32[8,128]{1,0:T(8,128)S(1)} collective-permute-done((f32[8,128]{1,0:T(8,128)S(1)}, f32[8,128]{1,0:T(8,128)S(1)}, u32[]{:S(2)}, u32[]{:S(2)}) %collective-permute-start.20) | collective-permute-done | bytes 4128 | tf_op jit(solution)/shard_map/ppermute | solution.py:18
  52.9 1.4 %collective-permute-start.24 = (f32[136,128]{1,0:T(8,128)S(1)}, f32[136,128]{1,0:T(8,128)S(1)}, u32[]{:S(2)}, u32[]{:S(2)}) collective-permute-start(f32[136,128]{1,0:T(8,128)S(1)} %combine.3.refs_0_), channel_id=1, source_target_pairs={{0,2},{1,3},{2,0},{3,1},{4,6},{5,7},{6,4},{7,5},{8,10},{9,11},{10,... | collective-permute-start | bytes 208904 | tf_op jit(solution)/shard_map/ppermute | solution.py:18
  54.3 2.3 %collective-permute-start.25 = (f32[136,128]{1,0:T(8,128)S(1)}, f32[136,128]{1,0:T(8,128)S(1)}, u32[]{:S(2)}, u32[]{:S(2)}) collective-permute-start(f32[136,128]{1,0:T(8,128)S(1)} %combine.3.refs_0_), channel_id=1, source_target_pairs={{0,3},{1,2},{2,1},{3,0},{4,7},{5,6},{6,5},{7,4},{8,11},{9,10},{10,... | collective-permute-start | bytes 208904 | tf_op jit(solution)/shard_map/ppermute | solution.py:18
  56.6 4.9 %collective-permute-done.24.refs_1_ = f32[136,128]{1,0:T(8,128)S(1)} collective-permute-done((f32[136,128]{1,0:T(8,128)S(1)}, f32[136,128]{1,0:T(8,128)S(1)}, u32[]{:S(2)}, u32[]{:S(2)}) %collective-permute-start.24) | collective-permute-done | bytes 69664 | tf_op jit(solution)/shard_map/ppermute | solution.py:18
  61.8 1.2 %last.1 = (f32[32,2048]{1,0:T(8,128)}, f32[32,2048]{1,0:T(8,128)}) custom-call(f32[32,2048]{1,0:T(8,128)S(1)} %copy-done, f32[32,2048]{1,0:T(8,128)S(1)} %get-tuple-element.38.near.left, f32[8,128]{1,0:T(8,128)S(1)} %get-tuple-element.39.stat_now, f32[136,128]{1,0:T(8,128)S(1)} %combine.3.refs_0_, f32[136,128]{1,0:T(8,128)S(1)} %collective-permute-done.24.refs_1_, ...), custom_call_target="tpu_custom_call" | custom-call | tf_op jit(solution)/shard_map/last/pallas_call | solution.py:371
  (55 shorter events, 7.9 us)
Async XLA Ops:
  0.7 7.2 %collective-permute-start = (f32[32,2048]{1,0:T(8,128)}, f32[32,2048]{1,0:T(8,128)S(1)}, u32[]{:S(2)}, u32[]{:S(2)}) collective-permute-start(f32[32,2048]{1,0:T(8,128)} %right.3), channel_id=1, source_target_pairs={{0,8},{1,5},{2,6},{3,11},{4,0},{5,13},{6,14},{7,3},{8,12},{9,1},{1... | collective-permute-start | bytes 786440 | tf_op jit(solution)/shard_map/ppermute | solution.py:27
  8.0 3.2 %collective-permute-start.2 = (f32[16,32,128]{2,1,0:T(8,128)S(1)}, f32[16,32,128]{2,1,0:T(8,128)S(1)}, u32[]{:S(2)}, u32[]{:S(2)}) collective-permute-start(f32[16,32,128]{2,1,0:T(8,128)S(1)} %get-tuple-element.27.mark.mirror), channel_id=1, source_target_pairs={{0,4},{4,0},{8,12},{12,8},{1,5},{5,1},{9,13},{13,9},{2,6},{6,2},{1... | collective-permute-start | bytes 786440 | tf_op jit(solution)/shard_map/ppermute | solution.py:18
  11.2 8.3 %collective-permute-start.4 = (f32[128,128]{1,0:T(8,128)S(1)}, f32[128,128]{1,0:T(8,128)S(1)}, u32[]{:S(2)}, u32[]{:S(2)}) collective-permute-start(f32[128,128]{1,0:T(8,128)S(1)} %get-tuple-element.32), channel_id=1, source_target_pairs={{0,4},{1,5},{2,8},{3,12},{4,0},{5,1},{6,9},{7,13},{8,2},{9,6},{10,... | collective-permute-start | bytes 196616 | tf_op jit(solution)/shard_map/ppermute | solution.py:27
  11.4 8.1 %collective-permute-start.5 = (f32[128,128]{1,0:T(8,128)S(1)}, f32[128,128]{1,0:T(8,128)S(1)}, u32[]{:S(2)}, u32[]{:S(2)}) collective-permute-start(f32[128,128]{1,0:T(8,128)S(1)} %get-tuple-element.33), channel_id=1, source_target_pairs={{0,8},{1,9},{2,10},{3,14},{4,12},{5,13},{6,11},{7,15},{8,0},{9,4},... | collective-permute-start | bytes 196616 | tf_op jit(solution)/shard_map/ppermute | solution.py:27
  15.8 3.1 %collective-permute-start.3 = (f32[8,128]{1,0:T(8,128)S(1)}, f32[8,128]{1,0:T(8,128)S(1)}, u32[]{:S(2)}, u32[]{:S(2)}) collective-permute-start(f32[8,128]{1,0:T(8,128)S(1)} %get-tuple-element.31.one), channel_id=1, source_target_pairs={{0,4},{4,0},{8,12},{12,8},{1,5},{5,1},{9,13},{13,9},{2,6},{6,2},{1... | collective-permute-start | bytes 12296 | tf_op jit(solution)/shard_map/ppermute | solution.py:18
  15.9 7.3 %collective-permute-start.7 = (f32[128,128]{1,0:T(8,128)S(1)}, f32[128,128]{1,0:T(8,128)S(1)}, u32[]{:S(2)}, u32[]{:S(2)}) collective-permute-start(f32[128,128]{1,0:T(8,128)S(1)} %get-tuple-element.35), channel_id=1, source_target_pairs={{0,2},{1,3},{2,0},{3,1},{4,6},{5,7},{6,4},{7,5},{8,10},{9,11},{10,... | collective-permute-start | bytes 196616 | tf_op jit(solution)/shard_map/ppermute | solution.py:18
  18.4 6.3 %collective-permute-start.8 = (f32[128,128]{1,0:T(8,128)S(1)}, f32[128,128]{1,0:T(8,128)S(1)}, u32[]{:S(2)}, u32[]{:S(2)}) collective-permute-start(f32[128,128]{1,0:T(8,128)S(1)} %get-tuple-element.36), channel_id=1, source_target_pairs={{0,3},{1,2},{2,1},{3,0},{4,7},{5,6},{6,5},{7,4},{8,11},{9,10},{10,... | collective-permute-start | bytes 196616 | tf_op jit(solution)/shard_map/ppermute | solution.py:18
  19.0 6.1 %collective-permute-start.9 = (f32[128,128]{1,0:T(8,128)S(1)}, f32[128,128]{1,0:T(8,128)S(1)}, u32[]{:S(2)}, u32[]{:S(2)}) collective-permute-start(f32[128,128]{1,0:T(8,128)S(1)} %get-tuple-element.37), channel_id=1, source_target_pairs={{0,1},{1,0},{2,3},{3,2},{4,5},{5,4},{6,7},{7,6},{8,9},{9,8},{10,11... | collective-permute-start | bytes 196616 | tf_op jit(solution)/shard_map/ppermute | solution.py:18
  19.5 3.7 %collective-permute-start.6 = (f32[8,128]{1,0:T(8,128)S(1)}, f32[8,128]{1,0:T(8,128)S(1)}, u32[]{:S(2)}, u32[]{:S(2)}) collective-permute-start(f32[8,128]{1,0:T(8,128)S(1)} %add_stat.4.one), channel_id=1, source_target_pairs={{0,8},{4,12},{8,0},{12,4},{1,9},{5,13},{9,1},{13,5},{2,10},{6,14},... | collective-permute-start | bytes 12296 | tf_op jit(solution)/shard_map/ppermute | solution.py:18
  25.2 9.1 %collective-permute-start.10 = (f32[136,128]{1,0:T(8,128)S(1)}, f32[136,128]{1,0:T(8,128)S(1)}, u32[]{:S(2)}, u32[]{:S(2)}) collective-permute-start(f32[136,128]{1,0:T(8,128)S(1)} %combine.2.refs_0_), channel_id=1, source_target_pairs={{0,2},{1,3},{2,0},{3,1},{4,6},{5,7},{6,4},{7,5},{8,10},{9,11},{10,... | collective-permute-start | bytes 208904 | tf_op jit(solution)/shard_map/ppermute | solution.py:18
  26.9 7.3 %collective-permute-start.11 = (f32[136,128]{1,0:T(8,128)S(1)}, f32[136,128]{1,0:T(8,128)S(1)}, u32[]{:S(2)}, u32[]{:S(2)}) collective-permute-start(f32[136,128]{1,0:T(8,128)S(1)} %combine.2.refs_0_), channel_id=1, source_target_pairs={{0,3},{1,2},{2,1},{3,0},{4,7},{5,6},{6,5},{7,4},{8,11},{9,10},{10,... | collective-permute-start | bytes 208904 | tf_op jit(solution)/shard_map/ppermute | solution.py:18
  28.3 5.9 %collective-permute-start.12 = (f32[136,128]{1,0:T(8,128)S(1)}, f32[136,128]{1,0:T(8,128)S(1)}, u32[]{:S(2)}, u32[]{:S(2)}) collective-permute-start(f32[136,128]{1,0:T(8,128)S(1)} %combine.2.refs_0_), channel_id=1, source_target_pairs={{0,1},{1,0},{2,3},{3,2},{4,5},{5,4},{6,7},{7,6},{8,9},{9,8},{10,11... | collective-permute-start | bytes 208904 | tf_op jit(solution)/shard_map/ppermute | solution.py:18
  28.7 5.5 %collective-permute-start.13 = (f32[136,128]{1,0:T(8,128)S(1)}, f32[136,128]{1,0:T(8,128)S(1)}, u32[]{:S(2)}, u32[]{:S(2)}) collective-permute-start(f32[136,128]{1,0:T(8,128)S(1)} %combine.2.refs_0_), channel_id=1, source_target_pairs={{0,4},{1,5},{2,8},{3,12},{4,0},{5,1},{6,9},{7,13},{8,2},{9,6},{10,... | collective-permute-start | bytes 208904 | tf_op jit(solution)/shard_map/ppermute | solution.py:27
  28.7 7.2 %collective-permute-start.14 = (f32[136,128]{1,0:T(8,128)S(1)}, f32[136,128]{1,0:T(8,128)S(1)}, u32[]{:S(2)}, u32[]{:S(2)}) collective-permute-start(f32[136,128]{1,0:T(8,128)S(1)} %combine.2.refs_0_), channel_id=1, source_target_pairs={{0,8},{1,12},{2,10},{3,11},{4,9},{5,13},{6,14},{7,15},{8,0},{9,1},... | collective-permute-start | bytes 208904 | tf_op jit(solution)/shard_map/ppermute | solution.py:27
  39.7 7.3 %collective-permute-start.18 = (f32[128,128]{1,0:T(8,128)S(1)}, f32[128,128]{1,0:T(8,128)S(1)}, u32[]{:S(2)}, u32[]{:S(2)}) collective-permute-start(f32[128,128]{1,0:T(8,128)S(1)} %get-tuple-element.44), channel_id=1, source_target_pairs={{0,4},{1,5},{2,8},{3,12},{4,0},{5,1},{6,9},{7,13},{8,2},{9,6},{10,... | collective-permute-start | bytes 196616 | tf_op jit(solution)/shard_map/ppermute | solution.py:27
  39.8 7.2 %collective-permute-start.19 = (f32[128,128]{1,0:T(8,128)S(1)}, f32[128,128]{1,0:T(8,128)S(1)}, u32[]{:S(2)}, u32[]{:S(2)}) collective-permute-start(f32[128,128]{1,0:T(8,128)S(1)} %get-tuple-element.45), channel_id=1, source_target_pairs={{0,8},{1,9},{2,10},{3,14},{4,12},{5,13},{6,11},{7,15},{8,0},{9,4},... | collective-permute-start | bytes 196616 | tf_op jit(solution)/shard_map/ppermute | solution.py:27
  43.3 3.5 %collective-permute-start.17 = (f32[8,128]{1,0:T(8,128)S(1)}, f32[8,128]{1,0:T(8,128)S(1)}, u32[]{:S(2)}, u32[]{:S(2)}) collective-permute-start(f32[8,128]{1,0:T(8,128)S(1)} %get-tuple-element.43.one), channel_id=1, source_target_pairs={{0,4},{4,0},{8,12},{12,8},{1,5},{5,1},{9,13},{13,9},{2,6},{6,2},{1... | collective-permute-start | bytes 12296 | tf_op jit(solution)/shard_map/ppermute | solution.py:18
  43.6 8.9 %collective-permute-start.21 = (f32[128,128]{1,0:T(8,128)S(1)}, f32[128,128]{1,0:T(8,128)S(1)}, u32[]{:S(2)}, u32[]{:S(2)}) collective-permute-start(f32[128,128]{1,0:T(8,128)S(1)} %get-tuple-element.47), channel_id=1, source_target_pairs={{0,2},{1,3},{2,0},{3,1},{4,6},{5,7},{6,4},{7,5},{8,10},{9,11},{10,... | collective-permute-start | bytes 196616 | tf_op jit(solution)/shard_map/ppermute | solution.py:18
  45.2 7.3 %collective-permute-start.22 = (f32[128,128]{1,0:T(8,128)S(1)}, f32[128,128]{1,0:T(8,128)S(1)}, u32[]{:S(2)}, u32[]{:S(2)}) collective-permute-start(f32[128,128]{1,0:T(8,128)S(1)} %get-tuple-element.48), channel_id=1, source_target_pairs={{0,3},{1,2},{2,1},{3,0},{4,7},{5,6},{6,5},{7,4},{8,11},{9,10},{10,... | collective-permute-start | bytes 196616 | tf_op jit(solution)/shard_map/ppermute | solution.py:18
  46.8 6.0 %collective-permute-start.23 = (f32[128,128]{1,0:T(8,128)S(1)}, f32[128,128]{1,0:T(8,128)S(1)}, u32[]{:S(2)}, u32[]{:S(2)}) collective-permute-start(f32[128,128]{1,0:T(8,128)S(1)} %get-tuple-element.49), channel_id=1, source_target_pairs={{0,1},{1,0},{2,3},{3,2},{4,5},{5,4},{6,7},{7,6},{8,9},{9,8},{10,11... | collective-permute-start | bytes 196616 | tf_op jit(solution)/shard_map/ppermute | solution.py:18
  47.1 4.9 %collective-permute-start.20 = (f32[8,128]{1,0:T(8,128)S(1)}, f32[8,128]{1,0:T(8,128)S(1)}, u32[]{:S(2)}, u32[]{:S(2)}) collective-permute-start(f32[8,128]{1,0:T(8,128)S(1)} %add_stat.6.one), channel_id=1, source_target_pairs={{0,8},{4,12},{8,0},{12,4},{1,9},{5,13},{9,1},{13,5},{2,10},{6,14},... | collective-permute-start | bytes 12296 | tf_op jit(solution)/shard_map/ppermute | solution.py:18
  52.9 8.6 %collective-permute-start.24 = (f32[136,128]{1,0:T(8,128)S(1)}, f32[136,128]{1,0:T(8,128)S(1)}, u32[]{:S(2)}, u32[]{:S(2)}) collective-permute-start(f32[136,128]{1,0:T(8,128)S(1)} %combine.3.refs_0_), channel_id=1, source_target_pairs={{0,2},{1,3},{2,0},{3,1},{4,6},{5,7},{6,4},{7,5},{8,10},{9,11},{10,... | collective-permute-start | bytes 208904 | tf_op jit(solution)/shard_map/ppermute | solution.py:18
  54.3 7.2 %collective-permute-start.25 = (f32[136,128]{1,0:T(8,128)S(1)}, f32[136,128]{1,0:T(8,128)S(1)}, u32[]{:S(2)}, u32[]{:S(2)}) collective-permute-start(f32[136,128]{1,0:T(8,128)S(1)} %combine.3.refs_0_), channel_id=1, source_target_pairs={{0,3},{1,2},{2,1},{3,0},{4,7},{5,6},{6,5},{7,4},{8,11},{9,10},{10,... | collective-permute-start | bytes 208904 | tf_op jit(solution)/shard_map/ppermute | solution.py:18
  56.6 5.2 %collective-permute-start.26 = (f32[136,128]{1,0:T(8,128)S(1)}, f32[136,128]{1,0:T(8,128)S(1)}, u32[]{:S(2)}, u32[]{:S(2)}) collective-permute-start(f32[136,128]{1,0:T(8,128)S(1)} %combine.3.refs_0_), channel_id=1, source_target_pairs={{0,1},{1,0},{2,3},{3,2},{4,5},{5,4},{6,7},{7,6},{8,9},{9,8},{10,11... | collective-permute-start | bytes 208904 | tf_op jit(solution)/shard_map/ppermute | solution.py:18
  (7 other events, 39.5 us)

commit v9 on v6

--- a/solution.py
+++ b/solution.py
@@ -89,22 +89,23 @@
         total[tile * width + part] += value[:, part * LANES:(part + 1) * LANES]
 
 
-def add_blocks(blocks, slot_rows, slot_cols, live, pairs, total, mirror, ready=None):
+def wide_group(blocks):
+    return 2 * GROUP if blocks.shape[0] % (2 * GROUP) == 0 else GROUP
+
+
+def add_blocks(blocks, slot_rows, slot_cols, live, pairs, total, mirror, group, ready=None):
     read, write, contract = (slot_rows, slot_cols, 0) if mirror else (slot_cols, slot_rows, 1)
 
     def body(step, carry):
         if ready is not None:
             ready(step)
-        values = []
-        for g in range(GROUP):
-            slot = step * GROUP + g
+        for g in range(group):
+            slot = step * group + g
             value = product(pairs[read[0, 0, slot]], blocks[slot], contract)
-            values.append((write[0, 0, slot], jnp.where(slot < live, value, 0.0)))
-        for tile, value in values:
-            accumulate(total, tile, value)
+            accumulate(total, write[0, 0, slot], jnp.where(slot < live, value, 0.0))
         return carry
 
-    lax.fori_loop(0, (live + GROUP - 1) // GROUP, body, 0)
+    lax.fori_loop(0, (live + group - 1) // group, body, 0)
 
 
 def image_part(parts, me, i, per, rhs):
@@ -168,7 +169,7 @@
         load_pair(pairs, tile, right[:, tile * tile_size:(tile + 1) * tile_size])
     for copy in copies:
         copy.wait()
-    add_blocks(blocks, slot_rows, slot_cols, live, pairs, total, True, lambda i: block_copy(i).wait())
+    add_blocks(blocks, slot_rows, slot_cols, live, pairs, total, True, GROUP, lambda i: block_copy(i).wait())
 
 
 def mirror_second_kernel(rows_any, cols_any, count, near, blocks, total, *scratch):
@@ -180,7 +181,7 @@
         load_pair(pairs, tile, near[:, tile * tile_size:(tile + 1) * tile_size])
     for copy in copies:
         copy.wait()
-    add_blocks(blocks, slot_rows, slot_cols, count[0, 0], pairs, total, True)
+    add_blocks(blocks, slot_rows, slot_cols, count[0, 0], pairs, total, True, wide_group(blocks))
 
 
 def finish_direct(total, near, noise, stat, n):
@@ -209,7 +210,7 @@
     total[...] = jnp.zeros_like(total)
     for copy in copies:
         copy.wait()
-    add_blocks(blocks, slot_rows, slot_cols, count[0, 0], pairs, total, False)
+    add_blocks(blocks, slot_rows, slot_cols, count[0, 0], pairs, total, False, wide_group(blocks))
     finish_direct(total, near, noise, stat, n)
 
 
@@ -230,7 +231,7 @@
     total[...] = jnp.zeros_like(total)
     for copy in copies:
         copy.wait()
-    add_blocks(blocks, slot_rows, slot_cols, count[0, 0], pairs, total, False)
+    add_blocks(blocks, slot_rows, slot_cols, count[0, 0], pairs, total, False, wide_group(blocks))
     finish_direct(total, near, noise, stat, n)
 
 
@@ -322,14 +323,14 @@
 
     @pl.when(jnp.logical_not(diagonal))
     def _():
-        for j, part in enumerate(parts):
+        for j, part in zip(range(n // 2)[::-1], parts):
             first = (row ^ 2 * j) * per
             for i in range(per):
                 held[first + i] = far[first + i] - size_now * part[i * rhs:(i + 1) * rhs, :]
 
 
-def last_kernel(right, left, stat_now, *refs):
-    parts, (solution, residual) = refs[:-2], refs[-2:]
+def last_kernel(n, right, left, stat_now, *refs):
+    parts, (solution_out, residual_out, solution, residual, sems) = refs[:n], refs[n:]
     rhs, width = right.shape
     data = parts[0].shape[0] - 8
     per = data // rhs
@@ -341,13 +342,23 @@
     ratio = norm_next / norm
     size_next = norm_next / (unpack_stat(both, 1, rhs) - ratio * norm_next / size_now)
     back = ratio / size_now
-    for i in range(width // LANES):
-        lanes = slice(i * LANES, (i + 1) * LANES)
-        first = right[:, lanes]
-        now = left[:, lanes]
-        solution[:, lanes] = size_now * first + size_next * (now + ratio * first)
-        image = image_part(parts, me, i, per, rhs) + back * (first - now)
-        residual[:, lanes] = now - size_next * image
+    copies = []
+    groups = 4
+    count = width // LANES // groups
+    for group in range(groups):
+        for i in range(group * count, (group + 1) * count):
+            lanes = slice(i * LANES, (i + 1) * LANES)
+            first = right[:, lanes]
+            now = left[:, lanes]
+            solution[:, lanes] = size_now * first + size_next * (now + ratio * first)
+            image = image_part(parts, me, i, per, rhs) + back * (first - now)
+            residual[:, lanes] = now - size_next * image
+        lanes = pl.ds(group * count * LANES, count * LANES)
+        for k, (source, target) in enumerate(((solution, solution_out), (residual, residual_out))):
+            copies.append(pltpu.make_async_copy(source.at[:, lanes], target.at[:, lanes], sems.at[k, group]))
+            copies[-1].start()
+    for copy in copies:
+        copy.wait()
 
 
 def shape_of(*shape):
@@ -427,7 +438,7 @@
         functools.partial(direct_first_kernel, n), "direct_first", [any_spec] * 2 + [smem] + [vmem] * 6,
         [total, tile, total], kernel_index, (*index, noise, blocks, right_sides, current, twin, mark), True)
     parts = gathered(right_sides, mirror, twin_mirror, others, direct, stat)
-    far_parts = [moved(parts[0], n, far_target(j)) for j in range(n // 2)]
+    far_parts = [moved(parts[0], n, far_target(j)) for j in range(n // 2)[::-1]]
 
     left, stat_now = call(left_kernel, "left", [vmem] * (n + 1), [field, tile], [], (right_sides, *parts))
     mirror, = call(mirror_second_kernel, "mirror_second", [any_spec] * 2 + [smem] + [vmem] * 2,
@@ -441,8 +452,15 @@
         functools.partial(direct_second_kernel, n), "direct_second", [any_spec] * 2 + [smem] + [vmem] * 6,
         [total, tile], kernel_index, (*index, noise, blocks, left, held, twin, mark), True)
     parts = gathered(left, mirror, twin_mirror, others, direct, stat)
-    return tuple(call(last_kernel, "last", [vmem] * (n + 3), [field, field], [],
-                      (right_sides, left, stat_now, *parts)))
+    return tuple(pl.pallas_call(
+        functools.partial(last_kernel, n),
+        in_specs=[vmem] * (n + 3),
+        out_specs=[any_spec] * 2,
+        out_shape=[field, field],
+        scratch_shapes=[pltpu.VMEM((rhs, width), F32), pltpu.VMEM((rhs, width), F32), pltpu.SemaphoreType.DMA((2, 4))],
+        compiler_params=params,
+        name="last",
+    )(right_sides, left, stat_now, *parts))
 
 
 def solution(mesh):

time: 61 us -> 61 us (level)
  Pallas kernels: 6.89 us -> 11.1 us
  starting transfers between devices: 36.8 us -> 33.3 us
    pallas_call x18 -> x17, Pallas kernels: 6.89 us -> 9.79 us  [call(): pl.pallas_call(kernel, in_specs=specs, out_specs=jax.tree.map(lambda _: v...]
    ppermute x7, starting transfers between devices: 11.7 us -> 9.85 us  [moved(): lax.ppermute(value, ('row', 'col'), [(s, t[0] * n + t[1]) for s, t in pai...]
    ppermute x20, starting transfers between devices: 25.2 us -> 23.4 us  [shifted(): return lax.ppermute(value, axis, [(i, i ^ d) for i in range(n)])]
    pallas_call x0 -> x1, Pallas kernels: none -> 1.27 us  [on_device(): pl.pallas_call(functools.partial(last_kernel, n), in_specs=[vmem] * (n +...]
    ppermute x7, waiting for transfers between devices: 1.78 us -> 0.53 us  [moved(): lax.ppermute(value, ('row', 'col'), [(s, t[0] * n + t[1]) for s, t in pai...]
    ppermute x20, waiting for transfers between devices: 13.2 us -> 14.2 us  [shifted(): return lax.ppermute(value, axis, [(i, i ^ d) for i in range(n)])]
  transfers between devices with their start and end apart: 27 -> 27, of which waited for: 10 -> 11; matrix products, arithmetic and copies ran while one was open for 0% -> 0% of each run, Pallas kernels for 9% -> 16%
where the time goes in v9:
time: 61 us; the launch traced here: 60.6 us
  starting transfers between devices  33.3 us (55%)
  waiting for transfers between devices  14.7 us (24%)
  Pallas kernels  11.1 us (18%)
  between operations  1.5 us (2%)
    ppermute x20, starting transfers between devices, shifted(): return lax.ppermute(value, axis, [(i, i ^ d) for i in range(n)])  23.4 us
    ppermute x20, waiting for transfers between devices, shifted(): return lax.ppermute(value, axis, [(i, i ^ d) for i in range(n)])  14.2 us
    ppermute x7, starting transfers between devices, moved(): lax.ppermute(value, ('row', 'col'), [(s, t[0] * n + t[1]) for s, t in pai...  9.85 us
    pallas_call x17, Pallas kernels, call(): pl.pallas_call(kernel, in_specs=specs, out_specs=jax.tree.map(lambda _: v...  9.79 us
    pallas_call x1, Pallas kernels, on_device(): pl.pallas_call(functools.partial(last_kernel, n), in_specs=[vmem] * (n +...  1.27 us
  transfers between devices with their start and end apart: 27, of which 11 were waited for; matrix products, arithmetic and copies ran while one was open for 0% of the time, Pallas kernels for 16%

profile of v9, /device:TPU:0, one launch (start us, length us, event | category | flops | bytes accessed | tf_op | source)
XLA Modules:
  0.0 60.6 jit_solution(12287434738521093500)
XLA Ops:
  0.7 3.0 %collective-permute-start = (f32[32,2048]{1,0:T(8,128)}, f32[32,2048]{1,0:T(8,128)S(1)}, u32[]{:S(2)}, u32[]{:S(2)}) collective-permute-start(f32[32,2048]{1,0:T(8,128)} %right.3), channel_id=1, source_target_pairs={{0,8},{1,5},{2,6},{3,11},{4,0},{5,13},{6,14},{7,3},{8,12},{9,1},{1... | collective-permute-start | bytes 786440 | tf_op jit(solution)/shard_map/ppermute | solution.py:27
  4.3 3.0 %mirror_first.1 = (f32[16,32,128]{2,1,0:T(8,128)S(1)}, bf16[32,256,256]{2,1,0:T(8,128)(2,1)S(1)}) custom-call(s32[1,1,32]{2,1,0:T(1,128)} %rows_any.5, s32[1,1,32]{2,1,0:T(1,128)} %cols_any.5, s32[1,1]{1,0:T(1,128)S(6)} %copy.8.count, f32[32,2048]{1,0:T(8,128)} %right.3, bf16[1,1,32,256,256]{4,3,2,1,0:T(8,128)(2,1)} %cov.1), custom_call_target="tpu_custom_call" | custom-call | flops 268435456 | bytes 4194304 | tf_op jit(solution)/shard_map/mirror_first/pallas_call | solution.py:393
  8.9 1.6 %collective-permute-start.5 = (f32[128,128]{1,0:T(8,128)S(1)}, f32[128,128]{1,0:T(8,128)S(1)}, u32[]{:S(2)}, u32[]{:S(2)}) collective-permute-start(f32[128,128]{1,0:T(8,128)S(1)} %get-tuple-element.31), channel_id=1, source_target_pairs={{0,8},{1,9},{2,10},{3,14},{4,12},{5,13},{6,11},{7,15},{8,0},{9,4},... | collective-permute-start | bytes 196616 | tf_op jit(solution)/shard_map/ppermute | solution.py:27
  10.7 2.3 %direct_first.1 = (f32[16,32,128]{2,1,0:T(8,128)S(1)}, f32[8,128]{1,0:T(8,128)S(1)}, f32[16,32,128]{2,1,0:T(8,128)S(1)}) custom-call(s32[1,1,32]{2,1,0:T(1,128)S(1)} %copy-done.2, s32[1,1,32]{2,1,0:T(1,128)S(1)} %copy-done.3, s32[1,1]{1,0:T(1,128)S(6)} %copy.8.count, f32[1,2048]{1,0:T(1,128)S(1)} %bitcast.1, ...), custom_call_target="tpu_custom_call" | custom-call | flops 268435456 | bytes 4194304 | tf_op jit(solution)/shard_map/direct_first/pallas_call | solution.py:393
  13.1 1.9 %collective-permute-start.7 = (f32[128,128]{1,0:T(8,128)S(1)}, f32[128,128]{1,0:T(8,128)S(1)}, u32[]{:S(2)}, u32[]{:S(2)}) collective-permute-start(f32[128,128]{1,0:T(8,128)S(1)} %get-tuple-element.33), channel_id=1, source_target_pairs={{0,2},{1,3},{2,0},{3,1},{4,6},{5,7},{6,4},{7,5},{8,10},{9,11},{10,... | collective-permute-start | bytes 196616 | tf_op jit(solution)/shard_map/ppermute | solution.py:18
  15.0 1.7 %collective-permute-start.8 = (f32[128,128]{1,0:T(8,128)S(1)}, f32[128,128]{1,0:T(8,128)S(1)}, u32[]{:S(2)}, u32[]{:S(2)}) collective-permute-start(f32[128,128]{1,0:T(8,128)S(1)} %get-tuple-element.34), channel_id=1, source_target_pairs={{0,3},{1,2},{2,1},{3,0},{4,7},{5,6},{6,5},{7,4},{8,11},{9,10},{10,... | collective-permute-start | bytes 196616 | tf_op jit(solution)/shard_map/ppermute | solution.py:18
  17.2 1.2 %collective-permute-done.3.two = f32[8,128]{1,0:T(8,128)S(1)} collective-permute-done((f32[8,128]{1,0:T(8,128)S(1)}, f32[8,128]{1,0:T(8,128)S(1)}, u32[]{:S(2)}, u32[]{:S(2)}) %collective-permute-start.3) | collective-permute-done | bytes 4128 | tf_op jit(solution)/shard_map/ppermute | solution.py:18
  18.4 2.6 %collective-permute-start.6 = (f32[8,128]{1,0:T(8,128)S(1)}, f32[8,128]{1,0:T(8,128)S(1)}, u32[]{:S(2)}, u32[]{:S(2)}) collective-permute-start(f32[8,128]{1,0:T(8,128)S(1)} %add_stat.4.one), channel_id=1, source_target_pairs={{0,8},{4,12},{8,0},{12,4},{1,9},{5,13},{9,1},{13,5},{2,10},{6,14},... | collective-permute-start | bytes 12296 | tf_op jit(solution)/shard_map/ppermute | solution.py:18
  21.0 1.6 %collective-permute-done.6.two = f32[8,128]{1,0:T(8,128)S(1)} collective-permute-done((f32[8,128]{1,0:T(8,128)S(1)}, f32[8,128]{1,0:T(8,128)S(1)}, u32[]{:S(2)}, u32[]{:S(2)}) %collective-permute-start.6) | collective-permute-done | bytes 4128 | tf_op jit(solution)/shard_map/ppermute | solution.py:18
  22.7 1.6 %collective-permute-start.12 = (f32[136,128]{1,0:T(8,128)S(1)}, f32[136,128]{1,0:T(8,128)S(1)}, u32[]{:S(2)}, u32[]{:S(2)}) collective-permute-start(f32[136,128]{1,0:T(8,128)S(1)} %combine.2.refs_0_), channel_id=1, source_target_pairs={{0,2},{1,3},{2,0},{3,1},{4,6},{5,7},{6,4},{7,5},{8,10},{9,11},{10,... | collective-permute-start | bytes 208904 | tf_op jit(solution)/shard_map/ppermute | solution.py:18
  24.3 2.8 %collective-permute-start.11 = (f32[136,128]{1,0:T(8,128)S(1)}, f32[136,128]{1,0:T(8,128)S(1)}, u32[]{:S(2)}, u32[]{:S(2)}) collective-permute-start(f32[136,128]{1,0:T(8,128)S(1)} %combine.2.refs_0_), channel_id=1, source_target_pairs={{0,3},{1,2},{2,1},{3,0},{4,7},{5,6},{6,5},{7,4},{8,11},{9,10},{10,... | collective-permute-start | bytes 208904 | tf_op jit(solution)/shard_map/ppermute | solution.py:18
  27.1 3.0 %collective-permute-start.13 = (f32[136,128]{1,0:T(8,128)S(1)}, f32[136,128]{1,0:T(8,128)S(1)}, u32[]{:S(2)}, u32[]{:S(2)}) collective-permute-start(f32[136,128]{1,0:T(8,128)S(1)} %combine.2.refs_0_), channel_id=1, source_target_pairs={{0,8},{1,12},{2,10},{3,11},{4,9},{5,13},{6,14},{7,15},{8,0},{9,1},... | collective-permute-start | bytes 208904 | tf_op jit(solution)/shard_map/ppermute | solution.py:27
  30.2 1.3 %collective-permute-done.12.refs_3_ = f32[136,128]{1,0:T(8,128)S(1)} collective-permute-done((f32[136,128]{1,0:T(8,128)S(1)}, f32[136,128]{1,0:T(8,128)S(1)}, u32[]{:S(2)}, u32[]{:S(2)}) %collective-permute-start.12) | collective-permute-done | bytes 69664 | tf_op jit(solution)/shard_map/ppermute | solution.py:18
  32.3 1.6 %mirror_second.1.mark.mirror = f32[16,32,128]{2,1,0:T(8,128)S(1)} custom-call(s32[1,1,32]{2,1,0:T(1,128)S(1)} %copy-done.2, s32[1,1,32]{2,1,0:T(1,128)S(1)} %copy-done.3, s32[1,1]{1,0:T(1,128)S(6)} %copy.8.count, f32[32,2048]{1,0:T(8,128)S(1)} %get-tuple-element.36.near.left, bf16[32,256,256]{2,1,0:T(8,128)(2,1)S(1)} %get-tuple-element.25.blocks), custom_call_target="tpu_custom_call" | custom-call | flops 268435456 | bytes 4194304 | tf_op jit(solution)/shard_map/mirror_second/pallas_call | solution.py:393
  35.5 2.0 %collective-permute-start.19 = (f32[128,128]{1,0:T(8,128)S(1)}, f32[128,128]{1,0:T(8,128)S(1)}, u32[]{:S(2)}, u32[]{:S(2)}) collective-permute-start(f32[128,128]{1,0:T(8,128)S(1)} %get-tuple-element.43), channel_id=1, source_target_pairs={{0,8},{1,9},{2,10},{3,14},{4,12},{5,13},{6,11},{7,15},{8,0},{9,4},... | collective-permute-start | bytes 196616 | tf_op jit(solution)/shard_map/ppermute | solution.py:27
  37.6 2.2 %direct_second.1 = (f32[16,32,128]{2,1,0:T(8,128)S(1)}, f32[8,128]{1,0:T(8,128)S(1)}) custom-call(s32[1,1,32]{2,1,0:T(1,128)S(1)} %copy-done.2, s32[1,1,32]{2,1,0:T(1,128)S(1)} %copy-done.3, s32[1,1]{1,0:T(1,128)S(6)} %copy.8.count, f32[1,2048]{1,0:T(1,128)S(1)} %bitcast.3, bf16[32,256,256]{2,1,0:T(8,128)(2,1)S(1)} %get-tuple-element.25.blocks, ...), custom_call_target="tpu_custom_call" | custom-call | flops 268435456 | bytes 4194304 | tf_op jit(solution)/shard_map/direct_second/pallas_call | solution.py:393
  40.0 2.2 %collective-permute-start.21 = (f32[128,128]{1,0:T(8,128)S(1)}, f32[128,128]{1,0:T(8,128)S(1)}, u32[]{:S(2)}, u32[]{:S(2)}) collective-permute-start(f32[128,128]{1,0:T(8,128)S(1)} %get-tuple-element.45), channel_id=1, source_target_pairs={{0,2},{1,3},{2,0},{3,1},{4,6},{5,7},{6,4},{7,5},{8,10},{9,11},{10,... | collective-permute-start | bytes 196616 | tf_op jit(solution)/shard_map/ppermute | solution.py:18
  42.1 2.1 %collective-permute-start.22 = (f32[128,128]{1,0:T(8,128)S(1)}, f32[128,128]{1,0:T(8,128)S(1)}, u32[]{:S(2)}, u32[]{:S(2)}) collective-permute-start(f32[128,128]{1,0:T(8,128)S(1)} %get-tuple-element.46), channel_id=1, source_target_pairs={{0,3},{1,2},{2,1},{3,0},{4,7},{5,6},{6,5},{7,4},{8,11},{9,10},{10,... | collective-permute-start | bytes 196616 | tf_op jit(solution)/shard_map/ppermute | solution.py:18
  44.7 3.1 %collective-permute-start.20 = (f32[8,128]{1,0:T(8,128)S(1)}, f32[8,128]{1,0:T(8,128)S(1)}, u32[]{:S(2)}, u32[]{:S(2)}) collective-permute-start(f32[8,128]{1,0:T(8,128)S(1)} %add_stat.6.one), channel_id=1, source_target_pairs={{0,8},{4,12},{8,0},{12,4},{1,9},{5,13},{9,1},{13,5},{2,10},{6,14},... | collective-permute-start | bytes 12296 | tf_op jit(solution)/shard_map/ppermute | solution.py:18
  47.9 1.6 %collective-permute-done.20.two = f32[8,128]{1,0:T(8,128)S(1)} collective-permute-done((f32[8,128]{1,0:T(8,128)S(1)}, f32[8,128]{1,0:T(8,128)S(1)}, u32[]{:S(2)}, u32[]{:S(2)}) %collective-permute-start.20) | collective-permute-done | bytes 4128 | tf_op jit(solution)/shard_map/ppermute | solution.py:18
  50.2 1.6 %collective-permute-start.26 = (f32[136,128]{1,0:T(8,128)S(1)}, f32[136,128]{1,0:T(8,128)S(1)}, u32[]{:S(2)}, u32[]{:S(2)}) collective-permute-start(f32[136,128]{1,0:T(8,128)S(1)} %combine.3.refs_0_), channel_id=1, source_target_pairs={{0,2},{1,3},{2,0},{3,1},{4,6},{5,7},{6,4},{7,5},{8,10},{9,11},{10,... | collective-permute-start | bytes 208904 | tf_op jit(solution)/shard_map/ppermute | solution.py:18
  51.8 1.6 %collective-permute-start.25 = (f32[136,128]{1,0:T(8,128)S(1)}, f32[136,128]{1,0:T(8,128)S(1)}, u32[]{:S(2)}, u32[]{:S(2)}) collective-permute-start(f32[136,128]{1,0:T(8,128)S(1)} %combine.3.refs_0_), channel_id=1, source_target_pairs={{0,3},{1,2},{2,1},{3,0},{4,7},{5,6},{6,5},{7,4},{8,11},{9,10},{10,... | collective-permute-start | bytes 208904 | tf_op jit(solution)/shard_map/ppermute | solution.py:18
  53.8 4.8 %collective-permute-done.26.refs_3_ = f32[136,128]{1,0:T(8,128)S(1)} collective-permute-done((f32[136,128]{1,0:T(8,128)S(1)}, f32[136,128]{1,0:T(8,128)S(1)}, u32[]{:S(2)}, u32[]{:S(2)}) %collective-permute-start.26) | collective-permute-done | bytes 69664 | tf_op jit(solution)/shard_map/ppermute | solution.py:18
  59.4 1.3 %last.1 = (f32[32,2048]{1,0:T(8,128)}, f32[32,2048]{1,0:T(8,128)}) custom-call(f32[32,2048]{1,0:T(8,128)S(1)} %copy-done, f32[32,2048]{1,0:T(8,128)S(1)} %get-tuple-element.36.near.left, f32[8,128]{1,0:T(8,128)S(1)} %get-tuple-element.37.stat.stat_now, f32[136,128]{1,0:T(8,128)S(1)} %combine.3.refs_0_, f32[136,128]{1,0:T(8,128)S(1)} %collective-permute-done.24.refs_1_, ...), custom_call_target="tpu_custom_call" | custom-call | tf_op jit(solution)/shard_map/last/pallas_call | solution.py:455
  (56 shorter events, 7.4 us)
Async XLA Ops:
  0.7 7.2 %collective-permute-start = (f32[32,2048]{1,0:T(8,128)}, f32[32,2048]{1,0:T(8,128)S(1)}, u32[]{:S(2)}, u32[]{:S(2)}) collective-permute-start(f32[32,2048]{1,0:T(8,128)} %right.3), channel_id=1, source_target_pairs={{0,8},{1,5},{2,6},{3,11},{4,0},{5,13},{6,14},{7,3},{8,12},{9,1},{1... | collective-permute-start | bytes 786440 | tf_op jit(solution)/shard_map/ppermute | solution.py:27
  7.9 2.8 %collective-permute-start.1 = (f32[32,2048]{1,0:T(8,128)S(1)}, f32[32,2048]{1,0:T(8,128)S(1)}, u32[]{:S(2)}, u32[]{:S(2)}) collective-permute-start(f32[32,2048]{1,0:T(8,128)S(1)} %pick.1.current), channel_id=1, source_target_pairs={{0,4},{4,0},{8,12},{12,8},{1,5},{5,1},{9,13},{13,9},{2,6},{6,2},{1... | collective-permute-start | bytes 786440 | tf_op jit(solution)/shard_map/ppermute | solution.py:18
  8.9 8.3 %collective-permute-start.5 = (f32[128,128]{1,0:T(8,128)S(1)}, f32[128,128]{1,0:T(8,128)S(1)}, u32[]{:S(2)}, u32[]{:S(2)}) collective-permute-start(f32[128,128]{1,0:T(8,128)S(1)} %get-tuple-element.31), channel_id=1, source_target_pairs={{0,8},{1,9},{2,10},{3,14},{4,12},{5,13},{6,11},{7,15},{8,0},{9,4},... | collective-permute-start | bytes 196616 | tf_op jit(solution)/shard_map/ppermute | solution.py:27
  10.5 6.8 %collective-permute-start.4 = (f32[128,128]{1,0:T(8,128)S(1)}, f32[128,128]{1,0:T(8,128)S(1)}, u32[]{:S(2)}, u32[]{:S(2)}) collective-permute-start(f32[128,128]{1,0:T(8,128)S(1)} %get-tuple-element.27.mark), channel_id=1, source_target_pairs={{0,4},{1,5},{2,8},{3,12},{4,0},{5,1},{6,9},{7,13},{8,2},{9,6},{10,... | collective-permute-start | bytes 196616 | tf_op jit(solution)/shard_map/ppermute | solution.py:27
  13.1 9.6 %collective-permute-start.7 = (f32[128,128]{1,0:T(8,128)S(1)}, f32[128,128]{1,0:T(8,128)S(1)}, u32[]{:S(2)}, u32[]{:S(2)}) collective-permute-start(f32[128,128]{1,0:T(8,128)S(1)} %get-tuple-element.33), channel_id=1, source_target_pairs={{0,2},{1,3},{2,0},{3,1},{4,6},{5,7},{6,4},{7,5},{8,10},{9,11},{10,... | collective-permute-start | bytes 196616 | tf_op jit(solution)/shard_map/ppermute | solution.py:18
  15.0 7.6 %collective-permute-start.8 = (f32[128,128]{1,0:T(8,128)S(1)}, f32[128,128]{1,0:T(8,128)S(1)}, u32[]{:S(2)}, u32[]{:S(2)}) collective-permute-start(f32[128,128]{1,0:T(8,128)S(1)} %get-tuple-element.34), channel_id=1, source_target_pairs={{0,3},{1,2},{2,1},{3,0},{4,7},{5,6},{6,5},{7,4},{8,11},{9,10},{10,... | collective-permute-start | bytes 196616 | tf_op jit(solution)/shard_map/ppermute | solution.py:18
  16.8 5.9 %collective-permute-start.9 = (f32[128,128]{1,0:T(8,128)S(1)}, f32[128,128]{1,0:T(8,128)S(1)}, u32[]{:S(2)}, u32[]{:S(2)}) collective-permute-start(f32[128,128]{1,0:T(8,128)S(1)} %get-tuple-element.35), channel_id=1, source_target_pairs={{0,1},{1,0},{2,3},{3,2},{4,5},{5,4},{6,7},{7,6},{8,9},{9,8},{10,11... | collective-permute-start | bytes 196616 | tf_op jit(solution)/shard_map/ppermute | solution.py:18
  18.4 4.2 %collective-permute-start.6 = (f32[8,128]{1,0:T(8,128)S(1)}, f32[8,128]{1,0:T(8,128)S(1)}, u32[]{:S(2)}, u32[]{:S(2)}) collective-permute-start(f32[8,128]{1,0:T(8,128)S(1)} %add_stat.4.one), channel_id=1, source_target_pairs={{0,8},{4,12},{8,0},{12,4},{1,9},{5,13},{9,1},{13,5},{2,10},{6,14},... | collective-permute-start | bytes 12296 | tf_op jit(solution)/shard_map/ppermute | solution.py:18
  22.7 8.8 %collective-permute-start.12 = (f32[136,128]{1,0:T(8,128)S(1)}, f32[136,128]{1,0:T(8,128)S(1)}, u32[]{:S(2)}, u32[]{:S(2)}) collective-permute-start(f32[136,128]{1,0:T(8,128)S(1)} %combine.2.refs_0_), channel_id=1, source_target_pairs={{0,2},{1,3},{2,0},{3,1},{4,6},{5,7},{6,4},{7,5},{8,10},{9,11},{10,... | collective-permute-start | bytes 208904 | tf_op jit(solution)/shard_map/ppermute | solution.py:18
  24.3 7.1 %collective-permute-start.11 = (f32[136,128]{1,0:T(8,128)S(1)}, f32[136,128]{1,0:T(8,128)S(1)}, u32[]{:S(2)}, u32[]{:S(2)}) collective-permute-start(f32[136,128]{1,0:T(8,128)S(1)} %combine.2.refs_0_), channel_id=1, source_target_pairs={{0,3},{1,2},{2,1},{3,0},{4,7},{5,6},{6,5},{7,4},{8,11},{9,10},{10,... | collective-permute-start | bytes 208904 | tf_op jit(solution)/shard_map/ppermute | solution.py:18
  27.1 4.9 %collective-permute-start.10 = (f32[136,128]{1,0:T(8,128)S(1)}, f32[136,128]{1,0:T(8,128)S(1)}, u32[]{:S(2)}, u32[]{:S(2)}) collective-permute-start(f32[136,128]{1,0:T(8,128)S(1)} %combine.2.refs_0_), channel_id=1, source_target_pairs={{0,1},{1,0},{2,3},{3,2},{4,5},{5,4},{6,7},{7,6},{8,9},{9,8},{10,11... | collective-permute-start | bytes 208904 | tf_op jit(solution)/shard_map/ppermute | solution.py:18
  27.1 6.8 %collective-permute-start.14 = (f32[136,128]{1,0:T(8,128)S(1)}, f32[136,128]{1,0:T(8,128)S(1)}, u32[]{:S(2)}, u32[]{:S(2)}) collective-permute-start(f32[136,128]{1,0:T(8,128)S(1)} %combine.2.refs_0_), channel_id=1, source_target_pairs={{0,4},{1,5},{2,8},{3,12},{4,0},{5,1},{6,9},{7,13},{8,2},{9,6},{10,... | collective-permute-start | bytes 208904 | tf_op jit(solution)/shard_map/ppermute | solution.py:27
  27.1 6.8 %collective-permute-start.13 = (f32[136,128]{1,0:T(8,128)S(1)}, f32[136,128]{1,0:T(8,128)S(1)}, u32[]{:S(2)}, u32[]{:S(2)}) collective-permute-start(f32[136,128]{1,0:T(8,128)S(1)} %combine.2.refs_0_), channel_id=1, source_target_pairs={{0,8},{1,12},{2,10},{3,11},{4,9},{5,13},{6,14},{7,15},{8,0},{9,1},... | collective-permute-start | bytes 208904 | tf_op jit(solution)/shard_map/ppermute | solution.py:27
  34.1 3.4 %collective-permute-start.15 = (f32[16,32,128]{2,1,0:T(8,128)S(1)}, f32[16,32,128]{2,1,0:T(8,128)S(1)}, u32[]{:S(2)}, u32[]{:S(2)}) collective-permute-start(f32[16,32,128]{2,1,0:T(8,128)S(1)} %held.1), channel_id=1, source_target_pairs={{0,4},{4,0},{8,12},{12,8},{1,5},{5,1},{9,13},{13,9},{2,6},{6,2},{1... | collective-permute-start | bytes 786440 | tf_op jit(solution)/shard_map/ppermute | solution.py:18
  35.5 9.2 %collective-permute-start.19 = (f32[128,128]{1,0:T(8,128)S(1)}, f32[128,128]{1,0:T(8,128)S(1)}, u32[]{:S(2)}, u32[]{:S(2)}) collective-permute-start(f32[128,128]{1,0:T(8,128)S(1)} %get-tuple-element.43), channel_id=1, source_target_pairs={{0,8},{1,9},{2,10},{3,14},{4,12},{5,13},{6,11},{7,15},{8,0},{9,4},... | collective-permute-start | bytes 196616 | tf_op jit(solution)/shard_map/ppermute | solution.py:27
  37.6 7.2 %collective-permute-start.18 = (f32[128,128]{1,0:T(8,128)S(1)}, f32[128,128]{1,0:T(8,128)S(1)}, u32[]{:S(2)}, u32[]{:S(2)}) collective-permute-start(f32[128,128]{1,0:T(8,128)S(1)} %get-tuple-element.39.mark), channel_id=1, source_target_pairs={{0,4},{1,5},{2,8},{3,12},{4,0},{5,1},{6,9},{7,13},{8,2},{9,6},{10,... | collective-permute-start | bytes 196616 | tf_op jit(solution)/shard_map/ppermute | solution.py:27
  39.9 4.3 %collective-permute-start.17 = (f32[8,128]{1,0:T(8,128)S(1)}, f32[8,128]{1,0:T(8,128)S(1)}, u32[]{:S(2)}, u32[]{:S(2)}) collective-permute-start(f32[8,128]{1,0:T(8,128)S(1)} %get-tuple-element.42.one), channel_id=1, source_target_pairs={{0,4},{4,0},{8,12},{12,8},{1,5},{5,1},{9,13},{13,9},{2,6},{6,2},{1... | collective-permute-start | bytes 12296 | tf_op jit(solution)/shard_map/ppermute | solution.py:18
  40.0 9.5 %collective-permute-start.21 = (f32[128,128]{1,0:T(8,128)S(1)}, f32[128,128]{1,0:T(8,128)S(1)}, u32[]{:S(2)}, u32[]{:S(2)}) collective-permute-start(f32[128,128]{1,0:T(8,128)S(1)} %get-tuple-element.45), channel_id=1, source_target_pairs={{0,2},{1,3},{2,0},{3,1},{4,6},{5,7},{6,4},{7,5},{8,10},{9,11},{10,... | collective-permute-start | bytes 196616 | tf_op jit(solution)/shard_map/ppermute | solution.py:18
  42.1 7.3 %collective-permute-start.22 = (f32[128,128]{1,0:T(8,128)S(1)}, f32[128,128]{1,0:T(8,128)S(1)}, u32[]{:S(2)}, u32[]{:S(2)}) collective-permute-start(f32[128,128]{1,0:T(8,128)S(1)} %get-tuple-element.46), channel_id=1, source_target_pairs={{0,3},{1,2},{2,1},{3,0},{4,7},{5,6},{6,5},{7,4},{8,11},{9,10},{10,... | collective-permute-start | bytes 196616 | tf_op jit(solution)/shard_map/ppermute | solution.py:18
  44.2 5.9 %collective-permute-start.23 = (f32[128,128]{1,0:T(8,128)S(1)}, f32[128,128]{1,0:T(8,128)S(1)}, u32[]{:S(2)}, u32[]{:S(2)}) collective-permute-start(f32[128,128]{1,0:T(8,128)S(1)} %get-tuple-element.47), channel_id=1, source_target_pairs={{0,1},{1,0},{2,3},{3,2},{4,5},{5,4},{6,7},{7,6},{8,9},{9,8},{10,11... | collective-permute-start | bytes 196616 | tf_op jit(solution)/shard_map/ppermute | solution.py:18
  44.7 4.7 %collective-permute-start.20 = (f32[8,128]{1,0:T(8,128)S(1)}, f32[8,128]{1,0:T(8,128)S(1)}, u32[]{:S(2)}, u32[]{:S(2)}) collective-permute-start(f32[8,128]{1,0:T(8,128)S(1)} %add_stat.6.one), channel_id=1, source_target_pairs={{0,8},{4,12},{8,0},{12,4},{1,9},{5,13},{9,1},{13,5},{2,10},{6,14},... | collective-permute-start | bytes 12296 | tf_op jit(solution)/shard_map/ppermute | solution.py:18
  50.2 8.4 %collective-permute-start.26 = (f32[136,128]{1,0:T(8,128)S(1)}, f32[136,128]{1,0:T(8,128)S(1)}, u32[]{:S(2)}, u32[]{:S(2)}) collective-permute-start(f32[136,128]{1,0:T(8,128)S(1)} %combine.3.refs_0_), channel_id=1, source_target_pairs={{0,2},{1,3},{2,0},{3,1},{4,6},{5,7},{6,4},{7,5},{8,10},{9,11},{10,... | collective-permute-start | bytes 208904 | tf_op jit(solution)/shard_map/ppermute | solution.py:18
  51.8 6.8 %collective-permute-start.25 = (f32[136,128]{1,0:T(8,128)S(1)}, f32[136,128]{1,0:T(8,128)S(1)}, u32[]{:S(2)}, u32[]{:S(2)}) collective-permute-start(f32[136,128]{1,0:T(8,128)S(1)} %combine.3.refs_0_), channel_id=1, source_target_pairs={{0,3},{1,2},{2,1},{3,0},{4,7},{5,6},{6,5},{7,4},{8,11},{9,10},{10,... | collective-permute-start | bytes 208904 | tf_op jit(solution)/shard_map/ppermute | solution.py:18
  53.4 6.0 %collective-permute-start.24 = (f32[136,128]{1,0:T(8,128)S(1)}, f32[136,128]{1,0:T(8,128)S(1)}, u32[]{:S(2)}, u32[]{:S(2)}) collective-permute-start(f32[136,128]{1,0:T(8,128)S(1)} %combine.3.refs_0_), channel_id=1, source_target_pairs={{0,1},{1,0},{2,3},{3,2},{4,5},{5,4},{6,7},{7,6},{8,9},{9,8},{10,11... | collective-permute-start | bytes 208904 | tf_op jit(solution)/shard_map/ppermute | solution.py:18
  (7 other events, 41.7 us)

commit v10 on v6

--- a/solution.py
+++ b/solution.py
@@ -18,8 +18,14 @@
     return lax.ppermute(value, axis, [(i, i ^ d) for i in range(n)])
 
 
-def distances(n):
-    return [d for d in range(n) if d > 1] + [1]
+def distances(row, n):
+    even = [d for d in range(n) if d > 1] + [1]
+    odd = [1] + [d for d in range(n) if d > 1]
+    return [e + (o - e) * (row & 1) for e, o in zip(even, odd)]
+
+
+def along_line(values, n):
+    return [moved(value, n, lambda r, c: (r, c ^ distances(r, n)[i])) for i, value in enumerate(values)]
 
 
 def moved(value, n, target):
@@ -89,28 +95,30 @@
         total[tile * width + part] += value[:, part * LANES:(part + 1) * LANES]
 
 
-def add_blocks(blocks, slot_rows, slot_cols, live, pairs, total, mirror, ready=None):
+def wide_group(blocks):
+    return 2 * GROUP if blocks.shape[0] % (2 * GROUP) == 0 else GROUP
+
+
+def add_blocks(blocks, slot_rows, slot_cols, live, pairs, total, mirror, group, ready=None):
     read, write, contract = (slot_rows, slot_cols, 0) if mirror else (slot_cols, slot_rows, 1)
 
     def body(step, carry):
         if ready is not None:
             ready(step)
-        values = []
-        for g in range(GROUP):
-            slot = step * GROUP + g
+        for g in range(group):
+            slot = step * group + g
             value = product(pairs[read[0, 0, slot]], blocks[slot], contract)
-            values.append((write[0, 0, slot], jnp.where(slot < live, value, 0.0)))
-        for tile, value in values:
-            accumulate(total, tile, value)
+            accumulate(total, write[0, 0, slot], jnp.where(slot < live, value, 0.0))
         return carry
 
-    lax.fori_loop(0, (live + GROUP - 1) // GROUP, body, 0)
-
-
-def image_part(parts, me, i, per, rhs):
+    lax.fori_loop(0, (live + group - 1) // group, body, 0)
+
+
+def image_part(parts, i, per, rhs):
+    row, me = lax.axis_index("row"), lax.axis_index("col")
     rows = slice((i % per) * rhs, (i % per + 1) * rhs)
     value = parts[0][rows, :]
-    for d, part in zip(distances(len(parts))[::-1], parts[1:]):
+    for d, part in zip(distances(row, len(parts))[::-1], parts[1:]):
         value = jnp.where(me ^ d == i // per, part[rows, :], value)
     return value
 
@@ -135,8 +143,11 @@
 
 
 def stat_sum(parts, data):
-    order = [0] + distances(len(parts))[::-1]
-    return tree_sum(parts[order.index(d)][data:, :] for d in range(len(parts)))
+    odd = (lax.axis_index("row") & 1) == 1
+    tiles = [part[data:, :] for part in parts]
+    even_order = [tiles[0]] + tiles[:0:-1][-1:] + tiles[:0:-1][:-1]
+    odd_order = [tiles[0]] + tiles[:0:-1]
+    return jnp.where(odd, tree_sum(odd_order), tree_sum(even_order))
 
 
 def fetch_index(sources, targets, sems):
@@ -168,7 +179,7 @@
         load_pair(pairs, tile, right[:, tile * tile_size:(tile + 1) * tile_size])
     for copy in copies:
         copy.wait()
-    add_blocks(blocks, slot_rows, slot_cols, live, pairs, total, True, lambda i: block_copy(i).wait())
+    add_blocks(blocks, slot_rows, slot_cols, live, pairs, total, True, GROUP, lambda i: block_copy(i).wait())
 
 
 def mirror_second_kernel(rows_any, cols_any, count, near, blocks, total, *scratch):
@@ -180,7 +191,7 @@
         load_pair(pairs, tile, near[:, tile * tile_size:(tile + 1) * tile_size])
     for copy in copies:
         copy.wait()
-    add_blocks(blocks, slot_rows, slot_cols, count[0, 0], pairs, total, True)
+    add_blocks(blocks, slot_rows, slot_cols, count[0, 0], pairs, total, True, wide_group(blocks))
 
 
 def finish_direct(total, near, noise, stat, n):
@@ -209,7 +220,7 @@
     total[...] = jnp.zeros_like(total)
     for copy in copies:
         copy.wait()
-    add_blocks(blocks, slot_rows, slot_cols, count[0, 0], pairs, total, False)
+    add_blocks(blocks, slot_rows, slot_cols, count[0, 0], pairs, total, False, wide_group(blocks))
     finish_direct(total, near, noise, stat, n)
 
 
@@ -230,7 +241,7 @@
     total[...] = jnp.zeros_like(total)
     for copy in copies:
         copy.wait()
-    add_blocks(blocks, slot_rows, slot_cols, count[0, 0], pairs, total, False)
+    add_blocks(blocks, slot_rows, slot_cols, count[0, 0], pairs, total, False, wide_group(blocks))
     finish_direct(total, near, noise, stat, n)
 
 
@@ -258,8 +269,9 @@
     rhs = direct.shape[1]
     me = lax.axis_index("col")
     diagonal = lax.axis_index("row") == me
-    outs[n][...] = stat[...]
-    for d, out in zip([0] + distances(n), outs):
+    if outs[n] is not None:
+        outs[n][...] = stat[...]
+    for d, out in zip([0] + distances(lax.axis_index("row"), n), outs):
         first = (me ^ d) * per
 
         @pl.when(diagonal)
@@ -273,9 +285,27 @@
                 out[i * rhs:(i + 1) * rhs, :] = direct[first + i]
 
 
-def combine_kernel(n, near, noise, stat, *refs):
-    parts, others, chunk = refs[:n], refs[n:-1], refs[-1]
+def merge_last_kernel(n, direct, mirror, twin, stat, *outs):
+    data = direct.shape[0] // n * direct.shape[1]
+    merge_kernel(n, direct, mirror, twin, stat, *[out.at[:data] for out in outs], None)
+    for out in outs:
+        out[data:, :] = stat[...]
+
+
+def pass_kernel(value, *refs):
+    refs[-1][...] = value[...]
+
+
+def combine_last_kernel(n, near, noise, *refs):
+    parts, others, (chunk, stat) = refs[:n], refs[n:-2], refs[-2:]
+    data = chunk.shape[0]
+    stat[...] = tree_sum(ref[data:, :] for ref in parts)
+    sum_chunk(near, noise, [ref.at[:data] for ref in parts], others, chunk)
+
+
+def sum_chunk(near, noise, parts, others, chunk):
     rhs = near.shape[0]
+    n = len(parts)
     data = parts[0].shape[0]
     per = data // rhs
     me = lax.axis_index("col")
@@ -284,7 +314,6 @@
     for j, other in enumerate(others):
         value += jnp.where(group == j, 0.0, other[...])
     chunk[:data, :] = value
-    chunk[data:, :] = stat[...]
     for k in range(n):
         @pl.when(me == k)
         def _():
@@ -293,18 +322,24 @@
                 chunk[i * rhs:(i + 1) * rhs, :] += near[:, lanes] * noise[:, lanes]
 
 
+def combine_kernel(n, near, noise, stat, *refs):
+    parts, others, chunk = refs[:n], refs[n:-1], refs[-1]
+    data = parts[0].shape[0]
+    sum_chunk(near, noise, parts, others, chunk)
+    chunk[data:, :] = stat[...]
+
+
 def left_kernel(right, *refs):
     parts, (left, stat) = refs[:-2], refs[-2:]
     rhs, width = right.shape
     data = parts[0].shape[0] - 8
     per = data // rhs
-    me = lax.axis_index("col")
     both = stat_sum(parts, data)
     stat[...] = both
     size_now = unpack_stat(both, 0, rhs) / unpack_stat(both, 1, rhs)
     for i in range(width // LANES):
         lanes = slice(i * LANES, (i + 1) * LANES)
-        left[:, lanes] = right[:, lanes] - size_now * image_part(parts, me, i, per, rhs)
+        left[:, lanes] = right[:, lanes] - size_now * image_part(parts, i, per, rhs)
 
 
 def held_kernel(n, left, stat, far, mark, *refs):
@@ -328,13 +363,11 @@
                 held[first + i] = far[first + i] - size_now * part[i * rhs:(i + 1) * rhs, :]
 
 
-def last_kernel(right, left, stat_now, *refs):
+def last_kernel(right, left, stat_now, stat_next, *refs):
     parts, (solution, residual) = refs[:-2], refs[-2:]
     rhs, width = right.shape
-    data = parts[0].shape[0] - 8
-    per = data // rhs
-    me = lax.axis_index("col")
-    both = stat_sum(parts, data)
+    per = parts[0].shape[0] // rhs
+    both = stat_next[...]
     norm = unpack_stat(stat_now[...], 0, rhs)
     norm_next = unpack_stat(both, 0, rhs)
     size_now = norm / unpack_stat(stat_now[...], 1, rhs)
@@ -346,7 +379,7 @@
         first = right[:, lanes]
         now = left[:, lanes]
         solution[:, lanes] = size_now * first + size_next * (now + ratio * first)
-        image = image_part(parts, me, i, per, rhs) + back * (first - now)
+        image = image_part(parts, i, per, rhs) + back * (first - now)
         residual[:, lanes] = now - size_next * image
 
 
@@ -400,14 +433,26 @@
     def gathered(near, mirror, twin, others, direct, stat):
         merged = call(functools.partial(merge_kernel, n), "merge", [vmem] * 4, [chunk] * n + [tile], [],
                       (direct, mirror, twin, stat))
-        parts = [merged[0]] + [shifted(value, "col", d, n) for d, value in zip(distances(n), merged[1:n])]
+        parts = [merged[0]] + along_line(merged[1:n], n)
         stat = merged[n]
         for b in bits(n):
             stat, = call(add_kernel, "add_stat", [vmem] * (2 + n // 2), [tile], [],
                          (stat, shifted(stat, "row", b, n), *others))
         own, = call(functools.partial(combine_kernel, n), "combine", [vmem] * (3 + n + n // 2), [loaded], [],
                     (near, noise, stat, *parts, *others))
-        return [own] + [shifted(own, "col", d, n) for d in distances(n)[::-1]]
+        return [own] + along_line([own] * (n - 1), n)[::-1]
+
+    def gathered_last(near, mirror, twin, others, direct, stat):
+        merged = call(functools.partial(merge_last_kernel, n), "merge_last", [vmem] * 4, [loaded] * n, [],
+                      (direct, mirror, twin, stat))
+        final, = call(pass_kernel, "pass_on", [vmem] * (1 + n // 2), [loaded], [], (merged[n - 1], *others))
+        parts = [merged[0]] + along_line([*merged[1:n - 1], final], n)
+        own, stat = call(functools.partial(combine_last_kernel, n), "combine_last", [vmem] * (2 + n + n // 2),
+                         [chunk, tile], [], (near, noise, *parts, *others))
+        parts = [own] + along_line([own] * (n - 1), n)[::-1]
+        for b in bits(n):
+            stat, = call(add_kernel, "add_stat", [vmem] * 2, [tile], [], (stat, shifted(stat, "row", b, n)))
+        return parts, stat
 
     current = right_sides
     for b in bits(n)[:0:-1]:
@@ -440,9 +485,9 @@
     direct, stat = call(
         functools.partial(direct_second_kernel, n), "direct_second", [any_spec] * 2 + [smem] + [vmem] * 6,
         [total, tile], kernel_index, (*index, noise, blocks, left, held, twin, mark), True)
-    parts = gathered(left, mirror, twin_mirror, others, direct, stat)
-    return tuple(call(last_kernel, "last", [vmem] * (n + 3), [field, field], [],
-                      (right_sides, left, stat_now, *parts)))
+    parts, stat_next = gathered_last(left, mirror, twin_mirror, others, direct, stat)
+    return tuple(call(last_kernel, "last", [vmem] * (n + 4), [field, field], [],
+                      (right_sides, left, stat_now, stat_next, *parts)))
 
 
 def solution(mesh):

time: 61 us -> 61.6 us (level)
  Pallas kernels: 6.89 us -> 11.3 us
  starting transfers between devices: 36.8 us -> 33.6 us
    ppermute x20 -> x8, starting transfers between devices: 25.2 us -> 4.68 us  [shifted(): return lax.ppermute(value, axis, [(i, i ^ d) for i in range(n)])]
    ppermute x7 -> x19, starting transfers between devices: 11.7 us -> 29 us  [moved(): lax.ppermute(value, ('row', 'col'), [(s, t[0] * n + t[1]) for s, t in pai...]
    ppermute x20 -> x8, waiting for transfers between devices: 13.2 us -> 7.65 us  [shifted(): return lax.ppermute(value, axis, [(i, i ^ d) for i in range(n)])]
    ppermute x7 -> x19, waiting for transfers between devices: 1.78 us -> 7.27 us  [moved(): lax.ppermute(value, ('row', 'col'), [(s, t[0] * n + t[1]) for s, t in pai...]
    pallas_call x18 -> x19, Pallas kernels: 6.89 us -> 11.3 us  [call(): pl.pallas_call(kernel, in_specs=specs, out_specs=jax.tree.map(lambda _: v...]
  transfers between devices with their start and end apart: 27 -> 27, of which waited for: 10 -> 12; matrix products, arithmetic and copies ran while one was open for 0% -> 0% of each run, Pallas kernels for 9% -> 16%
where the time goes in v10:
time: 61.6 us; the launch traced here: 61.4 us
  starting transfers between devices  33.6 us (55%)
  waiting for transfers between devices  14.9 us (24%)
  Pallas kernels  11.3 us (18%)
  between operations  1.49 us (2%)
    ppermute x19, starting transfers between devices, moved(): lax.ppermute(value, ('row', 'col'), [(s, t[0] * n + t[1]) for s, t in pai...  29 us
    pallas_call x19, Pallas kernels, call(): pl.pallas_call(kernel, in_specs=specs, out_specs=jax.tree.map(lambda _: v...  11.3 us
    ppermute x8, waiting for transfers between devices, shifted(): return lax.ppermute(value, axis, [(i, i ^ d) for i in range(n)])  7.65 us
    ppermute x19, waiting for transfers between devices, moved(): lax.ppermute(value, ('row', 'col'), [(s, t[0] * n + t[1]) for s, t in pai...  7.27 us
    ppermute x8, starting transfers between devices, shifted(): return lax.ppermute(value, axis, [(i, i ^ d) for i in range(n)])  4.68 us
  transfers between devices with their start and end apart: 27, of which 12 were waited for; matrix products, arithmetic and copies ran while one was open for 0% of the time, Pallas kernels for 16%

profile of v10, /device:TPU:0, one launch (start us, length us, event | category | flops | bytes accessed | tf_op | source)
XLA Modules:
  0.0 61.4 jit_solution(10352024377936306231)
XLA Ops:
  0.7 3.0 %collective-permute-start = (f32[32,2048]{1,0:T(8,128)}, f32[32,2048]{1,0:T(8,128)S(1)}, u32[]{:S(2)}, u32[]{:S(2)}) collective-permute-start(f32[32,2048]{1,0:T(8,128)} %right.3), channel_id=1, source_target_pairs={{0,8},{1,5},{2,6},{3,11},{4,0},{5,13},{6,14},{7,3},{8,12},{9,1},{1... | collective-permute-start | bytes 786440 | tf_op jit(solution)/shard_map/ppermute | solution.py:33
  4.3 3.3 %mirror_first.1 = (f32[16,32,128]{2,1,0:T(8,128)S(1)}, bf16[32,256,256]{2,1,0:T(8,128)(2,1)S(1)}) custom-call(s32[1,1,32]{2,1,0:T(1,128)} %rows_any.5, s32[1,1,32]{2,1,0:T(1,128)} %cols_any.5, s32[1,1]{1,0:T(1,128)S(6)} %copy.8.count, f32[32,2048]{1,0:T(8,128)} %right.3, bf16[1,1,32,256,256]{4,3,2,1,0:T(8,128)(2,1)} %cov.1), custom_call_target="tpu_custom_call" | custom-call | flops 268435456 | bytes 4194304 | tf_op jit(solution)/shard_map/mirror_first/pallas_call | solution.py:415
  9.2 1.3 %collective-permute-start.5 = (f32[128,128]{1,0:T(8,128)S(1)}, f32[128,128]{1,0:T(8,128)S(1)}, u32[]{:S(2)}, u32[]{:S(2)}) collective-permute-start(f32[128,128]{1,0:T(8,128)S(1)} %get-tuple-element.32), channel_id=1, source_target_pairs={{0,8},{1,9},{2,10},{3,14},{4,12},{5,13},{6,11},{7,15},{8,0},{9,4},... | collective-permute-start | bytes 196616 | tf_op jit(solution)/shard_map/ppermute | solution.py:33
  10.7 2.3 %direct_first.1 = (f32[16,32,128]{2,1,0:T(8,128)S(1)}, f32[8,128]{1,0:T(8,128)S(1)}, f32[16,32,128]{2,1,0:T(8,128)S(1)}) custom-call(s32[1,1,32]{2,1,0:T(1,128)S(1)} %copy-done.2, s32[1,1,32]{2,1,0:T(1,128)S(1)} %copy-done.3, s32[1,1]{1,0:T(1,128)S(6)} %copy.8.count, f32[1,2048]{1,0:T(1,128)S(1)} %bitcast.1, ...), custom_call_target="tpu_custom_call" | custom-call | flops 268435456 | bytes 4194304 | tf_op jit(solution)/shard_map/direct_first/pallas_call | solution.py:415
  13.1 2.3 %collective-permute-start.7 = (f32[128,128]{1,0:T(8,128)S(1)}, f32[128,128]{1,0:T(8,128)S(1)}, u32[]{:S(2)}, u32[]{:S(2)}) collective-permute-start(f32[128,128]{1,0:T(8,128)S(1)} %get-tuple-element.34), channel_id=1, source_target_pairs={{0,2},{1,3},{2,0},{3,1},{4,5},{5,4},{6,7},{7,6},{8,10},{9,11},{10,... | collective-permute-start | bytes 196616 | tf_op jit(solution)/shard_map/ppermute | solution.py:33
  15.3 2.2 %collective-permute-start.8 = (f32[128,128]{1,0:T(8,128)S(1)}, f32[128,128]{1,0:T(8,128)S(1)}, u32[]{:S(2)}, u32[]{:S(2)}) collective-permute-start(f32[128,128]{1,0:T(8,128)S(1)} %get-tuple-element.35), channel_id=1, source_target_pairs={{0,3},{1,2},{2,1},{3,0},{4,6},{5,7},{6,4},{7,5},{8,11},{9,10},{10,... | collective-permute-start | bytes 196616 | tf_op jit(solution)/shard_map/ppermute | solution.py:33
  19.2 1.9 %collective-permute-start.6 = (f32[8,128]{1,0:T(8,128)S(1)}, f32[8,128]{1,0:T(8,128)S(1)}, u32[]{:S(2)}, u32[]{:S(2)}) collective-permute-start(f32[8,128]{1,0:T(8,128)S(1)} %add_stat.4.one), channel_id=1, source_target_pairs={{0,8},{4,12},{8,0},{12,4},{1,9},{5,13},{9,1},{13,5},{2,10},{6,14},... | collective-permute-start | bytes 12296 | tf_op jit(solution)/shard_map/ppermute | solution.py:18
  21.0 1.8 %collective-permute-done.6.two = f32[8,128]{1,0:T(8,128)S(1)} collective-permute-done((f32[8,128]{1,0:T(8,128)S(1)}, f32[8,128]{1,0:T(8,128)S(1)}, u32[]{:S(2)}, u32[]{:S(2)}) %collective-permute-start.6) | collective-permute-done | bytes 4128 | tf_op jit(solution)/shard_map/ppermute | solution.py:18
  22.9 2.6 %collective-permute-start.12 = (f32[136,128]{1,0:T(8,128)S(1)}, f32[136,128]{1,0:T(8,128)S(1)}, u32[]{:S(2)}, u32[]{:S(2)}) collective-permute-start(f32[136,128]{1,0:T(8,128)S(1)} %combine.1.refs_0_), channel_id=1, source_target_pairs={{0,2},{1,3},{2,0},{3,1},{4,5},{5,4},{6,7},{7,6},{8,10},{9,11},{10,... | collective-permute-start | bytes 208904 | tf_op jit(solution)/shard_map/ppermute | solution.py:33
  25.4 1.7 %collective-permute-start.11 = (f32[136,128]{1,0:T(8,128)S(1)}, f32[136,128]{1,0:T(8,128)S(1)}, u32[]{:S(2)}, u32[]{:S(2)}) collective-permute-start(f32[136,128]{1,0:T(8,128)S(1)} %combine.1.refs_0_), channel_id=1, source_target_pairs={{0,3},{1,2},{2,1},{3,0},{4,6},{5,7},{6,4},{7,5},{8,11},{9,10},{10,... | collective-permute-start | bytes 208904 | tf_op jit(solution)/shard_map/ppermute | solution.py:33
  27.1 2.0 %collective-permute-start.14 = (f32[136,128]{1,0:T(8,128)S(1)}, f32[136,128]{1,0:T(8,128)S(1)}, u32[]{:S(2)}, u32[]{:S(2)}) collective-permute-start(f32[136,128]{1,0:T(8,128)S(1)} %combine.1.refs_0_), channel_id=1, source_target_pairs={{0,8},{1,12},{2,10},{3,11},{4,9},{5,13},{6,14},{7,15},{8,0},{9,1},... | collective-permute-start | bytes 208904 | tf_op jit(solution)/shard_map/ppermute | solution.py:33
  29.2 1.6 %collective-permute-start.13 = (f32[136,128]{1,0:T(8,128)S(1)}, f32[136,128]{1,0:T(8,128)S(1)}, u32[]{:S(2)}, u32[]{:S(2)}) collective-permute-start(f32[136,128]{1,0:T(8,128)S(1)} %combine.1.refs_0_), channel_id=1, source_target_pairs={{0,4},{1,5},{2,8},{3,12},{4,0},{5,1},{6,9},{7,13},{8,2},{9,6},{10,... | collective-permute-start | bytes 208904 | tf_op jit(solution)/shard_map/ppermute | solution.py:33
  30.7 1.7 %collective-permute-done.12.refs_3_ = f32[136,128]{1,0:T(8,128)S(1)} collective-permute-done((f32[136,128]{1,0:T(8,128)S(1)}, f32[136,128]{1,0:T(8,128)S(1)}, u32[]{:S(2)}, u32[]{:S(2)}) %collective-permute-start.12) | collective-permute-done | bytes 69664 | tf_op jit(solution)/shard_map/ppermute | solution.py:33
  32.8 1.6 %mirror_second.1.mark.mirror = f32[16,32,128]{2,1,0:T(8,128)S(1)} custom-call(s32[1,1,32]{2,1,0:T(1,128)S(1)} %copy-done.2, s32[1,1,32]{2,1,0:T(1,128)S(1)} %copy-done.3, s32[1,1]{1,0:T(1,128)S(6)} %copy.8.count, f32[32,2048]{1,0:T(8,128)S(1)} %get-tuple-element.37.near.left, bf16[32,256,256]{2,1,0:T(8,128)(2,1)S(1)} %get-tuple-element.26.blocks), custom_call_target="tpu_custom_call" | custom-call | flops 268435456 | bytes 4194304 | tf_op jit(solution)/shard_map/mirror_second/pallas_call | solution.py:415
  36.0 2.1 %collective-permute-start.20 = (f32[128,128]{1,0:T(8,128)S(1)}, f32[128,128]{1,0:T(8,128)S(1)}, u32[]{:S(2)}, u32[]{:S(2)}) collective-permute-start(f32[128,128]{1,0:T(8,128)S(1)} %get-tuple-element.47), channel_id=1, source_target_pairs={{0,8},{1,9},{2,10},{3,14},{4,12},{5,13},{6,11},{7,15},{8,0},{9,4},... | collective-permute-start | bytes 196616 | tf_op jit(solution)/shard_map/ppermute | solution.py:33
  38.3 2.2 %direct_second.1 = (f32[16,32,128]{2,1,0:T(8,128)S(1)}, f32[8,128]{1,0:T(8,128)S(1)}) custom-call(s32[1,1,32]{2,1,0:T(1,128)S(1)} %copy-done.2, s32[1,1,32]{2,1,0:T(1,128)S(1)} %copy-done.3, s32[1,1]{1,0:T(1,128)S(6)} %copy.8.count, f32[1,2048]{1,0:T(1,128)S(1)} %bitcast.3, bf16[32,256,256]{2,1,0:T(8,128)(2,1)S(1)} %get-tuple-element.26.blocks, ...), custom_call_target="tpu_custom_call" | custom-call | flops 268435456 | bytes 4194304 | tf_op jit(solution)/shard_map/direct_second/pallas_call | solution.py:415
  40.7 1.5 %collective-permute-start.17 = (f32[136,128]{1,0:T(8,128)S(1)}, f32[136,128]{1,0:T(8,128)S(1)}, u32[]{:S(2)}, u32[]{:S(2)}) collective-permute-start(f32[136,128]{1,0:T(8,128)S(1)} %get-tuple-element.44), channel_id=1, source_target_pairs={{0,2},{1,3},{2,0},{3,1},{4,5},{5,4},{6,7},{7,6},{8,10},{9,11},{10,... | collective-permute-start | bytes 208904 | tf_op jit(solution)/shard_map/ppermute | solution.py:33
  42.2 3.6 %collective-permute-start.18 = (f32[136,128]{1,0:T(8,128)S(1)}, f32[136,128]{1,0:T(8,128)S(1)}, u32[]{:S(2)}, u32[]{:S(2)}) collective-permute-start(f32[136,128]{1,0:T(8,128)S(1)} %get-tuple-element.45), channel_id=1, source_target_pairs={{0,3},{1,2},{2,1},{3,0},{4,6},{5,7},{6,4},{7,5},{8,11},{9,10},{10,... | collective-permute-start | bytes 208904 | tf_op jit(solution)/shard_map/ppermute | solution.py:33
  46.3 3.9 %collective-permute-done.17.refs_1_ = f32[136,128]{1,0:T(8,128)S(1)} collective-permute-done((f32[136,128]{1,0:T(8,128)S(1)}, f32[136,128]{1,0:T(8,128)S(1)}, u32[]{:S(2)}, u32[]{:S(2)}) %collective-permute-start.17) | collective-permute-done | bytes 69664 | tf_op jit(solution)/shard_map/ppermute | solution.py:33
  50.9 1.7 %collective-permute-start.26 = (f32[128,128]{1,0:T(8,128)S(1)}, f32[128,128]{1,0:T(8,128)S(1)}, u32[]{:S(2)}, u32[]{:S(2)}) collective-permute-start(f32[128,128]{1,0:T(8,128)S(1)} %get-tuple-element.49.refs_0_), channel_id=1, source_target_pairs={{0,2},{1,3},{2,0},{3,1},{4,5},{5,4},{6,7},{7,6},{8,10},{9,11},{10,... | collective-permute-start | bytes 196616 | tf_op jit(solution)/shard_map/ppermute | solution.py:33
  52.6 2.0 %collective-permute-start.25 = (f32[128,128]{1,0:T(8,128)S(1)}, f32[128,128]{1,0:T(8,128)S(1)}, u32[]{:S(2)}, u32[]{:S(2)}) collective-permute-start(f32[128,128]{1,0:T(8,128)S(1)} %get-tuple-element.49.refs_0_), channel_id=1, source_target_pairs={{0,3},{1,2},{2,1},{3,0},{4,6},{5,7},{6,4},{7,5},{8,11},{9,10},{10,... | collective-permute-start | bytes 196616 | tf_op jit(solution)/shard_map/ppermute | solution.py:33
  55.8 1.8 %collective-permute-start.23 = (f32[8,128]{1,0:T(8,128)S(1)}, f32[8,128]{1,0:T(8,128)S(1)}, u32[]{:S(2)}, u32[]{:S(2)}) collective-permute-start(f32[8,128]{1,0:T(8,128)S(1)} %add_stat.6.one), channel_id=1, source_target_pairs={{0,8},{4,12},{8,0},{12,4},{1,9},{5,13},{9,1},{13,5},{2,10},{6,14},... | collective-permute-start | bytes 12296 | tf_op jit(solution)/shard_map/ppermute | solution.py:18
  57.6 1.8 %collective-permute-done.23.two = f32[8,128]{1,0:T(8,128)S(1)} collective-permute-done((f32[8,128]{1,0:T(8,128)S(1)}, f32[8,128]{1,0:T(8,128)S(1)}, u32[]{:S(2)}, u32[]{:S(2)}) %collective-permute-start.23) | collective-permute-done | bytes 4128 | tf_op jit(solution)/shard_map/ppermute | solution.py:18
  60.2 1.2 %last.1 = (f32[32,2048]{1,0:T(8,128)}, f32[32,2048]{1,0:T(8,128)}) custom-call(f32[32,2048]{1,0:T(8,128)S(1)} %copy-done, f32[32,2048]{1,0:T(8,128)S(1)} %get-tuple-element.37.near.left, f32[8,128]{1,0:T(8,128)S(1)} %get-tuple-element.38.stat.stat_now, f32[8,128]{1,0:T(8,128)S(1)} %add_stat.7.stat_next, f32[128,128]{1,0:T(8,128)S(1)} %get-tuple-element.49.refs_0_, ...), custom_call_target="tpu_custom_call" | custom-call | tf_op jit(solution)/shard_map/last/pallas_call | solution.py:415
  (57 shorter events, 9.0 us)
Async XLA Ops:
  0.7 7.2 %collective-permute-start = (f32[32,2048]{1,0:T(8,128)}, f32[32,2048]{1,0:T(8,128)S(1)}, u32[]{:S(2)}, u32[]{:S(2)}) collective-permute-start(f32[32,2048]{1,0:T(8,128)} %right.3), channel_id=1, source_target_pairs={{0,8},{1,5},{2,6},{3,11},{4,0},{5,13},{6,14},{7,3},{8,12},{9,1},{1... | collective-permute-start | bytes 786440 | tf_op jit(solution)/shard_map/ppermute | solution.py:33
  7.9 2.8 %collective-permute-start.1 = (f32[32,2048]{1,0:T(8,128)S(1)}, f32[32,2048]{1,0:T(8,128)S(1)}, u32[]{:S(2)}, u32[]{:S(2)}) collective-permute-start(f32[32,2048]{1,0:T(8,128)S(1)} %pick.1.current), channel_id=1, source_target_pairs={{0,4},{4,0},{8,12},{12,8},{1,5},{5,1},{9,13},{13,9},{2,6},{6,2},{1... | collective-permute-start | bytes 786440 | tf_op jit(solution)/shard_map/ppermute | solution.py:18
  9.2 8.8 %collective-permute-start.5 = (f32[128,128]{1,0:T(8,128)S(1)}, f32[128,128]{1,0:T(8,128)S(1)}, u32[]{:S(2)}, u32[]{:S(2)}) collective-permute-start(f32[128,128]{1,0:T(8,128)S(1)} %get-tuple-element.32), channel_id=1, source_target_pairs={{0,8},{1,9},{2,10},{3,14},{4,12},{5,13},{6,11},{7,15},{8,0},{9,4},... | collective-permute-start | bytes 196616 | tf_op jit(solution)/shard_map/ppermute | solution.py:33
  10.5 7.5 %collective-permute-start.4 = (f32[128,128]{1,0:T(8,128)S(1)}, f32[128,128]{1,0:T(8,128)S(1)}, u32[]{:S(2)}, u32[]{:S(2)}) collective-permute-start(f32[128,128]{1,0:T(8,128)S(1)} %get-tuple-element.28.mark), channel_id=1, source_target_pairs={{0,4},{1,5},{2,8},{3,12},{4,0},{5,1},{6,9},{7,13},{8,2},{9,6},{10,... | collective-permute-start | bytes 196616 | tf_op jit(solution)/shard_map/ppermute | solution.py:33
  13.1 9.7 %collective-permute-start.7 = (f32[128,128]{1,0:T(8,128)S(1)}, f32[128,128]{1,0:T(8,128)S(1)}, u32[]{:S(2)}, u32[]{:S(2)}) collective-permute-start(f32[128,128]{1,0:T(8,128)S(1)} %get-tuple-element.34), channel_id=1, source_target_pairs={{0,2},{1,3},{2,0},{3,1},{4,5},{5,4},{6,7},{7,6},{8,10},{9,11},{10,... | collective-permute-start | bytes 196616 | tf_op jit(solution)/shard_map/ppermute | solution.py:33
  15.3 7.5 %collective-permute-start.8 = (f32[128,128]{1,0:T(8,128)S(1)}, f32[128,128]{1,0:T(8,128)S(1)}, u32[]{:S(2)}, u32[]{:S(2)}) collective-permute-start(f32[128,128]{1,0:T(8,128)S(1)} %get-tuple-element.35), channel_id=1, source_target_pairs={{0,3},{1,2},{2,1},{3,0},{4,6},{5,7},{6,4},{7,5},{8,11},{9,10},{10,... | collective-permute-start | bytes 196616 | tf_op jit(solution)/shard_map/ppermute | solution.py:33
  17.5 5.3 %collective-permute-start.9 = (f32[128,128]{1,0:T(8,128)S(1)}, f32[128,128]{1,0:T(8,128)S(1)}, u32[]{:S(2)}, u32[]{:S(2)}) collective-permute-start(f32[128,128]{1,0:T(8,128)S(1)} %get-tuple-element.36), channel_id=1, source_target_pairs={{0,1},{1,0},{2,3},{3,2},{4,7},{5,6},{6,5},{7,4},{8,9},{9,8},{10,11... | collective-permute-start | bytes 196616 | tf_op jit(solution)/shard_map/ppermute | solution.py:33
  19.2 3.6 %collective-permute-start.6 = (f32[8,128]{1,0:T(8,128)S(1)}, f32[8,128]{1,0:T(8,128)S(1)}, u32[]{:S(2)}, u32[]{:S(2)}) collective-permute-start(f32[8,128]{1,0:T(8,128)S(1)} %add_stat.4.one), channel_id=1, source_target_pairs={{0,8},{4,12},{8,0},{12,4},{1,9},{5,13},{9,1},{13,5},{2,10},{6,14},... | collective-permute-start | bytes 12296 | tf_op jit(solution)/shard_map/ppermute | solution.py:18
  22.9 9.6 %collective-permute-start.12 = (f32[136,128]{1,0:T(8,128)S(1)}, f32[136,128]{1,0:T(8,128)S(1)}, u32[]{:S(2)}, u32[]{:S(2)}) collective-permute-start(f32[136,128]{1,0:T(8,128)S(1)} %combine.1.refs_0_), channel_id=1, source_target_pairs={{0,2},{1,3},{2,0},{3,1},{4,5},{5,4},{6,7},{7,6},{8,10},{9,11},{10,... | collective-permute-start | bytes 208904 | tf_op jit(solution)/shard_map/ppermute | solution.py:33
  25.4 7.0 %collective-permute-start.11 = (f32[136,128]{1,0:T(8,128)S(1)}, f32[136,128]{1,0:T(8,128)S(1)}, u32[]{:S(2)}, u32[]{:S(2)}) collective-permute-start(f32[136,128]{1,0:T(8,128)S(1)} %combine.1.refs_0_), channel_id=1, source_target_pairs={{0,3},{1,2},{2,1},{3,0},{4,6},{5,7},{6,4},{7,5},{8,11},{9,10},{10,... | collective-permute-start | bytes 208904 | tf_op jit(solution)/shard_map/ppermute | solution.py:33
  27.1 5.4 %collective-permute-start.10 = (f32[136,128]{1,0:T(8,128)S(1)}, f32[136,128]{1,0:T(8,128)S(1)}, u32[]{:S(2)}, u32[]{:S(2)}) collective-permute-start(f32[136,128]{1,0:T(8,128)S(1)} %combine.1.refs_0_), channel_id=1, source_target_pairs={{0,1},{1,0},{2,3},{3,2},{4,7},{5,6},{6,5},{7,4},{8,9},{9,8},{10,11... | collective-permute-start | bytes 208904 | tf_op jit(solution)/shard_map/ppermute | solution.py:33
  27.1 7.3 %collective-permute-start.14 = (f32[136,128]{1,0:T(8,128)S(1)}, f32[136,128]{1,0:T(8,128)S(1)}, u32[]{:S(2)}, u32[]{:S(2)}) collective-permute-start(f32[136,128]{1,0:T(8,128)S(1)} %combine.1.refs_0_), channel_id=1, source_target_pairs={{0,8},{1,12},{2,10},{3,11},{4,9},{5,13},{6,14},{7,15},{8,0},{9,1},... | collective-permute-start | bytes 208904 | tf_op jit(solution)/shard_map/ppermute | solution.py:33
  29.2 5.3 %collective-permute-start.13 = (f32[136,128]{1,0:T(8,128)S(1)}, f32[136,128]{1,0:T(8,128)S(1)}, u32[]{:S(2)}, u32[]{:S(2)}) collective-permute-start(f32[136,128]{1,0:T(8,128)S(1)} %combine.1.refs_0_), channel_id=1, source_target_pairs={{0,4},{1,5},{2,8},{3,12},{4,0},{5,1},{6,9},{7,13},{8,2},{9,6},{10,... | collective-permute-start | bytes 208904 | tf_op jit(solution)/shard_map/ppermute | solution.py:33
  34.4 1.6 %collective-permute-start.16 = (f32[16,32,128]{2,1,0:T(8,128)S(1)}, f32[16,32,128]{2,1,0:T(8,128)S(1)}, u32[]{:S(2)}, u32[]{:S(2)}) collective-permute-start(f32[16,32,128]{2,1,0:T(8,128)S(1)} %mirror_second.1.mark.mirror), channel_id=1, source_target_pairs={{0,4},{4,0},{8,12},{12,8},{1,5},{5,1},{9,13},{13,9},{2,6},{6,2},{1... | collective-permute-start | bytes 786440 | tf_op jit(solution)/shard_map/ppermute | solution.py:18
  34.6 3.7 %collective-permute-start.15 = (f32[16,32,128]{2,1,0:T(8,128)S(1)}, f32[16,32,128]{2,1,0:T(8,128)S(1)}, u32[]{:S(2)}, u32[]{:S(2)}) collective-permute-start(f32[16,32,128]{2,1,0:T(8,128)S(1)} %held.1), channel_id=1, source_target_pairs={{0,4},{4,0},{8,12},{12,8},{1,5},{5,1},{9,13},{13,9},{2,6},{6,2},{1... | collective-permute-start | bytes 786440 | tf_op jit(solution)/shard_map/ppermute | solution.py:18
  36.0 9.8 %collective-permute-start.20 = (f32[128,128]{1,0:T(8,128)S(1)}, f32[128,128]{1,0:T(8,128)S(1)}, u32[]{:S(2)}, u32[]{:S(2)}) collective-permute-start(f32[128,128]{1,0:T(8,128)S(1)} %get-tuple-element.47), channel_id=1, source_target_pairs={{0,8},{1,9},{2,10},{3,14},{4,12},{5,13},{6,11},{7,15},{8,0},{9,4},... | collective-permute-start | bytes 196616 | tf_op jit(solution)/shard_map/ppermute | solution.py:33
  38.1 7.6 %collective-permute-start.19 = (f32[128,128]{1,0:T(8,128)S(1)}, f32[128,128]{1,0:T(8,128)S(1)}, u32[]{:S(2)}, u32[]{:S(2)}) collective-permute-start(f32[128,128]{1,0:T(8,128)S(1)} %get-tuple-element.40.mark), channel_id=1, source_target_pairs={{0,4},{1,5},{2,8},{3,12},{4,0},{5,1},{6,9},{7,13},{8,2},{9,6},{10,... | collective-permute-start | bytes 196616 | tf_op jit(solution)/shard_map/ppermute | solution.py:33
  40.7 9.5 %collective-permute-start.17 = (f32[136,128]{1,0:T(8,128)S(1)}, f32[136,128]{1,0:T(8,128)S(1)}, u32[]{:S(2)}, u32[]{:S(2)}) collective-permute-start(f32[136,128]{1,0:T(8,128)S(1)} %get-tuple-element.44), channel_id=1, source_target_pairs={{0,2},{1,3},{2,0},{3,1},{4,5},{5,4},{6,7},{7,6},{8,10},{9,11},{10,... | collective-permute-start | bytes 208904 | tf_op jit(solution)/shard_map/ppermute | solution.py:33
  42.2 8.0 %collective-permute-start.18 = (f32[136,128]{1,0:T(8,128)S(1)}, f32[136,128]{1,0:T(8,128)S(1)}, u32[]{:S(2)}, u32[]{:S(2)}) collective-permute-start(f32[136,128]{1,0:T(8,128)S(1)} %get-tuple-element.45), channel_id=1, source_target_pairs={{0,3},{1,2},{2,1},{3,0},{4,6},{5,7},{6,4},{7,5},{8,11},{9,10},{10,... | collective-permute-start | bytes 208904 | tf_op jit(solution)/shard_map/ppermute | solution.py:33
  45.8 5.1 %collective-permute-start.21 = (f32[136,128]{1,0:T(8,128)S(1)}, f32[136,128]{1,0:T(8,128)S(1)}, u32[]{:S(2)}, u32[]{:S(2)}) collective-permute-start(f32[136,128]{1,0:T(8,128)S(1)} %pass_on.1), channel_id=1, source_target_pairs={{0,1},{1,0},{2,3},{3,2},{4,7},{5,6},{6,5},{7,4},{8,9},{9,8},{10,11... | collective-permute-start | bytes 208904 | tf_op jit(solution)/shard_map/ppermute | solution.py:33
  50.9 8.7 %collective-permute-start.26 = (f32[128,128]{1,0:T(8,128)S(1)}, f32[128,128]{1,0:T(8,128)S(1)}, u32[]{:S(2)}, u32[]{:S(2)}) collective-permute-start(f32[128,128]{1,0:T(8,128)S(1)} %get-tuple-element.49.refs_0_), channel_id=1, source_target_pairs={{0,2},{1,3},{2,0},{3,1},{4,5},{5,4},{6,7},{7,6},{8,10},{9,11},{10,... | collective-permute-start | bytes 196616 | tf_op jit(solution)/shard_map/ppermute | solution.py:33
  52.6 7.0 %collective-permute-start.25 = (f32[128,128]{1,0:T(8,128)S(1)}, f32[128,128]{1,0:T(8,128)S(1)}, u32[]{:S(2)}, u32[]{:S(2)}) collective-permute-start(f32[128,128]{1,0:T(8,128)S(1)} %get-tuple-element.49.refs_0_), channel_id=1, source_target_pairs={{0,3},{1,2},{2,1},{3,0},{4,6},{5,7},{6,4},{7,5},{8,11},{9,10},{10,... | collective-permute-start | bytes 196616 | tf_op jit(solution)/shard_map/ppermute | solution.py:33
  54.6 5.6 %collective-permute-start.24 = (f32[128,128]{1,0:T(8,128)S(1)}, f32[128,128]{1,0:T(8,128)S(1)}, u32[]{:S(2)}, u32[]{:S(2)}) collective-permute-start(f32[128,128]{1,0:T(8,128)S(1)} %get-tuple-element.49.refs_0_), channel_id=1, source_target_pairs={{0,1},{1,0},{2,3},{3,2},{4,7},{5,6},{6,5},{7,4},{8,9},{9,8},{10,11... | collective-permute-start | bytes 196616 | tf_op jit(solution)/shard_map/ppermute | solution.py:33
  55.8 3.6 %collective-permute-start.23 = (f32[8,128]{1,0:T(8,128)S(1)}, f32[8,128]{1,0:T(8,128)S(1)}, u32[]{:S(2)}, u32[]{:S(2)}) collective-permute-start(f32[8,128]{1,0:T(8,128)S(1)} %add_stat.6.one), channel_id=1, source_target_pairs={{0,8},{4,12},{8,0},{12,4},{1,9},{5,13},{9,1},{13,5},{2,10},{6,14},... | collective-permute-start | bytes 12296 | tf_op jit(solution)/shard_map/ppermute | solution.py:18
  (7 other events, 41.3 us)

commit v11 on v8

--- a/solution.py
+++ b/solution.py
@@ -37,11 +37,6 @@
     return target
 
 
-def far_source(j, n):
-    back = {far_target(j)(r, c): (r, c) for r in range(n) for c in range(n)}
-    return lambda r, c: back[r, c]
-
-
 def spread_target(b):
     def target(r, c):
         o = r ^ c
@@ -49,6 +44,11 @@
         return r ^ move, c
 
     return target
+
+
+def collect_target(b, n):
+    back = {spread_target(b)(r, c): (r, c) for r in range(n) for c in range(n)}
+    return lambda r, c: back[r, c]
 
 
 def bits(n):
@@ -89,22 +89,23 @@
         total[tile * width + part] += value[:, part * LANES:(part + 1) * LANES]
 
 
-def add_blocks(blocks, slot_rows, slot_cols, live, pairs, total, mirror, ready=None):
+def wide_group(blocks):
+    return 2 * GROUP if blocks.shape[0] % (2 * GROUP) == 0 else GROUP
+
+
+def add_blocks(blocks, slot_rows, slot_cols, live, pairs, total, mirror, group, ready=None):
     read, write, contract = (slot_rows, slot_cols, 0) if mirror else (slot_cols, slot_rows, 1)
 
     def body(step, carry):
         if ready is not None:
             ready(step)
-        values = []
-        for g in range(GROUP):
-            slot = step * GROUP + g
+        for g in range(group):
+            slot = step * group + g
             value = product(pairs[read[0, 0, slot]], blocks[slot], contract)
-            values.append((write[0, 0, slot], jnp.where(slot < live, value, 0.0)))
-        for tile, value in values:
-            accumulate(total, tile, value)
+            accumulate(total, write[0, 0, slot], jnp.where(slot < live, value, 0.0))
         return carry
 
-    lax.fori_loop(0, (live + GROUP - 1) // GROUP, body, 0)
+    lax.fori_loop(0, (live + group - 1) // group, body, 0)
 
 
 def image_part(parts, me, i, per, rhs):
@@ -168,7 +169,7 @@
         load_pair(pairs, tile, right[:, tile * tile_size:(tile + 1) * tile_size])
     for copy in copies:
         copy.wait()
-    add_blocks(blocks, slot_rows, slot_cols, live, pairs, total, True, lambda i: block_copy(i).wait())
+    add_blocks(blocks, slot_rows, slot_cols, live, pairs, total, True, GROUP, lambda i: block_copy(i).wait())
 
 
 def mirror_second_kernel(rows_any, cols_any, count, near, blocks, total, *scratch):
@@ -180,7 +181,7 @@
         load_pair(pairs, tile, near[:, tile * tile_size:(tile + 1) * tile_size])
     for copy in copies:
         copy.wait()
-    add_blocks(blocks, slot_rows, slot_cols, count[0, 0], pairs, total, True)
+    add_blocks(blocks, slot_rows, slot_cols, count[0, 0], pairs, total, True, wide_group(blocks))
 
 
 def finish_direct(total, near, noise, stat, n):
@@ -209,7 +210,7 @@
     total[...] = jnp.zeros_like(total)
     for copy in copies:
         copy.wait()
-    add_blocks(blocks, slot_rows, slot_cols, count[0, 0], pairs, total, False)
+    add_blocks(blocks, slot_rows, slot_cols, count[0, 0], pairs, total, False, wide_group(blocks))
     finish_direct(total, near, noise, stat, n)
 
 
@@ -230,7 +231,7 @@
     total[...] = jnp.zeros_like(total)
     for copy in copies:
         copy.wait()
-    add_blocks(blocks, slot_rows, slot_cols, count[0, 0], pairs, total, False)
+    add_blocks(blocks, slot_rows, slot_cols, count[0, 0], pairs, total, False, wide_group(blocks))
     finish_direct(total, near, noise, stat, n)
 
 
@@ -243,29 +244,30 @@
     out[...] = jnp.where(there != 0, arrived[...], current[...])
 
 
-def split_kernel(n, mirror, twin, mark, *outs):
+def split_kernel(n, mirror, twin, far, near):
     per = mirror.shape[0] // n
-    rhs = mirror.shape[1]
-    row = lax.axis_index("row")
-    for j, out in enumerate(outs):
-        first = (row ^ 2 * j) * per
+    me = lax.axis_index("col")
+    for d in range(n):
+        first = (me ^ d) * per
+        out, start = (near, d * per) if d < 2 else (far, (d - 2) * per)
         for i in range(per):
-            out[i * rhs:(i + 1) * rhs, :] = mirror[first + i] + twin[first + i]
-
-
-def merge_kernel(n, direct, mirror, twin, stat, *outs):
+            out[start + i] = mirror[first + i] + twin[first + i]
+
+
+def merge_kernel(n, ways, direct, mirror, twin, arrived, mark, *outs):
     per = direct.shape[0] // n
     rhs = direct.shape[1]
     me = lax.axis_index("col")
     diagonal = lax.axis_index("row") == me
-    outs[n][...] = stat[...]
-    for d, out in zip([0] + distances(n), outs):
+    for d, out in zip(ways, outs):
         first = (me ^ d) * per
+        start = (d if d < 2 else d - 2) * per
 
         @pl.when(diagonal)
         def _():
             for i in range(per):
-                out[i * rhs:(i + 1) * rhs, :] = direct[first + i] + (mirror[first + i] + twin[first + i])
+                both = mirror[first + i] + twin[first + i]
+                out[i * rhs:(i + 1) * rhs, :] = direct[first + i] + (both + arrived[start + i])
 
         @pl.when(jnp.logical_not(diagonal))
         def _():
@@ -274,16 +276,12 @@
 
 
 def combine_kernel(n, near, noise, stat, *refs):
-    parts, others, chunk = refs[:n], refs[n:-1], refs[-1]
+    parts, chunk = refs[:n], refs[n]
     rhs = near.shape[0]
     data = parts[0].shape[0]
     per = data // rhs
     me = lax.axis_index("col")
-    group = (lax.axis_index("row") ^ me) // 2
-    value = tree_sum(ref[...] for ref in parts)
-    for j, other in enumerate(others):
-        value += jnp.where(group == j, 0.0, other[...])
-    chunk[:data, :] = value
+    chunk[:data, :] = tree_sum(ref[...] for ref in parts)
     chunk[data:, :] = stat[...]
     for k in range(n):
         @pl.when(me == k)
@@ -294,7 +292,7 @@
 
 
 def left_kernel(n, right, far, *refs):
-    parts, others, (left, stat, held) = refs[:n], refs[n:-3], refs[-3:]
+    others, parts, (left, stat, held) = refs[:n // 2], refs[n // 2:-3], refs[-3:]
     rhs, width = right.shape
     data = parts[0].shape[0] - 8
     per = data // rhs
@@ -364,6 +362,8 @@
     field = shape_of(rhs, width)
     total = shape_of(width // LANES, rhs, LANES)
     chunk = shape_of(data, LANES)
+    far_chunks = shape_of((n - 2) * per, rhs, LANES)
+    near_chunks = shape_of(2 * per, rhs, LANES)
     tile = shape_of(8, LANES)
     loaded = shape_of(size, LANES)
 
@@ -382,19 +382,27 @@
     in_hbm = functools.partial(pltpu.with_memory_space_constraint, memory_space=pltpu.HBM)
     kernel_index = index_scratch + [pair, index_sems]
 
-    def gathered(near, mirror, twin, direct, stat):
-        sent = call(functools.partial(split_kernel, n), "split", [vmem] * 3, [chunk] * (n // 2), [],
-                    (mirror, twin, stat))
-        others = [moved(value, n, far_source(j, n)) for j, value in enumerate(sent)]
-        merged = call(functools.partial(merge_kernel, n), "merge", [vmem] * 4, [chunk] * n + [tile], [],
-                      (direct, mirror, twin, stat))
-        parts = [merged[0]] + [shifted(value, "col", d, n) for d, value in zip(distances(n), merged[1:n])]
-        stat = merged[n]
+    def collected(mirror, twin):
+        far, near = call(functools.partial(split_kernel, n), "split", [vmem] * 2, [far_chunks, near_chunks], [],
+                         (mirror, twin))
+        for b in bits(n)[1:]:
+            arrived = [moved(value, n, collect_target(b, n)) for value in (far, near)]
+            if 2 * b < n:
+                far, near = [call(add_kernel, "add_sums", [vmem] * 2, [shape], [], (own, other))[0]
+                             for shape, own, other in zip((far_chunks, near_chunks), (far, near), arrived)]
+        return arrived
+
+    def gathered(near, mirror, twin, others, direct, stat):
+        ways = distances(n)[:-1]
+        sent = call(functools.partial(merge_kernel, n, ways), "merge_far", [vmem] * 5, [chunk] * (n - 2), [],
+                    (direct, mirror, twin, others[0], stat))
+        own, last = call(functools.partial(merge_kernel, n, (0, 1)), "merge_near", [vmem] * 5, [chunk] * 2, [],
+                         (direct, mirror, twin, others[1], stat))
+        parts = [own] + [shifted(value, "col", d, n) for d, value in zip(distances(n), (*sent, last))]
         for b in bits(n):
-            stat, = call(add_kernel, "add_stat", [vmem] * (2 + n // 2), [tile], [],
-                         (stat, shifted(stat, "row", b, n), *others))
-        own, = call(functools.partial(combine_kernel, n), "combine", [vmem] * (3 + n + n // 2), [loaded], [],
-                    (near, noise, stat, *parts, *others))
+            stat, = call(add_kernel, "add_stat", [vmem] * 3, [tile], [], (stat, shifted(stat, "row", b, n), sent[0]))
+        own, = call(functools.partial(combine_kernel, n), "combine", [vmem] * (3 + n), [loaded], [],
+                    (near, noise, stat, *parts))
         return [own] + [shifted(own, "col", d, n) for d in distances(n)]
 
     current = right_sides
@@ -410,23 +418,25 @@
             twin_mirror = shifted(mirror, "row", 1, n)
         current, = call(functools.partial(pick_kernel, b), "pick", [vmem] * 3, [field], [], (current, arrived, mirror))
     twin = shifted(current, "row", 1, n)
+    others = collected(mirror, twin_mirror)
     direct, stat, far = call(
         functools.partial(direct_first_kernel, n), "direct_first", [any_spec] * 2 + [smem] + [vmem] * 5,
         [total, tile, total], kernel_index, (*index, noise, blocks, right_sides, current, twin), True)
-    parts = gathered(right_sides, mirror, twin_mirror, direct, stat)
+    parts = gathered(right_sides, mirror, twin_mirror, others, direct, stat)
     far_parts = [moved(parts[0], n, far_target(j)) for j in range(n // 2)]
 
     left, stat_now, held = call(
         functools.partial(left_kernel, n), "left", [vmem] * (2 + n + n // 2), [field, tile, total], [],
-        (right_sides, far, *parts, *far_parts))
+        (right_sides, far, *far_parts, *parts))
     twin = shifted(held, "row", 1, n)
     mirror, = call(mirror_second_kernel, "mirror_second", [any_spec] * 2 + [smem] + [vmem] * 2,
                    [total], kernel_index, (*index, left, blocks), True)
     twin_mirror = shifted(mirror, "row", 1, n)
+    others = collected(mirror, twin_mirror)
     direct, stat = call(
         functools.partial(direct_second_kernel, n), "direct_second", [any_spec] * 2 + [smem] + [vmem] * 5,
         [total, tile], kernel_index, (*index, noise, blocks, left, held, twin), True)
-    parts = gathered(left, mirror, twin_mirror, direct, stat)
+    parts = gathered(left, mirror, twin_mirror, others, direct, stat)
     return tuple(call(last_kernel, "last", [vmem] * (n + 3), [field, field], [],
                       (right_sides, left, stat_now, *parts)))
 

time: 63.9 us -> 62.2 us (0.973); the launches traced: 63 us -> 62.3 us
  waiting for transfers between devices: 16.8 us -> 26.3 us
  starting transfers between devices: 36.1 us -> 26.9 us
  Pallas kernels: 8.57 us -> 7.58 us
    ppermute x20, waiting for transfers between devices: 13.9 us -> 20.1 us  [shifted(): return lax.ppermute(value, axis, [(i, i ^ d) for i in range(n)])]
    ppermute x7, starting transfers between devices: 15 us -> 8.97 us  [moved(): lax.ppermute(value, ('row', 'col'), [(s, t[0] * n + t[1]) for s, t in pai...]
    ppermute x7, waiting for transfers between devices: 2.97 us -> 6.2 us  [moved(): lax.ppermute(value, ('row', 'col'), [(s, t[0] * n + t[1]) for s, t in pai...]
    ppermute x20, starting transfers between devices: 21.1 us -> 17.9 us  [shifted(): return lax.ppermute(value, axis, [(i, i ^ d) for i in range(n)])]
    pallas_call x17 -> x19, Pallas kernels: 8.57 us -> 7.58 us  [call(): pl.pallas_call(kernel, in_specs=specs, out_specs=jax.tree.map(lambda _: v...]
  transfers between devices with their start and end apart: 27 -> 27, of which waited for: 12 -> 13; matrix products, arithmetic and copies ran while one was open for 0% -> 0% of each run, Pallas kernels for 11% -> 8%
where the time goes in v11:
time: 62.2 us; the launch traced here: 62.3 us
  starting transfers between devices  26.9 us (43%)
  waiting for transfers between devices  26.3 us (42%)
  Pallas kernels  7.58 us (12%)
  between operations  1.52 us (2%)
    ppermute x20, waiting for transfers between devices, shifted(): return lax.ppermute(value, axis, [(i, i ^ d) for i in range(n)])  20.1 us
    ppermute x20, starting transfers between devices, shifted(): return lax.ppermute(value, axis, [(i, i ^ d) for i in range(n)])  17.9 us
    ppermute x7, starting transfers between devices, moved(): lax.ppermute(value, ('row', 'col'), [(s, t[0] * n + t[1]) for s, t in pai...  8.97 us
    pallas_call x19, Pallas kernels, call(): pl.pallas_call(kernel, in_specs=specs, out_specs=jax.tree.map(lambda _: v...  7.58 us
    ppermute x7, waiting for transfers between devices, moved(): lax.ppermute(value, ('row', 'col'), [(s, t[0] * n + t[1]) for s, t in pai...  6.2 us
  transfers between devices with their start and end apart: 27, of which 13 were waited for; matrix products, arithmetic and copies ran while one was open for 0% of the time, Pallas kernels for 8%

profile of v11, /device:TPU:0, one launch (start us, length us, event | category | flops | bytes accessed | tf_op | source)
XLA Modules:
  0.0 62.3 jit_solution(2369636587932548914)
XLA Ops:
  0.7 3.0 %collective-permute-start = (f32[32,2048]{1,0:T(8,128)}, f32[32,2048]{1,0:T(8,128)S(1)}, u32[]{:S(2)}, u32[]{:S(2)}) collective-permute-start(f32[32,2048]{1,0:T(8,128)} %right.3), channel_id=1, source_target_pairs={{0,8},{1,5},{2,6},{3,11},{4,0},{5,13},{6,14},{7,3},{8,12},{9,1},{1... | collective-permute-start | bytes 786440 | tf_op jit(solution)/shard_map/ppermute | solution.py:27
  4.3 1.7 %mirror_first.1 = (f32[16,32,128]{2,1,0:T(8,128)S(1)}, bf16[32,256,256]{2,1,0:T(8,128)(2,1)S(1)}) custom-call(s32[1,1,32]{2,1,0:T(1,128)} %rows_any.5, s32[1,1,32]{2,1,0:T(1,128)} %cols_any.5, s32[1,1]{1,0:T(1,128)S(6)} %copy.8.count, f32[32,2048]{1,0:T(8,128)} %right.3, bf16[1,1,32,256,256]{4,3,2,1,0:T(8,128)(2,1)} %cov.1), custom_call_target="tpu_custom_call" | custom-call | flops 268435456 | bytes 4194304 | tf_op jit(solution)/shard_map/mirror_first/pallas_call | solution.py:371
  6.1 1.8 %collective-permute-done.arrived = f32[32,2048]{1,0:T(8,128)S(1)} collective-permute-done((f32[32,2048]{1,0:T(8,128)}, f32[32,2048]{1,0:T(8,128)S(1)}, u32[]{:S(2)}, u32[]{:S(2)}) %collective-permute-start) | collective-permute-done | bytes 262176 | tf_op jit(solution)/shard_map/ppermute | solution.py:27
  8.6 2.1 %collective-permute-start.6 = (f32[8,32,128]{2,1,0:T(8,128)S(1)}, f32[8,32,128]{2,1,0:T(8,128)S(1)}, u32[]{:S(2)}, u32[]{:S(2)}) collective-permute-start(f32[8,32,128]{2,1,0:T(8,128)S(1)} %get-tuple-element.31), channel_id=1, source_target_pairs={{0,4},{1,9},{2,10},{3,7},{4,12},{5,1},{6,2},{7,15},{8,0},{9,13},{1... | collective-permute-start | bytes 393224 | tf_op jit(solution)/shard_map/ppermute | solution.py:27
  10.7 1.5 %direct_first.1 = (f32[16,32,128]{2,1,0:T(8,128)S(1)}, f32[8,128]{1,0:T(8,128)S(1)}, f32[16,32,128]{2,1,0:T(8,128)S(1)}) custom-call(s32[1,1,32]{2,1,0:T(1,128)S(1)} %copy-done.2, s32[1,1,32]{2,1,0:T(1,128)S(1)} %copy-done.3, s32[1,1]{1,0:T(1,128)S(6)} %copy.8.count, f32[1,2048]{1,0:T(1,128)S(1)} %bitcast.1, ...), custom_call_target="tpu_custom_call" | custom-call | flops 268435456 | bytes 4194304 | tf_op jit(solution)/shard_map/direct_first/pallas_call | solution.py:371
  12.2 1.2 %collective-permute-done.4.arrived = f32[8,32,128]{2,1,0:T(8,128)S(1)} collective-permute-done((f32[8,32,128]{2,1,0:T(8,128)S(1)}, f32[8,32,128]{2,1,0:T(8,128)S(1)}, u32[]{:S(2)}, u32[]{:S(2)}) %collective-permute-start.4) | collective-permute-done | bytes 131104 | tf_op jit(solution)/shard_map/ppermute | solution.py:27
  13.5 1.9 %collective-permute-start.7 = (f32[128,128]{1,0:T(8,128)S(1)}, f32[128,128]{1,0:T(8,128)S(1)}, u32[]{:S(2)}, u32[]{:S(2)}) collective-permute-start(f32[128,128]{1,0:T(8,128)S(1)} %get-tuple-element.30.refs_0_), channel_id=1, source_target_pairs={{0,2},{1,3},{2,0},{3,1},{4,6},{5,7},{6,4},{7,5},{8,10},{9,11},{10,... | collective-permute-start | bytes 196616 | tf_op jit(solution)/shard_map/ppermute | solution.py:18
  15.4 2.6 %collective-permute-start.8 = (f32[128,128]{1,0:T(8,128)S(1)}, f32[128,128]{1,0:T(8,128)S(1)}, u32[]{:S(2)}, u32[]{:S(2)}) collective-permute-start(f32[128,128]{1,0:T(8,128)S(1)} %get-tuple-element.33), channel_id=1, source_target_pairs={{0,3},{1,2},{2,1},{3,0},{4,7},{5,6},{6,5},{7,4},{8,11},{9,10},{10,... | collective-permute-start | bytes 196616 | tf_op jit(solution)/shard_map/ppermute | solution.py:18
  18.6 1.2 %collective-permute-done.2.two = f32[8,128]{1,0:T(8,128)S(1)} collective-permute-done((f32[8,128]{1,0:T(8,128)S(1)}, f32[8,128]{1,0:T(8,128)S(1)}, u32[]{:S(2)}, u32[]{:S(2)}) %collective-permute-start.2) | collective-permute-done | bytes 4128 | tf_op jit(solution)/shard_map/ppermute | solution.py:18
  19.8 3.6 %collective-permute-done.5.two = f32[8,128]{1,0:T(8,128)S(1)} collective-permute-done((f32[8,128]{1,0:T(8,128)S(1)}, f32[8,128]{1,0:T(8,128)S(1)}, u32[]{:S(2)}, u32[]{:S(2)}) %collective-permute-start.5) | collective-permute-done | bytes 4128 | tf_op jit(solution)/shard_map/ppermute | solution.py:18
  23.5 3.0 %collective-permute-start.11 = (f32[136,128]{1,0:T(8,128)S(1)}, f32[136,128]{1,0:T(8,128)S(1)}, u32[]{:S(2)}, u32[]{:S(2)}) collective-permute-start(f32[136,128]{1,0:T(8,128)S(1)} %combine.2.refs_2_), channel_id=1, source_target_pairs={{0,8},{1,12},{2,10},{3,11},{4,9},{5,13},{6,14},{7,15},{8,0},{9,1},... | collective-permute-start | bytes 208904 | tf_op jit(solution)/shard_map/ppermute | solution.py:27
  26.5 4.9 %collective-permute-start.13 = (f32[136,128]{1,0:T(8,128)S(1)}, f32[136,128]{1,0:T(8,128)S(1)}, u32[]{:S(2)}, u32[]{:S(2)}) collective-permute-start(f32[136,128]{1,0:T(8,128)S(1)} %combine.2.refs_2_), channel_id=1, source_target_pairs={{0,3},{1,2},{2,1},{3,0},{4,7},{5,6},{6,5},{7,4},{8,11},{9,10},{10,... | collective-permute-start | bytes 208904 | tf_op jit(solution)/shard_map/ppermute | solution.py:18
  31.5 3.3 %collective-permute-done.12.refs_3_ = f32[136,128]{1,0:T(8,128)S(1)} collective-permute-done((f32[136,128]{1,0:T(8,128)S(1)}, f32[136,128]{1,0:T(8,128)S(1)}, u32[]{:S(2)}, u32[]{:S(2)}) %collective-permute-start.12) | collective-permute-done | bytes 69664 | tf_op jit(solution)/shard_map/ppermute | solution.py:18
  36.1 1.1 %mirror_second.1.mirror = f32[16,32,128]{2,1,0:T(8,128)S(1)} custom-call(s32[1,1,32]{2,1,0:T(1,128)S(1)} %copy-done.2, s32[1,1,32]{2,1,0:T(1,128)S(1)} %copy-done.3, s32[1,1]{1,0:T(1,128)S(6)} %copy.8.count, f32[32,2048]{1,0:T(8,128)S(1)} %get-tuple-element.35.near.left, bf16[32,256,256]{2,1,0:T(8,128)(2,1)S(1)} %get-tuple-element.24.blocks), custom_call_target="tpu_custom_call" | custom-call | flops 268435456 | bytes 4194304 | tf_op jit(solution)/shard_map/mirror_second/pallas_call | solution.py:371
  39.1 1.5 %direct_second.1 = (f32[16,32,128]{2,1,0:T(8,128)S(1)}, f32[8,128]{1,0:T(8,128)S(1)}) custom-call(s32[1,1,32]{2,1,0:T(1,128)S(1)} %copy-done.2, s32[1,1,32]{2,1,0:T(1,128)S(1)} %copy-done.3, s32[1,1]{1,0:T(1,128)S(6)} %copy.8.count, f32[1,2048]{1,0:T(1,128)S(1)} %bitcast.3, bf16[32,256,256]{2,1,0:T(8,128)(2,1)S(1)} %get-tuple-element.24.blocks, ...), custom_call_target="tpu_custom_call" | custom-call | flops 268435456 | bytes 4194304 | tf_op jit(solution)/shard_map/direct_second/pallas_call | solution.py:371
  40.6 3.2 %collective-permute-done.18.arrived = f32[8,32,128]{2,1,0:T(8,128)S(1)} collective-permute-done((f32[8,32,128]{2,1,0:T(8,128)S(1)}, f32[8,32,128]{2,1,0:T(8,128)S(1)}, u32[]{:S(2)}, u32[]{:S(2)}) %collective-permute-start.18) | collective-permute-done | bytes 131104 | tf_op jit(solution)/shard_map/ppermute | solution.py:27
  43.9 2.3 %collective-permute-start.22 = (f32[128,128]{1,0:T(8,128)S(1)}, f32[128,128]{1,0:T(8,128)S(1)}, u32[]{:S(2)}, u32[]{:S(2)}) collective-permute-start(f32[128,128]{1,0:T(8,128)S(1)} %get-tuple-element.44), channel_id=1, source_target_pairs={{0,3},{1,2},{2,1},{3,0},{4,7},{5,6},{6,5},{7,4},{8,11},{9,10},{10,... | collective-permute-start | bytes 196616 | tf_op jit(solution)/shard_map/ppermute | solution.py:18
  46.3 1.2 %collective-permute-start.23 = (f32[128,128]{1,0:T(8,128)S(1)}, f32[128,128]{1,0:T(8,128)S(1)}, u32[]{:S(2)}, u32[]{:S(2)}) collective-permute-start(f32[128,128]{1,0:T(8,128)S(1)} %get-tuple-element.45), channel_id=1, source_target_pairs={{0,1},{1,0},{2,3},{3,2},{4,5},{5,4},{6,7},{7,6},{8,9},{9,8},{10,11... | collective-permute-start | bytes 196616 | tf_op jit(solution)/shard_map/ppermute | solution.py:18
  47.5 1.2 %collective-permute-done.16.two = f32[8,128]{1,0:T(8,128)S(1)} collective-permute-done((f32[8,128]{1,0:T(8,128)S(1)}, f32[8,128]{1,0:T(8,128)S(1)}, u32[]{:S(2)}, u32[]{:S(2)}) %collective-permute-start.16) | collective-permute-done | bytes 4128 | tf_op jit(solution)/shard_map/ppermute | solution.py:18
  48.7 3.6 %collective-permute-done.19.two = f32[8,128]{1,0:T(8,128)S(1)} collective-permute-done((f32[8,128]{1,0:T(8,128)S(1)}, f32[8,128]{1,0:T(8,128)S(1)}, u32[]{:S(2)}, u32[]{:S(2)}) %collective-permute-start.19) | collective-permute-done | bytes 4128 | tf_op jit(solution)/shard_map/ppermute | solution.py:18
  52.4 1.3 %collective-permute-start.24 = (f32[136,128]{1,0:T(8,128)S(1)}, f32[136,128]{1,0:T(8,128)S(1)}, u32[]{:S(2)}, u32[]{:S(2)}) collective-permute-start(f32[136,128]{1,0:T(8,128)S(1)} %combine.3.refs_0_), channel_id=1, source_target_pairs={{0,2},{1,3},{2,0},{3,1},{4,6},{5,7},{6,4},{7,5},{8,10},{9,11},{10,... | collective-permute-start | bytes 208904 | tf_op jit(solution)/shard_map/ppermute | solution.py:18
  53.6 2.1 %collective-permute-start.25 = (f32[136,128]{1,0:T(8,128)S(1)}, f32[136,128]{1,0:T(8,128)S(1)}, u32[]{:S(2)}, u32[]{:S(2)}) collective-permute-start(f32[136,128]{1,0:T(8,128)S(1)} %combine.3.refs_0_), channel_id=1, source_target_pairs={{0,3},{1,2},{2,1},{3,0},{4,7},{5,6},{6,5},{7,4},{8,11},{9,10},{10,... | collective-permute-start | bytes 208904 | tf_op jit(solution)/shard_map/ppermute | solution.py:18
  55.9 4.4 %collective-permute-done.24.refs_1_ = f32[136,128]{1,0:T(8,128)S(1)} collective-permute-done((f32[136,128]{1,0:T(8,128)S(1)}, f32[136,128]{1,0:T(8,128)S(1)}, u32[]{:S(2)}, u32[]{:S(2)}) %collective-permute-start.24) | collective-permute-done | bytes 69664 | tf_op jit(solution)/shard_map/ppermute | solution.py:18
  61.0 1.2 %last.1 = (f32[32,2048]{1,0:T(8,128)}, f32[32,2048]{1,0:T(8,128)}) custom-call(f32[32,2048]{1,0:T(8,128)S(1)} %copy-done, f32[32,2048]{1,0:T(8,128)S(1)} %get-tuple-element.35.near.left, f32[8,128]{1,0:T(8,128)S(1)} %get-tuple-element.36.stat_now, f32[136,128]{1,0:T(8,128)S(1)} %combine.3.refs_0_, f32[136,128]{1,0:T(8,128)S(1)} %collective-permute-done.24.refs_1_, ...), custom_call_target="tpu_custom_call" | custom-call | tf_op jit(solution)/shard_map/last/pallas_call | solution.py:371
  (57 shorter events, 5.9 us)
Async XLA Ops:
  0.7 7.2 %collective-permute-start = (f32[32,2048]{1,0:T(8,128)}, f32[32,2048]{1,0:T(8,128)S(1)}, u32[]{:S(2)}, u32[]{:S(2)}) collective-permute-start(f32[32,2048]{1,0:T(8,128)} %right.3), channel_id=1, source_target_pairs={{0,8},{1,5},{2,6},{3,11},{4,0},{5,13},{6,14},{7,3},{8,12},{9,1},{1... | collective-permute-start | bytes 786440 | tf_op jit(solution)/shard_map/ppermute | solution.py:27
  6.0 2.0 %collective-permute-start.3 = (f32[16,32,128]{2,1,0:T(8,128)S(1)}, f32[16,32,128]{2,1,0:T(8,128)S(1)}, u32[]{:S(2)}, u32[]{:S(2)}) collective-permute-start(f32[16,32,128]{2,1,0:T(8,128)S(1)} %get-tuple-element.25.mark.mirror), channel_id=1, source_target_pairs={{0,4},{4,0},{8,12},{12,8},{1,5},{5,1},{9,13},{13,9},{2,6},{6,2},{1... | collective-permute-start | bytes 786440 | tf_op jit(solution)/shard_map/ppermute | solution.py:18
  7.9 2.8 %collective-permute-start.1 = (f32[32,2048]{1,0:T(8,128)S(1)}, f32[32,2048]{1,0:T(8,128)S(1)}, u32[]{:S(2)}, u32[]{:S(2)}) collective-permute-start(f32[32,2048]{1,0:T(8,128)S(1)} %pick.1.current), channel_id=1, source_target_pairs={{0,4},{4,0},{8,12},{12,8},{1,5},{5,1},{9,13},{13,9},{2,6},{6,2},{1... | collective-permute-start | bytes 786440 | tf_op jit(solution)/shard_map/ppermute | solution.py:18
  8.1 5.4 %collective-permute-start.4 = (f32[8,32,128]{2,1,0:T(8,128)S(1)}, f32[8,32,128]{2,1,0:T(8,128)S(1)}, u32[]{:S(2)}, u32[]{:S(2)}) collective-permute-start(f32[8,32,128]{2,1,0:T(8,128)S(1)} %get-tuple-element.29), channel_id=1, source_target_pairs={{0,4},{1,9},{2,10},{3,7},{4,12},{5,1},{6,2},{7,15},{8,0},{9,13},{1... | collective-permute-start | bytes 393224 | tf_op jit(solution)/shard_map/ppermute | solution.py:27
  8.6 9.4 %collective-permute-start.6 = (f32[8,32,128]{2,1,0:T(8,128)S(1)}, f32[8,32,128]{2,1,0:T(8,128)S(1)}, u32[]{:S(2)}, u32[]{:S(2)}) collective-permute-start(f32[8,32,128]{2,1,0:T(8,128)S(1)} %get-tuple-element.31), channel_id=1, source_target_pairs={{0,4},{1,9},{2,10},{3,7},{4,12},{5,1},{6,2},{7,15},{8,0},{9,13},{1... | collective-permute-start | bytes 393224 | tf_op jit(solution)/shard_map/ppermute | solution.py:27
  13.5 9.9 %collective-permute-start.7 = (f32[128,128]{1,0:T(8,128)S(1)}, f32[128,128]{1,0:T(8,128)S(1)}, u32[]{:S(2)}, u32[]{:S(2)}) collective-permute-start(f32[128,128]{1,0:T(8,128)S(1)} %get-tuple-element.30.refs_0_), channel_id=1, source_target_pairs={{0,2},{1,3},{2,0},{3,1},{4,6},{5,7},{6,4},{7,5},{8,10},{9,11},{10,... | collective-permute-start | bytes 196616 | tf_op jit(solution)/shard_map/ppermute | solution.py:18
  15.4 8.0 %collective-permute-start.8 = (f32[128,128]{1,0:T(8,128)S(1)}, f32[128,128]{1,0:T(8,128)S(1)}, u32[]{:S(2)}, u32[]{:S(2)}) collective-permute-start(f32[128,128]{1,0:T(8,128)S(1)} %get-tuple-element.33), channel_id=1, source_target_pairs={{0,3},{1,2},{2,1},{3,0},{4,7},{5,6},{6,5},{7,4},{8,11},{9,10},{10,... | collective-permute-start | bytes 196616 | tf_op jit(solution)/shard_map/ppermute | solution.py:18
  18.1 5.3 %collective-permute-start.9 = (f32[128,128]{1,0:T(8,128)S(1)}, f32[128,128]{1,0:T(8,128)S(1)}, u32[]{:S(2)}, u32[]{:S(2)}) collective-permute-start(f32[128,128]{1,0:T(8,128)S(1)} %get-tuple-element.34), channel_id=1, source_target_pairs={{0,1},{1,0},{2,3},{3,2},{4,5},{5,4},{6,7},{7,6},{8,9},{9,8},{10,11... | collective-permute-start | bytes 196616 | tf_op jit(solution)/shard_map/ppermute | solution.py:18
  19.8 3.6 %collective-permute-start.5 = (f32[8,128]{1,0:T(8,128)S(1)}, f32[8,128]{1,0:T(8,128)S(1)}, u32[]{:S(2)}, u32[]{:S(2)}) collective-permute-start(f32[8,128]{1,0:T(8,128)S(1)} %add_stat.4.one), channel_id=1, source_target_pairs={{0,8},{4,12},{8,0},{12,4},{1,9},{5,13},{9,1},{13,5},{2,10},{6,14},... | collective-permute-start | bytes 12296 | tf_op jit(solution)/shard_map/ppermute | solution.py:18
  23.5 8.0 %collective-permute-start.10 = (f32[136,128]{1,0:T(8,128)S(1)}, f32[136,128]{1,0:T(8,128)S(1)}, u32[]{:S(2)}, u32[]{:S(2)}) collective-permute-start(f32[136,128]{1,0:T(8,128)S(1)} %combine.2.refs_2_), channel_id=1, source_target_pairs={{0,4},{1,5},{2,8},{3,12},{4,0},{5,1},{6,9},{7,13},{8,2},{9,6},{10,... | collective-permute-start | bytes 208904 | tf_op jit(solution)/shard_map/ppermute | solution.py:27
  23.5 7.9 %collective-permute-start.11 = (f32[136,128]{1,0:T(8,128)S(1)}, f32[136,128]{1,0:T(8,128)S(1)}, u32[]{:S(2)}, u32[]{:S(2)}) collective-permute-start(f32[136,128]{1,0:T(8,128)S(1)} %combine.2.refs_2_), channel_id=1, source_target_pairs={{0,8},{1,12},{2,10},{3,11},{4,9},{5,13},{6,14},{7,15},{8,0},{9,1},... | collective-permute-start | bytes 208904 | tf_op jit(solution)/shard_map/ppermute | solution.py:27
  26.5 8.2 %collective-permute-start.12 = (f32[136,128]{1,0:T(8,128)S(1)}, f32[136,128]{1,0:T(8,128)S(1)}, u32[]{:S(2)}, u32[]{:S(2)}) collective-permute-start(f32[136,128]{1,0:T(8,128)S(1)} %combine.2.refs_2_), channel_id=1, source_target_pairs={{0,2},{1,3},{2,0},{3,1},{4,6},{5,7},{6,4},{7,5},{8,10},{9,11},{10,... | collective-permute-start | bytes 208904 | tf_op jit(solution)/shard_map/ppermute | solution.py:18
  26.5 8.2 %collective-permute-start.13 = (f32[136,128]{1,0:T(8,128)S(1)}, f32[136,128]{1,0:T(8,128)S(1)}, u32[]{:S(2)}, u32[]{:S(2)}) collective-permute-start(f32[136,128]{1,0:T(8,128)S(1)} %combine.2.refs_2_), channel_id=1, source_target_pairs={{0,3},{1,2},{2,1},{3,0},{4,7},{5,6},{6,5},{7,4},{8,11},{9,10},{10,... | collective-permute-start | bytes 208904 | tf_op jit(solution)/shard_map/ppermute | solution.py:18
  31.5 4.3 %collective-permute-start.14 = (f32[136,128]{1,0:T(8,128)S(1)}, f32[136,128]{1,0:T(8,128)S(1)}, u32[]{:S(2)}, u32[]{:S(2)}) collective-permute-start(f32[136,128]{1,0:T(8,128)S(1)} %combine.2.refs_2_), channel_id=1, source_target_pairs={{0,1},{1,0},{2,3},{3,2},{4,5},{5,4},{6,7},{7,6},{8,9},{9,8},{10,11... | collective-permute-start | bytes 208904 | tf_op jit(solution)/shard_map/ppermute | solution.py:18
  37.2 1.9 %collective-permute-start.15 = (f32[16,32,128]{2,1,0:T(8,128)S(1)}, f32[16,32,128]{2,1,0:T(8,128)S(1)}, u32[]{:S(2)}, u32[]{:S(2)}) collective-permute-start(f32[16,32,128]{2,1,0:T(8,128)S(1)} %get-tuple-element.37.held), channel_id=1, source_target_pairs={{0,4},{4,0},{8,12},{12,8},{1,5},{5,1},{9,13},{13,9},{2,6},{6,2},{1... | collective-permute-start | bytes 786440 | tf_op jit(solution)/shard_map/ppermute | solution.py:18
  38.8 5.0 %collective-permute-start.18 = (f32[8,32,128]{2,1,0:T(8,128)S(1)}, f32[8,32,128]{2,1,0:T(8,128)S(1)}, u32[]{:S(2)}, u32[]{:S(2)}) collective-permute-start(f32[8,32,128]{2,1,0:T(8,128)S(1)} %get-tuple-element.40), channel_id=1, source_target_pairs={{0,4},{1,9},{2,10},{3,7},{4,12},{5,1},{6,2},{7,15},{8,0},{9,13},{1... | collective-permute-start | bytes 393224 | tf_op jit(solution)/shard_map/ppermute | solution.py:27
  39.0 7.3 %collective-permute-start.20 = (f32[8,32,128]{2,1,0:T(8,128)S(1)}, f32[8,32,128]{2,1,0:T(8,128)S(1)}, u32[]{:S(2)}, u32[]{:S(2)}) collective-permute-start(f32[8,32,128]{2,1,0:T(8,128)S(1)} %get-tuple-element.42), channel_id=1, source_target_pairs={{0,4},{1,9},{2,10},{3,7},{4,12},{5,1},{6,2},{7,15},{8,0},{9,13},{1... | collective-permute-start | bytes 393224 | tf_op jit(solution)/shard_map/ppermute | solution.py:27
  43.9 8.4 %collective-permute-start.21 = (f32[128,128]{1,0:T(8,128)S(1)}, f32[128,128]{1,0:T(8,128)S(1)}, u32[]{:S(2)}, u32[]{:S(2)}) collective-permute-start(f32[128,128]{1,0:T(8,128)S(1)} %get-tuple-element.41.refs_0_), channel_id=1, source_target_pairs={{0,2},{1,3},{2,0},{3,1},{4,6},{5,7},{6,4},{7,5},{8,10},{9,11},{10,... | collective-permute-start | bytes 196616 | tf_op jit(solution)/shard_map/ppermute | solution.py:18
  43.9 8.4 %collective-permute-start.22 = (f32[128,128]{1,0:T(8,128)S(1)}, f32[128,128]{1,0:T(8,128)S(1)}, u32[]{:S(2)}, u32[]{:S(2)}) collective-permute-start(f32[128,128]{1,0:T(8,128)S(1)} %get-tuple-element.44), channel_id=1, source_target_pairs={{0,3},{1,2},{2,1},{3,0},{4,7},{5,6},{6,5},{7,4},{8,11},{9,10},{10,... | collective-permute-start | bytes 196616 | tf_op jit(solution)/shard_map/ppermute | solution.py:18
  46.3 6.0 %collective-permute-start.23 = (f32[128,128]{1,0:T(8,128)S(1)}, f32[128,128]{1,0:T(8,128)S(1)}, u32[]{:S(2)}, u32[]{:S(2)}) collective-permute-start(f32[128,128]{1,0:T(8,128)S(1)} %get-tuple-element.45), channel_id=1, source_target_pairs={{0,1},{1,0},{2,3},{3,2},{4,5},{5,4},{6,7},{7,6},{8,9},{9,8},{10,11... | collective-permute-start | bytes 196616 | tf_op jit(solution)/shard_map/ppermute | solution.py:18
  48.7 3.6 %collective-permute-start.19 = (f32[8,128]{1,0:T(8,128)S(1)}, f32[8,128]{1,0:T(8,128)S(1)}, u32[]{:S(2)}, u32[]{:S(2)}) collective-permute-start(f32[8,128]{1,0:T(8,128)S(1)} %add_stat.6.one), channel_id=1, source_target_pairs={{0,8},{4,12},{8,0},{12,4},{1,9},{5,13},{9,1},{13,5},{2,10},{6,14},... | collective-permute-start | bytes 12296 | tf_op jit(solution)/shard_map/ppermute | solution.py:18
  52.4 8.0 %collective-permute-start.24 = (f32[136,128]{1,0:T(8,128)S(1)}, f32[136,128]{1,0:T(8,128)S(1)}, u32[]{:S(2)}, u32[]{:S(2)}) collective-permute-start(f32[136,128]{1,0:T(8,128)S(1)} %combine.3.refs_0_), channel_id=1, source_target_pairs={{0,2},{1,3},{2,0},{3,1},{4,6},{5,7},{6,4},{7,5},{8,10},{9,11},{10,... | collective-permute-start | bytes 208904 | tf_op jit(solution)/shard_map/ppermute | solution.py:18
  53.6 6.7 %collective-permute-start.25 = (f32[136,128]{1,0:T(8,128)S(1)}, f32[136,128]{1,0:T(8,128)S(1)}, u32[]{:S(2)}, u32[]{:S(2)}) collective-permute-start(f32[136,128]{1,0:T(8,128)S(1)} %combine.3.refs_0_), channel_id=1, source_target_pairs={{0,3},{1,2},{2,1},{3,0},{4,7},{5,6},{6,5},{7,4},{8,11},{9,10},{10,... | collective-permute-start | bytes 208904 | tf_op jit(solution)/shard_map/ppermute | solution.py:18
  55.7 5.4 %collective-permute-start.26 = (f32[136,128]{1,0:T(8,128)S(1)}, f32[136,128]{1,0:T(8,128)S(1)}, u32[]{:S(2)}, u32[]{:S(2)}) collective-permute-start(f32[136,128]{1,0:T(8,128)S(1)} %combine.3.refs_0_), channel_id=1, source_target_pairs={{0,1},{1,0},{2,3},{3,2},{4,5},{5,4},{6,7},{7,6},{8,9},{9,8},{10,11... | collective-permute-start | bytes 208904 | tf_op jit(solution)/shard_map/ppermute | solution.py:18
  (7 other events, 41.3 us)

commit v12 on v6

--- a/solution.py
+++ b/solution.py
@@ -89,22 +89,27 @@
         total[tile * width + part] += value[:, part * LANES:(part + 1) * LANES]
 
 
-def add_blocks(blocks, slot_rows, slot_cols, live, pairs, total, mirror, ready=None):
+def add_blocks(blocks, slot_rows, slot_cols, live, pairs, total, mirror, wide, ready=None):
     read, write, contract = (slot_rows, slot_cols, 0) if mirror else (slot_cols, slot_rows, 1)
 
-    def body(step, carry):
-        if ready is not None:
-            ready(step)
-        values = []
-        for g in range(GROUP):
-            slot = step * GROUP + g
-            value = product(pairs[read[0, 0, slot]], blocks[slot], contract)
-            values.append((write[0, 0, slot], jnp.where(slot < live, value, 0.0)))
-        for tile, value in values:
-            accumulate(total, tile, value)
-        return carry
-
-    lax.fori_loop(0, (live + GROUP - 1) // GROUP, body, 0)
+    def steps(group, base):
+        def body(step, carry):
+            if ready is not None:
+                ready(step)
+            for g in range(group):
+                slot = base + step * group + g
+                value = product(pairs[read[0, 0, slot]], blocks[slot], contract)
+                accumulate(total, write[0, 0, slot], jnp.where(slot < live, value, 0.0))
+            return carry
+
+        return body
+
+    done = 0
+    if wide > GROUP:
+        count = live // wide
+        lax.fori_loop(0, count, steps(wide, 0), 0)
+        done = count * wide
+    lax.fori_loop(0, (live - done + GROUP - 1) // GROUP, steps(GROUP, done), 0)
 
 
 def image_part(parts, me, i, per, rhs):
@@ -168,7 +173,7 @@
         load_pair(pairs, tile, right[:, tile * tile_size:(tile + 1) * tile_size])
     for copy in copies:
         copy.wait()
-    add_blocks(blocks, slot_rows, slot_cols, live, pairs, total, True, lambda i: block_copy(i).wait())
+    add_blocks(blocks, slot_rows, slot_cols, live, pairs, total, True, GROUP, lambda i: block_copy(i).wait())
 
 
 def mirror_second_kernel(rows_any, cols_any, count, near, blocks, total, *scratch):
@@ -180,7 +185,7 @@
         load_pair(pairs, tile, near[:, tile * tile_size:(tile + 1) * tile_size])
     for copy in copies:
         copy.wait()
-    add_blocks(blocks, slot_rows, slot_cols, count[0, 0], pairs, total, True)
+    add_blocks(blocks, slot_rows, slot_cols, count[0, 0], pairs, total, True, 2 * GROUP)
 
 
 def finish_direct(total, near, noise, stat, n):
@@ -209,7 +214,7 @@
     total[...] = jnp.zeros_like(total)
     for copy in copies:
         copy.wait()
-    add_blocks(blocks, slot_rows, slot_cols, count[0, 0], pairs, total, False)
+    add_blocks(blocks, slot_rows, slot_cols, count[0, 0], pairs, total, False, 2 * GROUP)
     finish_direct(total, near, noise, stat, n)
 
 
@@ -230,7 +235,7 @@
     total[...] = jnp.zeros_like(total)
     for copy in copies:
         copy.wait()
-    add_blocks(blocks, slot_rows, slot_cols, count[0, 0], pairs, total, False)
+    add_blocks(blocks, slot_rows, slot_cols, count[0, 0], pairs, total, False, 2 * GROUP)
     finish_direct(total, near, noise, stat, n)
 
 

time: 61 us -> 60.8 us (level)
  Pallas kernels: 6.89 us -> 8.78 us
  waiting for transfers between devices: 15 us -> 13.5 us
  starting transfers between devices: 36.8 us -> 36.1 us
    pallas_call x18, Pallas kernels: 6.89 us -> 8.78 us  [call(): pl.pallas_call(kernel, in_specs=specs, out_specs=jax.tree.map(lambda _: v...]
    ppermute x20, waiting for transfers between devices: 13.2 us -> 12.3 us  [shifted(): return lax.ppermute(value, axis, [(i, i ^ d) for i in range(n)])]
    ppermute x20, starting transfers between devices: 25.2 us -> 24.5 us  [shifted(): return lax.ppermute(value, axis, [(i, i ^ d) for i in range(n)])]
    ppermute x7, waiting for transfers between devices: 1.78 us -> 1.15 us  [moved(): lax.ppermute(value, ('row', 'col'), [(s, t[0] * n + t[1]) for s, t in pai...]
  transfers between devices with their start and end apart: 27 -> 27, of which waited for: 10 -> 14; matrix products, arithmetic and copies ran while one was open for 0% -> 0% of each run, Pallas kernels for 9% -> 12%
where the time goes in v12:
time: 60.8 us; the launch traced here: 59.9 us
  starting transfers between devices  36.1 us (59%)
  waiting for transfers between devices  13.5 us (22%)
  Pallas kernels  8.78 us (14%)
  between operations  1.49 us (2%)
    ppermute x20, starting transfers between devices, shifted(): return lax.ppermute(value, axis, [(i, i ^ d) for i in range(n)])  24.5 us
    ppermute x20, waiting for transfers between devices, shifted(): return lax.ppermute(value, axis, [(i, i ^ d) for i in range(n)])  12.3 us
    ppermute x7, starting transfers between devices, moved(): lax.ppermute(value, ('row', 'col'), [(s, t[0] * n + t[1]) for s, t in pai...  11.6 us
    pallas_call x18, Pallas kernels, call(): pl.pallas_call(kernel, in_specs=specs, out_specs=jax.tree.map(lambda _: v...  8.78 us
  transfers between devices with their start and end apart: 27, of which 14 were waited for; matrix products, arithmetic and copies ran while one was open for 0% of the time, Pallas kernels for 12%

profile of v12, /device:TPU:0, one launch (start us, length us, event | category | flops | bytes accessed | tf_op | source)
XLA Modules:
  0.0 59.9 jit_solution(5840733688097808664)
XLA Ops:
  0.7 3.0 %collective-permute-start = (f32[32,2048]{1,0:T(8,128)}, f32[32,2048]{1,0:T(8,128)S(1)}, u32[]{:S(2)}, u32[]{:S(2)}) collective-permute-start(f32[32,2048]{1,0:T(8,128)} %right.3), channel_id=1, source_target_pairs={{0,8},{1,5},{2,6},{3,11},{4,0},{5,13},{6,14},{7,3},{8,12},{9,1},{1... | collective-permute-start | bytes 786440 | tf_op jit(solution)/shard_map/ppermute | solution.py:27
  4.3 2.3 %mirror_first.1 = (f32[16,32,128]{2,1,0:T(8,128)S(1)}, bf16[32,256,256]{2,1,0:T(8,128)(2,1)S(1)}) custom-call(s32[1,1,32]{2,1,0:T(1,128)} %rows_any.5, s32[1,1,32]{2,1,0:T(1,128)} %cols_any.5, s32[1,1]{1,0:T(1,128)S(6)} %copy.8.count, f32[32,2048]{1,0:T(8,128)} %right.3, bf16[1,1,32,256,256]{4,3,2,1,0:T(8,128)(2,1)} %cov.1), custom_call_target="tpu_custom_call" | custom-call | flops 268435456 | bytes 4194304 | tf_op jit(solution)/shard_map/mirror_first/pallas_call | solution.py:387
  6.7 1.1 %collective-permute-done.arrived = f32[32,2048]{1,0:T(8,128)S(1)} collective-permute-done((f32[32,2048]{1,0:T(8,128)}, f32[32,2048]{1,0:T(8,128)S(1)}, u32[]{:S(2)}, u32[]{:S(2)}) %collective-permute-start) | collective-permute-done | bytes 262176 | tf_op jit(solution)/shard_map/ppermute | solution.py:27
  8.3 2.2 %collective-permute-start.5 = (f32[128,128]{1,0:T(8,128)S(1)}, f32[128,128]{1,0:T(8,128)S(1)}, u32[]{:S(2)}, u32[]{:S(2)}) collective-permute-start(f32[128,128]{1,0:T(8,128)S(1)} %get-tuple-element.31), channel_id=1, source_target_pairs={{0,8},{1,9},{2,10},{3,14},{4,12},{5,13},{6,11},{7,15},{8,0},{9,4},... | collective-permute-start | bytes 196616 | tf_op jit(solution)/shard_map/ppermute | solution.py:27
  10.7 1.6 %direct_first.1 = (f32[16,32,128]{2,1,0:T(8,128)S(1)}, f32[8,128]{1,0:T(8,128)S(1)}, f32[16,32,128]{2,1,0:T(8,128)S(1)}) custom-call(s32[1,1,32]{2,1,0:T(1,128)S(1)} %copy-done.2, s32[1,1,32]{2,1,0:T(1,128)S(1)} %copy-done.3, s32[1,1]{1,0:T(1,128)S(6)} %copy.8.count, f32[1,2048]{1,0:T(1,128)S(1)} %bitcast.1, ...), custom_call_target="tpu_custom_call" | custom-call | flops 268435456 | bytes 4194304 | tf_op jit(solution)/shard_map/direct_first/pallas_call | solution.py:387
  12.4 1.9 %collective-permute-start.7 = (f32[128,128]{1,0:T(8,128)S(1)}, f32[128,128]{1,0:T(8,128)S(1)}, u32[]{:S(2)}, u32[]{:S(2)}) collective-permute-start(f32[128,128]{1,0:T(8,128)S(1)} %get-tuple-element.33), channel_id=1, source_target_pairs={{0,2},{1,3},{2,0},{3,1},{4,6},{5,7},{6,4},{7,5},{8,10},{9,11},{10,... | collective-permute-start | bytes 196616 | tf_op jit(solution)/shard_map/ppermute | solution.py:18
  14.3 2.6 %collective-permute-start.8 = (f32[128,128]{1,0:T(8,128)S(1)}, f32[128,128]{1,0:T(8,128)S(1)}, u32[]{:S(2)}, u32[]{:S(2)}) collective-permute-start(f32[128,128]{1,0:T(8,128)S(1)} %get-tuple-element.34), channel_id=1, source_target_pairs={{0,3},{1,2},{2,1},{3,0},{4,7},{5,6},{6,5},{7,4},{8,11},{9,10},{10,... | collective-permute-start | bytes 196616 | tf_op jit(solution)/shard_map/ppermute | solution.py:18
  17.4 1.2 %collective-permute-done.3.two = f32[8,128]{1,0:T(8,128)S(1)} collective-permute-done((f32[8,128]{1,0:T(8,128)S(1)}, f32[8,128]{1,0:T(8,128)S(1)}, u32[]{:S(2)}, u32[]{:S(2)}) %collective-permute-start.3) | collective-permute-done | bytes 4128 | tf_op jit(solution)/shard_map/ppermute | solution.py:18
  18.5 2.2 %collective-permute-start.6 = (f32[8,128]{1,0:T(8,128)S(1)}, f32[8,128]{1,0:T(8,128)S(1)}, u32[]{:S(2)}, u32[]{:S(2)}) collective-permute-start(f32[8,128]{1,0:T(8,128)S(1)} %add_stat.4.one), channel_id=1, source_target_pairs={{0,8},{4,12},{8,0},{12,4},{1,9},{5,13},{9,1},{13,5},{2,10},{6,14},... | collective-permute-start | bytes 12296 | tf_op jit(solution)/shard_map/ppermute | solution.py:18
  20.7 1.6 %collective-permute-done.6.two = f32[8,128]{1,0:T(8,128)S(1)} collective-permute-done((f32[8,128]{1,0:T(8,128)S(1)}, f32[8,128]{1,0:T(8,128)S(1)}, u32[]{:S(2)}, u32[]{:S(2)}) %collective-permute-start.6) | collective-permute-done | bytes 4128 | tf_op jit(solution)/shard_map/ppermute | solution.py:18
  22.4 1.6 %collective-permute-start.12 = (f32[136,128]{1,0:T(8,128)S(1)}, f32[136,128]{1,0:T(8,128)S(1)}, u32[]{:S(2)}, u32[]{:S(2)}) collective-permute-start(f32[136,128]{1,0:T(8,128)S(1)} %combine.2.refs_0_), channel_id=1, source_target_pairs={{0,2},{1,3},{2,0},{3,1},{4,6},{5,7},{6,4},{7,5},{8,10},{9,11},{10,... | collective-permute-start | bytes 208904 | tf_op jit(solution)/shard_map/ppermute | solution.py:18
  24.0 2.9 %collective-permute-start.11 = (f32[136,128]{1,0:T(8,128)S(1)}, f32[136,128]{1,0:T(8,128)S(1)}, u32[]{:S(2)}, u32[]{:S(2)}) collective-permute-start(f32[136,128]{1,0:T(8,128)S(1)} %combine.2.refs_0_), channel_id=1, source_target_pairs={{0,3},{1,2},{2,1},{3,0},{4,7},{5,6},{6,5},{7,4},{8,11},{9,10},{10,... | collective-permute-start | bytes 208904 | tf_op jit(solution)/shard_map/ppermute | solution.py:18
  26.8 2.0 %collective-permute-start.14 = (f32[136,128]{1,0:T(8,128)S(1)}, f32[136,128]{1,0:T(8,128)S(1)}, u32[]{:S(2)}, u32[]{:S(2)}) collective-permute-start(f32[136,128]{1,0:T(8,128)S(1)} %combine.2.refs_0_), channel_id=1, source_target_pairs={{0,8},{1,12},{2,10},{3,11},{4,9},{5,13},{6,14},{7,15},{8,0},{9,1},... | collective-permute-start | bytes 208904 | tf_op jit(solution)/shard_map/ppermute | solution.py:27
  28.9 1.6 %collective-permute-start.13 = (f32[136,128]{1,0:T(8,128)S(1)}, f32[136,128]{1,0:T(8,128)S(1)}, u32[]{:S(2)}, u32[]{:S(2)}) collective-permute-start(f32[136,128]{1,0:T(8,128)S(1)} %combine.2.refs_0_), channel_id=1, source_target_pairs={{0,4},{1,5},{2,8},{3,12},{4,0},{5,1},{6,9},{7,13},{8,2},{9,6},{10,... | collective-permute-start | bytes 208904 | tf_op jit(solution)/shard_map/ppermute | solution.py:27
  31.8 1.2 %mirror_second.1.mark.mirror = f32[16,32,128]{2,1,0:T(8,128)S(1)} custom-call(s32[1,1,32]{2,1,0:T(1,128)S(1)} %copy-done.2, s32[1,1,32]{2,1,0:T(1,128)S(1)} %copy-done.3, s32[1,1]{1,0:T(1,128)S(6)} %copy.8.count, f32[32,2048]{1,0:T(8,128)S(1)} %get-tuple-element.36.near.left, bf16[32,256,256]{2,1,0:T(8,128)(2,1)S(1)} %get-tuple-element.25.blocks), custom_call_target="tpu_custom_call" | custom-call | flops 268435456 | bytes 4194304 | tf_op jit(solution)/shard_map/mirror_second/pallas_call | solution.py:387
  34.6 2.6 %collective-permute-start.19 = (f32[128,128]{1,0:T(8,128)S(1)}, f32[128,128]{1,0:T(8,128)S(1)}, u32[]{:S(2)}, u32[]{:S(2)}) collective-permute-start(f32[128,128]{1,0:T(8,128)S(1)} %get-tuple-element.43), channel_id=1, source_target_pairs={{0,8},{1,9},{2,10},{3,14},{4,12},{5,13},{6,11},{7,15},{8,0},{9,4},... | collective-permute-start | bytes 196616 | tf_op jit(solution)/shard_map/ppermute | solution.py:27
  37.3 1.6 %direct_second.1 = (f32[16,32,128]{2,1,0:T(8,128)S(1)}, f32[8,128]{1,0:T(8,128)S(1)}) custom-call(s32[1,1,32]{2,1,0:T(1,128)S(1)} %copy-done.2, s32[1,1,32]{2,1,0:T(1,128)S(1)} %copy-done.3, s32[1,1]{1,0:T(1,128)S(6)} %copy.8.count, f32[1,2048]{1,0:T(1,128)S(1)} %bitcast.3, bf16[32,256,256]{2,1,0:T(8,128)(2,1)S(1)} %get-tuple-element.25.blocks, ...), custom_call_target="tpu_custom_call" | custom-call | flops 268435456 | bytes 4194304 | tf_op jit(solution)/shard_map/direct_second/pallas_call | solution.py:387
  39.1 4.3 %collective-permute-start.21 = (f32[128,128]{1,0:T(8,128)S(1)}, f32[128,128]{1,0:T(8,128)S(1)}, u32[]{:S(2)}, u32[]{:S(2)}) collective-permute-start(f32[128,128]{1,0:T(8,128)S(1)} %get-tuple-element.45), channel_id=1, source_target_pairs={{0,2},{1,3},{2,0},{3,1},{4,6},{5,7},{6,4},{7,5},{8,10},{9,11},{10,... | collective-permute-start | bytes 196616 | tf_op jit(solution)/shard_map/ppermute | solution.py:18
  44.0 3.6 %collective-permute-start.20 = (f32[8,128]{1,0:T(8,128)S(1)}, f32[8,128]{1,0:T(8,128)S(1)}, u32[]{:S(2)}, u32[]{:S(2)}) collective-permute-start(f32[8,128]{1,0:T(8,128)S(1)} %add_stat.6.one), channel_id=1, source_target_pairs={{0,8},{4,12},{8,0},{12,4},{1,9},{5,13},{9,1},{13,5},{2,10},{6,14},... | collective-permute-start | bytes 12296 | tf_op jit(solution)/shard_map/ppermute | solution.py:18
  47.5 1.6 %collective-permute-done.20.two = f32[8,128]{1,0:T(8,128)S(1)} collective-permute-done((f32[8,128]{1,0:T(8,128)S(1)}, f32[8,128]{1,0:T(8,128)S(1)}, u32[]{:S(2)}, u32[]{:S(2)}) %collective-permute-start.20) | collective-permute-done | bytes 4128 | tf_op jit(solution)/shard_map/ppermute | solution.py:18
  49.9 1.7 %collective-permute-start.26 = (f32[136,128]{1,0:T(8,128)S(1)}, f32[136,128]{1,0:T(8,128)S(1)}, u32[]{:S(2)}, u32[]{:S(2)}) collective-permute-start(f32[136,128]{1,0:T(8,128)S(1)} %combine.3.refs_0_), channel_id=1, source_target_pairs={{0,2},{1,3},{2,0},{3,1},{4,6},{5,7},{6,4},{7,5},{8,10},{9,11},{10,... | collective-permute-start | bytes 208904 | tf_op jit(solution)/shard_map/ppermute | solution.py:18
  51.6 2.0 %collective-permute-start.25 = (f32[136,128]{1,0:T(8,128)S(1)}, f32[136,128]{1,0:T(8,128)S(1)}, u32[]{:S(2)}, u32[]{:S(2)}) collective-permute-start(f32[136,128]{1,0:T(8,128)S(1)} %combine.3.refs_0_), channel_id=1, source_target_pairs={{0,3},{1,2},{2,1},{3,0},{4,7},{5,6},{6,5},{7,4},{8,11},{9,10},{10,... | collective-permute-start | bytes 208904 | tf_op jit(solution)/shard_map/ppermute | solution.py:18
  53.7 4.0 %collective-permute-done.26.refs_3_ = f32[136,128]{1,0:T(8,128)S(1)} collective-permute-done((f32[136,128]{1,0:T(8,128)S(1)}, f32[136,128]{1,0:T(8,128)S(1)}, u32[]{:S(2)}, u32[]{:S(2)}) %collective-permute-start.26) | collective-permute-done | bytes 69664 | tf_op jit(solution)/shard_map/ppermute | solution.py:18
  58.7 1.2 %last.1 = (f32[32,2048]{1,0:T(8,128)}, f32[32,2048]{1,0:T(8,128)}) custom-call(f32[32,2048]{1,0:T(8,128)S(1)} %copy-done, f32[32,2048]{1,0:T(8,128)S(1)} %get-tuple-element.36.near.left, f32[8,128]{1,0:T(8,128)S(1)} %get-tuple-element.37.stat.stat_now, f32[136,128]{1,0:T(8,128)S(1)} %combine.3.refs_0_, f32[136,128]{1,0:T(8,128)S(1)} %collective-permute-done.24.refs_1_, ...), custom_call_target="tpu_custom_call" | custom-call | tf_op jit(solution)/shard_map/last/pallas_call | solution.py:387
  (56 shorter events, 6.9 us)
Async XLA Ops:
  0.7 7.2 %collective-permute-start = (f32[32,2048]{1,0:T(8,128)}, f32[32,2048]{1,0:T(8,128)S(1)}, u32[]{:S(2)}, u32[]{:S(2)}) collective-permute-start(f32[32,2048]{1,0:T(8,128)} %right.3), channel_id=1, source_target_pairs={{0,8},{1,5},{2,6},{3,11},{4,0},{5,13},{6,14},{7,3},{8,12},{9,1},{1... | collective-permute-start | bytes 786440 | tf_op jit(solution)/shard_map/ppermute | solution.py:27
  7.9 2.8 %collective-permute-start.1 = (f32[32,2048]{1,0:T(8,128)S(1)}, f32[32,2048]{1,0:T(8,128)S(1)}, u32[]{:S(2)}, u32[]{:S(2)}) collective-permute-start(f32[32,2048]{1,0:T(8,128)S(1)} %pick.1.current), channel_id=1, source_target_pairs={{0,4},{4,0},{8,12},{12,8},{1,5},{5,1},{9,13},{13,9},{2,6},{6,2},{1... | collective-permute-start | bytes 786440 | tf_op jit(solution)/shard_map/ppermute | solution.py:18
  8.3 9.1 %collective-permute-start.5 = (f32[128,128]{1,0:T(8,128)S(1)}, f32[128,128]{1,0:T(8,128)S(1)}, u32[]{:S(2)}, u32[]{:S(2)}) collective-permute-start(f32[128,128]{1,0:T(8,128)S(1)} %get-tuple-element.31), channel_id=1, source_target_pairs={{0,8},{1,9},{2,10},{3,14},{4,12},{5,13},{6,11},{7,15},{8,0},{9,4},... | collective-permute-start | bytes 196616 | tf_op jit(solution)/shard_map/ppermute | solution.py:27
  10.5 6.9 %collective-permute-start.4 = (f32[128,128]{1,0:T(8,128)S(1)}, f32[128,128]{1,0:T(8,128)S(1)}, u32[]{:S(2)}, u32[]{:S(2)}) collective-permute-start(f32[128,128]{1,0:T(8,128)S(1)} %get-tuple-element.27.mark), channel_id=1, source_target_pairs={{0,4},{1,5},{2,8},{3,12},{4,0},{5,1},{6,9},{7,13},{8,2},{9,6},{10,... | collective-permute-start | bytes 196616 | tf_op jit(solution)/shard_map/ppermute | solution.py:27
  12.4 9.9 %collective-permute-start.7 = (f32[128,128]{1,0:T(8,128)S(1)}, f32[128,128]{1,0:T(8,128)S(1)}, u32[]{:S(2)}, u32[]{:S(2)}) collective-permute-start(f32[128,128]{1,0:T(8,128)S(1)} %get-tuple-element.33), channel_id=1, source_target_pairs={{0,2},{1,3},{2,0},{3,1},{4,6},{5,7},{6,4},{7,5},{8,10},{9,11},{10,... | collective-permute-start | bytes 196616 | tf_op jit(solution)/shard_map/ppermute | solution.py:18
  14.3 8.0 %collective-permute-start.8 = (f32[128,128]{1,0:T(8,128)S(1)}, f32[128,128]{1,0:T(8,128)S(1)}, u32[]{:S(2)}, u32[]{:S(2)}) collective-permute-start(f32[128,128]{1,0:T(8,128)S(1)} %get-tuple-element.34), channel_id=1, source_target_pairs={{0,3},{1,2},{2,1},{3,0},{4,7},{5,6},{6,5},{7,4},{8,11},{9,10},{10,... | collective-permute-start | bytes 196616 | tf_op jit(solution)/shard_map/ppermute | solution.py:18
  16.9 5.4 %collective-permute-start.9 = (f32[128,128]{1,0:T(8,128)S(1)}, f32[128,128]{1,0:T(8,128)S(1)}, u32[]{:S(2)}, u32[]{:S(2)}) collective-permute-start(f32[128,128]{1,0:T(8,128)S(1)} %get-tuple-element.35), channel_id=1, source_target_pairs={{0,1},{1,0},{2,3},{3,2},{4,5},{5,4},{6,7},{7,6},{8,9},{9,8},{10,11... | collective-permute-start | bytes 196616 | tf_op jit(solution)/shard_map/ppermute | solution.py:18
  18.5 3.8 %collective-permute-start.6 = (f32[8,128]{1,0:T(8,128)S(1)}, f32[8,128]{1,0:T(8,128)S(1)}, u32[]{:S(2)}, u32[]{:S(2)}) collective-permute-start(f32[8,128]{1,0:T(8,128)S(1)} %add_stat.4.one), channel_id=1, source_target_pairs={{0,8},{4,12},{8,0},{12,4},{1,9},{5,13},{9,1},{13,5},{2,10},{6,14},... | collective-permute-start | bytes 12296 | tf_op jit(solution)/shard_map/ppermute | solution.py:18
  22.4 8.1 %collective-permute-start.12 = (f32[136,128]{1,0:T(8,128)S(1)}, f32[136,128]{1,0:T(8,128)S(1)}, u32[]{:S(2)}, u32[]{:S(2)}) collective-permute-start(f32[136,128]{1,0:T(8,128)S(1)} %combine.2.refs_0_), channel_id=1, source_target_pairs={{0,2},{1,3},{2,0},{3,1},{4,6},{5,7},{6,4},{7,5},{8,10},{9,11},{10,... | collective-permute-start | bytes 208904 | tf_op jit(solution)/shard_map/ppermute | solution.py:18
  24.0 7.2 %collective-permute-start.11 = (f32[136,128]{1,0:T(8,128)S(1)}, f32[136,128]{1,0:T(8,128)S(1)}, u32[]{:S(2)}, u32[]{:S(2)}) collective-permute-start(f32[136,128]{1,0:T(8,128)S(1)} %combine.2.refs_0_), channel_id=1, source_target_pairs={{0,3},{1,2},{2,1},{3,0},{4,7},{5,6},{6,5},{7,4},{8,11},{9,10},{10,... | collective-permute-start | bytes 208904 | tf_op jit(solution)/shard_map/ppermute | solution.py:18
  26.8 4.7 %collective-permute-start.10 = (f32[136,128]{1,0:T(8,128)S(1)}, f32[136,128]{1,0:T(8,128)S(1)}, u32[]{:S(2)}, u32[]{:S(2)}) collective-permute-start(f32[136,128]{1,0:T(8,128)S(1)} %combine.2.refs_0_), channel_id=1, source_target_pairs={{0,1},{1,0},{2,3},{3,2},{4,5},{5,4},{6,7},{7,6},{8,9},{9,8},{10,11... | collective-permute-start | bytes 208904 | tf_op jit(solution)/shard_map/ppermute | solution.py:18
  26.8 6.3 %collective-permute-start.14 = (f32[136,128]{1,0:T(8,128)S(1)}, f32[136,128]{1,0:T(8,128)S(1)}, u32[]{:S(2)}, u32[]{:S(2)}) collective-permute-start(f32[136,128]{1,0:T(8,128)S(1)} %combine.2.refs_0_), channel_id=1, source_target_pairs={{0,8},{1,12},{2,10},{3,11},{4,9},{5,13},{6,14},{7,15},{8,0},{9,1},... | collective-permute-start | bytes 208904 | tf_op jit(solution)/shard_map/ppermute | solution.py:27
  28.9 4.2 %collective-permute-start.13 = (f32[136,128]{1,0:T(8,128)S(1)}, f32[136,128]{1,0:T(8,128)S(1)}, u32[]{:S(2)}, u32[]{:S(2)}) collective-permute-start(f32[136,128]{1,0:T(8,128)S(1)} %combine.2.refs_0_), channel_id=1, source_target_pairs={{0,4},{1,5},{2,8},{3,12},{4,0},{5,1},{6,9},{7,13},{8,2},{9,6},{10,... | collective-permute-start | bytes 208904 | tf_op jit(solution)/shard_map/ppermute | solution.py:27
  33.3 4.0 %collective-permute-start.15 = (f32[16,32,128]{2,1,0:T(8,128)S(1)}, f32[16,32,128]{2,1,0:T(8,128)S(1)}, u32[]{:S(2)}, u32[]{:S(2)}) collective-permute-start(f32[16,32,128]{2,1,0:T(8,128)S(1)} %held.1), channel_id=1, source_target_pairs={{0,4},{4,0},{8,12},{12,8},{1,5},{5,1},{9,13},{13,9},{2,6},{6,2},{1... | collective-permute-start | bytes 786440 | tf_op jit(solution)/shard_map/ppermute | solution.py:18
  34.6 9.3 %collective-permute-start.19 = (f32[128,128]{1,0:T(8,128)S(1)}, f32[128,128]{1,0:T(8,128)S(1)}, u32[]{:S(2)}, u32[]{:S(2)}) collective-permute-start(f32[128,128]{1,0:T(8,128)S(1)} %get-tuple-element.43), channel_id=1, source_target_pairs={{0,8},{1,9},{2,10},{3,14},{4,12},{5,13},{6,11},{7,15},{8,0},{9,4},... | collective-permute-start | bytes 196616 | tf_op jit(solution)/shard_map/ppermute | solution.py:27
  37.3 6.7 %collective-permute-start.18 = (f32[128,128]{1,0:T(8,128)S(1)}, f32[128,128]{1,0:T(8,128)S(1)}, u32[]{:S(2)}, u32[]{:S(2)}) collective-permute-start(f32[128,128]{1,0:T(8,128)S(1)} %get-tuple-element.39.mark), channel_id=1, source_target_pairs={{0,4},{1,5},{2,8},{3,12},{4,0},{5,1},{6,9},{7,13},{8,2},{9,6},{10,... | collective-permute-start | bytes 196616 | tf_op jit(solution)/shard_map/ppermute | solution.py:27
  39.0 4.4 %collective-permute-start.17 = (f32[8,128]{1,0:T(8,128)S(1)}, f32[8,128]{1,0:T(8,128)S(1)}, u32[]{:S(2)}, u32[]{:S(2)}) collective-permute-start(f32[8,128]{1,0:T(8,128)S(1)} %get-tuple-element.42.one), channel_id=1, source_target_pairs={{0,4},{4,0},{8,12},{12,8},{1,5},{5,1},{9,13},{13,9},{2,6},{6,2},{1... | collective-permute-start | bytes 12296 | tf_op jit(solution)/shard_map/ppermute | solution.py:18
  39.1 10.0 %collective-permute-start.21 = (f32[128,128]{1,0:T(8,128)S(1)}, f32[128,128]{1,0:T(8,128)S(1)}, u32[]{:S(2)}, u32[]{:S(2)}) collective-permute-start(f32[128,128]{1,0:T(8,128)S(1)} %get-tuple-element.45), channel_id=1, source_target_pairs={{0,2},{1,3},{2,0},{3,1},{4,6},{5,7},{6,4},{7,5},{8,10},{9,11},{10,... | collective-permute-start | bytes 196616 | tf_op jit(solution)/shard_map/ppermute | solution.py:18
  43.4 6.4 %collective-permute-start.22 = (f32[128,128]{1,0:T(8,128)S(1)}, f32[128,128]{1,0:T(8,128)S(1)}, u32[]{:S(2)}, u32[]{:S(2)}) collective-permute-start(f32[128,128]{1,0:T(8,128)S(1)} %get-tuple-element.46), channel_id=1, source_target_pairs={{0,3},{1,2},{2,1},{3,0},{4,7},{5,6},{6,5},{7,4},{8,11},{9,10},{10,... | collective-permute-start | bytes 196616 | tf_op jit(solution)/shard_map/ppermute | solution.py:18
  43.4 6.5 %collective-permute-start.23 = (f32[128,128]{1,0:T(8,128)S(1)}, f32[128,128]{1,0:T(8,128)S(1)}, u32[]{:S(2)}, u32[]{:S(2)}) collective-permute-start(f32[128,128]{1,0:T(8,128)S(1)} %get-tuple-element.47), channel_id=1, source_target_pairs={{0,1},{1,0},{2,3},{3,2},{4,5},{5,4},{6,7},{7,6},{8,9},{9,8},{10,11... | collective-permute-start | bytes 196616 | tf_op jit(solution)/shard_map/ppermute | solution.py:18
  44.0 5.2 %collective-permute-start.20 = (f32[8,128]{1,0:T(8,128)S(1)}, f32[8,128]{1,0:T(8,128)S(1)}, u32[]{:S(2)}, u32[]{:S(2)}) collective-permute-start(f32[8,128]{1,0:T(8,128)S(1)} %add_stat.6.one), channel_id=1, source_target_pairs={{0,8},{4,12},{8,0},{12,4},{1,9},{5,13},{9,1},{13,5},{2,10},{6,14},... | collective-permute-start | bytes 12296 | tf_op jit(solution)/shard_map/ppermute | solution.py:18
  49.9 7.7 %collective-permute-start.26 = (f32[136,128]{1,0:T(8,128)S(1)}, f32[136,128]{1,0:T(8,128)S(1)}, u32[]{:S(2)}, u32[]{:S(2)}) collective-permute-start(f32[136,128]{1,0:T(8,128)S(1)} %combine.3.refs_0_), channel_id=1, source_target_pairs={{0,2},{1,3},{2,0},{3,1},{4,6},{5,7},{6,4},{7,5},{8,10},{9,11},{10,... | collective-permute-start | bytes 208904 | tf_op jit(solution)/shard_map/ppermute | solution.py:18
  51.6 6.8 %collective-permute-start.25 = (f32[136,128]{1,0:T(8,128)S(1)}, f32[136,128]{1,0:T(8,128)S(1)}, u32[]{:S(2)}, u32[]{:S(2)}) collective-permute-start(f32[136,128]{1,0:T(8,128)S(1)} %combine.3.refs_0_), channel_id=1, source_target_pairs={{0,3},{1,2},{2,1},{3,0},{4,7},{5,6},{6,5},{7,4},{8,11},{9,10},{10,... | collective-permute-start | bytes 208904 | tf_op jit(solution)/shard_map/ppermute | solution.py:18
  53.7 5.0 %collective-permute-start.24 = (f32[136,128]{1,0:T(8,128)S(1)}, f32[136,128]{1,0:T(8,128)S(1)}, u32[]{:S(2)}, u32[]{:S(2)}) collective-permute-start(f32[136,128]{1,0:T(8,128)S(1)} %combine.3.refs_0_), channel_id=1, source_target_pairs={{0,1},{1,0},{2,3},{3,2},{4,5},{5,4},{6,7},{7,6},{8,9},{9,8},{10,11... | collective-permute-start | bytes 208904 | tf_op jit(solution)/shard_map/ppermute | solution.py:18
  (7 other events, 41.7 us)

commit v13 on v12

--- a/solution.py
+++ b/solution.py
@@ -19,7 +19,7 @@
 
 
 def distances(n):
-    return [d for d in range(n) if d > 1] + [1]
+    return list(range(n - 1, 0, -1))
 
 
 def moved(value, n, target):

time: 60.8 us -> 60.9 us (level); the launches traced: 59.9 us -> 60.7 us
  starting transfers between devices: 36.1 us -> 30.6 us
  waiting for transfers between devices: 13.5 us -> 18.4 us
  Pallas kernels: 8.78 us -> 10.2 us
    ppermute x20, waiting for transfers between devices: 12.3 us -> 17.9 us  [shifted(): return lax.ppermute(value, axis, [(i, i ^ d) for i in range(n)])]
    ppermute x7, starting transfers between devices: 11.6 us -> 7.28 us  [moved(): lax.ppermute(value, ('row', 'col'), [(s, t[0] * n + t[1]) for s, t in pai...]
    pallas_call x18, Pallas kernels: 8.78 us -> 10.2 us  [call(): pl.pallas_call(kernel, in_specs=specs, out_specs=jax.tree.map(lambda _: v...]
    ppermute x20, starting transfers between devices: 24.5 us -> 23.3 us  [shifted(): return lax.ppermute(value, axis, [(i, i ^ d) for i in range(n)])]
    ppermute x7, waiting for transfers between devices: 1.15 us -> 0.53 us  [moved(): lax.ppermute(value, ('row', 'col'), [(s, t[0] * n + t[1]) for s, t in pai...]
  transfers between devices with their start and end apart: 27 -> 27, of which waited for: 14 -> 12; matrix products, arithmetic and copies ran while one was open for 0% -> 0% of each run, Pallas kernels for 12% -> 15%
where the time goes in v13:
time: 60.9 us; the launch traced here: 60.7 us
  starting transfers between devices  30.6 us (50%)
  waiting for transfers between devices  18.4 us (30%)
  Pallas kernels  10.2 us (17%)
  between operations  1.48 us (2%)
    ppermute x20, starting transfers between devices, shifted(): return lax.ppermute(value, axis, [(i, i ^ d) for i in range(n)])  23.3 us
    ppermute x20, waiting for transfers between devices, shifted(): return lax.ppermute(value, axis, [(i, i ^ d) for i in range(n)])  17.9 us
    pallas_call x18, Pallas kernels, call(): pl.pallas_call(kernel, in_specs=specs, out_specs=jax.tree.map(lambda _: v...  10.2 us
    ppermute x7, starting transfers between devices, moved(): lax.ppermute(value, ('row', 'col'), [(s, t[0] * n + t[1]) for s, t in pai...  7.28 us
  transfers between devices with their start and end apart: 27, of which 12 were waited for; matrix products, arithmetic and copies ran while one was open for 0% of the time, Pallas kernels for 15%

profile of v13, /device:TPU:0, one launch (start us, length us, event | category | flops | bytes accessed | tf_op | source)
XLA Modules:
  0.0 60.7 jit_solution(622771679995339401)
XLA Ops:
  0.7 3.0 %collective-permute-start = (f32[32,2048]{1,0:T(8,128)}, f32[32,2048]{1,0:T(8,128)S(1)}, u32[]{:S(2)}, u32[]{:S(2)}) collective-permute-start(f32[32,2048]{1,0:T(8,128)} %right.3), channel_id=1, source_target_pairs={{0,8},{1,5},{2,6},{3,11},{4,0},{5,13},{6,14},{7,3},{8,12},{9,1},{1... | collective-permute-start | bytes 786440 | tf_op jit(solution)/shard_map/ppermute | solution.py:27
  4.3 3.0 %mirror_first.1 = (f32[16,32,128]{2,1,0:T(8,128)S(1)}, bf16[32,256,256]{2,1,0:T(8,128)(2,1)S(1)}) custom-call(s32[1,1,32]{2,1,0:T(1,128)} %rows_any.5, s32[1,1,32]{2,1,0:T(1,128)} %cols_any.5, s32[1,1]{1,0:T(1,128)S(6)} %copy.8.count, f32[32,2048]{1,0:T(8,128)} %right.3, bf16[1,1,32,256,256]{4,3,2,1,0:T(8,128)(2,1)} %cov.1), custom_call_target="tpu_custom_call" | custom-call | flops 268435456 | bytes 4194304 | tf_op jit(solution)/shard_map/mirror_first/pallas_call | solution.py:387
  8.9 1.6 %collective-permute-start.5 = (f32[128,128]{1,0:T(8,128)S(1)}, f32[128,128]{1,0:T(8,128)S(1)}, u32[]{:S(2)}, u32[]{:S(2)}) collective-permute-start(f32[128,128]{1,0:T(8,128)S(1)} %get-tuple-element.31), channel_id=1, source_target_pairs={{0,8},{1,9},{2,10},{3,14},{4,12},{5,13},{6,11},{7,15},{8,0},{9,4},... | collective-permute-start | bytes 196616 | tf_op jit(solution)/shard_map/ppermute | solution.py:27
  10.7 1.9 %direct_first.1 = (f32[16,32,128]{2,1,0:T(8,128)S(1)}, f32[8,128]{1,0:T(8,128)S(1)}, f32[16,32,128]{2,1,0:T(8,128)S(1)}) custom-call(s32[1,1,32]{2,1,0:T(1,128)S(1)} %copy-done.2, s32[1,1,32]{2,1,0:T(1,128)S(1)} %copy-done.3, s32[1,1]{1,0:T(1,128)S(6)} %copy.8.count, f32[1,2048]{1,0:T(1,128)S(1)} %bitcast.1, ...), custom_call_target="tpu_custom_call" | custom-call | flops 268435456 | bytes 4194304 | tf_op jit(solution)/shard_map/direct_first/pallas_call | solution.py:387
  12.7 3.9 %collective-permute-start.7 = (f32[128,128]{1,0:T(8,128)S(1)}, f32[128,128]{1,0:T(8,128)S(1)}, u32[]{:S(2)}, u32[]{:S(2)}) collective-permute-start(f32[128,128]{1,0:T(8,128)S(1)} %get-tuple-element.33), channel_id=1, source_target_pairs={{0,3},{1,2},{2,1},{3,0},{4,7},{5,6},{6,5},{7,4},{8,11},{9,10},{10,... | collective-permute-start | bytes 196616 | tf_op jit(solution)/shard_map/ppermute | solution.py:18
  17.3 1.2 %collective-permute-done.3.two = f32[8,128]{1,0:T(8,128)S(1)} collective-permute-done((f32[8,128]{1,0:T(8,128)S(1)}, f32[8,128]{1,0:T(8,128)S(1)}, u32[]{:S(2)}, u32[]{:S(2)}) %collective-permute-start.3) | collective-permute-done | bytes 4128 | tf_op jit(solution)/shard_map/ppermute | solution.py:18
  18.5 2.7 %collective-permute-start.6 = (f32[8,128]{1,0:T(8,128)S(1)}, f32[8,128]{1,0:T(8,128)S(1)}, u32[]{:S(2)}, u32[]{:S(2)}) collective-permute-start(f32[8,128]{1,0:T(8,128)S(1)} %add_stat.4.one), channel_id=1, source_target_pairs={{0,8},{4,12},{8,0},{12,4},{1,9},{5,13},{9,1},{13,5},{2,10},{6,14},... | collective-permute-start | bytes 12296 | tf_op jit(solution)/shard_map/ppermute | solution.py:18
  21.2 1.6 %collective-permute-done.6.two = f32[8,128]{1,0:T(8,128)S(1)} collective-permute-done((f32[8,128]{1,0:T(8,128)S(1)}, f32[8,128]{1,0:T(8,128)S(1)}, u32[]{:S(2)}, u32[]{:S(2)}) %collective-permute-start.6) | collective-permute-done | bytes 4128 | tf_op jit(solution)/shard_map/ppermute | solution.py:18
  23.2 2.8 %collective-permute-start.12 = (f32[136,128]{1,0:T(8,128)S(1)}, f32[136,128]{1,0:T(8,128)S(1)}, u32[]{:S(2)}, u32[]{:S(2)}) collective-permute-start(f32[136,128]{1,0:T(8,128)S(1)} %combine.2.refs_0_), channel_id=1, source_target_pairs={{0,3},{1,2},{2,1},{3,0},{4,7},{5,6},{6,5},{7,4},{8,11},{9,10},{10,... | collective-permute-start | bytes 208904 | tf_op jit(solution)/shard_map/ppermute | solution.py:18
  26.0 1.7 %collective-permute-start.10 = (f32[136,128]{1,0:T(8,128)S(1)}, f32[136,128]{1,0:T(8,128)S(1)}, u32[]{:S(2)}, u32[]{:S(2)}) collective-permute-start(f32[136,128]{1,0:T(8,128)S(1)} %combine.2.refs_0_), channel_id=1, source_target_pairs={{0,1},{1,0},{2,3},{3,2},{4,5},{5,4},{6,7},{7,6},{8,9},{9,8},{10,11... | collective-permute-start | bytes 208904 | tf_op jit(solution)/shard_map/ppermute | solution.py:18
  27.7 2.0 %collective-permute-start.14 = (f32[136,128]{1,0:T(8,128)S(1)}, f32[136,128]{1,0:T(8,128)S(1)}, u32[]{:S(2)}, u32[]{:S(2)}) collective-permute-start(f32[136,128]{1,0:T(8,128)S(1)} %combine.2.refs_0_), channel_id=1, source_target_pairs={{0,8},{1,12},{2,10},{3,11},{4,9},{5,13},{6,14},{7,15},{8,0},{9,1},... | collective-permute-start | bytes 208904 | tf_op jit(solution)/shard_map/ppermute | solution.py:27
  30.2 4.3 %collective-permute-done.11.refs_2_ = f32[136,128]{1,0:T(8,128)S(1)} collective-permute-done((f32[136,128]{1,0:T(8,128)S(1)}, f32[136,128]{1,0:T(8,128)S(1)}, u32[]{:S(2)}, u32[]{:S(2)}) %collective-permute-start.11) | collective-permute-done | bytes 69664 | tf_op jit(solution)/shard_map/ppermute | solution.py:18
  34.7 1.4 %mirror_second.1.mark.mirror = f32[16,32,128]{2,1,0:T(8,128)S(1)} custom-call(s32[1,1,32]{2,1,0:T(1,128)S(1)} %copy-done.2, s32[1,1,32]{2,1,0:T(1,128)S(1)} %copy-done.3, s32[1,1]{1,0:T(1,128)S(6)} %copy.8.count, f32[32,2048]{1,0:T(8,128)S(1)} %get-tuple-element.36.near.left, bf16[32,256,256]{2,1,0:T(8,128)(2,1)S(1)} %get-tuple-element.25.blocks), custom_call_target="tpu_custom_call" | custom-call | flops 268435456 | bytes 4194304 | tf_op jit(solution)/shard_map/mirror_second/pallas_call | solution.py:387
  38.2 1.9 %direct_second.1 = (f32[16,32,128]{2,1,0:T(8,128)S(1)}, f32[8,128]{1,0:T(8,128)S(1)}) custom-call(s32[1,1,32]{2,1,0:T(1,128)S(1)} %copy-done.2, s32[1,1,32]{2,1,0:T(1,128)S(1)} %copy-done.3, s32[1,1]{1,0:T(1,128)S(6)} %copy.8.count, f32[1,2048]{1,0:T(1,128)S(1)} %bitcast.3, bf16[32,256,256]{2,1,0:T(8,128)(2,1)S(1)} %get-tuple-element.25.blocks, ...), custom_call_target="tpu_custom_call" | custom-call | flops 268435456 | bytes 4194304 | tf_op jit(solution)/shard_map/direct_second/pallas_call | solution.py:387
  40.5 2.5 %collective-permute-start.21 = (f32[128,128]{1,0:T(8,128)S(1)}, f32[128,128]{1,0:T(8,128)S(1)}, u32[]{:S(2)}, u32[]{:S(2)}) collective-permute-start(f32[128,128]{1,0:T(8,128)S(1)} %get-tuple-element.45), channel_id=1, source_target_pairs={{0,3},{1,2},{2,1},{3,0},{4,7},{5,6},{6,5},{7,4},{8,11},{9,10},{10,... | collective-permute-start | bytes 196616 | tf_op jit(solution)/shard_map/ppermute | solution.py:18
  43.0 1.1 %collective-permute-start.22 = (f32[128,128]{1,0:T(8,128)S(1)}, f32[128,128]{1,0:T(8,128)S(1)}, u32[]{:S(2)}, u32[]{:S(2)}) collective-permute-start(f32[128,128]{1,0:T(8,128)S(1)} %get-tuple-element.46), channel_id=1, source_target_pairs={{0,2},{1,3},{2,0},{3,1},{4,6},{5,7},{6,4},{7,5},{8,10},{9,11},{10,... | collective-permute-start | bytes 196616 | tf_op jit(solution)/shard_map/ppermute | solution.py:18
  44.9 1.9 %collective-permute-start.20 = (f32[8,128]{1,0:T(8,128)S(1)}, f32[8,128]{1,0:T(8,128)S(1)}, u32[]{:S(2)}, u32[]{:S(2)}) collective-permute-start(f32[8,128]{1,0:T(8,128)S(1)} %add_stat.6.one), channel_id=1, source_target_pairs={{0,8},{4,12},{8,0},{12,4},{1,9},{5,13},{9,1},{13,5},{2,10},{6,14},... | collective-permute-start | bytes 12296 | tf_op jit(solution)/shard_map/ppermute | solution.py:18
  46.8 1.8 %collective-permute-done.20.two = f32[8,128]{1,0:T(8,128)S(1)} collective-permute-done((f32[8,128]{1,0:T(8,128)S(1)}, f32[8,128]{1,0:T(8,128)S(1)}, u32[]{:S(2)}, u32[]{:S(2)}) %collective-permute-start.20) | collective-permute-done | bytes 4128 | tf_op jit(solution)/shard_map/ppermute | solution.py:18
  48.6 2.1 %collective-permute-done.22.refs_2_ = f32[128,128]{1,0:T(8,128)S(1)} collective-permute-done((f32[128,128]{1,0:T(8,128)S(1)}, f32[128,128]{1,0:T(8,128)S(1)}, u32[]{:S(2)}, u32[]{:S(2)}) %collective-permute-start.22) | collective-permute-done | bytes 65568 | tf_op jit(solution)/shard_map/ppermute | solution.py:18
  50.7 2.7 %collective-permute-start.26 = (f32[136,128]{1,0:T(8,128)S(1)}, f32[136,128]{1,0:T(8,128)S(1)}, u32[]{:S(2)}, u32[]{:S(2)}) collective-permute-start(f32[136,128]{1,0:T(8,128)S(1)} %combine.3.refs_0_), channel_id=1, source_target_pairs={{0,3},{1,2},{2,1},{3,0},{4,7},{5,6},{6,5},{7,4},{8,11},{9,10},{10,... | collective-permute-start | bytes 208904 | tf_op jit(solution)/shard_map/ppermute | solution.py:18
  53.4 1.7 %collective-permute-start.24 = (f32[136,128]{1,0:T(8,128)S(1)}, f32[136,128]{1,0:T(8,128)S(1)}, u32[]{:S(2)}, u32[]{:S(2)}) collective-permute-start(f32[136,128]{1,0:T(8,128)S(1)} %combine.3.refs_0_), channel_id=1, source_target_pairs={{0,1},{1,0},{2,3},{3,2},{4,5},{5,4},{6,7},{7,6},{8,9},{9,8},{10,11... | collective-permute-start | bytes 208904 | tf_op jit(solution)/shard_map/ppermute | solution.py:18
  55.2 2.2 %collective-permute-done.26.refs_3_ = f32[136,128]{1,0:T(8,128)S(1)} collective-permute-done((f32[136,128]{1,0:T(8,128)S(1)}, f32[136,128]{1,0:T(8,128)S(1)}, u32[]{:S(2)}, u32[]{:S(2)}) %collective-permute-start.26) | collective-permute-done | bytes 69664 | tf_op jit(solution)/shard_map/ppermute | solution.py:18
  57.3 2.1 %collective-permute-done.25.refs_2_ = f32[136,128]{1,0:T(8,128)S(1)} collective-permute-done((f32[136,128]{1,0:T(8,128)S(1)}, f32[136,128]{1,0:T(8,128)S(1)}, u32[]{:S(2)}, u32[]{:S(2)}) %collective-permute-start.25) | collective-permute-done | bytes 69664 | tf_op jit(solution)/shard_map/ppermute | solution.py:18
  59.5 1.2 %last.1 = (f32[32,2048]{1,0:T(8,128)}, f32[32,2048]{1,0:T(8,128)}) custom-call(f32[32,2048]{1,0:T(8,128)S(1)} %copy-done, f32[32,2048]{1,0:T(8,128)S(1)} %get-tuple-element.36.near.left, f32[8,128]{1,0:T(8,128)S(1)} %get-tuple-element.37.stat.stat_now, f32[136,128]{1,0:T(8,128)S(1)} %combine.3.refs_0_, f32[136,128]{1,0:T(8,128)S(1)} %collective-permute-done.24.refs_1_, ...), custom_call_target="tpu_custom_call" | custom-call | tf_op jit(solution)/shard_map/last/pallas_call | solution.py:387
  (56 shorter events, 7.0 us)
Async XLA Ops:
  0.7 7.2 %collective-permute-start = (f32[32,2048]{1,0:T(8,128)}, f32[32,2048]{1,0:T(8,128)S(1)}, u32[]{:S(2)}, u32[]{:S(2)}) collective-permute-start(f32[32,2048]{1,0:T(8,128)} %right.3), channel_id=1, source_target_pairs={{0,8},{1,5},{2,6},{3,11},{4,0},{5,13},{6,14},{7,3},{8,12},{9,1},{1... | collective-permute-start | bytes 786440 | tf_op jit(solution)/shard_map/ppermute | solution.py:27
  7.9 2.8 %collective-permute-start.1 = (f32[32,2048]{1,0:T(8,128)S(1)}, f32[32,2048]{1,0:T(8,128)S(1)}, u32[]{:S(2)}, u32[]{:S(2)}) collective-permute-start(f32[32,2048]{1,0:T(8,128)S(1)} %pick.1.current), channel_id=1, source_target_pairs={{0,4},{4,0},{8,12},{12,8},{1,5},{5,1},{9,13},{13,9},{2,6},{6,2},{1... | collective-permute-start | bytes 786440 | tf_op jit(solution)/shard_map/ppermute | solution.py:18
  8.9 8.4 %collective-permute-start.5 = (f32[128,128]{1,0:T(8,128)S(1)}, f32[128,128]{1,0:T(8,128)S(1)}, u32[]{:S(2)}, u32[]{:S(2)}) collective-permute-start(f32[128,128]{1,0:T(8,128)S(1)} %get-tuple-element.31), channel_id=1, source_target_pairs={{0,8},{1,9},{2,10},{3,14},{4,12},{5,13},{6,11},{7,15},{8,0},{9,4},... | collective-permute-start | bytes 196616 | tf_op jit(solution)/shard_map/ppermute | solution.py:27
  10.5 6.8 %collective-permute-start.4 = (f32[128,128]{1,0:T(8,128)S(1)}, f32[128,128]{1,0:T(8,128)S(1)}, u32[]{:S(2)}, u32[]{:S(2)}) collective-permute-start(f32[128,128]{1,0:T(8,128)S(1)} %get-tuple-element.27.mark), channel_id=1, source_target_pairs={{0,4},{1,5},{2,8},{3,12},{4,0},{5,1},{6,9},{7,13},{8,2},{9,6},{10,... | collective-permute-start | bytes 196616 | tf_op jit(solution)/shard_map/ppermute | solution.py:27
  12.7 10.0 %collective-permute-start.7 = (f32[128,128]{1,0:T(8,128)S(1)}, f32[128,128]{1,0:T(8,128)S(1)}, u32[]{:S(2)}, u32[]{:S(2)}) collective-permute-start(f32[128,128]{1,0:T(8,128)S(1)} %get-tuple-element.33), channel_id=1, source_target_pairs={{0,3},{1,2},{2,1},{3,0},{4,7},{5,6},{6,5},{7,4},{8,11},{9,10},{10,... | collective-permute-start | bytes 196616 | tf_op jit(solution)/shard_map/ppermute | solution.py:18
  16.7 6.5 %collective-permute-start.8 = (f32[128,128]{1,0:T(8,128)S(1)}, f32[128,128]{1,0:T(8,128)S(1)}, u32[]{:S(2)}, u32[]{:S(2)}) collective-permute-start(f32[128,128]{1,0:T(8,128)S(1)} %get-tuple-element.34), channel_id=1, source_target_pairs={{0,2},{1,3},{2,0},{3,1},{4,6},{5,7},{6,4},{7,5},{8,10},{9,11},{10,... | collective-permute-start | bytes 196616 | tf_op jit(solution)/shard_map/ppermute | solution.py:18
  16.7 6.5 %collective-permute-start.9 = (f32[128,128]{1,0:T(8,128)S(1)}, f32[128,128]{1,0:T(8,128)S(1)}, u32[]{:S(2)}, u32[]{:S(2)}) collective-permute-start(f32[128,128]{1,0:T(8,128)S(1)} %get-tuple-element.35), channel_id=1, source_target_pairs={{0,1},{1,0},{2,3},{3,2},{4,5},{5,4},{6,7},{7,6},{8,9},{9,8},{10,11... | collective-permute-start | bytes 196616 | tf_op jit(solution)/shard_map/ppermute | solution.py:18
  18.5 4.3 %collective-permute-start.6 = (f32[8,128]{1,0:T(8,128)S(1)}, f32[8,128]{1,0:T(8,128)S(1)}, u32[]{:S(2)}, u32[]{:S(2)}) collective-permute-start(f32[8,128]{1,0:T(8,128)S(1)} %add_stat.4.one), channel_id=1, source_target_pairs={{0,8},{4,12},{8,0},{12,4},{1,9},{5,13},{9,1},{13,5},{2,10},{6,14},... | collective-permute-start | bytes 12296 | tf_op jit(solution)/shard_map/ppermute | solution.py:18
  23.2 7.0 %collective-permute-start.12 = (f32[136,128]{1,0:T(8,128)S(1)}, f32[136,128]{1,0:T(8,128)S(1)}, u32[]{:S(2)}, u32[]{:S(2)}) collective-permute-start(f32[136,128]{1,0:T(8,128)S(1)} %combine.2.refs_0_), channel_id=1, source_target_pairs={{0,3},{1,2},{2,1},{3,0},{4,7},{5,6},{6,5},{7,4},{8,11},{9,10},{10,... | collective-permute-start | bytes 208904 | tf_op jit(solution)/shard_map/ppermute | solution.py:18
  26.0 8.5 %collective-permute-start.11 = (f32[136,128]{1,0:T(8,128)S(1)}, f32[136,128]{1,0:T(8,128)S(1)}, u32[]{:S(2)}, u32[]{:S(2)}) collective-permute-start(f32[136,128]{1,0:T(8,128)S(1)} %combine.2.refs_0_), channel_id=1, source_target_pairs={{0,2},{1,3},{2,0},{3,1},{4,6},{5,7},{6,4},{7,5},{8,10},{9,11},{10,... | collective-permute-start | bytes 208904 | tf_op jit(solution)/shard_map/ppermute | solution.py:18
  26.0 8.5 %collective-permute-start.10 = (f32[136,128]{1,0:T(8,128)S(1)}, f32[136,128]{1,0:T(8,128)S(1)}, u32[]{:S(2)}, u32[]{:S(2)}) collective-permute-start(f32[136,128]{1,0:T(8,128)S(1)} %combine.2.refs_0_), channel_id=1, source_target_pairs={{0,1},{1,0},{2,3},{3,2},{4,5},{5,4},{6,7},{7,6},{8,9},{9,8},{10,11... | collective-permute-start | bytes 208904 | tf_op jit(solution)/shard_map/ppermute | solution.py:18
  27.7 8.5 %collective-permute-start.14 = (f32[136,128]{1,0:T(8,128)S(1)}, f32[136,128]{1,0:T(8,128)S(1)}, u32[]{:S(2)}, u32[]{:S(2)}) collective-permute-start(f32[136,128]{1,0:T(8,128)S(1)} %combine.2.refs_0_), channel_id=1, source_target_pairs={{0,8},{1,12},{2,10},{3,11},{4,9},{5,13},{6,14},{7,15},{8,0},{9,1},... | collective-permute-start | bytes 208904 | tf_op jit(solution)/shard_map/ppermute | solution.py:27
  29.7 6.5 %collective-permute-start.13 = (f32[136,128]{1,0:T(8,128)S(1)}, f32[136,128]{1,0:T(8,128)S(1)}, u32[]{:S(2)}, u32[]{:S(2)}) collective-permute-start(f32[136,128]{1,0:T(8,128)S(1)} %combine.2.refs_0_), channel_id=1, source_target_pairs={{0,4},{1,5},{2,8},{3,12},{4,0},{5,1},{6,9},{7,13},{8,2},{9,6},{10,... | collective-permute-start | bytes 208904 | tf_op jit(solution)/shard_map/ppermute | solution.py:27
  36.4 1.9 %collective-permute-start.15 = (f32[16,32,128]{2,1,0:T(8,128)S(1)}, f32[16,32,128]{2,1,0:T(8,128)S(1)}, u32[]{:S(2)}, u32[]{:S(2)}) collective-permute-start(f32[16,32,128]{2,1,0:T(8,128)S(1)} %held.1), channel_id=1, source_target_pairs={{0,4},{4,0},{8,12},{12,8},{1,5},{5,1},{9,13},{13,9},{2,6},{6,2},{1... | collective-permute-start | bytes 786440 | tf_op jit(solution)/shard_map/ppermute | solution.py:18
  37.7 7.2 %collective-permute-start.19 = (f32[128,128]{1,0:T(8,128)S(1)}, f32[128,128]{1,0:T(8,128)S(1)}, u32[]{:S(2)}, u32[]{:S(2)}) collective-permute-start(f32[128,128]{1,0:T(8,128)S(1)} %get-tuple-element.43), channel_id=1, source_target_pairs={{0,8},{1,9},{2,10},{3,14},{4,12},{5,13},{6,11},{7,15},{8,0},{9,4},... | collective-permute-start | bytes 196616 | tf_op jit(solution)/shard_map/ppermute | solution.py:27
  38.2 6.7 %collective-permute-start.18 = (f32[128,128]{1,0:T(8,128)S(1)}, f32[128,128]{1,0:T(8,128)S(1)}, u32[]{:S(2)}, u32[]{:S(2)}) collective-permute-start(f32[128,128]{1,0:T(8,128)S(1)} %get-tuple-element.39.mark), channel_id=1, source_target_pairs={{0,4},{1,5},{2,8},{3,12},{4,0},{5,1},{6,9},{7,13},{8,2},{9,6},{10,... | collective-permute-start | bytes 196616 | tf_op jit(solution)/shard_map/ppermute | solution.py:27
  40.3 3.9 %collective-permute-start.17 = (f32[8,128]{1,0:T(8,128)S(1)}, f32[8,128]{1,0:T(8,128)S(1)}, u32[]{:S(2)}, u32[]{:S(2)}) collective-permute-start(f32[8,128]{1,0:T(8,128)S(1)} %get-tuple-element.42.one), channel_id=1, source_target_pairs={{0,4},{4,0},{8,12},{12,8},{1,5},{5,1},{9,13},{13,9},{2,6},{6,2},{1... | collective-permute-start | bytes 12296 | tf_op jit(solution)/shard_map/ppermute | solution.py:18
  40.5 8.1 %collective-permute-start.21 = (f32[128,128]{1,0:T(8,128)S(1)}, f32[128,128]{1,0:T(8,128)S(1)}, u32[]{:S(2)}, u32[]{:S(2)}) collective-permute-start(f32[128,128]{1,0:T(8,128)S(1)} %get-tuple-element.45), channel_id=1, source_target_pairs={{0,3},{1,2},{2,1},{3,0},{4,7},{5,6},{6,5},{7,4},{8,11},{9,10},{10,... | collective-permute-start | bytes 196616 | tf_op jit(solution)/shard_map/ppermute | solution.py:18
  43.0 7.7 %collective-permute-start.22 = (f32[128,128]{1,0:T(8,128)S(1)}, f32[128,128]{1,0:T(8,128)S(1)}, u32[]{:S(2)}, u32[]{:S(2)}) collective-permute-start(f32[128,128]{1,0:T(8,128)S(1)} %get-tuple-element.46), channel_id=1, source_target_pairs={{0,2},{1,3},{2,0},{3,1},{4,6},{5,7},{6,4},{7,5},{8,10},{9,11},{10,... | collective-permute-start | bytes 196616 | tf_op jit(solution)/shard_map/ppermute | solution.py:18
  44.1 6.5 %collective-permute-start.23 = (f32[128,128]{1,0:T(8,128)S(1)}, f32[128,128]{1,0:T(8,128)S(1)}, u32[]{:S(2)}, u32[]{:S(2)}) collective-permute-start(f32[128,128]{1,0:T(8,128)S(1)} %get-tuple-element.47), channel_id=1, source_target_pairs={{0,1},{1,0},{2,3},{3,2},{4,5},{5,4},{6,7},{7,6},{8,9},{9,8},{10,11... | collective-permute-start | bytes 196616 | tf_op jit(solution)/shard_map/ppermute | solution.py:18
  44.9 3.7 %collective-permute-start.20 = (f32[8,128]{1,0:T(8,128)S(1)}, f32[8,128]{1,0:T(8,128)S(1)}, u32[]{:S(2)}, u32[]{:S(2)}) collective-permute-start(f32[8,128]{1,0:T(8,128)S(1)} %add_stat.6.one), channel_id=1, source_target_pairs={{0,8},{4,12},{8,0},{12,4},{1,9},{5,13},{9,1},{13,5},{2,10},{6,14},... | collective-permute-start | bytes 12296 | tf_op jit(solution)/shard_map/ppermute | solution.py:18
  50.7 6.6 %collective-permute-start.26 = (f32[136,128]{1,0:T(8,128)S(1)}, f32[136,128]{1,0:T(8,128)S(1)}, u32[]{:S(2)}, u32[]{:S(2)}) collective-permute-start(f32[136,128]{1,0:T(8,128)S(1)} %combine.3.refs_0_), channel_id=1, source_target_pairs={{0,3},{1,2},{2,1},{3,0},{4,7},{5,6},{6,5},{7,4},{8,11},{9,10},{10,... | collective-permute-start | bytes 208904 | tf_op jit(solution)/shard_map/ppermute | solution.py:18
  53.4 6.1 %collective-permute-start.25 = (f32[136,128]{1,0:T(8,128)S(1)}, f32[136,128]{1,0:T(8,128)S(1)}, u32[]{:S(2)}, u32[]{:S(2)}) collective-permute-start(f32[136,128]{1,0:T(8,128)S(1)} %combine.3.refs_0_), channel_id=1, source_target_pairs={{0,2},{1,3},{2,0},{3,1},{4,6},{5,7},{6,4},{7,5},{8,10},{9,11},{10,... | collective-permute-start | bytes 208904 | tf_op jit(solution)/shard_map/ppermute | solution.py:18
  53.4 6.1 %collective-permute-start.24 = (f32[136,128]{1,0:T(8,128)S(1)}, f32[136,128]{1,0:T(8,128)S(1)}, u32[]{:S(2)}, u32[]{:S(2)}) collective-permute-start(f32[136,128]{1,0:T(8,128)S(1)} %combine.3.refs_0_), channel_id=1, source_target_pairs={{0,1},{1,0},{2,3},{3,2},{4,5},{5,4},{6,7},{7,6},{8,9},{9,8},{10,11... | collective-permute-start | bytes 208904 | tf_op jit(solution)/shard_map/ppermute | solution.py:18
  (7 other events, 41.7 us)

commit v14 on v13

--- a/solution.py
+++ b/solution.py
@@ -407,7 +407,7 @@
                       (direct, mirror, twin, stat))
         parts = [merged[0]] + [shifted(value, "col", d, n) for d, value in zip(distances(n), merged[1:n])]
         stat = merged[n]
-        for b in bits(n):
+        for b in bits(n)[::-1]:
             stat, = call(add_kernel, "add_stat", [vmem] * (2 + n // 2), [tile], [],
                          (stat, shifted(stat, "row", b, n), *others))
         own, = call(functools.partial(combine_kernel, n), "combine", [vmem] * (3 + n + n // 2), [loaded], [],

time: 60.9 us -> 60.5 us (level)
  Pallas kernels: 10.2 us -> 6.94 us
  starting transfers between devices: 30.6 us -> 32 us
  waiting for transfers between devices: 18.4 us -> 19.6 us
    pallas_call x18, Pallas kernels: 10.2 us -> 6.94 us  [call(): pl.pallas_call(kernel, in_specs=specs, out_specs=jax.tree.map(lambda _: v...]
    ppermute x7, waiting for transfers between devices: 0.53 us -> 1.78 us  [moved(): lax.ppermute(value, ('row', 'col'), [(s, t[0] * n + t[1]) for s, t in pai...]
    ppermute x7, starting transfers between devices: 7.28 us -> 8.23 us  [moved(): lax.ppermute(value, ('row', 'col'), [(s, t[0] * n + t[1]) for s, t in pai...]
  transfers between devices with their start and end apart: 27 -> 27, of which waited for: 12 -> 13; matrix products, arithmetic and copies ran while one was open for 0% -> 0% of each run, Pallas kernels for 15% -> 9%
where the time goes in v14:
time: 60.5 us; the launch traced here: 60.1 us
  starting transfers between devices  32 us (53%)
  waiting for transfers between devices  19.6 us (32%)
  Pallas kernels  6.94 us (11%)
  between operations  1.5 us (2%)
    ppermute x20, starting transfers between devices, shifted(): return lax.ppermute(value, axis, [(i, i ^ d) for i in range(n)])  23.7 us
    ppermute x20, waiting for transfers between devices, shifted(): return lax.ppermute(value, axis, [(i, i ^ d) for i in range(n)])  17.9 us
    ppermute x7, starting transfers between devices, moved(): lax.ppermute(value, ('row', 'col'), [(s, t[0] * n + t[1]) for s, t in pai...  8.23 us
    pallas_call x18, Pallas kernels, call(): pl.pallas_call(kernel, in_specs=specs, out_specs=jax.tree.map(lambda _: v...  6.94 us
    ppermute x7, waiting for transfers between devices, moved(): lax.ppermute(value, ('row', 'col'), [(s, t[0] * n + t[1]) for s, t in pai...  1.78 us
  transfers between devices with their start and end apart: 27, of which 13 were waited for; matrix products, arithmetic and copies ran while one was open for 0% of the time, Pallas kernels for 9%

profile of v14, /device:TPU:0, one launch (start us, length us, event | category | flops | bytes accessed | tf_op | source)
XLA Modules:
  0.0 60.1 jit_solution(2907068710926080581)
XLA Ops:
  0.7 3.0 %collective-permute-start = (f32[32,2048]{1,0:T(8,128)}, f32[32,2048]{1,0:T(8,128)S(1)}, u32[]{:S(2)}, u32[]{:S(2)}) collective-permute-start(f32[32,2048]{1,0:T(8,128)} %right.3), channel_id=1, source_target_pairs={{0,8},{1,5},{2,6},{3,11},{4,0},{5,13},{6,14},{7,3},{8,12},{9,1},{1... | collective-permute-start | bytes 786440 | tf_op jit(solution)/shard_map/ppermute | solution.py:27
  4.3 1.7 %mirror_first.1 = (f32[16,32,128]{2,1,0:T(8,128)S(1)}, bf16[32,256,256]{2,1,0:T(8,128)(2,1)S(1)}) custom-call(s32[1,1,32]{2,1,0:T(1,128)} %rows_any.5, s32[1,1,32]{2,1,0:T(1,128)} %cols_any.5, s32[1,1]{1,0:T(1,128)S(6)} %copy.8.count, f32[32,2048]{1,0:T(8,128)} %right.3, bf16[1,1,32,256,256]{4,3,2,1,0:T(8,128)(2,1)} %cov.1), custom_call_target="tpu_custom_call" | custom-call | flops 268435456 | bytes 4194304 | tf_op jit(solution)/shard_map/mirror_first/pallas_call | solution.py:387
  6.1 1.8 %collective-permute-done.arrived = f32[32,2048]{1,0:T(8,128)S(1)} collective-permute-done((f32[32,2048]{1,0:T(8,128)}, f32[32,2048]{1,0:T(8,128)S(1)}, u32[]{:S(2)}, u32[]{:S(2)}) %collective-permute-start) | collective-permute-done | bytes 262176 | tf_op jit(solution)/shard_map/ppermute | solution.py:27
  8.0 2.4 %collective-permute-start.5 = (f32[128,128]{1,0:T(8,128)S(1)}, f32[128,128]{1,0:T(8,128)S(1)}, u32[]{:S(2)}, u32[]{:S(2)}) collective-permute-start(f32[128,128]{1,0:T(8,128)S(1)} %get-tuple-element.31), channel_id=1, source_target_pairs={{0,8},{1,9},{2,10},{3,14},{4,12},{5,13},{6,11},{7,15},{8,0},{9,4},... | collective-permute-start | bytes 196616 | tf_op jit(solution)/shard_map/ppermute | solution.py:27
  10.7 1.2 %direct_first.1 = (f32[16,32,128]{2,1,0:T(8,128)S(1)}, f32[8,128]{1,0:T(8,128)S(1)}, f32[16,32,128]{2,1,0:T(8,128)S(1)}) custom-call(s32[1,1,32]{2,1,0:T(1,128)S(1)} %copy-done.2, s32[1,1,32]{2,1,0:T(1,128)S(1)} %copy-done.3, s32[1,1]{1,0:T(1,128)S(6)} %copy.8.count, f32[1,2048]{1,0:T(1,128)S(1)} %bitcast.1, ...), custom_call_target="tpu_custom_call" | custom-call | flops 268435456 | bytes 4194304 | tf_op jit(solution)/shard_map/direct_first/pallas_call | solution.py:387
  12.0 4.4 %collective-permute-start.7 = (f32[128,128]{1,0:T(8,128)S(1)}, f32[128,128]{1,0:T(8,128)S(1)}, u32[]{:S(2)}, u32[]{:S(2)}) collective-permute-start(f32[128,128]{1,0:T(8,128)S(1)} %get-tuple-element.33), channel_id=1, source_target_pairs={{0,3},{1,2},{2,1},{3,0},{4,7},{5,6},{6,5},{7,4},{8,11},{9,10},{10,... | collective-permute-start | bytes 196616 | tf_op jit(solution)/shard_map/ppermute | solution.py:18
  17.0 2.4 %collective-permute-start.3 = (f32[8,128]{1,0:T(8,128)S(1)}, f32[8,128]{1,0:T(8,128)S(1)}, u32[]{:S(2)}, u32[]{:S(2)}) collective-permute-start(f32[8,128]{1,0:T(8,128)S(1)} %get-tuple-element.30.one), channel_id=1, source_target_pairs={{0,8},{4,12},{8,0},{12,4},{1,9},{5,13},{9,1},{13,5},{2,10},{6,14},... | collective-permute-start | bytes 12296 | tf_op jit(solution)/shard_map/ppermute | solution.py:18
  19.4 1.6 %collective-permute-done.3.two = f32[8,128]{1,0:T(8,128)S(1)} collective-permute-done((f32[8,128]{1,0:T(8,128)S(1)}, f32[8,128]{1,0:T(8,128)S(1)}, u32[]{:S(2)}, u32[]{:S(2)}) %collective-permute-start.3) | collective-permute-done | bytes 4128 | tf_op jit(solution)/shard_map/ppermute | solution.py:18
  21.0 1.2 %collective-permute-done.6.two = f32[8,128]{1,0:T(8,128)S(1)} collective-permute-done((f32[8,128]{1,0:T(8,128)S(1)}, f32[8,128]{1,0:T(8,128)S(1)}, u32[]{:S(2)}, u32[]{:S(2)}) %collective-permute-start.6) | collective-permute-done | bytes 4128 | tf_op jit(solution)/shard_map/ppermute | solution.py:18
  22.9 2.7 %collective-permute-start.12 = (f32[136,128]{1,0:T(8,128)S(1)}, f32[136,128]{1,0:T(8,128)S(1)}, u32[]{:S(2)}, u32[]{:S(2)}) collective-permute-start(f32[136,128]{1,0:T(8,128)S(1)} %combine.2.refs_0_), channel_id=1, source_target_pairs={{0,3},{1,2},{2,1},{3,0},{4,7},{5,6},{6,5},{7,4},{8,11},{9,10},{10,... | collective-permute-start | bytes 208904 | tf_op jit(solution)/shard_map/ppermute | solution.py:18
  25.8 1.6 %collective-permute-start.10 = (f32[136,128]{1,0:T(8,128)S(1)}, f32[136,128]{1,0:T(8,128)S(1)}, u32[]{:S(2)}, u32[]{:S(2)}) collective-permute-start(f32[136,128]{1,0:T(8,128)S(1)} %combine.2.refs_0_), channel_id=1, source_target_pairs={{0,1},{1,0},{2,3},{3,2},{4,5},{5,4},{6,7},{7,6},{8,9},{9,8},{10,11... | collective-permute-start | bytes 208904 | tf_op jit(solution)/shard_map/ppermute | solution.py:18
  27.4 2.2 %collective-permute-start.14 = (f32[136,128]{1,0:T(8,128)S(1)}, f32[136,128]{1,0:T(8,128)S(1)}, u32[]{:S(2)}, u32[]{:S(2)}) collective-permute-start(f32[136,128]{1,0:T(8,128)S(1)} %combine.2.refs_0_), channel_id=1, source_target_pairs={{0,8},{1,12},{2,10},{3,11},{4,9},{5,13},{6,14},{7,15},{8,0},{9,1},... | collective-permute-start | bytes 208904 | tf_op jit(solution)/shard_map/ppermute | solution.py:27
  29.8 4.7 %collective-permute-done.11.refs_2_ = f32[136,128]{1,0:T(8,128)S(1)} collective-permute-done((f32[136,128]{1,0:T(8,128)S(1)}, f32[136,128]{1,0:T(8,128)S(1)}, u32[]{:S(2)}, u32[]{:S(2)}) %collective-permute-start.11) | collective-permute-done | bytes 69664 | tf_op jit(solution)/shard_map/ppermute | solution.py:18
  37.7 1.2 %direct_second.1 = (f32[16,32,128]{2,1,0:T(8,128)S(1)}, f32[8,128]{1,0:T(8,128)S(1)}) custom-call(s32[1,1,32]{2,1,0:T(1,128)S(1)} %copy-done.2, s32[1,1,32]{2,1,0:T(1,128)S(1)} %copy-done.3, s32[1,1]{1,0:T(1,128)S(6)} %copy.8.count, f32[1,2048]{1,0:T(1,128)S(1)} %bitcast.3, bf16[32,256,256]{2,1,0:T(8,128)(2,1)S(1)} %get-tuple-element.25.blocks, ...), custom_call_target="tpu_custom_call" | custom-call | flops 268435456 | bytes 4194304 | tf_op jit(solution)/shard_map/direct_second/pallas_call | solution.py:387
  39.0 2.2 %collective-permute-start.17 = (f32[8,128]{1,0:T(8,128)S(1)}, f32[8,128]{1,0:T(8,128)S(1)}, u32[]{:S(2)}, u32[]{:S(2)}) collective-permute-start(f32[8,128]{1,0:T(8,128)S(1)} %get-tuple-element.42.one), channel_id=1, source_target_pairs={{0,8},{4,12},{8,0},{12,4},{1,9},{5,13},{9,1},{13,5},{2,10},{6,14},... | collective-permute-start | bytes 12296 | tf_op jit(solution)/shard_map/ppermute | solution.py:18
  41.2 1.8 %collective-permute-start.21 = (f32[128,128]{1,0:T(8,128)S(1)}, f32[128,128]{1,0:T(8,128)S(1)}, u32[]{:S(2)}, u32[]{:S(2)}) collective-permute-start(f32[128,128]{1,0:T(8,128)S(1)} %get-tuple-element.45), channel_id=1, source_target_pairs={{0,3},{1,2},{2,1},{3,0},{4,7},{5,6},{6,5},{7,4},{8,11},{9,10},{10,... | collective-permute-start | bytes 196616 | tf_op jit(solution)/shard_map/ppermute | solution.py:18
  43.0 2.6 %collective-permute-start.22 = (f32[128,128]{1,0:T(8,128)S(1)}, f32[128,128]{1,0:T(8,128)S(1)}, u32[]{:S(2)}, u32[]{:S(2)}) collective-permute-start(f32[128,128]{1,0:T(8,128)S(1)} %get-tuple-element.46), channel_id=1, source_target_pairs={{0,2},{1,3},{2,0},{3,1},{4,6},{5,7},{6,4},{7,5},{8,10},{9,11},{10,... | collective-permute-start | bytes 196616 | tf_op jit(solution)/shard_map/ppermute | solution.py:18
  45.8 1.2 %collective-permute-done.20.two = f32[8,128]{1,0:T(8,128)S(1)} collective-permute-done((f32[8,128]{1,0:T(8,128)S(1)}, f32[8,128]{1,0:T(8,128)S(1)}, u32[]{:S(2)}, u32[]{:S(2)}) %collective-permute-start.20) | collective-permute-done | bytes 4128 | tf_op jit(solution)/shard_map/ppermute | solution.py:18
  47.6 3.0 %collective-permute-done.22.refs_2_ = f32[128,128]{1,0:T(8,128)S(1)} collective-permute-done((f32[128,128]{1,0:T(8,128)S(1)}, f32[128,128]{1,0:T(8,128)S(1)}, u32[]{:S(2)}, u32[]{:S(2)}) %collective-permute-start.22) | collective-permute-done | bytes 65568 | tf_op jit(solution)/shard_map/ppermute | solution.py:18
  50.8 1.7 %collective-permute-start.26 = (f32[136,128]{1,0:T(8,128)S(1)}, f32[136,128]{1,0:T(8,128)S(1)}, u32[]{:S(2)}, u32[]{:S(2)}) collective-permute-start(f32[136,128]{1,0:T(8,128)S(1)} %combine.3.refs_0_), channel_id=1, source_target_pairs={{0,3},{1,2},{2,1},{3,0},{4,7},{5,6},{6,5},{7,4},{8,11},{9,10},{10,... | collective-permute-start | bytes 208904 | tf_op jit(solution)/shard_map/ppermute | solution.py:18
  52.5 2.7 %collective-permute-start.24 = (f32[136,128]{1,0:T(8,128)S(1)}, f32[136,128]{1,0:T(8,128)S(1)}, u32[]{:S(2)}, u32[]{:S(2)}) collective-permute-start(f32[136,128]{1,0:T(8,128)S(1)} %combine.3.refs_0_), channel_id=1, source_target_pairs={{0,1},{1,0},{2,3},{3,2},{4,5},{5,4},{6,7},{7,6},{8,9},{9,8},{10,11... | collective-permute-start | bytes 208904 | tf_op jit(solution)/shard_map/ppermute | solution.py:18
  55.2 2.2 %collective-permute-done.26.refs_3_ = f32[136,128]{1,0:T(8,128)S(1)} collective-permute-done((f32[136,128]{1,0:T(8,128)S(1)}, f32[136,128]{1,0:T(8,128)S(1)}, u32[]{:S(2)}, u32[]{:S(2)}) %collective-permute-start.26) | collective-permute-done | bytes 69664 | tf_op jit(solution)/shard_map/ppermute | solution.py:18
  57.4 1.4 %collective-permute-done.25.refs_2_ = f32[136,128]{1,0:T(8,128)S(1)} collective-permute-done((f32[136,128]{1,0:T(8,128)S(1)}, f32[136,128]{1,0:T(8,128)S(1)}, u32[]{:S(2)}, u32[]{:S(2)}) %collective-permute-start.25) | collective-permute-done | bytes 69664 | tf_op jit(solution)/shard_map/ppermute | solution.py:18
  58.9 1.2 %last.1 = (f32[32,2048]{1,0:T(8,128)}, f32[32,2048]{1,0:T(8,128)}) custom-call(f32[32,2048]{1,0:T(8,128)S(1)} %copy-done, f32[32,2048]{1,0:T(8,128)S(1)} %get-tuple-element.36.near.left, f32[8,128]{1,0:T(8,128)S(1)} %get-tuple-element.37.stat.stat_now, f32[136,128]{1,0:T(8,128)S(1)} %combine.3.refs_0_, f32[136,128]{1,0:T(8,128)S(1)} %collective-permute-done.24.refs_1_, ...), custom_call_target="tpu_custom_call" | custom-call | tf_op jit(solution)/shard_map/last/pallas_call | solution.py:387
  (56 shorter events, 6.6 us)
Async XLA Ops:
  0.7 7.2 %collective-permute-start = (f32[32,2048]{1,0:T(8,128)}, f32[32,2048]{1,0:T(8,128)S(1)}, u32[]{:S(2)}, u32[]{:S(2)}) collective-permute-start(f32[32,2048]{1,0:T(8,128)} %right.3), channel_id=1, source_target_pairs={{0,8},{1,5},{2,6},{3,11},{4,0},{5,13},{6,14},{7,3},{8,12},{9,1},{1... | collective-permute-start | bytes 786440 | tf_op jit(solution)/shard_map/ppermute | solution.py:27
  6.0 2.0 %collective-permute-start.2 = (f32[16,32,128]{2,1,0:T(8,128)S(1)}, f32[16,32,128]{2,1,0:T(8,128)S(1)}, u32[]{:S(2)}, u32[]{:S(2)}) collective-permute-start(f32[16,32,128]{2,1,0:T(8,128)S(1)} %get-tuple-element.26.mark.mirror), channel_id=1, source_target_pairs={{0,4},{4,0},{8,12},{12,8},{1,5},{5,1},{9,13},{13,9},{2,6},{6,2},{1... | collective-permute-start | bytes 786440 | tf_op jit(solution)/shard_map/ppermute | solution.py:18
  7.9 2.8 %collective-permute-start.1 = (f32[32,2048]{1,0:T(8,128)S(1)}, f32[32,2048]{1,0:T(8,128)S(1)}, u32[]{:S(2)}, u32[]{:S(2)}) collective-permute-start(f32[32,2048]{1,0:T(8,128)S(1)} %pick.1.current), channel_id=1, source_target_pairs={{0,4},{4,0},{8,12},{12,8},{1,5},{5,1},{9,13},{13,9},{2,6},{6,2},{1... | collective-permute-start | bytes 786440 | tf_op jit(solution)/shard_map/ppermute | solution.py:18
  8.0 9.0 %collective-permute-start.5 = (f32[128,128]{1,0:T(8,128)S(1)}, f32[128,128]{1,0:T(8,128)S(1)}, u32[]{:S(2)}, u32[]{:S(2)}) collective-permute-start(f32[128,128]{1,0:T(8,128)S(1)} %get-tuple-element.31), channel_id=1, source_target_pairs={{0,8},{1,9},{2,10},{3,14},{4,12},{5,13},{6,11},{7,15},{8,0},{9,4},... | collective-permute-start | bytes 196616 | tf_op jit(solution)/shard_map/ppermute | solution.py:27
  10.5 8.9 %collective-permute-start.4 = (f32[128,128]{1,0:T(8,128)S(1)}, f32[128,128]{1,0:T(8,128)S(1)}, u32[]{:S(2)}, u32[]{:S(2)}) collective-permute-start(f32[128,128]{1,0:T(8,128)S(1)} %get-tuple-element.27.mark), channel_id=1, source_target_pairs={{0,4},{1,5},{2,8},{3,12},{4,0},{5,1},{6,9},{7,13},{8,2},{9,6},{10,... | collective-permute-start | bytes 196616 | tf_op jit(solution)/shard_map/ppermute | solution.py:27
  12.0 10.2 %collective-permute-start.7 = (f32[128,128]{1,0:T(8,128)S(1)}, f32[128,128]{1,0:T(8,128)S(1)}, u32[]{:S(2)}, u32[]{:S(2)}) collective-permute-start(f32[128,128]{1,0:T(8,128)S(1)} %get-tuple-element.33), channel_id=1, source_target_pairs={{0,3},{1,2},{2,1},{3,0},{4,7},{5,6},{6,5},{7,4},{8,11},{9,10},{10,... | collective-permute-start | bytes 196616 | tf_op jit(solution)/shard_map/ppermute | solution.py:18
  16.4 6.5 %collective-permute-start.8 = (f32[128,128]{1,0:T(8,128)S(1)}, f32[128,128]{1,0:T(8,128)S(1)}, u32[]{:S(2)}, u32[]{:S(2)}) collective-permute-start(f32[128,128]{1,0:T(8,128)S(1)} %get-tuple-element.34), channel_id=1, source_target_pairs={{0,2},{1,3},{2,0},{3,1},{4,6},{5,7},{6,4},{7,5},{8,10},{9,11},{10,... | collective-permute-start | bytes 196616 | tf_op jit(solution)/shard_map/ppermute | solution.py:18
  16.4 6.5 %collective-permute-start.9 = (f32[128,128]{1,0:T(8,128)S(1)}, f32[128,128]{1,0:T(8,128)S(1)}, u32[]{:S(2)}, u32[]{:S(2)}) collective-permute-start(f32[128,128]{1,0:T(8,128)S(1)} %get-tuple-element.35), channel_id=1, source_target_pairs={{0,1},{1,0},{2,3},{3,2},{4,5},{5,4},{6,7},{7,6},{8,9},{9,8},{10,11... | collective-permute-start | bytes 196616 | tf_op jit(solution)/shard_map/ppermute | solution.py:18
  17.0 4.0 %collective-permute-start.3 = (f32[8,128]{1,0:T(8,128)S(1)}, f32[8,128]{1,0:T(8,128)S(1)}, u32[]{:S(2)}, u32[]{:S(2)}) collective-permute-start(f32[8,128]{1,0:T(8,128)S(1)} %get-tuple-element.30.one), channel_id=1, source_target_pairs={{0,8},{4,12},{8,0},{12,4},{1,9},{5,13},{9,1},{13,5},{2,10},{6,14},... | collective-permute-start | bytes 12296 | tf_op jit(solution)/shard_map/ppermute | solution.py:18
  22.9 6.9 %collective-permute-start.12 = (f32[136,128]{1,0:T(8,128)S(1)}, f32[136,128]{1,0:T(8,128)S(1)}, u32[]{:S(2)}, u32[]{:S(2)}) collective-permute-start(f32[136,128]{1,0:T(8,128)S(1)} %combine.2.refs_0_), channel_id=1, source_target_pairs={{0,3},{1,2},{2,1},{3,0},{4,7},{5,6},{6,5},{7,4},{8,11},{9,10},{10,... | collective-permute-start | bytes 208904 | tf_op jit(solution)/shard_map/ppermute | solution.py:18
  25.7 8.9 %collective-permute-start.11 = (f32[136,128]{1,0:T(8,128)S(1)}, f32[136,128]{1,0:T(8,128)S(1)}, u32[]{:S(2)}, u32[]{:S(2)}) collective-permute-start(f32[136,128]{1,0:T(8,128)S(1)} %combine.2.refs_0_), channel_id=1, source_target_pairs={{0,2},{1,3},{2,0},{3,1},{4,6},{5,7},{6,4},{7,5},{8,10},{9,11},{10,... | collective-permute-start | bytes 208904 | tf_op jit(solution)/shard_map/ppermute | solution.py:18
  25.8 8.7 %collective-permute-start.10 = (f32[136,128]{1,0:T(8,128)S(1)}, f32[136,128]{1,0:T(8,128)S(1)}, u32[]{:S(2)}, u32[]{:S(2)}) collective-permute-start(f32[136,128]{1,0:T(8,128)S(1)} %combine.2.refs_0_), channel_id=1, source_target_pairs={{0,1},{1,0},{2,3},{3,2},{4,5},{5,4},{6,7},{7,6},{8,9},{9,8},{10,11... | collective-permute-start | bytes 208904 | tf_op jit(solution)/shard_map/ppermute | solution.py:18
  27.4 8.4 %collective-permute-start.14 = (f32[136,128]{1,0:T(8,128)S(1)}, f32[136,128]{1,0:T(8,128)S(1)}, u32[]{:S(2)}, u32[]{:S(2)}) collective-permute-start(f32[136,128]{1,0:T(8,128)S(1)} %combine.2.refs_0_), channel_id=1, source_target_pairs={{0,8},{1,12},{2,10},{3,11},{4,9},{5,13},{6,14},{7,15},{8,0},{9,1},... | collective-permute-start | bytes 208904 | tf_op jit(solution)/shard_map/ppermute | solution.py:27
  29.6 6.2 %collective-permute-start.13 = (f32[136,128]{1,0:T(8,128)S(1)}, f32[136,128]{1,0:T(8,128)S(1)}, u32[]{:S(2)}, u32[]{:S(2)}) collective-permute-start(f32[136,128]{1,0:T(8,128)S(1)} %combine.2.refs_0_), channel_id=1, source_target_pairs={{0,4},{1,5},{2,8},{3,12},{4,0},{5,1},{6,9},{7,13},{8,2},{9,6},{10,... | collective-permute-start | bytes 208904 | tf_op jit(solution)/shard_map/ppermute | solution.py:27
  35.9 1.8 %collective-permute-start.15 = (f32[16,32,128]{2,1,0:T(8,128)S(1)}, f32[16,32,128]{2,1,0:T(8,128)S(1)}, u32[]{:S(2)}, u32[]{:S(2)}) collective-permute-start(f32[16,32,128]{2,1,0:T(8,128)S(1)} %held.1), channel_id=1, source_target_pairs={{0,4},{4,0},{8,12},{12,8},{1,5},{5,1},{9,13},{13,9},{2,6},{6,2},{1... | collective-permute-start | bytes 786440 | tf_op jit(solution)/shard_map/ppermute | solution.py:18
  37.3 8.4 %collective-permute-start.19 = (f32[128,128]{1,0:T(8,128)S(1)}, f32[128,128]{1,0:T(8,128)S(1)}, u32[]{:S(2)}, u32[]{:S(2)}) collective-permute-start(f32[128,128]{1,0:T(8,128)S(1)} %get-tuple-element.43), channel_id=1, source_target_pairs={{0,8},{1,9},{2,10},{3,14},{4,12},{5,13},{6,11},{7,15},{8,0},{9,4},... | collective-permute-start | bytes 196616 | tf_op jit(solution)/shard_map/ppermute | solution.py:27
  37.7 7.9 %collective-permute-start.18 = (f32[128,128]{1,0:T(8,128)S(1)}, f32[128,128]{1,0:T(8,128)S(1)}, u32[]{:S(2)}, u32[]{:S(2)}) collective-permute-start(f32[128,128]{1,0:T(8,128)S(1)} %get-tuple-element.39.mark), channel_id=1, source_target_pairs={{0,4},{1,5},{2,8},{3,12},{4,0},{5,1},{6,9},{7,13},{8,2},{9,6},{10,... | collective-permute-start | bytes 196616 | tf_op jit(solution)/shard_map/ppermute | solution.py:27
  39.0 6.5 %collective-permute-start.17 = (f32[8,128]{1,0:T(8,128)S(1)}, f32[8,128]{1,0:T(8,128)S(1)}, u32[]{:S(2)}, u32[]{:S(2)}) collective-permute-start(f32[8,128]{1,0:T(8,128)S(1)} %get-tuple-element.42.one), channel_id=1, source_target_pairs={{0,8},{4,12},{8,0},{12,4},{1,9},{5,13},{9,1},{13,5},{2,10},{6,14},... | collective-permute-start | bytes 12296 | tf_op jit(solution)/shard_map/ppermute | solution.py:18
  41.2 6.4 %collective-permute-start.21 = (f32[128,128]{1,0:T(8,128)S(1)}, f32[128,128]{1,0:T(8,128)S(1)}, u32[]{:S(2)}, u32[]{:S(2)}) collective-permute-start(f32[128,128]{1,0:T(8,128)S(1)} %get-tuple-element.45), channel_id=1, source_target_pairs={{0,3},{1,2},{2,1},{3,0},{4,7},{5,6},{6,5},{7,4},{8,11},{9,10},{10,... | collective-permute-start | bytes 196616 | tf_op jit(solution)/shard_map/ppermute | solution.py:18
  43.0 7.6 %collective-permute-start.22 = (f32[128,128]{1,0:T(8,128)S(1)}, f32[128,128]{1,0:T(8,128)S(1)}, u32[]{:S(2)}, u32[]{:S(2)}) collective-permute-start(f32[128,128]{1,0:T(8,128)S(1)} %get-tuple-element.46), channel_id=1, source_target_pairs={{0,2},{1,3},{2,0},{3,1},{4,6},{5,7},{6,4},{7,5},{8,10},{9,11},{10,... | collective-permute-start | bytes 196616 | tf_op jit(solution)/shard_map/ppermute | solution.py:18
  45.5 5.2 %collective-permute-start.23 = (f32[128,128]{1,0:T(8,128)S(1)}, f32[128,128]{1,0:T(8,128)S(1)}, u32[]{:S(2)}, u32[]{:S(2)}) collective-permute-start(f32[128,128]{1,0:T(8,128)S(1)} %get-tuple-element.47), channel_id=1, source_target_pairs={{0,1},{1,0},{2,3},{3,2},{4,5},{5,4},{6,7},{7,6},{8,9},{9,8},{10,11... | collective-permute-start | bytes 196616 | tf_op jit(solution)/shard_map/ppermute | solution.py:18
  50.8 6.6 %collective-permute-start.26 = (f32[136,128]{1,0:T(8,128)S(1)}, f32[136,128]{1,0:T(8,128)S(1)}, u32[]{:S(2)}, u32[]{:S(2)}) collective-permute-start(f32[136,128]{1,0:T(8,128)S(1)} %combine.3.refs_0_), channel_id=1, source_target_pairs={{0,3},{1,2},{2,1},{3,0},{4,7},{5,6},{6,5},{7,4},{8,11},{9,10},{10,... | collective-permute-start | bytes 208904 | tf_op jit(solution)/shard_map/ppermute | solution.py:18
  52.5 6.3 %collective-permute-start.25 = (f32[136,128]{1,0:T(8,128)S(1)}, f32[136,128]{1,0:T(8,128)S(1)}, u32[]{:S(2)}, u32[]{:S(2)}) collective-permute-start(f32[136,128]{1,0:T(8,128)S(1)} %combine.3.refs_0_), channel_id=1, source_target_pairs={{0,2},{1,3},{2,0},{3,1},{4,6},{5,7},{6,4},{7,5},{8,10},{9,11},{10,... | collective-permute-start | bytes 208904 | tf_op jit(solution)/shard_map/ppermute | solution.py:18
  52.5 6.3 %collective-permute-start.24 = (f32[136,128]{1,0:T(8,128)S(1)}, f32[136,128]{1,0:T(8,128)S(1)}, u32[]{:S(2)}, u32[]{:S(2)}) collective-permute-start(f32[136,128]{1,0:T(8,128)S(1)} %combine.3.refs_0_), channel_id=1, source_target_pairs={{0,1},{1,0},{2,3},{3,2},{4,5},{5,4},{6,7},{7,6},{8,9},{9,8},{10,11... | collective-permute-start | bytes 208904 | tf_op jit(solution)/shard_map/ppermute | solution.py:18
  (7 other events, 41.3 us)

commit v15 on v13

--- a/solution.py
+++ b/solution.py
@@ -408,8 +408,8 @@
         parts = [merged[0]] + [shifted(value, "col", d, n) for d, value in zip(distances(n), merged[1:n])]
         stat = merged[n]
         for b in bits(n):
-            stat, = call(add_kernel, "add_stat", [vmem] * (2 + n // 2), [tile], [],
-                         (stat, shifted(stat, "row", b, n), *others))
+            stat, = call(add_kernel, "add_stat", [vmem] * 3, [tile], [],
+                         (stat, shifted(stat, "row", b, n), others[-1]))
         own, = call(functools.partial(combine_kernel, n), "combine", [vmem] * (3 + n + n // 2), [loaded], [],
                     (near, noise, stat, *parts, *others))
         return [own] + [shifted(own, "col", d, n) for d in distances(n)[::-1]]

time: 60.9 us -> 61 us (level)
  starting transfers between devices: 30.6 us -> 34.2 us
  Pallas kernels: 10.2 us -> 6.93 us
    pallas_call x18, Pallas kernels: 10.2 us -> 6.93 us  [call(): pl.pallas_call(kernel, in_specs=specs, out_specs=jax.tree.map(lambda _: v...]
    ppermute x7, starting transfers between devices: 7.28 us -> 9.95 us  [moved(): lax.ppermute(value, ('row', 'col'), [(s, t[0] * n + t[1]) for s, t in pai...]
    ppermute x20, waiting for transfers between devices: 17.9 us -> 16.4 us  [shifted(): return lax.ppermute(value, axis, [(i, i ^ d) for i in range(n)])]
    ppermute x7, waiting for transfers between devices: 0.53 us -> 1.78 us  [moved(): lax.ppermute(value, ('row', 'col'), [(s, t[0] * n + t[1]) for s, t in pai...]
    ppermute x20, starting transfers between devices: 23.3 us -> 24.3 us  [shifted(): return lax.ppermute(value, axis, [(i, i ^ d) for i in range(n)])]
  transfers between devices with their start and end apart: 27 -> 27, of which waited for: 12 -> 10; matrix products, arithmetic and copies ran while one was open for 0% -> 0% of each run, Pallas kernels for 15% -> 9%
where the time goes in v15:
time: 61 us; the launch traced here: 60.8 us
  starting transfers between devices  34.2 us (56%)
  waiting for transfers between devices  18.2 us (30%)
  Pallas kernels  6.93 us (11%)
  between operations  1.48 us (2%)
    ppermute x20, starting transfers between devices, shifted(): return lax.ppermute(value, axis, [(i, i ^ d) for i in range(n)])  24.3 us
    ppermute x20, waiting for transfers between devices, shifted(): return lax.ppermute(value, axis, [(i, i ^ d) for i in range(n)])  16.4 us
    ppermute x7, starting transfers between devices, moved(): lax.ppermute(value, ('row', 'col'), [(s, t[0] * n + t[1]) for s, t in pai...  9.95 us
    pallas_call x18, Pallas kernels, call(): pl.pallas_call(kernel, in_specs=specs, out_specs=jax.tree.map(lambda _: v...  6.93 us
    ppermute x7, waiting for transfers between devices, moved(): lax.ppermute(value, ('row', 'col'), [(s, t[0] * n + t[1]) for s, t in pai...  1.78 us
  transfers between devices with their start and end apart: 27, of which 10 were waited for; matrix products, arithmetic and copies ran while one was open for 0% of the time, Pallas kernels for 9%

profile of v15, /device:TPU:0, one launch (start us, length us, event | category | flops | bytes accessed | tf_op | source)
XLA Modules:
  0.0 60.8 jit_solution(14720955748155244204)
XLA Ops:
  0.7 3.0 %collective-permute-start = (f32[32,2048]{1,0:T(8,128)}, f32[32,2048]{1,0:T(8,128)S(1)}, u32[]{:S(2)}, u32[]{:S(2)}) collective-permute-start(f32[32,2048]{1,0:T(8,128)} %right.3), channel_id=1, source_target_pairs={{0,8},{1,5},{2,6},{3,11},{4,0},{5,13},{6,14},{7,3},{8,12},{9,1},{1... | collective-permute-start | bytes 786440 | tf_op jit(solution)/shard_map/ppermute | solution.py:27
  4.3 1.7 %mirror_first.1 = (f32[16,32,128]{2,1,0:T(8,128)S(1)}, bf16[32,256,256]{2,1,0:T(8,128)(2,1)S(1)}) custom-call(s32[1,1,32]{2,1,0:T(1,128)} %rows_any.5, s32[1,1,32]{2,1,0:T(1,128)} %cols_any.5, s32[1,1]{1,0:T(1,128)S(6)} %copy.8.count, f32[32,2048]{1,0:T(8,128)} %right.3, bf16[1,1,32,256,256]{4,3,2,1,0:T(8,128)(2,1)} %cov.1), custom_call_target="tpu_custom_call" | custom-call | flops 268435456 | bytes 4194304 | tf_op jit(solution)/shard_map/mirror_first/pallas_call | solution.py:387
  6.1 1.8 %collective-permute-done.arrived = f32[32,2048]{1,0:T(8,128)S(1)} collective-permute-done((f32[32,2048]{1,0:T(8,128)}, f32[32,2048]{1,0:T(8,128)S(1)}, u32[]{:S(2)}, u32[]{:S(2)}) %collective-permute-start) | collective-permute-done | bytes 262176 | tf_op jit(solution)/shard_map/ppermute | solution.py:27
  8.0 2.4 %collective-permute-start.4 = (f32[128,128]{1,0:T(8,128)S(1)}, f32[128,128]{1,0:T(8,128)S(1)}, u32[]{:S(2)}, u32[]{:S(2)}) collective-permute-start(f32[128,128]{1,0:T(8,128)S(1)} %get-tuple-element.31), channel_id=1, source_target_pairs={{0,8},{1,9},{2,10},{3,14},{4,12},{5,13},{6,11},{7,15},{8,0},{9,4},... | collective-permute-start | bytes 196616 | tf_op jit(solution)/shard_map/ppermute | solution.py:27
  10.7 1.2 %direct_first.1 = (f32[16,32,128]{2,1,0:T(8,128)S(1)}, f32[8,128]{1,0:T(8,128)S(1)}, f32[16,32,128]{2,1,0:T(8,128)S(1)}) custom-call(s32[1,1,32]{2,1,0:T(1,128)S(1)} %copy-done.2, s32[1,1,32]{2,1,0:T(1,128)S(1)} %copy-done.3, s32[1,1]{1,0:T(1,128)S(6)} %copy.8.count, f32[1,2048]{1,0:T(1,128)S(1)} %bitcast.1, ...), custom_call_target="tpu_custom_call" | custom-call | flops 268435456 | bytes 4194304 | tf_op jit(solution)/shard_map/direct_first/pallas_call | solution.py:387
  12.0 4.8 %collective-permute-start.6 = (f32[128,128]{1,0:T(8,128)S(1)}, f32[128,128]{1,0:T(8,128)S(1)}, u32[]{:S(2)}, u32[]{:S(2)}) collective-permute-start(f32[128,128]{1,0:T(8,128)S(1)} %get-tuple-element.33), channel_id=1, source_target_pairs={{0,3},{1,2},{2,1},{3,0},{4,7},{5,6},{6,5},{7,4},{8,11},{9,10},{10,... | collective-permute-start | bytes 196616 | tf_op jit(solution)/shard_map/ppermute | solution.py:18
  18.6 2.0 %collective-permute-start.5 = (f32[8,128]{1,0:T(8,128)S(1)}, f32[8,128]{1,0:T(8,128)S(1)}, u32[]{:S(2)}, u32[]{:S(2)}) collective-permute-start(f32[8,128]{1,0:T(8,128)S(1)} %add_stat.4.one), channel_id=1, source_target_pairs={{0,8},{4,12},{8,0},{12,4},{1,9},{5,13},{9,1},{13,5},{2,10},{6,14},... | collective-permute-start | bytes 12296 | tf_op jit(solution)/shard_map/ppermute | solution.py:18
  20.6 1.6 %collective-permute-done.5.two = f32[8,128]{1,0:T(8,128)S(1)} collective-permute-done((f32[8,128]{1,0:T(8,128)S(1)}, f32[8,128]{1,0:T(8,128)S(1)}, u32[]{:S(2)}, u32[]{:S(2)}) %collective-permute-start.5) | collective-permute-done | bytes 4128 | tf_op jit(solution)/shard_map/ppermute | solution.py:18
  22.8 3.3 %collective-permute-start.12 = (f32[136,128]{1,0:T(8,128)S(1)}, f32[136,128]{1,0:T(8,128)S(1)}, u32[]{:S(2)}, u32[]{:S(2)}) collective-permute-start(f32[136,128]{1,0:T(8,128)S(1)} %combine.2.refs_0_), channel_id=1, source_target_pairs={{0,3},{1,2},{2,1},{3,0},{4,7},{5,6},{6,5},{7,4},{8,11},{9,10},{10,... | collective-permute-start | bytes 208904 | tf_op jit(solution)/shard_map/ppermute | solution.py:18
  27.3 2.7 %collective-permute-start.14 = (f32[136,128]{1,0:T(8,128)S(1)}, f32[136,128]{1,0:T(8,128)S(1)}, u32[]{:S(2)}, u32[]{:S(2)}) collective-permute-start(f32[136,128]{1,0:T(8,128)S(1)} %combine.2.refs_0_), channel_id=1, source_target_pairs={{0,8},{1,12},{2,10},{3,11},{4,9},{5,13},{6,14},{7,15},{8,0},{9,1},... | collective-permute-start | bytes 208904 | tf_op jit(solution)/shard_map/ppermute | solution.py:27
  30.0 3.3 %collective-permute-done.11.refs_2_ = f32[136,128]{1,0:T(8,128)S(1)} collective-permute-done((f32[136,128]{1,0:T(8,128)S(1)}, f32[136,128]{1,0:T(8,128)S(1)}, u32[]{:S(2)}, u32[]{:S(2)}) %collective-permute-start.11) | collective-permute-done | bytes 69664 | tf_op jit(solution)/shard_map/ppermute | solution.py:18
  36.0 1.6 %collective-permute-start.18 = (f32[128,128]{1,0:T(8,128)S(1)}, f32[128,128]{1,0:T(8,128)S(1)}, u32[]{:S(2)}, u32[]{:S(2)}) collective-permute-start(f32[128,128]{1,0:T(8,128)S(1)} %get-tuple-element.43), channel_id=1, source_target_pairs={{0,8},{1,9},{2,10},{3,14},{4,12},{5,13},{6,11},{7,15},{8,0},{9,4},... | collective-permute-start | bytes 196616 | tf_op jit(solution)/shard_map/ppermute | solution.py:27
  37.6 1.2 %direct_second.1 = (f32[16,32,128]{2,1,0:T(8,128)S(1)}, f32[8,128]{1,0:T(8,128)S(1)}) custom-call(s32[1,1,32]{2,1,0:T(1,128)S(1)} %copy-done.2, s32[1,1,32]{2,1,0:T(1,128)S(1)} %copy-done.3, s32[1,1]{1,0:T(1,128)S(6)} %copy.8.count, f32[1,2048]{1,0:T(1,128)S(1)} %bitcast.3, bf16[32,256,256]{2,1,0:T(8,128)(2,1)S(1)} %get-tuple-element.25.blocks, ...), custom_call_target="tpu_custom_call" | custom-call | flops 268435456 | bytes 4194304 | tf_op jit(solution)/shard_map/direct_second/pallas_call | solution.py:387
  38.9 1.3 %collective-permute-start.17 = (f32[8,128]{1,0:T(8,128)S(1)}, f32[8,128]{1,0:T(8,128)S(1)}, u32[]{:S(2)}, u32[]{:S(2)}) collective-permute-start(f32[8,128]{1,0:T(8,128)S(1)} %get-tuple-element.42.one), channel_id=1, source_target_pairs={{0,4},{4,0},{8,12},{12,8},{1,5},{5,1},{9,13},{13,9},{2,6},{6,2},{1... | collective-permute-start | bytes 12296 | tf_op jit(solution)/shard_map/ppermute | solution.py:18
  40.2 1.3 %collective-permute-start.20 = (f32[128,128]{1,0:T(8,128)S(1)}, f32[128,128]{1,0:T(8,128)S(1)}, u32[]{:S(2)}, u32[]{:S(2)}) collective-permute-start(f32[128,128]{1,0:T(8,128)S(1)} %get-tuple-element.45), channel_id=1, source_target_pairs={{0,3},{1,2},{2,1},{3,0},{4,7},{5,6},{6,5},{7,4},{8,11},{9,10},{10,... | collective-permute-start | bytes 196616 | tf_op jit(solution)/shard_map/ppermute | solution.py:18
  41.6 3.0 %collective-permute-start.22 = (f32[128,128]{1,0:T(8,128)S(1)}, f32[128,128]{1,0:T(8,128)S(1)}, u32[]{:S(2)}, u32[]{:S(2)}) collective-permute-start(f32[128,128]{1,0:T(8,128)S(1)} %get-tuple-element.47), channel_id=1, source_target_pairs={{0,1},{1,0},{2,3},{3,2},{4,5},{5,4},{6,7},{7,6},{8,9},{9,8},{10,11... | collective-permute-start | bytes 196616 | tf_op jit(solution)/shard_map/ppermute | solution.py:18
  44.6 1.5 %collective-permute-start.19 = (f32[8,128]{1,0:T(8,128)S(1)}, f32[8,128]{1,0:T(8,128)S(1)}, u32[]{:S(2)}, u32[]{:S(2)}) collective-permute-start(f32[8,128]{1,0:T(8,128)S(1)} %add_stat.6.one), channel_id=1, source_target_pairs={{0,8},{4,12},{8,0},{12,4},{1,9},{5,13},{9,1},{13,5},{2,10},{6,14},... | collective-permute-start | bytes 12296 | tf_op jit(solution)/shard_map/ppermute | solution.py:18
  46.1 2.2 %collective-permute-done.19.two = f32[8,128]{1,0:T(8,128)S(1)} collective-permute-done((f32[8,128]{1,0:T(8,128)S(1)}, f32[8,128]{1,0:T(8,128)S(1)}, u32[]{:S(2)}, u32[]{:S(2)}) %collective-permute-start.19) | collective-permute-done | bytes 4128 | tf_op jit(solution)/shard_map/ppermute | solution.py:18
  48.3 2.1 %collective-permute-done.21.refs_2_ = f32[128,128]{1,0:T(8,128)S(1)} collective-permute-done((f32[128,128]{1,0:T(8,128)S(1)}, f32[128,128]{1,0:T(8,128)S(1)}, u32[]{:S(2)}, u32[]{:S(2)}) %collective-permute-start.21) | collective-permute-done | bytes 65568 | tf_op jit(solution)/shard_map/ppermute | solution.py:18
  50.5 2.2 %collective-permute-start.26 = (f32[136,128]{1,0:T(8,128)S(1)}, f32[136,128]{1,0:T(8,128)S(1)}, u32[]{:S(2)}, u32[]{:S(2)}) collective-permute-start(f32[136,128]{1,0:T(8,128)S(1)} %combine.3.refs_0_), channel_id=1, source_target_pairs={{0,3},{1,2},{2,1},{3,0},{4,7},{5,6},{6,5},{7,4},{8,11},{9,10},{10,... | collective-permute-start | bytes 208904 | tf_op jit(solution)/shard_map/ppermute | solution.py:18
  52.7 2.2 %collective-permute-start.24 = (f32[136,128]{1,0:T(8,128)S(1)}, f32[136,128]{1,0:T(8,128)S(1)}, u32[]{:S(2)}, u32[]{:S(2)}) collective-permute-start(f32[136,128]{1,0:T(8,128)S(1)} %combine.3.refs_0_), channel_id=1, source_target_pairs={{0,1},{1,0},{2,3},{3,2},{4,5},{5,4},{6,7},{7,6},{8,9},{9,8},{10,11... | collective-permute-start | bytes 208904 | tf_op jit(solution)/shard_map/ppermute | solution.py:18
  54.9 2.3 %collective-permute-done.26.refs_3_ = f32[136,128]{1,0:T(8,128)S(1)} collective-permute-done((f32[136,128]{1,0:T(8,128)S(1)}, f32[136,128]{1,0:T(8,128)S(1)}, u32[]{:S(2)}, u32[]{:S(2)}) %collective-permute-start.26) | collective-permute-done | bytes 69664 | tf_op jit(solution)/shard_map/ppermute | solution.py:18
  57.2 2.4 %collective-permute-done.25.refs_2_ = f32[136,128]{1,0:T(8,128)S(1)} collective-permute-done((f32[136,128]{1,0:T(8,128)S(1)}, f32[136,128]{1,0:T(8,128)S(1)}, u32[]{:S(2)}, u32[]{:S(2)}) %collective-permute-start.25) | collective-permute-done | bytes 69664 | tf_op jit(solution)/shard_map/ppermute | solution.py:18
  59.6 1.2 %last.1 = (f32[32,2048]{1,0:T(8,128)}, f32[32,2048]{1,0:T(8,128)}) custom-call(f32[32,2048]{1,0:T(8,128)S(1)} %copy-done, f32[32,2048]{1,0:T(8,128)S(1)} %get-tuple-element.36.near.left, f32[8,128]{1,0:T(8,128)S(1)} %get-tuple-element.37.stat.stat_now, f32[136,128]{1,0:T(8,128)S(1)} %combine.3.refs_0_, f32[136,128]{1,0:T(8,128)S(1)} %collective-permute-done.24.refs_1_, ...), custom_call_target="tpu_custom_call" | custom-call | tf_op jit(solution)/shard_map/last/pallas_call | solution.py:387
  (56 shorter events, 6.9 us)
Async XLA Ops:
  0.7 7.2 %collective-permute-start = (f32[32,2048]{1,0:T(8,128)}, f32[32,2048]{1,0:T(8,128)S(1)}, u32[]{:S(2)}, u32[]{:S(2)}) collective-permute-start(f32[32,2048]{1,0:T(8,128)} %right.3), channel_id=1, source_target_pairs={{0,8},{1,5},{2,6},{3,11},{4,0},{5,13},{6,14},{7,3},{8,12},{9,1},{1... | collective-permute-start | bytes 786440 | tf_op jit(solution)/shard_map/ppermute | solution.py:27
  7.9 2.8 %collective-permute-start.1 = (f32[32,2048]{1,0:T(8,128)S(1)}, f32[32,2048]{1,0:T(8,128)S(1)}, u32[]{:S(2)}, u32[]{:S(2)}) collective-permute-start(f32[32,2048]{1,0:T(8,128)S(1)} %pick.1.current), channel_id=1, source_target_pairs={{0,4},{4,0},{8,12},{12,8},{1,5},{5,1},{9,13},{13,9},{2,6},{6,2},{1... | collective-permute-start | bytes 786440 | tf_op jit(solution)/shard_map/ppermute | solution.py:18
  8.0 9.4 %collective-permute-start.4 = (f32[128,128]{1,0:T(8,128)S(1)}, f32[128,128]{1,0:T(8,128)S(1)}, u32[]{:S(2)}, u32[]{:S(2)}) collective-permute-start(f32[128,128]{1,0:T(8,128)S(1)} %get-tuple-element.31), channel_id=1, source_target_pairs={{0,8},{1,9},{2,10},{3,14},{4,12},{5,13},{6,11},{7,15},{8,0},{9,4},... | collective-permute-start | bytes 196616 | tf_op jit(solution)/shard_map/ppermute | solution.py:27
  10.5 11.8 %collective-permute-start.9 = (f32[128,128]{1,0:T(8,128)S(1)}, f32[128,128]{1,0:T(8,128)S(1)}, u32[]{:S(2)}, u32[]{:S(2)}) collective-permute-start(f32[128,128]{1,0:T(8,128)S(1)} %get-tuple-element.27.mark), channel_id=1, source_target_pairs={{0,4},{1,5},{2,8},{3,12},{4,0},{5,1},{6,9},{7,13},{8,2},{9,6},{10,... | collective-permute-start | bytes 196616 | tf_op jit(solution)/shard_map/ppermute | solution.py:27
  12.0 10.3 %collective-permute-start.6 = (f32[128,128]{1,0:T(8,128)S(1)}, f32[128,128]{1,0:T(8,128)S(1)}, u32[]{:S(2)}, u32[]{:S(2)}) collective-permute-start(f32[128,128]{1,0:T(8,128)S(1)} %get-tuple-element.33), channel_id=1, source_target_pairs={{0,3},{1,2},{2,1},{3,0},{4,7},{5,6},{6,5},{7,4},{8,11},{9,10},{10,... | collective-permute-start | bytes 196616 | tf_op jit(solution)/shard_map/ppermute | solution.py:18
  16.8 5.9 %collective-permute-start.7 = (f32[128,128]{1,0:T(8,128)S(1)}, f32[128,128]{1,0:T(8,128)S(1)}, u32[]{:S(2)}, u32[]{:S(2)}) collective-permute-start(f32[128,128]{1,0:T(8,128)S(1)} %get-tuple-element.34), channel_id=1, source_target_pairs={{0,2},{1,3},{2,0},{3,1},{4,6},{5,7},{6,4},{7,5},{8,10},{9,11},{10,... | collective-permute-start | bytes 196616 | tf_op jit(solution)/shard_map/ppermute | solution.py:18
  16.8 5.9 %collective-permute-start.8 = (f32[128,128]{1,0:T(8,128)S(1)}, f32[128,128]{1,0:T(8,128)S(1)}, u32[]{:S(2)}, u32[]{:S(2)}) collective-permute-start(f32[128,128]{1,0:T(8,128)S(1)} %get-tuple-element.35), channel_id=1, source_target_pairs={{0,1},{1,0},{2,3},{3,2},{4,5},{5,4},{6,7},{7,6},{8,9},{9,8},{10,11... | collective-permute-start | bytes 196616 | tf_op jit(solution)/shard_map/ppermute | solution.py:18
  18.6 3.6 %collective-permute-start.5 = (f32[8,128]{1,0:T(8,128)S(1)}, f32[8,128]{1,0:T(8,128)S(1)}, u32[]{:S(2)}, u32[]{:S(2)}) collective-permute-start(f32[8,128]{1,0:T(8,128)S(1)} %add_stat.4.one), channel_id=1, source_target_pairs={{0,8},{4,12},{8,0},{12,4},{1,9},{5,13},{9,1},{13,5},{2,10},{6,14},... | collective-permute-start | bytes 12296 | tf_op jit(solution)/shard_map/ppermute | solution.py:18
  22.8 7.2 %collective-permute-start.12 = (f32[136,128]{1,0:T(8,128)S(1)}, f32[136,128]{1,0:T(8,128)S(1)}, u32[]{:S(2)}, u32[]{:S(2)}) collective-permute-start(f32[136,128]{1,0:T(8,128)S(1)} %combine.2.refs_0_), channel_id=1, source_target_pairs={{0,3},{1,2},{2,1},{3,0},{4,7},{5,6},{6,5},{7,4},{8,11},{9,10},{10,... | collective-permute-start | bytes 208904 | tf_op jit(solution)/shard_map/ppermute | solution.py:18
  26.1 7.1 %collective-permute-start.11 = (f32[136,128]{1,0:T(8,128)S(1)}, f32[136,128]{1,0:T(8,128)S(1)}, u32[]{:S(2)}, u32[]{:S(2)}) collective-permute-start(f32[136,128]{1,0:T(8,128)S(1)} %combine.2.refs_0_), channel_id=1, source_target_pairs={{0,2},{1,3},{2,0},{3,1},{4,6},{5,7},{6,4},{7,5},{8,10},{9,11},{10,... | collective-permute-start | bytes 208904 | tf_op jit(solution)/shard_map/ppermute | solution.py:18
  26.1 7.1 %collective-permute-start.10 = (f32[136,128]{1,0:T(8,128)S(1)}, f32[136,128]{1,0:T(8,128)S(1)}, u32[]{:S(2)}, u32[]{:S(2)}) collective-permute-start(f32[136,128]{1,0:T(8,128)S(1)} %combine.2.refs_0_), channel_id=1, source_target_pairs={{0,1},{1,0},{2,3},{3,2},{4,5},{5,4},{6,7},{7,6},{8,9},{9,8},{10,11... | collective-permute-start | bytes 208904 | tf_op jit(solution)/shard_map/ppermute | solution.py:18
  27.3 7.4 %collective-permute-start.14 = (f32[136,128]{1,0:T(8,128)S(1)}, f32[136,128]{1,0:T(8,128)S(1)}, u32[]{:S(2)}, u32[]{:S(2)}) collective-permute-start(f32[136,128]{1,0:T(8,128)S(1)} %combine.2.refs_0_), channel_id=1, source_target_pairs={{0,8},{1,12},{2,10},{3,11},{4,9},{5,13},{6,14},{7,15},{8,0},{9,1},... | collective-permute-start | bytes 208904 | tf_op jit(solution)/shard_map/ppermute | solution.py:27
  30.0 4.7 %collective-permute-start.13 = (f32[136,128]{1,0:T(8,128)S(1)}, f32[136,128]{1,0:T(8,128)S(1)}, u32[]{:S(2)}, u32[]{:S(2)}) collective-permute-start(f32[136,128]{1,0:T(8,128)S(1)} %combine.2.refs_0_), channel_id=1, source_target_pairs={{0,4},{1,5},{2,8},{3,12},{4,0},{5,1},{6,9},{7,13},{8,2},{9,6},{10,... | collective-permute-start | bytes 208904 | tf_op jit(solution)/shard_map/ppermute | solution.py:27
  34.8 2.8 %collective-permute-start.15 = (f32[16,32,128]{2,1,0:T(8,128)S(1)}, f32[16,32,128]{2,1,0:T(8,128)S(1)}, u32[]{:S(2)}, u32[]{:S(2)}) collective-permute-start(f32[16,32,128]{2,1,0:T(8,128)S(1)} %held.1), channel_id=1, source_target_pairs={{0,4},{4,0},{8,12},{12,8},{1,5},{5,1},{9,13},{13,9},{2,6},{6,2},{1... | collective-permute-start | bytes 786440 | tf_op jit(solution)/shard_map/ppermute | solution.py:18
  36.0 8.6 %collective-permute-start.18 = (f32[128,128]{1,0:T(8,128)S(1)}, f32[128,128]{1,0:T(8,128)S(1)}, u32[]{:S(2)}, u32[]{:S(2)}) collective-permute-start(f32[128,128]{1,0:T(8,128)S(1)} %get-tuple-element.43), channel_id=1, source_target_pairs={{0,8},{1,9},{2,10},{3,14},{4,12},{5,13},{6,11},{7,15},{8,0},{9,4},... | collective-permute-start | bytes 196616 | tf_op jit(solution)/shard_map/ppermute | solution.py:27
  38.9 5.7 %collective-permute-start.17 = (f32[8,128]{1,0:T(8,128)S(1)}, f32[8,128]{1,0:T(8,128)S(1)}, u32[]{:S(2)}, u32[]{:S(2)}) collective-permute-start(f32[8,128]{1,0:T(8,128)S(1)} %get-tuple-element.42.one), channel_id=1, source_target_pairs={{0,4},{4,0},{8,12},{12,8},{1,5},{5,1},{9,13},{13,9},{2,6},{6,2},{1... | collective-permute-start | bytes 12296 | tf_op jit(solution)/shard_map/ppermute | solution.py:18
  40.2 8.1 %collective-permute-start.20 = (f32[128,128]{1,0:T(8,128)S(1)}, f32[128,128]{1,0:T(8,128)S(1)}, u32[]{:S(2)}, u32[]{:S(2)}) collective-permute-start(f32[128,128]{1,0:T(8,128)S(1)} %get-tuple-element.45), channel_id=1, source_target_pairs={{0,3},{1,2},{2,1},{3,0},{4,7},{5,6},{6,5},{7,4},{8,11},{9,10},{10,... | collective-permute-start | bytes 196616 | tf_op jit(solution)/shard_map/ppermute | solution.py:18
  41.6 8.8 %collective-permute-start.21 = (f32[128,128]{1,0:T(8,128)S(1)}, f32[128,128]{1,0:T(8,128)S(1)}, u32[]{:S(2)}, u32[]{:S(2)}) collective-permute-start(f32[128,128]{1,0:T(8,128)S(1)} %get-tuple-element.46), channel_id=1, source_target_pairs={{0,2},{1,3},{2,0},{3,1},{4,6},{5,7},{6,4},{7,5},{8,10},{9,11},{10,... | collective-permute-start | bytes 196616 | tf_op jit(solution)/shard_map/ppermute | solution.py:18
  41.6 8.8 %collective-permute-start.22 = (f32[128,128]{1,0:T(8,128)S(1)}, f32[128,128]{1,0:T(8,128)S(1)}, u32[]{:S(2)}, u32[]{:S(2)}) collective-permute-start(f32[128,128]{1,0:T(8,128)S(1)} %get-tuple-element.47), channel_id=1, source_target_pairs={{0,1},{1,0},{2,3},{3,2},{4,5},{5,4},{6,7},{7,6},{8,9},{9,8},{10,11... | collective-permute-start | bytes 196616 | tf_op jit(solution)/shard_map/ppermute | solution.py:18
  44.6 5.8 %collective-permute-start.23 = (f32[128,128]{1,0:T(8,128)S(1)}, f32[128,128]{1,0:T(8,128)S(1)}, u32[]{:S(2)}, u32[]{:S(2)}) collective-permute-start(f32[128,128]{1,0:T(8,128)S(1)} %get-tuple-element.39.mark), channel_id=1, source_target_pairs={{0,4},{1,5},{2,8},{3,12},{4,0},{5,1},{6,9},{7,13},{8,2},{9,6},{10,... | collective-permute-start | bytes 196616 | tf_op jit(solution)/shard_map/ppermute | solution.py:27
  44.6 3.7 %collective-permute-start.19 = (f32[8,128]{1,0:T(8,128)S(1)}, f32[8,128]{1,0:T(8,128)S(1)}, u32[]{:S(2)}, u32[]{:S(2)}) collective-permute-start(f32[8,128]{1,0:T(8,128)S(1)} %add_stat.6.one), channel_id=1, source_target_pairs={{0,8},{4,12},{8,0},{12,4},{1,9},{5,13},{9,1},{13,5},{2,10},{6,14},... | collective-permute-start | bytes 12296 | tf_op jit(solution)/shard_map/ppermute | solution.py:18
  50.5 6.7 %collective-permute-start.26 = (f32[136,128]{1,0:T(8,128)S(1)}, f32[136,128]{1,0:T(8,128)S(1)}, u32[]{:S(2)}, u32[]{:S(2)}) collective-permute-start(f32[136,128]{1,0:T(8,128)S(1)} %combine.3.refs_0_), channel_id=1, source_target_pairs={{0,3},{1,2},{2,1},{3,0},{4,7},{5,6},{6,5},{7,4},{8,11},{9,10},{10,... | collective-permute-start | bytes 208904 | tf_op jit(solution)/shard_map/ppermute | solution.py:18
  52.7 6.9 %collective-permute-start.25 = (f32[136,128]{1,0:T(8,128)S(1)}, f32[136,128]{1,0:T(8,128)S(1)}, u32[]{:S(2)}, u32[]{:S(2)}) collective-permute-start(f32[136,128]{1,0:T(8,128)S(1)} %combine.3.refs_0_), channel_id=1, source_target_pairs={{0,2},{1,3},{2,0},{3,1},{4,6},{5,7},{6,4},{7,5},{8,10},{9,11},{10,... | collective-permute-start | bytes 208904 | tf_op jit(solution)/shard_map/ppermute | solution.py:18
  52.7 6.9 %collective-permute-start.24 = (f32[136,128]{1,0:T(8,128)S(1)}, f32[136,128]{1,0:T(8,128)S(1)}, u32[]{:S(2)}, u32[]{:S(2)}) collective-permute-start(f32[136,128]{1,0:T(8,128)S(1)} %combine.3.refs_0_), channel_id=1, source_target_pairs={{0,1},{1,0},{2,3},{3,2},{4,5},{5,4},{6,7},{7,6},{8,9},{9,8},{10,11... | collective-permute-start | bytes 208904 | tf_op jit(solution)/shard_map/ppermute | solution.py:18
  (7 other events, 42.1 us)

commit v16 on v14

--- a/solution.py
+++ b/solution.py
@@ -10,6 +10,7 @@
 ITERS = 2
 LANES = 128
 GROUP = 8
+WIDTHS = (16, 8, 4)
 BF16 = jnp.bfloat16
 F32 = jnp.float32
 
@@ -89,7 +90,7 @@
         total[tile * width + part] += value[:, part * LANES:(part + 1) * LANES]
 
 
-def add_blocks(blocks, slot_rows, slot_cols, live, pairs, total, mirror, wide, ready=None):
+def add_blocks(blocks, slot_rows, slot_cols, live, pairs, total, mirror, widths, ready=None):
     read, write, contract = (slot_rows, slot_cols, 0) if mirror else (slot_cols, slot_rows, 1)
 
     def steps(group, base):
@@ -105,11 +106,11 @@
         return body
 
     done = 0
-    if wide > GROUP:
-        count = live // wide
-        lax.fori_loop(0, count, steps(wide, 0), 0)
-        done = count * wide
-    lax.fori_loop(0, (live - done + GROUP - 1) // GROUP, steps(GROUP, done), 0)
+    for group in widths[:-1]:
+        count = (live - done) // group
+        lax.fori_loop(0, count, steps(group, done), 0)
+        done += count * group
+    lax.fori_loop(0, (live - done + widths[-1] - 1) // widths[-1], steps(widths[-1], done), 0)
 
 
 def image_part(parts, me, i, per, rhs):
@@ -173,7 +174,7 @@
         load_pair(pairs, tile, right[:, tile * tile_size:(tile + 1) * tile_size])
     for copy in copies:
         copy.wait()
-    add_blocks(blocks, slot_rows, slot_cols, live, pairs, total, True, GROUP, lambda i: block_copy(i).wait())
+    add_blocks(blocks, slot_rows, slot_cols, live, pairs, total, True, (GROUP,), lambda i: block_copy(i).wait())
 
 
 def mirror_second_kernel(rows_any, cols_any, count, near, blocks, total, *scratch):
@@ -185,7 +186,7 @@
         load_pair(pairs, tile, near[:, tile * tile_size:(tile + 1) * tile_size])
     for copy in copies:
         copy.wait()
-    add_blocks(blocks, slot_rows, slot_cols, count[0, 0], pairs, total, True, 2 * GROUP)
+    add_blocks(blocks, slot_rows, slot_cols, count[0, 0], pairs, total, True, WIDTHS)
 
 
 def finish_direct(total, near, noise, stat, n):
@@ -214,7 +215,7 @@
     total[...] = jnp.zeros_like(total)
     for copy in copies:
         copy.wait()
-    add_blocks(blocks, slot_rows, slot_cols, count[0, 0], pairs, total, False, 2 * GROUP)
+    add_blocks(blocks, slot_rows, slot_cols, count[0, 0], pairs, total, False, WIDTHS)
     finish_direct(total, near, noise, stat, n)
 
 
@@ -235,7 +236,7 @@
     total[...] = jnp.zeros_like(total)
     for copy in copies:
         copy.wait()
-    add_blocks(blocks, slot_rows, slot_cols, count[0, 0], pairs, total, False, 2 * GROUP)
+    add_blocks(blocks, slot_rows, slot_cols, count[0, 0], pairs, total, False, WIDTHS)
     finish_direct(total, near, noise, stat, n)
 
 

time: 60.5 us -> 61.3 us (1.013); the launches traced: 60.1 us -> 61.8 us
  waiting for transfers between devices: 19.6 us -> 16.6 us
  Pallas kernels: 6.94 us -> 9.83 us
  starting transfers between devices: 32 us -> 33.8 us
    pallas_call x18, Pallas kernels: 6.94 us -> 9.83 us  [call(): pl.pallas_call(kernel, in_specs=specs, out_specs=jax.tree.map(lambda _: v...]
    ppermute x20, waiting for transfers between devices: 17.9 us -> 16.1 us  [shifted(): return lax.ppermute(value, axis, [(i, i ^ d) for i in range(n)])]
    ppermute x20, starting transfers between devices: 23.7 us -> 25.2 us  [shifted(): return lax.ppermute(value, axis, [(i, i ^ d) for i in range(n)])]
    ppermute x7, waiting for transfers between devices: 1.78 us -> 0.52 us  [moved(): lax.ppermute(value, ('row', 'col'), [(s, t[0] * n + t[1]) for s, t in pai...]
  transfers between devices with their start and end apart: 27 -> 27, of which waited for: 13 -> 12; matrix products, arithmetic and copies ran while one was open for 0% -> 0% of each run, Pallas kernels for 9% -> 14%
where the time goes in v16:
time: 61.3 us; the launch traced here: 61.8 us
  starting transfers between devices  33.8 us (55%)
  waiting for transfers between devices  16.6 us (27%)
  Pallas kernels  9.83 us (16%)
  between operations  1.5 us (2%)
    ppermute x20, starting transfers between devices, shifted(): return lax.ppermute(value, axis, [(i, i ^ d) for i in range(n)])  25.2 us
    ppermute x20, waiting for transfers between devices, shifted(): return lax.ppermute(value, axis, [(i, i ^ d) for i in range(n)])  16.1 us
    pallas_call x18, Pallas kernels, call(): pl.pallas_call(kernel, in_specs=specs, out_specs=jax.tree.map(lambda _: v...  9.83 us
    ppermute x7, starting transfers between devices, moved(): lax.ppermute(value, ('row', 'col'), [(s, t[0] * n + t[1]) for s, t in pai...  8.61 us
  transfers between devices with their start and end apart: 27, of which 12 were waited for; matrix products, arithmetic and copies ran while one was open for 0% of the time, Pallas kernels for 14%

profile of v16, /device:TPU:0, one launch (start us, length us, event | category | flops | bytes accessed | tf_op | source)
XLA Modules:
  0.0 61.8 jit_solution(12019289631878679683)
XLA Ops:
  0.7 3.0 %collective-permute-start = (f32[32,2048]{1,0:T(8,128)}, f32[32,2048]{1,0:T(8,128)S(1)}, u32[]{:S(2)}, u32[]{:S(2)}) collective-permute-start(f32[32,2048]{1,0:T(8,128)} %right.3), channel_id=1, source_target_pairs={{0,8},{1,5},{2,6},{3,11},{4,0},{5,13},{6,14},{7,3},{8,12},{9,1},{1... | collective-permute-start | bytes 786440 | tf_op jit(solution)/shard_map/ppermute | solution.py:28
  4.3 3.0 %mirror_first.1 = (f32[16,32,128]{2,1,0:T(8,128)S(1)}, bf16[32,256,256]{2,1,0:T(8,128)(2,1)S(1)}) custom-call(s32[1,1,32]{2,1,0:T(1,128)} %rows_any.5, s32[1,1,32]{2,1,0:T(1,128)} %cols_any.5, s32[1,1]{1,0:T(1,128)S(6)} %copy.8.count, f32[32,2048]{1,0:T(8,128)} %right.3, bf16[1,1,32,256,256]{4,3,2,1,0:T(8,128)(2,1)} %cov.1), custom_call_target="tpu_custom_call" | custom-call | flops 268435456 | bytes 4194304 | tf_op jit(solution)/shard_map/mirror_first/pallas_call | solution.py:388
  8.9 1.6 %collective-permute-start.5 = (f32[128,128]{1,0:T(8,128)S(1)}, f32[128,128]{1,0:T(8,128)S(1)}, u32[]{:S(2)}, u32[]{:S(2)}) collective-permute-start(f32[128,128]{1,0:T(8,128)S(1)} %get-tuple-element.31), channel_id=1, source_target_pairs={{0,8},{1,9},{2,10},{3,14},{4,12},{5,13},{6,11},{7,15},{8,0},{9,4},... | collective-permute-start | bytes 196616 | tf_op jit(solution)/shard_map/ppermute | solution.py:28
  10.7 1.8 %direct_first.1 = (f32[16,32,128]{2,1,0:T(8,128)S(1)}, f32[8,128]{1,0:T(8,128)S(1)}, f32[16,32,128]{2,1,0:T(8,128)S(1)}) custom-call(s32[1,1,32]{2,1,0:T(1,128)S(1)} %copy-done.2, s32[1,1,32]{2,1,0:T(1,128)S(1)} %copy-done.3, s32[1,1]{1,0:T(1,128)S(6)} %copy.8.count, f32[1,2048]{1,0:T(1,128)S(1)} %bitcast.1, ...), custom_call_target="tpu_custom_call" | custom-call | flops 268435456 | bytes 4194304 | tf_op jit(solution)/shard_map/direct_first/pallas_call | solution.py:388
  12.6 4.7 %collective-permute-start.7 = (f32[128,128]{1,0:T(8,128)S(1)}, f32[128,128]{1,0:T(8,128)S(1)}, u32[]{:S(2)}, u32[]{:S(2)}) collective-permute-start(f32[128,128]{1,0:T(8,128)S(1)} %get-tuple-element.33), channel_id=1, source_target_pairs={{0,3},{1,2},{2,1},{3,0},{4,7},{5,6},{6,5},{7,4},{8,11},{9,10},{10,... | collective-permute-start | bytes 196616 | tf_op jit(solution)/shard_map/ppermute | solution.py:19
  17.9 3.1 %collective-permute-start.3 = (f32[8,128]{1,0:T(8,128)S(1)}, f32[8,128]{1,0:T(8,128)S(1)}, u32[]{:S(2)}, u32[]{:S(2)}) collective-permute-start(f32[8,128]{1,0:T(8,128)S(1)} %get-tuple-element.30.one), channel_id=1, source_target_pairs={{0,8},{4,12},{8,0},{12,4},{1,9},{5,13},{9,1},{13,5},{2,10},{6,14},... | collective-permute-start | bytes 12296 | tf_op jit(solution)/shard_map/ppermute | solution.py:19
  21.0 1.6 %collective-permute-done.3.two = f32[8,128]{1,0:T(8,128)S(1)} collective-permute-done((f32[8,128]{1,0:T(8,128)S(1)}, f32[8,128]{1,0:T(8,128)S(1)}, u32[]{:S(2)}, u32[]{:S(2)}) %collective-permute-start.3) | collective-permute-done | bytes 4128 | tf_op jit(solution)/shard_map/ppermute | solution.py:19
  22.5 1.2 %collective-permute-done.6.two = f32[8,128]{1,0:T(8,128)S(1)} collective-permute-done((f32[8,128]{1,0:T(8,128)S(1)}, f32[8,128]{1,0:T(8,128)S(1)}, u32[]{:S(2)}, u32[]{:S(2)}) %collective-permute-start.6) | collective-permute-done | bytes 4128 | tf_op jit(solution)/shard_map/ppermute | solution.py:19
  23.8 2.8 %collective-permute-start.12 = (f32[136,128]{1,0:T(8,128)S(1)}, f32[136,128]{1,0:T(8,128)S(1)}, u32[]{:S(2)}, u32[]{:S(2)}) collective-permute-start(f32[136,128]{1,0:T(8,128)S(1)} %combine.2.refs_0_), channel_id=1, source_target_pairs={{0,3},{1,2},{2,1},{3,0},{4,7},{5,6},{6,5},{7,4},{8,11},{9,10},{10,... | collective-permute-start | bytes 208904 | tf_op jit(solution)/shard_map/ppermute | solution.py:19
  26.6 1.7 %collective-permute-start.10 = (f32[136,128]{1,0:T(8,128)S(1)}, f32[136,128]{1,0:T(8,128)S(1)}, u32[]{:S(2)}, u32[]{:S(2)}) collective-permute-start(f32[136,128]{1,0:T(8,128)S(1)} %combine.2.refs_0_), channel_id=1, source_target_pairs={{0,1},{1,0},{2,3},{3,2},{4,5},{5,4},{6,7},{7,6},{8,9},{9,8},{10,11... | collective-permute-start | bytes 208904 | tf_op jit(solution)/shard_map/ppermute | solution.py:19
  28.3 2.1 %collective-permute-start.14 = (f32[136,128]{1,0:T(8,128)S(1)}, f32[136,128]{1,0:T(8,128)S(1)}, u32[]{:S(2)}, u32[]{:S(2)}) collective-permute-start(f32[136,128]{1,0:T(8,128)S(1)} %combine.2.refs_0_), channel_id=1, source_target_pairs={{0,8},{1,12},{2,10},{3,11},{4,9},{5,13},{6,14},{7,15},{8,0},{9,1},... | collective-permute-start | bytes 208904 | tf_op jit(solution)/shard_map/ppermute | solution.py:28
  30.7 3.0 %collective-permute-done.11.refs_2_ = f32[136,128]{1,0:T(8,128)S(1)} collective-permute-done((f32[136,128]{1,0:T(8,128)S(1)}, f32[136,128]{1,0:T(8,128)S(1)}, u32[]{:S(2)}, u32[]{:S(2)}) %collective-permute-start.11) | collective-permute-done | bytes 69664 | tf_op jit(solution)/shard_map/ppermute | solution.py:19
  34.0 1.3 %mirror_second.1.mark.mirror = f32[16,32,128]{2,1,0:T(8,128)S(1)} custom-call(s32[1,1,32]{2,1,0:T(1,128)S(1)} %copy-done.2, s32[1,1,32]{2,1,0:T(1,128)S(1)} %copy-done.3, s32[1,1]{1,0:T(1,128)S(6)} %copy.8.count, f32[32,2048]{1,0:T(8,128)S(1)} %get-tuple-element.36.near.left, bf16[32,256,256]{2,1,0:T(8,128)(2,1)S(1)} %get-tuple-element.25.blocks), custom_call_target="tpu_custom_call" | custom-call | flops 268435456 | bytes 4194304 | tf_op jit(solution)/shard_map/mirror_second/pallas_call | solution.py:388
  36.9 1.8 %collective-permute-start.19 = (f32[128,128]{1,0:T(8,128)S(1)}, f32[128,128]{1,0:T(8,128)S(1)}, u32[]{:S(2)}, u32[]{:S(2)}) collective-permute-start(f32[128,128]{1,0:T(8,128)S(1)} %get-tuple-element.43), channel_id=1, source_target_pairs={{0,8},{1,9},{2,10},{3,14},{4,12},{5,13},{6,11},{7,15},{8,0},{9,4},... | collective-permute-start | bytes 196616 | tf_op jit(solution)/shard_map/ppermute | solution.py:28
  38.7 1.8 %direct_second.1 = (f32[16,32,128]{2,1,0:T(8,128)S(1)}, f32[8,128]{1,0:T(8,128)S(1)}) custom-call(s32[1,1,32]{2,1,0:T(1,128)S(1)} %copy-done.2, s32[1,1,32]{2,1,0:T(1,128)S(1)} %copy-done.3, s32[1,1]{1,0:T(1,128)S(6)} %copy.8.count, f32[1,2048]{1,0:T(1,128)S(1)} %bitcast.3, bf16[32,256,256]{2,1,0:T(8,128)(2,1)S(1)} %get-tuple-element.25.blocks, ...), custom_call_target="tpu_custom_call" | custom-call | flops 268435456 | bytes 4194304 | tf_op jit(solution)/shard_map/direct_second/pallas_call | solution.py:388
  40.6 2.8 %collective-permute-start.17 = (f32[8,128]{1,0:T(8,128)S(1)}, f32[8,128]{1,0:T(8,128)S(1)}, u32[]{:S(2)}, u32[]{:S(2)}) collective-permute-start(f32[8,128]{1,0:T(8,128)S(1)} %get-tuple-element.42.one), channel_id=1, source_target_pairs={{0,8},{4,12},{8,0},{12,4},{1,9},{5,13},{9,1},{13,5},{2,10},{6,14},... | collective-permute-start | bytes 12296 | tf_op jit(solution)/shard_map/ppermute | solution.py:19
  45.3 2.5 %collective-permute-start.23 = (f32[128,128]{1,0:T(8,128)S(1)}, f32[128,128]{1,0:T(8,128)S(1)}, u32[]{:S(2)}, u32[]{:S(2)}) collective-permute-start(f32[128,128]{1,0:T(8,128)S(1)} %get-tuple-element.47), channel_id=1, source_target_pairs={{0,1},{1,0},{2,3},{3,2},{4,5},{5,4},{6,7},{7,6},{8,9},{9,8},{10,11... | collective-permute-start | bytes 196616 | tf_op jit(solution)/shard_map/ppermute | solution.py:19
  49.0 1.2 %collective-permute-done.21.refs_1_ = f32[128,128]{1,0:T(8,128)S(1)} collective-permute-done((f32[128,128]{1,0:T(8,128)S(1)}, f32[128,128]{1,0:T(8,128)S(1)}, u32[]{:S(2)}, u32[]{:S(2)}) %collective-permute-start.21) | collective-permute-done | bytes 65568 | tf_op jit(solution)/shard_map/ppermute | solution.py:19
  50.2 1.7 %collective-permute-done.22.refs_2_ = f32[128,128]{1,0:T(8,128)S(1)} collective-permute-done((f32[128,128]{1,0:T(8,128)S(1)}, f32[128,128]{1,0:T(8,128)S(1)}, u32[]{:S(2)}, u32[]{:S(2)}) %collective-permute-start.22) | collective-permute-done | bytes 65568 | tf_op jit(solution)/shard_map/ppermute | solution.py:19
  52.0 1.6 %collective-permute-start.26 = (f32[136,128]{1,0:T(8,128)S(1)}, f32[136,128]{1,0:T(8,128)S(1)}, u32[]{:S(2)}, u32[]{:S(2)}) collective-permute-start(f32[136,128]{1,0:T(8,128)S(1)} %combine.3.refs_0_), channel_id=1, source_target_pairs={{0,3},{1,2},{2,1},{3,0},{4,7},{5,6},{6,5},{7,4},{8,11},{9,10},{10,... | collective-permute-start | bytes 208904 | tf_op jit(solution)/shard_map/ppermute | solution.py:19
  53.7 2.7 %collective-permute-start.24 = (f32[136,128]{1,0:T(8,128)S(1)}, f32[136,128]{1,0:T(8,128)S(1)}, u32[]{:S(2)}, u32[]{:S(2)}) collective-permute-start(f32[136,128]{1,0:T(8,128)S(1)} %combine.3.refs_0_), channel_id=1, source_target_pairs={{0,1},{1,0},{2,3},{3,2},{4,5},{5,4},{6,7},{7,6},{8,9},{9,8},{10,11... | collective-permute-start | bytes 208904 | tf_op jit(solution)/shard_map/ppermute | solution.py:19
  56.5 2.5 %collective-permute-done.26.refs_3_ = f32[136,128]{1,0:T(8,128)S(1)} collective-permute-done((f32[136,128]{1,0:T(8,128)S(1)}, f32[136,128]{1,0:T(8,128)S(1)}, u32[]{:S(2)}, u32[]{:S(2)}) %collective-permute-start.26) | collective-permute-done | bytes 69664 | tf_op jit(solution)/shard_map/ppermute | solution.py:19
  58.9 1.6 %collective-permute-done.25.refs_2_ = f32[136,128]{1,0:T(8,128)S(1)} collective-permute-done((f32[136,128]{1,0:T(8,128)S(1)}, f32[136,128]{1,0:T(8,128)S(1)}, u32[]{:S(2)}, u32[]{:S(2)}) %collective-permute-start.25) | collective-permute-done | bytes 69664 | tf_op jit(solution)/shard_map/ppermute | solution.py:19
  60.5 1.2 %last.1 = (f32[32,2048]{1,0:T(8,128)}, f32[32,2048]{1,0:T(8,128)}) custom-call(f32[32,2048]{1,0:T(8,128)S(1)} %copy-done, f32[32,2048]{1,0:T(8,128)S(1)} %get-tuple-element.36.near.left, f32[8,128]{1,0:T(8,128)S(1)} %get-tuple-element.37.stat.stat_now, f32[136,128]{1,0:T(8,128)S(1)} %combine.3.refs_0_, f32[136,128]{1,0:T(8,128)S(1)} %collective-permute-done.24.refs_1_, ...), custom_call_target="tpu_custom_call" | custom-call | tf_op jit(solution)/shard_map/last/pallas_call | solution.py:388
  (56 shorter events, 8.3 us)
Async XLA Ops:
  0.7 7.2 %collective-permute-start = (f32[32,2048]{1,0:T(8,128)}, f32[32,2048]{1,0:T(8,128)S(1)}, u32[]{:S(2)}, u32[]{:S(2)}) collective-permute-start(f32[32,2048]{1,0:T(8,128)} %right.3), channel_id=1, source_target_pairs={{0,8},{1,5},{2,6},{3,11},{4,0},{5,13},{6,14},{7,3},{8,12},{9,1},{1... | collective-permute-start | bytes 786440 | tf_op jit(solution)/shard_map/ppermute | solution.py:28
  7.3 1.6 %collective-permute-start.2 = (f32[16,32,128]{2,1,0:T(8,128)S(1)}, f32[16,32,128]{2,1,0:T(8,128)S(1)}, u32[]{:S(2)}, u32[]{:S(2)}) collective-permute-start(f32[16,32,128]{2,1,0:T(8,128)S(1)} %get-tuple-element.26.mark.mirror), channel_id=1, source_target_pairs={{0,4},{4,0},{8,12},{12,8},{1,5},{5,1},{9,13},{13,9},{2,6},{6,2},{1... | collective-permute-start | bytes 786440 | tf_op jit(solution)/shard_map/ppermute | solution.py:19
  7.9 2.8 %collective-permute-start.1 = (f32[32,2048]{1,0:T(8,128)S(1)}, f32[32,2048]{1,0:T(8,128)S(1)}, u32[]{:S(2)}, u32[]{:S(2)}) collective-permute-start(f32[32,2048]{1,0:T(8,128)S(1)} %pick.1.current), channel_id=1, source_target_pairs={{0,4},{4,0},{8,12},{12,8},{1,5},{5,1},{9,13},{13,9},{2,6},{6,2},{1... | collective-permute-start | bytes 786440 | tf_op jit(solution)/shard_map/ppermute | solution.py:19
  8.9 9.0 %collective-permute-start.5 = (f32[128,128]{1,0:T(8,128)S(1)}, f32[128,128]{1,0:T(8,128)S(1)}, u32[]{:S(2)}, u32[]{:S(2)}) collective-permute-start(f32[128,128]{1,0:T(8,128)S(1)} %get-tuple-element.31), channel_id=1, source_target_pairs={{0,8},{1,9},{2,10},{3,14},{4,12},{5,13},{6,11},{7,15},{8,0},{9,4},... | collective-permute-start | bytes 196616 | tf_op jit(solution)/shard_map/ppermute | solution.py:28
  10.5 10.5 %collective-permute-start.4 = (f32[128,128]{1,0:T(8,128)S(1)}, f32[128,128]{1,0:T(8,128)S(1)}, u32[]{:S(2)}, u32[]{:S(2)}) collective-permute-start(f32[128,128]{1,0:T(8,128)S(1)} %get-tuple-element.27.mark), channel_id=1, source_target_pairs={{0,4},{1,5},{2,8},{3,12},{4,0},{5,1},{6,9},{7,13},{8,2},{9,6},{10,... | collective-permute-start | bytes 196616 | tf_op jit(solution)/shard_map/ppermute | solution.py:28
  12.6 11.1 %collective-permute-start.7 = (f32[128,128]{1,0:T(8,128)S(1)}, f32[128,128]{1,0:T(8,128)S(1)}, u32[]{:S(2)}, u32[]{:S(2)}) collective-permute-start(f32[128,128]{1,0:T(8,128)S(1)} %get-tuple-element.33), channel_id=1, source_target_pairs={{0,3},{1,2},{2,1},{3,0},{4,7},{5,6},{6,5},{7,4},{8,11},{9,10},{10,... | collective-permute-start | bytes 196616 | tf_op jit(solution)/shard_map/ppermute | solution.py:19
  17.2 6.5 %collective-permute-start.8 = (f32[128,128]{1,0:T(8,128)S(1)}, f32[128,128]{1,0:T(8,128)S(1)}, u32[]{:S(2)}, u32[]{:S(2)}) collective-permute-start(f32[128,128]{1,0:T(8,128)S(1)} %get-tuple-element.34), channel_id=1, source_target_pairs={{0,2},{1,3},{2,0},{3,1},{4,6},{5,7},{6,4},{7,5},{8,10},{9,11},{10,... | collective-permute-start | bytes 196616 | tf_op jit(solution)/shard_map/ppermute | solution.py:19
  17.3 6.5 %collective-permute-start.9 = (f32[128,128]{1,0:T(8,128)S(1)}, f32[128,128]{1,0:T(8,128)S(1)}, u32[]{:S(2)}, u32[]{:S(2)}) collective-permute-start(f32[128,128]{1,0:T(8,128)S(1)} %get-tuple-element.35), channel_id=1, source_target_pairs={{0,1},{1,0},{2,3},{3,2},{4,5},{5,4},{6,7},{7,6},{8,9},{9,8},{10,11... | collective-permute-start | bytes 196616 | tf_op jit(solution)/shard_map/ppermute | solution.py:19
  17.9 4.6 %collective-permute-start.3 = (f32[8,128]{1,0:T(8,128)S(1)}, f32[8,128]{1,0:T(8,128)S(1)}, u32[]{:S(2)}, u32[]{:S(2)}) collective-permute-start(f32[8,128]{1,0:T(8,128)S(1)} %get-tuple-element.30.one), channel_id=1, source_target_pairs={{0,8},{4,12},{8,0},{12,4},{1,9},{5,13},{9,1},{13,5},{2,10},{6,14},... | collective-permute-start | bytes 12296 | tf_op jit(solution)/shard_map/ppermute | solution.py:19
  23.8 6.9 %collective-permute-start.12 = (f32[136,128]{1,0:T(8,128)S(1)}, f32[136,128]{1,0:T(8,128)S(1)}, u32[]{:S(2)}, u32[]{:S(2)}) collective-permute-start(f32[136,128]{1,0:T(8,128)S(1)} %combine.2.refs_0_), channel_id=1, source_target_pairs={{0,3},{1,2},{2,1},{3,0},{4,7},{5,6},{6,5},{7,4},{8,11},{9,10},{10,... | collective-permute-start | bytes 208904 | tf_op jit(solution)/shard_map/ppermute | solution.py:19
  26.6 7.2 %collective-permute-start.11 = (f32[136,128]{1,0:T(8,128)S(1)}, f32[136,128]{1,0:T(8,128)S(1)}, u32[]{:S(2)}, u32[]{:S(2)}) collective-permute-start(f32[136,128]{1,0:T(8,128)S(1)} %combine.2.refs_0_), channel_id=1, source_target_pairs={{0,2},{1,3},{2,0},{3,1},{4,6},{5,7},{6,4},{7,5},{8,10},{9,11},{10,... | collective-permute-start | bytes 208904 | tf_op jit(solution)/shard_map/ppermute | solution.py:19
  26.6 7.2 %collective-permute-start.10 = (f32[136,128]{1,0:T(8,128)S(1)}, f32[136,128]{1,0:T(8,128)S(1)}, u32[]{:S(2)}, u32[]{:S(2)}) collective-permute-start(f32[136,128]{1,0:T(8,128)S(1)} %combine.2.refs_0_), channel_id=1, source_target_pairs={{0,1},{1,0},{2,3},{3,2},{4,5},{5,4},{6,7},{7,6},{8,9},{9,8},{10,11... | collective-permute-start | bytes 208904 | tf_op jit(solution)/shard_map/ppermute | solution.py:19
  28.3 7.1 %collective-permute-start.14 = (f32[136,128]{1,0:T(8,128)S(1)}, f32[136,128]{1,0:T(8,128)S(1)}, u32[]{:S(2)}, u32[]{:S(2)}) collective-permute-start(f32[136,128]{1,0:T(8,128)S(1)} %combine.2.refs_0_), channel_id=1, source_target_pairs={{0,8},{1,12},{2,10},{3,11},{4,9},{5,13},{6,14},{7,15},{8,0},{9,1},... | collective-permute-start | bytes 208904 | tf_op jit(solution)/shard_map/ppermute | solution.py:28
  30.3 5.1 %collective-permute-start.13 = (f32[136,128]{1,0:T(8,128)S(1)}, f32[136,128]{1,0:T(8,128)S(1)}, u32[]{:S(2)}, u32[]{:S(2)}) collective-permute-start(f32[136,128]{1,0:T(8,128)S(1)} %combine.2.refs_0_), channel_id=1, source_target_pairs={{0,4},{1,5},{2,8},{3,12},{4,0},{5,1},{6,9},{7,13},{8,2},{9,6},{10,... | collective-permute-start | bytes 208904 | tf_op jit(solution)/shard_map/ppermute | solution.py:28
  35.6 3.2 %collective-permute-start.15 = (f32[16,32,128]{2,1,0:T(8,128)S(1)}, f32[16,32,128]{2,1,0:T(8,128)S(1)}, u32[]{:S(2)}, u32[]{:S(2)}) collective-permute-start(f32[16,32,128]{2,1,0:T(8,128)S(1)} %held.1), channel_id=1, source_target_pairs={{0,4},{4,0},{8,12},{12,8},{1,5},{5,1},{9,13},{13,9},{2,6},{6,2},{1... | collective-permute-start | bytes 786440 | tf_op jit(solution)/shard_map/ppermute | solution.py:19
  36.9 10.9 %collective-permute-start.19 = (f32[128,128]{1,0:T(8,128)S(1)}, f32[128,128]{1,0:T(8,128)S(1)}, u32[]{:S(2)}, u32[]{:S(2)}) collective-permute-start(f32[128,128]{1,0:T(8,128)S(1)} %get-tuple-element.43), channel_id=1, source_target_pairs={{0,8},{1,9},{2,10},{3,14},{4,12},{5,13},{6,11},{7,15},{8,0},{9,4},... | collective-permute-start | bytes 196616 | tf_op jit(solution)/shard_map/ppermute | solution.py:28
  38.7 9.1 %collective-permute-start.18 = (f32[128,128]{1,0:T(8,128)S(1)}, f32[128,128]{1,0:T(8,128)S(1)}, u32[]{:S(2)}, u32[]{:S(2)}) collective-permute-start(f32[128,128]{1,0:T(8,128)S(1)} %get-tuple-element.39.mark), channel_id=1, source_target_pairs={{0,4},{1,5},{2,8},{3,12},{4,0},{5,1},{6,9},{7,13},{8,2},{9,6},{10,... | collective-permute-start | bytes 196616 | tf_op jit(solution)/shard_map/ppermute | solution.py:28
  40.6 4.7 %collective-permute-start.17 = (f32[8,128]{1,0:T(8,128)S(1)}, f32[8,128]{1,0:T(8,128)S(1)}, u32[]{:S(2)}, u32[]{:S(2)}) collective-permute-start(f32[8,128]{1,0:T(8,128)S(1)} %get-tuple-element.42.one), channel_id=1, source_target_pairs={{0,8},{4,12},{8,0},{12,4},{1,9},{5,13},{9,1},{13,5},{2,10},{6,14},... | collective-permute-start | bytes 12296 | tf_op jit(solution)/shard_map/ppermute | solution.py:19
  43.4 6.8 %collective-permute-start.21 = (f32[128,128]{1,0:T(8,128)S(1)}, f32[128,128]{1,0:T(8,128)S(1)}, u32[]{:S(2)}, u32[]{:S(2)}) collective-permute-start(f32[128,128]{1,0:T(8,128)S(1)} %get-tuple-element.45), channel_id=1, source_target_pairs={{0,3},{1,2},{2,1},{3,0},{4,7},{5,6},{6,5},{7,4},{8,11},{9,10},{10,... | collective-permute-start | bytes 196616 | tf_op jit(solution)/shard_map/ppermute | solution.py:19
  44.3 7.6 %collective-permute-start.22 = (f32[128,128]{1,0:T(8,128)S(1)}, f32[128,128]{1,0:T(8,128)S(1)}, u32[]{:S(2)}, u32[]{:S(2)}) collective-permute-start(f32[128,128]{1,0:T(8,128)S(1)} %get-tuple-element.46), channel_id=1, source_target_pairs={{0,2},{1,3},{2,0},{3,1},{4,6},{5,7},{6,4},{7,5},{8,10},{9,11},{10,... | collective-permute-start | bytes 196616 | tf_op jit(solution)/shard_map/ppermute | solution.py:19
  45.3 6.7 %collective-permute-start.23 = (f32[128,128]{1,0:T(8,128)S(1)}, f32[128,128]{1,0:T(8,128)S(1)}, u32[]{:S(2)}, u32[]{:S(2)}) collective-permute-start(f32[128,128]{1,0:T(8,128)S(1)} %get-tuple-element.47), channel_id=1, source_target_pairs={{0,1},{1,0},{2,3},{3,2},{4,5},{5,4},{6,7},{7,6},{8,9},{9,8},{10,11... | collective-permute-start | bytes 196616 | tf_op jit(solution)/shard_map/ppermute | solution.py:19
  52.0 6.9 %collective-permute-start.26 = (f32[136,128]{1,0:T(8,128)S(1)}, f32[136,128]{1,0:T(8,128)S(1)}, u32[]{:S(2)}, u32[]{:S(2)}) collective-permute-start(f32[136,128]{1,0:T(8,128)S(1)} %combine.3.refs_0_), channel_id=1, source_target_pairs={{0,3},{1,2},{2,1},{3,0},{4,7},{5,6},{6,5},{7,4},{8,11},{9,10},{10,... | collective-permute-start | bytes 208904 | tf_op jit(solution)/shard_map/ppermute | solution.py:19
  53.6 7.0 %collective-permute-start.25 = (f32[136,128]{1,0:T(8,128)S(1)}, f32[136,128]{1,0:T(8,128)S(1)}, u32[]{:S(2)}, u32[]{:S(2)}) collective-permute-start(f32[136,128]{1,0:T(8,128)S(1)} %combine.3.refs_0_), channel_id=1, source_target_pairs={{0,2},{1,3},{2,0},{3,1},{4,6},{5,7},{6,4},{7,5},{8,10},{9,11},{10,... | collective-permute-start | bytes 208904 | tf_op jit(solution)/shard_map/ppermute | solution.py:19
  53.7 6.8 %collective-permute-start.24 = (f32[136,128]{1,0:T(8,128)S(1)}, f32[136,128]{1,0:T(8,128)S(1)}, u32[]{:S(2)}, u32[]{:S(2)}) collective-permute-start(f32[136,128]{1,0:T(8,128)S(1)} %combine.3.refs_0_), channel_id=1, source_target_pairs={{0,1},{1,0},{2,3},{3,2},{4,5},{5,4},{6,7},{7,6},{8,9},{9,8},{10,11... | collective-permute-start | bytes 208904 | tf_op jit(solution)/shard_map/ppermute | solution.py:19
  (7 other events, 41.3 us)
